TPU v7x, 32 devices: a whole 2x2x4 slice. The times are simulated.
32 devices in a mesh: dp: 8 (over z, y), tensor: 4 (over x, core).
Axes of the slice: x: 2, y: 2, z: 4, core: 2. Of those that a mesh axis runs over, the one named last changes fastest.
Arguments:
- embedded: bfloat16 [18912, 768], P('dp'), may hold values from -6 to 6
- attn_gain: bfloat16 [768], replicated, may hold values from 0.5 to 1.5
- attn_shift: bfloat16 [768], replicated, may hold values from -1 to 1
- qkv_weight: bfloat16 [3, 768, 768], P(None, None, 'tensor'), may hold values from -0.21875 to 0.21875
- qv_bias: bfloat16 [2, 768], P(None, 'tensor'), may hold values from -1 to 1
- out_weight: bfloat16 [768, 768], P('tensor'), may hold values from -1.25 to 1.25
- out_bias: bfloat16 [768], replicated, may hold values from -0.59765625 to 0.59765625
- moe_gain: bfloat16 [768], replicated, may hold values from 0.5 to 1.5
- moe_shift: bfloat16 [768], replicated, may hold values from -1 to 1
- router_weight: bfloat16 [768, 8], replicated, may hold values from -0.15625 to 0.15625
- up_weight: bfloat16 [8, 768, 3072], P(None, None, 'tensor'), may hold values from -0.21875 to 0.21875
- up_bias: bfloat16 [8, 3072], P(None, 'tensor'), may hold values from -0.59765625 to 0.59765625
- down_weight: bfloat16 [8, 3072, 768], P(None, 'tensor'), may hold values from -0.5 to 0.5
- down_bias: bfloat16 [8, 768], replicated, may hold values from -3 to 3
- routes: int32 [18912, 2], P('dp'), may hold values from 0 to 7, all different within a row; in each aligned block of 2364 rows (0 to 2363, 2364 to 4727, ...) at most 768 rows name the same one
- cotangent: bfloat16 [18912, 768], P('dp'), may hold values from -6 to 6
Outputs:
- layer_out: bfloat16 [18912, 768], P('dp')
- grad_embedded: float32 [18912, 768], P('dp')
- grad_attn_gain: float32 [768], replicated
- grad_attn_shift: float32 [768], replicated
- grad_qkv_weight: float32 [3, 768, 768], P(None, 'dp', 'tensor')
- grad_qv_bias: float32 [2, 768], P(None, 'tensor')
- grad_out_weight: float32 [768, 768], P('tensor', 'dp')
- grad_out_bias: float32 [768], replicated
- grad_moe_gain: float32 [768], replicated
- grad_moe_shift: float32 [768], replicated
- grad_router_weight: float32 [768, 8], replicated
- grad_up_weight: float32 [8, 768, 3072], P(None, 'dp', 'tensor')
- grad_up_bias: float32 [8, 3072], P(None, 'tensor')
- grad_down_weight: float32 [8, 3072, 768], P(None, 'tensor', 'dp')
- grad_down_bias: float32 [8, 768], replicated
Inputs may be any that keep to these rules, and one draw needn't show every extreme that they name: `routes`: each token names 2 different experts; among the rows of one device no expert is named more than 768 times, and in every draw some expert is named exactly 768 times among some device's rows.
All inputs are finite; a program needn't handle non-finite values.
Results may differ from a plain program's by a relative error of at most 0.028.
Values may be sent and summed in bfloat16 or wider, within the bound.
No kernel may reach another device: no remote copies, remote signals or barrier semaphores. Data moves between devices by JAX's collectives and lax.ppermute only.
A program may use at most 256 MiB of HBM per device.

v0:
```python
import jax
import jax.numpy as jnp
from jax import lax
from jax.sharding import PartitionSpec as P

TOP = 2
SEQ = 197
HD = 64
CAP = 768


EPSILON = 1e-06
HIGHEST = lax.Precision.HIGHEST


def layer_norm(inputs, gain_vec, shift_vec):
    row_mean = jnp.mean(inputs, axis=-1, keepdims=True)
    centered = inputs - row_mean
    row_var = jnp.mean(centered * centered, axis=-1, keepdims=True)
    return centered * lax.rsqrt(row_var + EPSILON) * gain_vec + shift_vec


def on_device(
    embedded,
    attn_gain,
    attn_shift,
    qkv_weight,
    qv_bias,
    out_weight,
    out_bias,
    moe_gain,
    moe_shift,
    router_weight,
    up_weight,
    up_bias,
    down_weight,
    down_bias,
    routes,
    cotangent,
):
    tok_rows = embedded.shape[0]
    images = tok_rows // SEQ
    head_width = qkv_weight.shape[2]
    heads_here = head_width // HD
    expert_count = up_weight.shape[0]
    score_scale = HD ** (-0.5)
    embedded_f = embedded.astype(jnp.float32)
    attn_norm, attn_norm_back = jax.vjp(
        layer_norm, embedded_f, attn_gain.astype(jnp.float32), attn_shift.astype(jnp.float32)
    )
    normed = attn_norm.astype(jnp.bfloat16)
    bias_rows = jnp.stack([qv_bias[0], jnp.zeros_like(qv_bias[0]), qv_bias[1]]).astype(jnp.float32)
    projected = (
        jnp.einsum("td,cdh->cth", normed, qkv_weight, preferred_element_type=jnp.float32)
        + bias_rows[:, None, :]
    )
    projected = projected.astype(jnp.bfloat16)
    queries, key_rows, value_rows = projected.reshape(3, images, SEQ, heads_here, HD)
    scores = (
        jnp.einsum("bqhd,bkhd->bhqk", queries, key_rows, preferred_element_type=jnp.float32)
        * score_scale
    )
    top_score = jnp.max(scores, axis=-1, keepdims=True)
    log_total = top_score + jnp.log(jnp.sum(jnp.exp(scores - top_score), axis=-1, keepdims=True))
    probs_low = jnp.exp(scores - log_total).astype(jnp.bfloat16)
    mixed_heads = jnp.einsum(
        "bhqk,bkhd->bqhd", probs_low, value_rows, preferred_element_type=jnp.float32
    )
    mixed_low = mixed_heads.astype(jnp.bfloat16).reshape(tok_rows, head_width)
    attn_part = jnp.dot(mixed_low, out_weight, preferred_element_type=jnp.float32)
    attn_total = lax.psum(attn_part.astype(jnp.bfloat16), "tensor").astype(jnp.float32)
    middle = embedded_f + attn_total + out_bias.astype(jnp.float32)
    moe_norm, moe_norm_back = jax.vjp(
        layer_norm, middle, moe_gain.astype(jnp.float32), moe_shift.astype(jnp.float32)
    )
    moe_normed = moe_norm.astype(jnp.bfloat16)
    logits = jnp.dot(moe_normed, router_weight, preferred_element_type=jnp.float32)
    gate_probs = jax.nn.softmax(logits, axis=-1)
    choose = (
        routes[:, :, None] == jnp.arange(expert_count, dtype=jnp.int32)[None, None, :]
    ).astype(jnp.float32)
    mixing = gate_probs * jnp.sum(choose, axis=1)
    picked = jnp.sum(gate_probs[:, None, :] * choose, axis=-1)
    flat_expert = routes.reshape(-1)
    route_hot = choose.reshape(-1, expert_count).astype(jnp.int32)
    before = jnp.cumsum(route_hot, axis=0) - route_hot
    slot_index = jnp.sum(before * route_hot, axis=1)
    target = flat_expert * CAP + slot_index
    route_count = flat_expert.shape[0]
    route_of_slot = (
        jnp.full((expert_count * CAP,), route_count, jnp.int32)
        .at[target]
        .set(jnp.arange(route_count, dtype=jnp.int32))
    )
    token_of_slot = route_of_slot // TOP
    padded = jnp.concatenate(
        [moe_normed, jnp.zeros((1, moe_normed.shape[1]), jnp.bfloat16)], axis=0
    )
    buffers = padded[token_of_slot].reshape(expert_count, CAP, moe_normed.shape[1])
    pre_act = (
        jnp.einsum("ecd,edf->ecf", buffers, up_weight, preferred_element_type=jnp.float32)
        + up_bias.astype(jnp.float32)[:, None, :]
    )
    activated, gelu_back = jax.vjp(jax.nn.gelu, pre_act)
    activated_low = activated.astype(jnp.bfloat16)
    expert_out = jnp.einsum(
        "ecf,efd->ecd", activated_low, down_weight, preferred_element_type=jnp.float32
    )
    route_out = expert_out.reshape(expert_count * CAP, -1)[target].reshape(tok_rows, TOP, -1)
    moe_part = jnp.sum(picked[:, :, None] * route_out, axis=1)
    moe_total = lax.psum(moe_part.astype(jnp.bfloat16), "tensor").astype(jnp.float32)
    down_bias_f = down_bias.astype(jnp.float32)
    layer_out = middle + moe_total + jnp.dot(mixing, down_bias_f, precision=HIGHEST)
    upstream = cotangent.astype(jnp.float32)
    grad_down_bias = jnp.dot(mixing.T, upstream, precision=HIGHEST)
    bias_dot = jnp.dot(cotangent, down_bias.T, preferred_element_type=jnp.float32)
    route_dot_part = jnp.sum(route_out * upstream[:, None, :], axis=-1)
    route_dot = lax.psum(route_dot_part, "tensor")
    grad_picked = route_dot + jnp.sum(bias_dot[:, None, :] * choose, axis=-1)
    grad_gates = jnp.sum(choose * grad_picked[:, :, None], axis=1)
    grad_logits = gate_probs * (
        grad_gates - jnp.sum(gate_probs * grad_gates, axis=-1, keepdims=True)
    )
    grad_logits_low = grad_logits.astype(jnp.bfloat16)
    grad_router = lax.dot_general(
        moe_normed, grad_logits_low, (((0,), (0,)), ((), ())), preferred_element_type=jnp.float32
    )
    router_back = lax.dot_general(
        grad_logits_low, router_weight, (((1,), (1,)), ((), ())), preferred_element_type=jnp.float32
    )
    route_grad = (
        (picked[:, :, None] * upstream[:, None, :]).astype(jnp.bfloat16).reshape(route_count, -1)
    )
    route_grad_pad = jnp.concatenate(
        [route_grad, jnp.zeros((1, route_grad.shape[1]), jnp.bfloat16)], axis=0
    )
    slot_grad = route_grad_pad[route_of_slot].reshape(expert_count, CAP, -1)
    grad_down = jnp.einsum(
        "ecf,ecd->efd", activated_low, slot_grad, preferred_element_type=jnp.float32
    )
    hidden_grad = jnp.einsum(
        "ecd,efd->ecf", slot_grad, down_weight, preferred_element_type=jnp.float32
    )
    pre_grad = gelu_back(hidden_grad)[0].astype(jnp.bfloat16)
    grad_up_bias = jnp.sum(pre_grad, axis=1, dtype=jnp.float32)
    grad_up = jnp.einsum("ecd,ecf->edf", buffers, pre_grad, preferred_element_type=jnp.float32)
    slot_back = jnp.einsum("ecf,edf->ecd", pre_grad, up_weight, preferred_element_type=jnp.float32)
    back_part = jnp.sum(
        slot_back.reshape(expert_count * CAP, -1)[target].reshape(tok_rows, TOP, -1), axis=1
    )
    back_total = lax.psum(back_part.astype(jnp.bfloat16), "tensor").astype(jnp.float32)
    normed2_grad = back_total + router_back
    middle_grad_ln, grad_moe_gain, grad_moe_shift = moe_norm_back(normed2_grad)
    middle_grad = upstream + middle_grad_ln
    attn_grad = middle_grad.astype(jnp.bfloat16)
    grad_out_bias = jnp.sum(attn_grad, axis=0, dtype=jnp.float32)
    grad_out = lax.dot_general(
        mixed_low, attn_grad, (((0,), (0,)), ((), ())), preferred_element_type=jnp.float32
    )
    mixed_grad = lax.dot_general(
        attn_grad, out_weight, (((1,), (1,)), ((), ())), preferred_element_type=jnp.float32
    )
    mixed_grad = mixed_grad.astype(jnp.bfloat16).reshape(images, SEQ, heads_here, HD)
    scores_again = (
        jnp.einsum("bqhd,bkhd->bhqk", queries, key_rows, preferred_element_type=jnp.float32)
        * score_scale
    )
    attn_probs = jnp.exp(scores_again - log_total)
    probs_again = attn_probs.astype(jnp.bfloat16)
    grad_values = jnp.einsum(
        "bhqk,bqhd->bkhd", probs_again, mixed_grad, preferred_element_type=jnp.float32
    )
    grad_probs = jnp.einsum(
        "bqhd,bkhd->bhqk", mixed_grad, value_rows, preferred_element_type=jnp.float32
    )
    row_dot = jnp.sum(attn_probs * grad_probs, axis=-1, keepdims=True)
    grad_scores = (attn_probs * (grad_probs - row_dot)).astype(jnp.bfloat16)
    grad_queries = (
        jnp.einsum("bhqk,bkhd->bqhd", grad_scores, key_rows, preferred_element_type=jnp.float32)
        * score_scale
    )
    grad_keys = (
        jnp.einsum("bhqk,bqhd->bkhd", grad_scores, queries, preferred_element_type=jnp.float32)
        * score_scale
    )
    grad_proj = (
        jnp.stack([grad_queries, grad_keys, grad_values])
        .astype(jnp.bfloat16)
        .reshape(3, tok_rows, head_width)
    )
    grad_qkv = jnp.einsum("td,cth->cdh", normed, grad_proj, preferred_element_type=jnp.float32)
    grad_qv_bias = jnp.sum(jnp.stack([grad_proj[0], grad_proj[2]]), axis=1, dtype=jnp.float32)
    normed_back = jnp.einsum(
        "cth,cdh->td", grad_proj, qkv_weight, preferred_element_type=jnp.float32
    )
    normed_grad = lax.psum(normed_back.astype(jnp.bfloat16), "tensor").astype(jnp.float32)
    embed_grad_ln, grad_attn_gain, grad_attn_shift = attn_norm_back(normed_grad)
    grad_embedded = middle_grad + embed_grad_ln
    smalls = lax.psum(
        (
            grad_attn_gain,
            grad_attn_shift,
            grad_qv_bias,
            grad_out_bias,
            grad_moe_gain,
            grad_moe_shift,
            grad_router,
            grad_up_bias,
            grad_down_bias,
        ),
        "dp",
    )
    grad_qkv, grad_out, grad_up, grad_down = (
        lax.psum_scatter(grad_qkv, "dp", scatter_dimension=1, tiled=True),
        lax.psum_scatter(grad_out, "dp", scatter_dimension=1, tiled=True),
        lax.psum_scatter(grad_up, "dp", scatter_dimension=1, tiled=True),
        lax.psum_scatter(grad_down, "dp", scatter_dimension=2, tiled=True),
    )
    return (
        layer_out.astype(jnp.bfloat16),
        grad_embedded,
        smalls[0],
        smalls[1],
        grad_qkv,
        smalls[2],
        grad_out,
        smalls[3],
        smalls[4],
        smalls[5],
        smalls[6],
        grad_up,
        smalls[7],
        grad_down,
        smalls[8],
    )


def solution(mesh):
    return jax.shard_map(
        on_device,
        mesh=mesh,
        in_specs=(
            P("dp", None),
            P(),
            P(),
            P(None, None, "tensor"),
            P(None, "tensor"),
            P("tensor", None),
            P(),
            P(),
            P(),
            P(),
            P(None, None, "tensor"),
            P(None, "tensor"),
            P(None, "tensor", None),
            P(),
            P("dp", None),
            P("dp", None),
        ),
        out_specs=(
            P("dp", None),
            P("dp", None),
            P(),
            P(),
            P(None, "dp", "tensor"),
            P(None, "tensor"),
            P("tensor", "dp"),
            P(),
            P(),
            P(),
            P(),
            P(None, "dp", "tensor"),
            P(None, "tensor"),
            P(None, "tensor", "dp"),
            P(),
        ),
        check_vma=False,
    )
```

profile of v0, /device:TPU:0, one launch (start us, length us, event | category | flops | bytes accessed | tf_op | source)
XLA Modules:
  0.0 1571.9 jit_solution(3117372554019732186)
XLA Ops:
  20.2 5.5 unstack.21
  25.7 4.4 unstack.23
  33.8 5.1 multiply_reduce_fusion.6
  45.2 4.2 convolution_convert_fusion
  54.9 5.8 convert_element_type.155
  60.6 15.1 mul.286
  75.8 18.0 %mul.287 = f32[4728,768]{1,0:T(8,128)} reshape(f32[2364,2,768]{2,1,0:T(2,128)} %mul.286) | data formatting | bytes 29048832 | tf_op jit(solution)/shard_map/mul | solution.py:132
  93.9 22.9 %scatter_custom_fusion = s32[6144]{0:T(1024)S(1)} fusion(s32[4728]{0:T(1024)S(1)} %fusion.56, s32[4728]{0:T(1024)S(1)} %iota.9, s32[]{:T(128)} %constant.55.clone.1), kind=kCustom, calls=%fused_computation.127 | custom fusion | bytes 24580 | tf_op jit(solution)/shard_map/scatter | solution.py:93
  120.6 8.1 all-reduce.10.cloned.1.call-done
  128.7 4.6 fusion.20
  144.4 8.9 multiply_convert_fusion.1
  153.3 6.5 concatenate.13
  159.8 30.7 %gather_fusion = bf16[6144,768]{1,0:T(8,128)(2,1)} fusion(bf16[2365,768]{1,0:T(8,128)(2,1)} %concatenate.12, s32[6144]{0:T(1024)S(1)} %get-tuple-element.139), kind=kCustom, calls=%fused_computation | custom fusion | bytes 18898944 | tf_op jit(solution)/shard_map/gather | solution.py:99
  190.5 32.2 %gather_fusion.2 = bf16[6144,768]{1,0:T(8,128)(2,1)} fusion(bf16[4729,768]{1,0:T(8,128)(2,1)} %concatenate.13, s32[6144]{0:T(1024)S(1)} %get-tuple-element.138), kind=kCustom, calls=%fused_computation.2 | custom fusion | bytes 18898944 | tf_op jit(solution)/shard_map/gather | solution.py:137
  222.7 16.4 %fusion.74 = f32[8,768,768]{2,1,0:T(8,128)} fusion(bf16[8,768,768]{2,1,0:T(8,128)(2,1)} %bitcast.102, bf16[8,768,768]{2,1,0:T(8,128)(2,1)} %param.26), kind=kOutput, calls=%fused_computation.149 | convolution fusion | flops 7247757312 | bytes 37748736 | tf_op jit(solution)/shard_map/ecd,edf->ecf/dot_general | solution.py:101
  239.1 19.2 %fusion.67 = f32[8,768,768]{2,1,0:T(8,128)} fusion(bf16[8,768,768]{2,1,0:T(8,128)(2,1)} %param.28, f32[8,768,768]{2,1,0:T(8,128)} %fusion.74, f32[8,768]{1,0:T(8,128)S(1)} %convert_element_type.149), kind=kOutput, calls=%fused_computation.144 | convolution fusion | flops 7294943232 | bytes 47210496 | tf_op jit(solution)/shard_map/ecf,efd->ecd/dot_general | solution.py:106
  258.3 27.3 %convert_reduce_fusion = (f32[8,768]{1,0:T(8,128)}, bf16[8,768,768]{2,1,0:T(8,128)(2,1)}) fusion(f32[8,768,768]{2,1,0:T(8,128)} %fusion.74, f32[8,768]{1,0:T(8,128)S(1)} %convert_element_type.149, bf16[8,768,768]{2,1,0:T(8,128)(2,1)} %bitcast.100, bf16[8,768,768]{2,1,0:T(8,128)(2,1)} %param.28), kind=kOutput, calls=%fused_computation.14 | convolution fusion | flops 7356278784 | bytes 47235072 | tf_op jit(solution)/shard_map/ecd,efd->ecf/dot_general | solution.py:141
  285.7 16.8 %fusion.75 = f32[8,768,768]{2,1,0:T(8,128)} fusion(bf16[8,768,768]{2,1,0:T(8,128)(2,1)} %get-tuple-element.130, bf16[8,768,768]{2,1,0:T(8,128)(2,1)} %param.26), kind=kOutput, calls=%fused_computation.150 | convolution fusion | flops 7247757312 | bytes 37748736 | tf_op jit(solution)/shard_map/ecf,edf->ecd/dot_general | solution.py:147
  302.4 24.7 %gather_fusion.3 = f32[4728,768]{1,0:T(8,128)} fusion(f32[6144,768]{1,0:T(8,128)} %bitcast.96, s32[5120]{0:T(1024)S(1)} %copy-done.41), kind=kCustom, calls=%fused_computation.3 | custom fusion | bytes 29067744 | tf_op jit(solution)/shard_map/gather | solution.py:149
  327.1 17.2 %reshape.241 = f32[2364,2,768]{2,1,0:T(2,128)} reshape(f32[4728,768]{1,0:T(8,128)} %gather_fusion.3) | data formatting | bytes 29048832 | tf_op jit(solution)/shard_map/reshape | solution.py:149
  344.4 61.4 %reduce_sum.288 = bf16[2364,768]{1,0:T(8,128)(2,1)} reduce(f32[2364,2,768]{2,1,0:T(2,128)} %reshape.241, f32[]{:T(128)} %constant.22.clone.1), dimensions={1}, to_apply=%region_17.18 | reduce | flops 1815552 | bytes 18155524 | tf_op jit(solution)/shard_map/reduce_sum | solution.py:148
  405.8 25.3 %gather_fusion.1 = f32[4728,768]{1,0:T(8,128)} fusion(f32[6144,768]{1,0:T(8,128)} %bitcast.95, s32[5120]{0:T(1024)S(1)} %copy-done.41), kind=kCustom, calls=%fused_computation.1 | custom fusion | bytes 29067744 | tf_op jit(solution)/shard_map/gather | solution.py:109
  431.1 17.5 %reshape.238 = f32[2364,2,768]{2,1,0:T(2,128)} reshape(f32[4728,768]{1,0:T(8,128)} %gather_fusion.1) | data formatting | bytes 29048832 | tf_op jit(solution)/shard_map/reshape | solution.py:109
  448.7 36.5 %multiply_reduce_fusion = (f32[2364,2]{1,0:T(8,128)S(1)}, bf16[2364,768]{1,0:T(8,128)(2,1)}) fusion(f32[2364,2,768]{2,1,0:T(2,128)} %reshape.238, f32[2364,768]{1,0:T(8,128)} %convert_element_type.155, f32[2364,2]{1,0:T(8,128)S(1)} %copy-done.15), kind=kLoop, calls=%fused_computation.16 | loop fusion | flops 12704136 | bytes 25455552 | tf_op jit(solution)/shard_map/reduce_sum | solution.py:117
  485.6 10.5 psum.101
  496.4 10.1 multiply_reduce_fusion.3
  506.6 10.8 fusion.70
  517.4 4.6 convert_reduce_fusion.3
  525.2 4.5 reshape.242
  529.6 5.4 fusion.33
  535.1 5.8 multiply_reduce_fusion.2
  564.7 4.9 bitcast_convert_fusion
  569.7 4.8 convolution_bitcast_fusion
  574.6 7.7 fusion.27
  582.3 4.4 copy.180
  586.7 4.7 reshape.289
  600.0 105.6 %all-reduce.16.cloned.1.call-done = (bf16[2364,768]{1,0:T(8,128)(2,1)}, bf16[2364,768]{1,0:T(8,128)(2,1)}) async-done(((bf16[2364,768]{1,0:T(8,128)(2,1)}, bf16[2364,768]{1,0:T(8,128)(2,1)}), (bf16[2364,768]{1,0:T(8,128)(2,1)}, bf16[2364,768]{1,0:T(8,128)(2,1)})) %all-reduce.16.cloned.1.call-update) | async-done | bytes 7262224 | tf_op jit(solution)/shard_map/psum | solution.py:111
  705.5 6.3 convert_reduce_fusion.1
  711.9 4.6 fusion.18
  716.5 16.6 %fusion.78 = f32[8,768,768]{2,1,0:T(8,128)} fusion(bf16[8,768,768]{2,1,0:T(8,128)(2,1)} %bitcast.103, bf16[8,768,768]{2,1,0:T(8,128)(2,1)} %get-tuple-element.130), kind=kOutput, calls=%fused_computation.153 | convolution fusion | flops 7247757312 | bytes 37748736 | tf_op jit(solution)/shard_map/ecd,ecf->edf/dot_general | solution.py:146
  733.8 22.7 %fusion.66 = f32[8,768,768]{1,2,0:T(8,128)} fusion(bf16[8,768,768]{2,1,0:T(8,128)(2,1)} %bitcast.101, f32[8,768,768]{2,1,0:T(8,128)} %fusion.74, f32[8,768]{1,0:T(8,128)S(1)} %copy-done.62), kind=kOutput, calls=%fused_computation.143 | convolution fusion | flops 7294943232 | bytes 47210496 | tf_op jit(solution)/shard_map/ecf,ecd->efd/dot_general | solution.py:138
  756.5 15.2 reduce-scatter.15.cloned.1.call-done
  773.4 67.5 %reduce-scatter.13.cloned.1.call-done = f32[96,576]{1,0:T(8,128)} async-done(((f32[768,576]{1,0:T(8,128)}), f32[96,576]{1,0:T(8,128)}) %reduce-scatter.13.cloned.1.call-update) | async-done | bytes 221200
  842.9 10.4 add_convert_fusion
  853.3 8.2 add_add_fusion.2
  861.5 56.6 %all-reduce.14.cloned.1.call-done = (f32[768]{0:T(1024)}, f32[768]{0:T(1024)}, f32[2,192]{1,0:T(2,128)}, f32[768]{0:T(1024)}, f32[768]{0:T(1024)}, /*index=5*/f3...) async-done(((f32[768]{0:T(1024)}, f32[768]{0:T(1024)}, f32[2,192]{1,0:T(2,128)}, f32[768]{0:T(1024)}, f32[768]{0:T(1024)}, /*index=5*/f32[768]{0:T(1024)}, ...) | async-done | bytes 90640 | tf_op jit(solution)/shard_map/psum | solution.py:199
  918.2 317.6 %reduce-scatter.9.cloned.1.call-done = f32[8,96,768]{2,1,0:T(8,128)} async-done(((f32[8,768,768]{2,1,0:T(8,128)}), f32[8,96,768]{2,1,0:T(8,128)}) %reduce-scatter.9.cloned.1.call-update) | async-done | bytes 2359312 | tf_op jit(solution)/shard_map/reduce_scatter | solution.py:216
  1235.8 317.4 %reduce-scatter.11.cloned.1.call-done = f32[8,768,96]{1,2,0:T(8,128)} async-done(((f32[8,768,768]{1,2,0:T(8,128)}), f32[8,768,96]{1,2,0:T(8,128)}) %reduce-scatter.11.cloned.1.call-update) | async-done | bytes 2359312 | tf_op jit(solution)/shard_map/reduce_scatter | solution.py:217
  (251 shorter events, 95.3 us)
Async XLA Ops:
  7.2 8.8 copy-start
  7.2 121.5 %all-reduce.10.cloned.1.call-start = ((), (), s32[]{:S(2)}) async-start(), calls=%async_computation.4 | async-start | bytes 7274496 | tf_op jit(solution)/shard_map/psum | solution.py:71
  7.2 8.7 copy-start.1
  9.3 9.4 copy-start.55
  9.9 8.7 copy-start.65
  33.7 6.6 copy-start.16
  42.9 6.5 copy-start.67
  43.0 6.5 copy-start.68
  43.0 6.5 copy-start.69
  43.0 6.6 copy-start.63
  43.0 6.6 copy-start.30
  49.4 446.9 %all-reduce.12.cloned.1.call-start = ((), (), s32[]{:S(2)}) async-start(), calls=%async_computation.5 | async-start | bytes 7274496 | tf_op jit(solution)/shard_map/psum | solution.py:151
  49.5 86.3 %copy-start.44 = (f32[768]{0:T(1024)}, f32[768]{0:T(1024)S(1)}, u32[]{:S(2)}) copy-start(f32[768]{0:T(1024)S(1)} %convert_element_type.141) | copy-start | bytes 9220
  49.5 86.3 %copy-start.59 = (f32[768]{0:T(1024)}, f32[768]{0:T(1024)S(1)}, u32[]{:S(2)}) copy-start(f32[768]{0:T(1024)S(1)} %convert_element_type.142) | copy-start | bytes 9220
  49.6 208.7 %copy-start.61 = (f32[8,768]{1,0:T(8,128)}, f32[8,768]{1,0:T(8,128)S(1)}, u32[]{:S(2)}) copy-start(f32[8,768]{1,0:T(8,128)S(1)} %convert_element_type.149) | copy-start | bytes 73732
  75.8 41.7 %copy-start.57 = (bf16[8,768]{1,0:T(8,128)(2,1)S(1)}, bf16[8,768]{1,0:T(8,128)(2,1)}, u32[]{:S(2)}) copy-start(bf16[8,768]{1,0:T(8,128)(2,1)} %param.29) | copy-start | bytes 36868
  143.9 9.4 copy-start.14
  285.7 16.8 %copy-start.41 = (s32[5120]{0:T(1024)S(1)}, s32[5120]{0:T(1024)}, u32[]{:S(2)}) copy-start(s32[5120]{0:T(1024)} %pad_clamp_fusion) | copy-start | bytes 61444
  405.8 299.8 %all-reduce.16.cloned.1.call-start = ((), (), s32[]{:S(2)}) async-start(), calls=%async_computation.11 | async-start | bytes 14548992 | tf_op jit(solution)/shard_map/psum | solution.py:111
  431.1 17.5 %copy-start.15 = (f32[2364,2]{1,0:T(8,128)S(1)}, f32[2364,2]{1,0:T(8,128)}, u32[]{:S(2)}) copy-start(f32[2364,2]{1,0:T(8,128)} %copy-done.14) | copy-start | bytes 56740
  448.7 47.5 %copy-start.54 = (f32[2364,2]{0,1:T(2,128)S(1)}, f32[2364,2]{0,1:T(2,128)}, u32[]{:S(2)}) copy-start(f32[2364,2]{0,1:T(2,128)} %get-tuple-element.116) | copy-start | bytes 56740
  448.7 47.5 %copy-start.31 = (s32[2364,2]{0,1:T(2,128)S(1)}, s32[2364,2]{0,1:T(2,128)}, u32[]{:S(2)}) copy-start(s32[2364,2]{0,1:T(2,128)} %param.30) | copy-start | bytes 56740
  448.7 47.5 %copy-start.24 = (f32[2364,8]{0,1:T(8,128)S(1)}, f32[2364,8]{0,1:T(8,128)}, u32[]{:S(2)}) copy-start(f32[2364,8]{0,1:T(8,128)} %copy-done.23) | copy-start | bytes 226948
  448.7 47.5 %copy-start.35 = (f32[2364]{0:T(1024)S(1)}, f32[2364]{0:T(1024)}, u32[]{:S(2)}) copy-start(f32[2364]{0:T(1024)} %copy-done.34) | copy-start | bytes 28372
  448.7 47.5 %copy-start.38 = (f32[2364]{0:T(1024)S(1)}, f32[2364]{0:T(1024)}, u32[]{:S(2)}) copy-start(f32[2364]{0:T(1024)} %copy-done.37) | copy-start | bytes 28372
  448.7 47.7 %copy-start.40 = (f32[2364]{0:T(1024)S(1)}, f32[2364]{0:T(1024)}, u32[]{:S(2)}) copy-start(f32[2364]{0:T(1024)} %copy-done.39) | copy-start | bytes 28372
  448.7 47.7 %copy-start.45 = (f32[768]{0:T(1024)S(1)}, f32[768]{0:T(1024)}, u32[]{:S(2)}) copy-start(f32[768]{0:T(1024)} %copy-done.44) | copy-start | bytes 9220
  448.7 47.7 %copy-start.49 = (f32[2364]{0:T(1024)S(1)}, f32[2364]{0:T(1024)}, u32[]{:S(2)}) copy-start(f32[2364]{0:T(1024)} %copy-done.48) | copy-start | bytes 28372
  448.7 47.7 %copy-start.60 = (f32[768]{0:T(1024)S(1)}, f32[768]{0:T(1024)}, u32[]{:S(2)}) copy-start(f32[768]{0:T(1024)} %copy-done.59) | copy-start | bytes 9220
  496.3 10.2 copy-start.42
  496.3 10.2 copy-start.53
  496.4 10.2 copy-start.3
  506.6 10.8 copy-start.8
  522.0 7.7 copy-start.28
  525.2 9.9 copy-start.17
  529.6 11.3 slice-start
  569.7 202.1 %reduce-scatter.15.cloned.1.call-start = ((), (), s32[]{:S(2)}) async-start(), calls=%async_computation.9 | async-start | bytes 884736
  574.6 266.4 %reduce-scatter.13.cloned.1.call-start = ((), (), s32[]{:S(2)}) async-start(), calls=%async_computation.8 | async-start | bytes 2211840
  582.3 9.3 copy-start.43
  582.3 12.5 copy-start.26
  591.4 326.8 %all-reduce.14.cloned.1.call-start = ((), (), s32[]{:S(2)}) async-start(), calls=%async_computation.10 | async-start | bytes 192512 | tf_op jit(solution)/shard_map/psum | solution.py:199
  594.9 116.9 %copy-start.51 = (f32[2364]{0:T(1024)S(1)}, f32[2364]{0:T(1024)}, u32[]{:S(2)}) copy-start(f32[2364]{0:T(1024)} %copy-done.50) | copy-start | bytes 28372
  716.5 519.3 %reduce-scatter.9.cloned.1.call-start = ((), (), s32[]{:S(2)}) async-start(), calls=%async_computation.6 | async-start | bytes 21233664 | tf_op jit(solution)/shard_map/reduce_scatter | solution.py:216
  733.1 820.1 %reduce-scatter.11.cloned.1.call-start = ((), (), s32[]{:S(2)}) async-start(), calls=%async_computation.7 | async-start | bytes 21233664 | tf_op jit(solution)/shard_map/reduce_scatter | solution.py:217
  756.5 86.3 %copy-start.58 = (bf16[8,768]{1,0:T(8,128)(2,1)S(1)}, bf16[8,768]{1,0:T(8,128)(2,1)}, u32[]{:S(2)}) copy-start(bf16[8,768]{1,0:T(8,128)(2,1)} %param.29) | copy-start | bytes 36868
  842.9 10.4 copy-start.5
  842.9 10.4 copy-start.9
  842.9 10.4 copy-start.13
  (32 other events, 129.1 us)
Sparse Core Ops, SparseCore 0:
  49.5 79.0 all-reduce.9
  405.9 76.5 all-reduce.11
  569.8 135.6 all-reduce.15
  709.0 62.7 reduce-scatter.14
  775.1 65.8 reduce-scatter.12
  847.2 70.9 all-reduce.13
  923.1 312.6 reduce-scatter.8
  1240.7 312.4 reduce-scatter.10
where the time goes:
time: 1580 us; the launch traced here: 1570 us
  waiting for transfers between devices  888 us (56%)
  local copies, waits for them, and re-layouts  285 us (18%)
  matrix products  199 us (13%)
  other arithmetic  173 us (11%)
    reduce_scatter x1, waiting for transfers between devices, on_device(): lax.psum_scatter(grad_up, 'dp', scatter_dimension=1, tiled=True)  318 us
    reduce_scatter x1, waiting for transfers between devices, on_device(): lax.psum_scatter(grad_down, 'dp', scatter_dimension=2, tiled=True)  317 us
    psum x1, waiting for transfers between devices, on_device(): lax.psum(moe_part.astype(jnp.bfloat16), 'tensor').astype(jnp.float32)  106 us
    unnamed x10, waiting for transfers between devices  82.9 us
    reduce_sum x1, other arithmetic, on_device(): jnp.sum(slot_back.reshape(expert_count * CAP, -1)[target].reshape(tok_row...  61.4 us
    psum x1, waiting for transfers between devices, on_device(): lax.psum((grad_attn_gain, grad_attn_shift, grad_qv_bias, grad_out_bias, g...  56.6 us
    reduce_sum x1, other arithmetic, on_device(): route_dot_part = jnp.sum(route_out * upstream[:, None, :], axis=-1)  36.5 us
    mul x2, local copies, waits for them, and re-layouts, on_device(): picked[:, :, None] * upstream[:, None, :]  33.1 us
  transfers between devices with their start and end apart: 8, of which 7 were waited for; matrix products, arithmetic and copies ran while one was open for 16% of the time, Pallas kernels for 0%

commit v1 on v0

--- a/solution.py
+++ b/solution.py
@@ -18,6 +18,64 @@
     centered = inputs - row_mean
     row_var = jnp.mean(centered * centered, axis=-1, keepdims=True)
     return centered * lax.rsqrt(row_var + EPSILON) * gain_vec + shift_vec
+
+
+RING = (0, 2, 4, 6, 7, 5, 3, 1)
+
+
+def pairs(count, bit):
+    return [(i, i ^ bit) for i in range(count)]
+
+
+def tensor_sum(part):
+    if lax.axis_size("tensor") != 4:
+        return lax.psum(part, "tensor").astype(jnp.float32)
+    rows, cols = part.shape
+    half = cols // 2
+    core = lax.axis_index("tensor") % 2
+    theirs = lax.dynamic_slice(part, (0, (1 - core) * half), (rows, half))
+    mine = lax.dynamic_slice(part, (0, core * half), (rows, half))
+    got = lax.ppermute(theirs, "tensor", pairs(4, 1))
+    both = (mine.astype(jnp.float32) + got.astype(jnp.float32)).astype(jnp.bfloat16)
+    far = lax.ppermute(both, "tensor", pairs(4, 2))
+    total = (both.astype(jnp.float32) + far.astype(jnp.float32)).astype(jnp.bfloat16)
+    other = lax.ppermute(total, "tensor", pairs(4, 1))
+    low = jnp.where(core == 0, total, other)
+    high = jnp.where(core == 0, other, total)
+    return jnp.concatenate([low, high], axis=1).astype(jnp.float32)
+
+
+def small_sum(values, axis):
+    count = lax.axis_size(axis)
+    if count not in (4, 8):
+        return lax.psum(values, axis)
+    bit = 1
+    while bit < count:
+        values = values + lax.ppermute(values, axis, pairs(count, bit))
+        bit *= 2
+    return values
+
+
+def ring_scatter(values, way):
+    count = lax.axis_size("dp")
+    if count != 8:
+        return lax.psum_scatter(values, "dp", scatter_dimension=1, tiled=True).astype(jnp.float32)
+    chunk = values.shape[1] // count
+    order = jnp.array(RING, jnp.int32)
+    place = jnp.array([RING.index(i) for i in range(count)], jnp.int32)[lax.axis_index("dp")]
+    path = [(RING[i], RING[(i + way) % count]) for i in range(count)]
+
+    def local(step):
+        owner = order[(place - way * (step + 1)) % count]
+        start = (0, owner * chunk, 0)
+        return lax.dynamic_slice(values, start, (values.shape[0], chunk, values.shape[2]))
+
+    moving = local(0)
+    for step in range(1, count):
+        got = lax.ppermute(moving, "dp", path)
+        total = got.astype(jnp.float32) + local(step).astype(jnp.float32)
+        moving = total.astype(jnp.bfloat16) if step < count - 1 else total
+    return moving
 
 
 def on_device(
@@ -68,7 +126,7 @@
     )
     mixed_low = mixed_heads.astype(jnp.bfloat16).reshape(tok_rows, head_width)
     attn_part = jnp.dot(mixed_low, out_weight, preferred_element_type=jnp.float32)
-    attn_total = lax.psum(attn_part.astype(jnp.bfloat16), "tensor").astype(jnp.float32)
+    attn_total = tensor_sum(attn_part.astype(jnp.bfloat16))
     middle = embedded_f + attn_total + out_bias.astype(jnp.float32)
     moe_norm, moe_norm_back = jax.vjp(
         layer_norm, middle, moe_gain.astype(jnp.float32), moe_shift.astype(jnp.float32)
@@ -108,14 +166,14 @@
     )
     route_out = expert_out.reshape(expert_count * CAP, -1)[target].reshape(tok_rows, TOP, -1)
     moe_part = jnp.sum(picked[:, :, None] * route_out, axis=1)
-    moe_total = lax.psum(moe_part.astype(jnp.bfloat16), "tensor").astype(jnp.float32)
+    moe_total = tensor_sum(moe_part.astype(jnp.bfloat16))
     down_bias_f = down_bias.astype(jnp.float32)
     layer_out = middle + moe_total + jnp.dot(mixing, down_bias_f, precision=HIGHEST)
     upstream = cotangent.astype(jnp.float32)
     grad_down_bias = jnp.dot(mixing.T, upstream, precision=HIGHEST)
     bias_dot = jnp.dot(cotangent, down_bias.T, preferred_element_type=jnp.float32)
     route_dot_part = jnp.sum(route_out * upstream[:, None, :], axis=-1)
-    route_dot = lax.psum(route_dot_part, "tensor")
+    route_dot = small_sum(route_dot_part, "tensor")
     grad_picked = route_dot + jnp.sum(bias_dot[:, None, :] * choose, axis=-1)
     grad_gates = jnp.sum(choose * grad_picked[:, :, None], axis=1)
     grad_logits = gate_probs * (
@@ -136,7 +194,7 @@
     )
     slot_grad = route_grad_pad[route_of_slot].reshape(expert_count, CAP, -1)
     grad_down = jnp.einsum(
-        "ecf,ecd->efd", activated_low, slot_grad, preferred_element_type=jnp.float32
+        "ecf,ecd->edf", activated_low, slot_grad, preferred_element_type=jnp.float32
     )
     hidden_grad = jnp.einsum(
         "ecd,efd->ecf", slot_grad, down_weight, preferred_element_type=jnp.float32
@@ -148,7 +206,7 @@
     back_part = jnp.sum(
         slot_back.reshape(expert_count * CAP, -1)[target].reshape(tok_rows, TOP, -1), axis=1
     )
-    back_total = lax.psum(back_part.astype(jnp.bfloat16), "tensor").astype(jnp.float32)
+    back_total = tensor_sum(back_part.astype(jnp.bfloat16))
     normed2_grad = back_total + router_back
     middle_grad_ln, grad_moe_gain, grad_moe_shift = moe_norm_back(normed2_grad)
     middle_grad = upstream + middle_grad_ln
@@ -193,45 +251,47 @@
     normed_back = jnp.einsum(
         "cth,cdh->td", grad_proj, qkv_weight, preferred_element_type=jnp.float32
     )
-    normed_grad = lax.psum(normed_back.astype(jnp.bfloat16), "tensor").astype(jnp.float32)
+    normed_grad = tensor_sum(normed_back.astype(jnp.bfloat16))
     embed_grad_ln, grad_attn_gain, grad_attn_shift = attn_norm_back(normed_grad)
     grad_embedded = middle_grad + embed_grad_ln
-    smalls = lax.psum(
-        (
-            grad_attn_gain,
-            grad_attn_shift,
-            grad_qv_bias,
-            grad_out_bias,
-            grad_moe_gain,
-            grad_moe_shift,
-            grad_router,
-            grad_up_bias,
-            grad_down_bias,
-        ),
-        "dp",
-    )
-    grad_qkv, grad_out, grad_up, grad_down = (
-        lax.psum_scatter(grad_qkv, "dp", scatter_dimension=1, tiled=True),
-        lax.psum_scatter(grad_out, "dp", scatter_dimension=1, tiled=True),
-        lax.psum_scatter(grad_up, "dp", scatter_dimension=1, tiled=True),
-        lax.psum_scatter(grad_down, "dp", scatter_dimension=2, tiled=True),
-    )
+    width = embedded.shape[1]
+    pieces = (
+        grad_attn_gain[None],
+        grad_attn_shift[None],
+        grad_out_bias[None],
+        grad_moe_gain[None],
+        grad_moe_shift[None],
+        jnp.pad(grad_qv_bias, ((0, 0), (0, width - head_width))),
+        grad_router.T,
+        grad_up_bias,
+        grad_down_bias,
+    )
+    packed = small_sum(jnp.concatenate(pieces, axis=0), "dp")
+    grad_attn_gain, grad_attn_shift, grad_out_bias, grad_moe_gain, grad_moe_shift = packed[:5]
+    grad_qv_bias = packed[5:7, :head_width]
+    grad_router = packed[7 : 7 + expert_count].T
+    grad_up_bias = packed[7 + expert_count : 7 + 2 * expert_count]
+    grad_down_bias = packed[7 + 2 * expert_count :]
+    grad_up = ring_scatter(grad_up.astype(jnp.bfloat16), 1)
+    grad_down = ring_scatter(grad_down.astype(jnp.bfloat16), -1).transpose(0, 2, 1)
+    grad_qkv = ring_scatter(grad_qkv.astype(jnp.bfloat16), 1)
+    grad_out = ring_scatter(grad_out.T[None].astype(jnp.bfloat16), -1)[0].T
     return (
         layer_out.astype(jnp.bfloat16),
         grad_embedded,
-        smalls[0],
-        smalls[1],
+        grad_attn_gain,
+        grad_attn_shift,
         grad_qkv,
-        smalls[2],
+        grad_qv_bias,
         grad_out,
-        smalls[3],
-        smalls[4],
-        smalls[5],
-        smalls[6],
+        grad_out_bias,
+        grad_moe_gain,
+        grad_moe_shift,
+        grad_router,
         grad_up,
-        smalls[7],
+        grad_up_bias,
         grad_down,
-        smalls[8],
+        grad_down_bias,
     )
 
 

time: 1580 us -> 917 us (0.58)
  waiting for transfers between devices: 888 us -> 165 us
  starting transfers between devices: 0.71 us -> 46.3 us
  other arithmetic: 173 us -> 208 us
  matrix products: 199 us -> 173 us
    reduce_scatter x2 -> x0, waiting for transfers between devices: 635 us -> none  [the longest x1 318 us: on_device(): lax.psum_scatter(grad_up, 'dp', scatter_dimension=1, tiled=True)]
    psum x4 -> x0, waiting for transfers between devices: 170 us -> none  [the longest x1 106 us: on_device(): lax.psum(moe_part.astype(jnp.bfloat16), 'tensor').astype(jnp.float32)]
    ppermute x0 -> x45, waiting for transfers between devices: none -> 165 us  [the longest x28 89.7 us: ring_scatter(): got = lax.ppermute(moving, 'dp', path)]
    unnamed x10 -> x0, waiting for transfers between devices: 82.9 us -> none
    ppermute x0 -> x45, starting transfers between devices: none -> 46.3 us  [the longest x28 32 us: ring_scatter(): got = lax.ppermute(moving, 'dp', path)]
    convert_element_type x0 -> x32, other arithmetic: none -> 36.6 us  [the longest x24 27.2 us: ring_scatter(): moving = total.astype(jnp.bfloat16) if step < count - 1 else total]
  transfers between devices with their start and end apart: 8 -> 45, of which waited for: 7 -> 18; matrix products, arithmetic and copies ran while one was open for 16% -> 45% of each run, Pallas kernels for 0% -> 0%
where the time goes in v1:
time: 917 us; the launch traced here: 910 us
  local copies, waits for them, and re-layouts  293 us (32%)
  other arithmetic  208 us (23%)
  matrix products  173 us (19%)
  waiting for transfers between devices  165 us (18%)
  starting transfers between devices  46.3 us (5%)
  between operations  24 us (3%)
    ppermute x28, waiting for transfers between devices, ring_scatter(): got = lax.ppermute(moving, 'dp', path)  89.7 us
    ppermute x4, waiting for transfers between devices, tensor_sum(): far = lax.ppermute(both, 'tensor', pairs(4, 2))  66.3 us
    reduce_sum x1, other arithmetic, on_device(): jnp.sum(slot_back.reshape(expert_count * CAP, -1)[target].reshape(tok_row...  61.6 us
    reduce_sum x1, other arithmetic, on_device(): route_dot_part = jnp.sum(route_out * upstream[:, None, :], axis=-1)  36.4 us
    mul x2, local copies, waits for them, and re-layouts, on_device(): picked[:, :, None] * upstream[:, None, :]  33.1 us
    gather x1, local copies, waits for them, and re-layouts, on_device(): slot_grad = route_grad_pad[route_of_slot].reshape(expert_count, CAP, -1)  32 us
    ppermute x28, starting transfers between devices, ring_scatter(): got = lax.ppermute(moving, 'dp', path)  32 us
    gather x1, local copies, waits for them, and re-layouts, on_device(): padded[token_of_slot].reshape(expert_count, CAP, moe_normed.shape[1])  30.5 us
  transfers between devices with their start and end apart: 45, of which 18 were waited for; matrix products, arithmetic and copies ran while one was open for 45% of the time, Pallas kernels for 0%

profile of v1, /device:TPU:0, one launch (start us, length us, event | category | flops | bytes accessed | tf_op | source)
XLA Modules:
  0.0 910.2 jit_solution(8368845199051180253)
XLA Ops:
  9.9 4.9 unstack.51
  14.8 5.7 unstack.53
  20.5 4.0 multiply_reduce_fusion.6
  27.5 3.6 unstack.49
  31.1 5.5 fusion.32
  38.4 3.4 reshape.392
  46.8 3.7 collective-permute-done
  67.9 28.1 %collective-permute-done.1 = bf16[2364,384]{1,0:T(8,128)(2,1)} collective-permute-done((bf16[2364,384]{1,0:T(8,128)(2,1)S(1)}, bf16[2364,384]{1,0:T(8,128)(2,1)}, u32[]{:S(2)}, u32[]{:S(2)}) %collective-permute-start.1) | collective-permute-done | bytes 1815584 | tf_op jit(solution)/shard_map/ppermute | solution.py:40
  115.3 5.8 convert_element_type.537
  121.1 15.2 %mul.492 = f32[2364,2,768]{2,1,0:T(2,128)} broadcast(bf16[2364,768]{1,0:T(8,128)(2,1)S(1)} %copy-done.8), dimensions={0,2} | broadcast | bytes 18155520 | tf_op jit(solution)/shard_map/mul | solution.py:190
  136.2 18.0 %mul.493 = f32[4728,768]{1,0:T(8,128)} reshape(f32[2364,2,768]{2,1,0:T(2,128)} %mul.492) | data formatting | bytes 29048832 | tf_op jit(solution)/shard_map/mul | solution.py:190
  158.3 22.9 %scatter_custom_fusion = s32[6144]{0:T(1024)S(1)} fusion(s32[4728]{0:T(1024)S(1)} %fusion.72, s32[4728]{0:T(1024)S(1)} %iota.9, s32[]{:T(128)} %constant.332.clone.1), kind=kCustom, calls=%fused_computation.193 | custom fusion | bytes 24580 | tf_op jit(solution)/shard_map/scatter | solution.py:151
  200.6 8.9 multiply_convert_fusion.1
  209.5 6.5 concatenate.30
  216.0 32.0 %gather_fusion.2 = bf16[6144,768]{1,0:T(8,128)(2,1)} fusion(bf16[4729,768]{1,0:T(8,128)(2,1)} %concatenate.30, s32[6144]{0:T(1024)S(1)} %get-tuple-element.142), kind=kCustom, calls=%fused_computation.2 | custom fusion | bytes 18898944 | tf_op jit(solution)/shard_map/gather | solution.py:195
  248.0 30.5 %gather_fusion = bf16[6144,768]{1,0:T(8,128)(2,1)} fusion(bf16[2365,768]{1,0:T(8,128)(2,1)} %concatenate.28, s32[6144]{0:T(1024)S(1)} %get-tuple-element.143), kind=kCustom, calls=%fused_computation | custom fusion | bytes 18898944 | tf_op jit(solution)/shard_map/gather | solution.py:157
  278.6 16.6 %fusion.92 = f32[8,768,768]{2,1,0:T(8,128)} fusion(bf16[8,768,768]{2,1,0:T(8,128)(2,1)} %bitcast.181, bf16[8,768,768]{2,1,0:T(8,128)(2,1)} %param.34), kind=kOutput, calls=%fused_computation.228 | convolution fusion | flops 7247757312 | bytes 37748736 | tf_op jit(solution)/shard_map/ecd,edf->ecf/dot_general | solution.py:159
  295.1 17.6 %convolution_convert_fusion = bf16[8,768,768]{2,1,0:T(8,128)(2,1)} fusion(bf16[8,768,768]{2,1,0:T(8,128)(2,1)} %bitcast.183, f32[8,768,768]{2,1,0:T(8,128)} %fusion.92, f32[8,768]{1,0:T(8,128)S(1)} %convert_element_type.525), kind=kOutput, calls=%fused_computation.53 | convolution fusion | flops 7299661824 | bytes 37773312 | tf_op jit(solution)/shard_map/ecf,ecd->edf/dot_general | solution.py:196
  312.7 27.5 %convert_reduce_fusion = (f32[8,768]{1,0:T(8,128)}, bf16[8,768,768]{2,1,0:T(8,128)(2,1)}) fusion(f32[8,768,768]{2,1,0:T(8,128)} %fusion.92, f32[8,768]{1,0:T(8,128)S(1)} %convert_element_type.525, bf16[8,768,768]{2,1,0:T(8,128)(2,1)} %bitcast.184, bf16[8,768,768]{2,1,0:T(8,128)(2,1)} %param.36), kind=kOutput, calls=%fused_computation.14 | convolution fusion | flops 7356278784 | bytes 47235072 | tf_op jit(solution)/shard_map/ecd,efd->ecf/dot_general | solution.py:199
  340.3 19.0 %fusion.83 = f32[8,768,768]{2,1,0:T(8,128)} fusion(bf16[8,768,768]{2,1,0:T(8,128)(2,1)} %param.36, f32[8,768,768]{2,1,0:T(8,128)} %fusion.92, f32[8,768]{1,0:T(8,128)S(1)} %convert_element_type.525), kind=kOutput, calls=%fused_computation.221 | convolution fusion | flops 7294943232 | bytes 47210496 | tf_op jit(solution)/shard_map/ecf,efd->ecd/dot_general | solution.py:164
  359.3 15.4 %convolution_convert_fusion.1 = bf16[8,768,768]{2,1,0:T(8,128)(2,1)} fusion(bf16[8,768,768]{2,1,0:T(8,128)(2,1)} %bitcast.182, bf16[8,768,768]{2,1,0:T(8,128)(2,1)} %get-tuple-element.123), kind=kOutput, calls=%fused_computation.54 | convolution fusion | flops 7252475904 | bytes 28311552 | tf_op jit(solution)/shard_map/ecd,ecf->edf/dot_general | solution.py:204
  374.7 16.4 %fusion.93 = f32[8,768,768]{2,1,0:T(8,128)} fusion(bf16[8,768,768]{2,1,0:T(8,128)(2,1)} %get-tuple-element.123, bf16[8,768,768]{2,1,0:T(8,128)(2,1)} %param.34), kind=kOutput, calls=%fused_computation.229 | convolution fusion | flops 7247757312 | bytes 37748736 | tf_op jit(solution)/shard_map/ecf,edf->ecd/dot_general | solution.py:205
  397.9 24.9 %gather_fusion.1 = f32[4728,768]{1,0:T(8,128)} fusion(f32[6144,768]{1,0:T(8,128)} %bitcast.178, s32[5120]{0:T(1024)S(1)} %copy-done.57), kind=kCustom, calls=%fused_computation.1 | custom fusion | bytes 29067744 | tf_op jit(solution)/shard_map/gather | solution.py:167
  422.8 17.3 %reshape.397 = f32[2364,2,768]{2,1,0:T(2,128)} reshape(f32[4728,768]{1,0:T(8,128)} %gather_fusion.1) | data formatting | bytes 29048832 | tf_op jit(solution)/shard_map/reshape | solution.py:167
  440.2 36.4 %multiply_reduce_fusion = (f32[2364,2]{1,0:T(8,128)S(1)}, bf16[2364,768]{1,0:T(8,128)(2,1)}) fusion(f32[2364,2,768]{2,1,0:T(2,128)} %reshape.397, f32[2364,768]{1,0:T(8,128)} %convert_element_type.537, f32[2364,2]{1,0:T(8,128)S(1)} %copy-done.23), kind=kLoop, calls=%fused_computation.16 | loop fusion | flops 12704136 | bytes 25455552 | tf_op jit(solution)/shard_map/reduce_sum | solution.py:175
  477.0 24.7 %gather_fusion.3 = f32[4728,768]{1,0:T(8,128)} fusion(f32[6144,768]{1,0:T(8,128)} %bitcast.177, s32[5120]{0:T(1024)S(1)} %copy-done.57), kind=kCustom, calls=%fused_computation.3 | custom fusion | bytes 29067744 | tf_op jit(solution)/shard_map/gather | solution.py:207
  501.7 17.2 %reshape.400 = f32[2364,2,768]{2,1,0:T(2,128)} reshape(f32[4728,768]{1,0:T(8,128)} %gather_fusion.3) | data formatting | bytes 29048832 | tf_op jit(solution)/shard_map/reshape | solution.py:207
  519.0 61.6 %reduce_sum.288 = bf16[2364,768]{1,0:T(8,128)(2,1)} reduce(f32[2364,2,768]{2,1,0:T(2,128)} %reshape.400, f32[]{:T(128)} %constant.324.clone.1), dimensions={1}, to_apply=%region_15.16 | reduce | flops 1815552 | bytes 18155524 | tf_op jit(solution)/shard_map/reduce_sum | solution.py:206
  595.5 20.5 %collective-permute-done.39 = bf16[8,96,768]{2,1,0:T(8,128)(2,1)S(1)} collective-permute-done((bf16[8,96,768]{2,1,0:T(8,128)(2,1)S(1)}, bf16[8,96,768]{2,1,0:T(8,128)(2,1)S(1)}, u32[]{:S(2)}, u32[]{:S(2)}) %collective-permute-start.39) | collective-permute-done | bytes 1179680 | tf_op jit(solution)/shard_map/ppermute | solution.py:75
  625.1 18.5 %collective-permute-done.40 = bf16[8,96,768]{2,1,0:T(8,128)(2,1)S(1)} collective-permute-done((bf16[8,96,768]{2,1,0:T(8,128)(2,1)S(1)}, bf16[8,96,768]{2,1,0:T(8,128)(2,1)S(1)}, u32[]{:S(2)}, u32[]{:S(2)}) %collective-permute-start.40) | collective-permute-done | bytes 1179680 | tf_op jit(solution)/shard_map/ppermute | solution.py:75
  651.0 21.7 %collective-permute-done.4 = bf16[2364,384]{1,0:T(8,128)(2,1)S(1)} collective-permute-done((bf16[2364,384]{1,0:T(8,128)(2,1)S(1)}, bf16[2364,384]{1,0:T(8,128)(2,1)S(1)}, u32[]{:S(2)}, u32[]{:S(2)}) %collective-permute-start.4) | collective-permute-done | bytes 1815584 | tf_op jit(solution)/shard_map/ppermute | solution.py:40
  685.9 8.7 multiply_reduce_fusion.3
  694.6 8.2 fusion.86
  709.2 5.3 reshape.401
  714.6 5.4 fusion.33
  720.0 5.6 multiply_reduce_fusion.2
  735.6 3.8 stack.25
  742.5 3.8 stack.24
  749.4 3.8 stack.23
  766.9 8.0 add_convert_fusion
  794.3 4.0 collective-permute-done.20
  805.8 16.5 %collective-permute-done.12 = bf16[2364,384]{1,0:T(8,128)(2,1)S(1)} collective-permute-done((bf16[2364,384]{1,0:T(8,128)(2,1)S(1)}, bf16[2364,384]{1,0:T(8,128)(2,1)S(1)}, u32[]{:S(2)}, u32[]{:S(2)}) %collective-permute-start.12) | collective-permute-done | bytes 1815584 | tf_op jit(solution)/shard_map/ppermute | solution.py:40
  832.9 22.5 %collective-permute-done.30 = bf16[1,96,192]{1,2,0:T(8,128)(2,1)S(1)} collective-permute-done((bf16[1,96,192]{1,2,0:T(8,128)(2,1)S(1)}, bf16[1,96,192]{1,2,0:T(8,128)(2,1)S(1)}, u32[]{:S(2)}, u32[]{:S(2)}) %collective-permute-start.30) | collective-permute-done | bytes 36896 | tf_op jit(solution)/shard_map/ppermute | solution.py:75
  861.8 3.4 add_bitcast_fusion
  869.7 4.0 fusion.18
  874.4 14.4 %collective-permute-done.37 = bf16[8,96,768]{2,1,0:T(8,128)(2,1)} collective-permute-done((bf16[8,96,768]{2,1,0:T(8,128)(2,1)}, bf16[8,96,768]{2,1,0:T(8,128)(2,1)}, u32[]{:S(2)}, u32[]{:S(2)}) %collective-permute-start.37) | collective-permute-done | bytes 1179680 | tf_op jit(solution)/shard_map/ppermute | solution.py:75
  893.0 3.7 collective-permute-done.15
  898.7 9.1 %add_add_fusion.2 = f32[2364,768]{1,0:T(8,128)} fusion(bf16[2364,768]{1,0:T(8,128)(2,1)S(1)} %copy-done.6, f32[2364]{0:T(1024)S(1)} %negate_multiply_fusion, f32[2364]{0:T(1024)S(1)} %multiply_multiply_fusion.2, f32[768]{0:T(1024)S(1)} %copy-done.71, f32[2364]{0:T(1024)S(1)} %copy-done.64, f32[2364]{0:T(1024)S(1)} %copy-done.50, f32[2364,768]{1,0:T(8,128)} %copy-done.12, ...), kind=kLoop, calls=%fused_computation.46 | loop fusion | flops 29048832 | bytes 25468080 | tf_op jit(solution)/shard_map/add | solution.py:256
  (405 shorter events, 201.8 us)
Async XLA Ops:
  46.3 4.2 collective-permute-start
  53.0 43.0 %collective-permute-start.1 = (bf16[2364,384]{1,0:T(8,128)(2,1)S(1)}, bf16[2364,384]{1,0:T(8,128)(2,1)}, u32[]{:S(2)}, u32[]{:S(2)}) collective-permute-start(bf16[2364,384]{1,0:T(8,128)(2,1)S(1)} %add_convert_fusion.10), channel_id=1, source_target_pairs={{0,2},{1,3},{2,0},{3,1},{4,6},{5,7},{6,4},{7,5},{8,10},{9,11},{10,... | collective-permute-start | bytes 5446664 | tf_op jit(solution)/shard_map/ppermute | solution.py:40
  65.2 50.1 %copy-start.87 = (bf16[768]{0:T(1024)(128)(2,1)S(1)}, bf16[768]{0:T(1024)(128)(2,1)}, u32[]{:S(2)}) copy-start(bf16[768]{0:T(1024)(128)(2,1)} %param.32) | copy-start | bytes 4612
  98.5 86.4 %collective-permute-start.2 = (bf16[2364,384]{1,0:T(8,128)(2,1)S(1)}, bf16[2364,384]{1,0:T(8,128)(2,1)}, u32[]{:S(2)}, u32[]{:S(2)}) collective-permute-start(bf16[2364,384]{1,0:T(8,128)(2,1)S(1)} %add_convert_fusion.9), channel_id=1, source_target_pairs={{0,1},{1,0},{2,3},{3,2},{4,5},{5,4},{6,7},{7,6},{8,9},{9,8},{10,11... | collective-permute-start | bytes 5446664 | tf_op jit(solution)/shard_map/ppermute | solution.py:42
  115.2 76.7 %copy-start.67 = (f32[768]{0:T(1024)}, f32[768]{0:T(1024)S(1)}, u32[]{:S(2)}) copy-start(f32[768]{0:T(1024)S(1)} %convert_element_type.517) | copy-start | bytes 9220
  115.3 76.7 %copy-start.72 = (f32[768]{0:T(1024)}, f32[768]{0:T(1024)S(1)}, u32[]{:S(2)}) copy-start(f32[768]{0:T(1024)S(1)} %convert_element_type.518) | copy-start | bytes 9220
  393.5 193.5 %collective-permute-start.38 = (bf16[8,96,768]{2,1,0:T(8,128)(2,1)}, bf16[8,96,768]{2,1,0:T(8,128)(2,1)}, u32[]{:S(2)}, u32[]{:S(2)}) collective-permute-start(bf16[8,96,768]{2,1,0:T(8,128)(2,1)} %constant_dynamic-slice_fusion), channel_id=1, source_target_pairs={{0,4},{8,0},{16,8},{24,16},{28,24},{20,28},{12,20},{4,12},{1,5},{9... | collective-permute-start | bytes 3538952 | tf_op jit(solution)/shard_map/ppermute | solution.py:75
  397.7 193.3 %collective-permute-start.31 = (bf16[8,96,768]{2,1,0:T(8,128)(2,1)}, bf16[8,96,768]{2,1,0:T(8,128)(2,1)}, u32[]{:S(2)}, u32[]{:S(2)}) collective-permute-start(bf16[8,96,768]{2,1,0:T(8,128)(2,1)} %constant_dynamic-slice_fusion.1), channel_id=1, source_target_pairs={{0,8},{8,16},{16,24},{24,28},{28,20},{20,12},{12,4},{4,0},{1,9},{9... | collective-permute-start | bytes 3538952 | tf_op jit(solution)/shard_map/ppermute | solution.py:75
  476.9 106.0 %collective-permute-start.9 = (f32[2364,2]{0,1:T(2,128)S(1)}, f32[2364,2]{0,1:T(2,128)S(1)}, u32[]{:S(2)}, u32[]{:S(2)}) collective-permute-start(f32[2364,2]{0,1:T(2,128)S(1)} %copy.177), channel_id=1, source_target_pairs={{0,1},{1,0},{2,3},{3,2},{4,5},{5,4},{6,7},{7,6},{8,9},{9,8},{10,11... | collective-permute-start | bytes 56744 | tf_op jit(solution)/shard_map/ppermute | solution.py:54
  582.4 10.8 %collective-permute-start.6 = (bf16[2364,384]{1,0:T(8,128)(2,1)S(1)}, bf16[2364,384]{1,0:T(8,128)(2,1)S(1)}, u32[]{:S(2)}, u32[]{:S(2)}) collective-permute-start(bf16[2364,384]{1,0:T(8,128)(2,1)S(1)} %constant_dynamic-slice_fusion.3), channel_id=1, source_target_pairs={{0,1},{1,0},{2,3},{3,2},{4,5},{5,4},{6,7},{7,6},{8,9},{9,8},{10,11... | collective-permute-start | bytes 5446664 | tf_op jit(solution)/shard_map/ppermute | solution.py:38
  583.0 3.8 collective-permute-start.10
  585.0 34.3 %collective-permute-start.3 = (bf16[2364,384]{1,0:T(8,128)(2,1)S(1)}, bf16[2364,384]{1,0:T(8,128)(2,1)S(1)}, u32[]{:S(2)}, u32[]{:S(2)}) collective-permute-start(bf16[2364,384]{1,0:T(8,128)(2,1)S(1)} %constant_dynamic-slice_fusion.4), channel_id=1, source_target_pairs={{0,1},{1,0},{2,3},{3,2},{4,5},{5,4},{6,7},{7,6},{8,9},{9,8},{10,11... | collective-permute-start | bytes 5446664 | tf_op jit(solution)/shard_map/ppermute | solution.py:38
  589.1 26.9 %collective-permute-start.39 = (bf16[8,96,768]{2,1,0:T(8,128)(2,1)S(1)}, bf16[8,96,768]{2,1,0:T(8,128)(2,1)S(1)}, u32[]{:S(2)}, u32[]{:S(2)}) collective-permute-start(bf16[8,96,768]{2,1,0:T(8,128)(2,1)S(1)} %add_convert_fusion.16), channel_id=1, source_target_pairs={{0,4},{8,0},{16,8},{24,16},{28,24},{20,28},{12,20},{4,12},{1,5},{9... | collective-permute-start | bytes 3538952 | tf_op jit(solution)/shard_map/ppermute | solution.py:75
  592.9 28.5 %collective-permute-start.32 = (bf16[8,96,768]{2,1,0:T(8,128)(2,1)S(1)}, bf16[8,96,768]{2,1,0:T(8,128)(2,1)S(1)}, u32[]{:S(2)}, u32[]{:S(2)}) collective-permute-start(bf16[8,96,768]{2,1,0:T(8,128)(2,1)S(1)} %add_convert_fusion.22), channel_id=1, source_target_pairs={{0,8},{8,16},{16,24},{24,28},{28,20},{20,12},{12,4},{4,0},{1,9},{9... | collective-permute-start | bytes 3538952 | tf_op jit(solution)/shard_map/ppermute | solution.py:75
  593.7 53.1 %collective-permute-start.7 = (bf16[2364,384]{1,0:T(8,128)(2,1)S(1)}, bf16[2364,384]{1,0:T(8,128)(2,1)S(1)}, u32[]{:S(2)}, u32[]{:S(2)}) collective-permute-start(bf16[2364,384]{1,0:T(8,128)(2,1)S(1)} %add_convert_fusion.6), channel_id=1, source_target_pairs={{0,2},{1,3},{2,0},{3,1},{4,6},{5,7},{6,4},{7,5},{8,10},{9,11},{10,... | collective-permute-start | bytes 5446664 | tf_op jit(solution)/shard_map/ppermute | solution.py:40
  617.6 26.0 %collective-permute-start.40 = (bf16[8,96,768]{2,1,0:T(8,128)(2,1)S(1)}, bf16[8,96,768]{2,1,0:T(8,128)(2,1)S(1)}, u32[]{:S(2)}, u32[]{:S(2)}) collective-permute-start(bf16[8,96,768]{2,1,0:T(8,128)(2,1)S(1)} %add_convert_fusion.15), channel_id=1, source_target_pairs={{0,4},{8,0},{16,8},{24,16},{28,24},{20,28},{12,20},{4,12},{1,5},{9... | collective-permute-start | bytes 3538952 | tf_op jit(solution)/shard_map/ppermute | solution.py:75
  619.8 52.9 %collective-permute-start.4 = (bf16[2364,384]{1,0:T(8,128)(2,1)S(1)}, bf16[2364,384]{1,0:T(8,128)(2,1)S(1)}, u32[]{:S(2)}, u32[]{:S(2)}) collective-permute-start(bf16[2364,384]{1,0:T(8,128)(2,1)S(1)} %add_convert_fusion.8), channel_id=1, source_target_pairs={{0,2},{1,3},{2,0},{3,1},{4,6},{5,7},{6,4},{7,5},{8,10},{9,11},{10,... | collective-permute-start | bytes 5446664 | tf_op jit(solution)/shard_map/ppermute | solution.py:40
  623.0 25.3 %collective-permute-start.33 = (bf16[8,96,768]{2,1,0:T(8,128)(2,1)S(1)}, bf16[8,96,768]{2,1,0:T(8,128)(2,1)S(1)}, u32[]{:S(2)}, u32[]{:S(2)}) collective-permute-start(bf16[8,96,768]{2,1,0:T(8,128)(2,1)S(1)} %add_convert_fusion.21), channel_id=1, source_target_pairs={{0,8},{8,16},{16,24},{24,28},{28,20},{20,12},{12,4},{4,0},{1,9},{9... | collective-permute-start | bytes 3538952 | tf_op jit(solution)/shard_map/ppermute | solution.py:75
  645.1 29.3 %collective-permute-start.41 = (bf16[8,96,768]{2,1,0:T(8,128)(2,1)S(1)}, bf16[8,96,768]{2,1,0:T(8,128)(2,1)S(1)}, u32[]{:S(2)}, u32[]{:S(2)}) collective-permute-start(bf16[8,96,768]{2,1,0:T(8,128)(2,1)S(1)} %add_convert_fusion.14), channel_id=1, source_target_pairs={{0,4},{8,0},{16,8},{24,16},{28,24},{20,28},{12,20},{4,12},{1,5},{9... | collective-permute-start | bytes 3538952 | tf_op jit(solution)/shard_map/ppermute | solution.py:75
  647.3 35.0 %collective-permute-start.8 = (bf16[2364,384]{1,0:T(8,128)(2,1)S(1)}, bf16[2364,384]{1,0:T(8,128)(2,1)S(1)}, u32[]{:S(2)}, u32[]{:S(2)}) collective-permute-start(bf16[2364,384]{1,0:T(8,128)(2,1)S(1)} %add_convert_fusion.5), channel_id=1, source_target_pairs={{0,1},{1,0},{2,3},{3,2},{4,5},{5,4},{6,7},{7,6},{8,9},{9,8},{10,11... | collective-permute-start | bytes 5446664 | tf_op jit(solution)/shard_map/ppermute | solution.py:42
  649.9 28.9 %collective-permute-start.34 = (bf16[8,96,768]{2,1,0:T(8,128)(2,1)S(1)}, bf16[8,96,768]{2,1,0:T(8,128)(2,1)S(1)}, u32[]{:S(2)}, u32[]{:S(2)}) collective-permute-start(bf16[8,96,768]{2,1,0:T(8,128)(2,1)S(1)} %add_convert_fusion.20), channel_id=1, source_target_pairs={{0,8},{8,16},{16,24},{24,28},{28,20},{20,12},{12,4},{4,0},{1,9},{9... | collective-permute-start | bytes 3538952 | tf_op jit(solution)/shard_map/ppermute | solution.py:75
  674.5 89.8 %collective-permute-start.5 = (bf16[2364,384]{1,0:T(8,128)(2,1)}, bf16[2364,384]{1,0:T(8,128)(2,1)}, u32[]{:S(2)}, u32[]{:S(2)}) collective-permute-start(bf16[2364,384]{1,0:T(8,128)(2,1)} %add_convert_fusion.7), channel_id=1, source_target_pairs={{0,1},{1,0},{2,3},{3,2},{4,5},{5,4},{6,7},{7,6},{8,9},{9,8},{10,11... | collective-permute-start | bytes 5446664 | tf_op jit(solution)/shard_map/ppermute | solution.py:42
  677.1 121.9 %collective-permute-start.42 = (bf16[8,96,768]{2,1,0:T(8,128)(2,1)}, bf16[8,96,768]{2,1,0:T(8,128)(2,1)}, u32[]{:S(2)}, u32[]{:S(2)}) collective-permute-start(bf16[8,96,768]{2,1,0:T(8,128)(2,1)} %add_convert_fusion.13), channel_id=1, source_target_pairs={{0,4},{8,0},{16,8},{24,16},{28,24},{20,28},{12,20},{4,12},{1,5},{9... | collective-permute-start | bytes 3538952 | tf_op jit(solution)/shard_map/ppermute | solution.py:75
  681.4 121.0 %collective-permute-start.35 = (bf16[8,96,768]{2,1,0:T(8,128)(2,1)}, bf16[8,96,768]{2,1,0:T(8,128)(2,1)}, u32[]{:S(2)}, u32[]{:S(2)}) collective-permute-start(bf16[8,96,768]{2,1,0:T(8,128)(2,1)} %add_convert_fusion.19), channel_id=1, source_target_pairs={{0,8},{8,16},{16,24},{24,28},{28,20},{20,12},{12,4},{4,0},{1,9},{9... | collective-permute-start | bytes 3538952 | tf_op jit(solution)/shard_map/ppermute | solution.py:75
  732.1 42.8 %collective-permute-start.24 = (bf16[1,96,192]{1,2,0:T(8,128)(2,1)S(1)}, bf16[1,96,192]{1,2,0:T(8,128)(2,1)S(1)}, u32[]{:S(2)}, u32[]{:S(2)}) collective-permute-start(bf16[1,96,192]{1,2,0:T(8,128)(2,1)S(1)} %dynamic-slice_bitcast_fusion.1), channel_id=1, source_target_pairs={{0,4},{8,0},{16,8},{24,16},{28,24},{20,28},{12,20},{4,12},{1,5},{9... | collective-permute-start | bytes 110600 | tf_op jit(solution)/shard_map/ppermute | solution.py:75
  760.3 20.6 %collective-permute-start.17 = (bf16[3,96,192]{1,2,0:T(8,128)(2,1)S(1)}, bf16[3,96,192]{1,2,0:T(8,128)(2,1)S(1)}, u32[]{:S(2)}, u32[]{:S(2)}) collective-permute-start(bf16[3,96,192]{1,2,0:T(8,128)(2,1)S(1)} %dynamic-slice_bitcast_fusion), channel_id=1, source_target_pairs={{0,8},{8,16},{16,24},{24,28},{28,20},{20,12},{12,4},{4,0},{1,9},{9... | collective-permute-start | bytes 331784 | tf_op jit(solution)/shard_map/ppermute | solution.py:75
  764.3 17.2 %collective-permute-start.11 = (bf16[2364,384]{1,0:T(8,128)(2,1)S(1)}, bf16[2364,384]{1,0:T(8,128)(2,1)S(1)}, u32[]{:S(2)}, u32[]{:S(2)}) collective-permute-start(bf16[2364,384]{1,0:T(8,128)(2,1)S(1)} %constant_dynamic-slice_fusion.2), channel_id=1, source_target_pairs={{0,1},{1,0},{2,3},{3,2},{4,5},{5,4},{6,7},{7,6},{8,9},{9,8},{10,11... | collective-permute-start | bytes 5446664 | tf_op jit(solution)/shard_map/ppermute | solution.py:38
  775.0 4.2 collective-permute-start.25
  779.3 4.3 collective-permute-start.26
  781.0 5.2 collective-permute-start.18
  782.1 40.3 %collective-permute-start.12 = (bf16[2364,384]{1,0:T(8,128)(2,1)S(1)}, bf16[2364,384]{1,0:T(8,128)(2,1)S(1)}, u32[]{:S(2)}, u32[]{:S(2)}) collective-permute-start(bf16[2364,384]{1,0:T(8,128)(2,1)S(1)} %add_convert_fusion.4), channel_id=1, source_target_pairs={{0,2},{1,3},{2,0},{3,1},{4,6},{5,7},{6,4},{7,5},{8,10},{9,11},{10,... | collective-permute-start | bytes 5446664 | tf_op jit(solution)/shard_map/ppermute | solution.py:40
  783.7 4.1 collective-permute-start.27
  786.3 5.5 collective-permute-start.19
  787.9 4.7 collective-permute-start.28
  791.9 6.4 collective-permute-start.20
  792.7 35.1 %collective-permute-start.29 = (bf16[1,96,192]{1,2,0:T(8,128)(2,1)S(1)}, bf16[1,96,192]{1,2,0:T(8,128)(2,1)S(1)}, u32[]{:S(2)}, u32[]{:S(2)}) collective-permute-start(bf16[1,96,192]{1,2,0:T(8,128)(2,1)S(1)} %fusion.55), channel_id=1, source_target_pairs={{0,4},{8,0},{16,8},{24,16},{28,24},{20,28},{12,20},{4,12},{1,5},{9... | collective-permute-start | bytes 110600 | tf_op jit(solution)/shard_map/ppermute | solution.py:75
  798.4 24.5 %collective-permute-start.21 = (bf16[3,96,192]{1,2,0:T(8,128)(2,1)S(1)}, bf16[3,96,192]{1,2,0:T(8,128)(2,1)S(1)}, u32[]{:S(2)}, u32[]{:S(2)}) collective-permute-start(bf16[3,96,192]{1,2,0:T(8,128)(2,1)S(1)} %fusion.48), channel_id=1, source_target_pairs={{0,8},{8,16},{16,24},{24,28},{28,20},{20,12},{12,4},{4,0},{1,9},{9... | collective-permute-start | bytes 331784 | tf_op jit(solution)/shard_map/ppermute | solution.py:75
  800.8 22.6 %collective-permute-start.43 = (bf16[8,96,768]{2,1,0:T(8,128)(2,1)S(1)}, bf16[8,96,768]{2,1,0:T(8,128)(2,1)S(1)}, u32[]{:S(2)}, u32[]{:S(2)}) collective-permute-start(bf16[8,96,768]{2,1,0:T(8,128)(2,1)S(1)} %add_convert_fusion.12), channel_id=1, source_target_pairs={{0,4},{8,0},{16,8},{24,16},{28,24},{20,28},{12,20},{4,12},{1,5},{9... | collective-permute-start | bytes 3538952 | tf_op jit(solution)/shard_map/ppermute | solution.py:75
  805.4 51.8 %collective-permute-start.36 = (bf16[8,96,768]{2,1,0:T(8,128)(2,1)}, bf16[8,96,768]{2,1,0:T(8,128)(2,1)}, u32[]{:S(2)}, u32[]{:S(2)}) collective-permute-start(bf16[8,96,768]{2,1,0:T(8,128)(2,1)} %add_convert_fusion.18), channel_id=1, source_target_pairs={{0,8},{8,16},{16,24},{24,28},{28,20},{20,12},{12,4},{4,0},{1,9},{9... | collective-permute-start | bytes 3538952 | tf_op jit(solution)/shard_map/ppermute | solution.py:75
  822.9 42.4 %collective-permute-start.13 = (bf16[2364,384]{1,0:T(8,128)(2,1)S(1)}, bf16[2364,384]{1,0:T(8,128)(2,1)}, u32[]{:S(2)}, u32[]{:S(2)}) collective-permute-start(bf16[2364,384]{1,0:T(8,128)(2,1)S(1)} %add_convert_fusion.3), channel_id=1, source_target_pairs={{0,1},{1,0},{2,3},{3,2},{4,5},{5,4},{6,7},{7,6},{8,9},{9,8},{10,11... | collective-permute-start | bytes 5446664 | tf_op jit(solution)/shard_map/ppermute | solution.py:42
  823.1 9.0 collective-permute-start.22
  826.1 35.7 %collective-permute-start.44 = (bf16[8,96,768]{2,1,0:T(8,128)(2,1)}, bf16[8,96,768]{2,1,0:T(8,128)(2,1)}, u32[]{:S(2)}, u32[]{:S(2)}) collective-permute-start(bf16[8,96,768]{2,1,0:T(8,128)(2,1)} %add_convert_fusion.11), channel_id=1, source_target_pairs={{0,4},{8,0},{16,8},{24,16},{28,24},{20,28},{12,20},{4,12},{1,5},{9... | collective-permute-start | bytes 3538952 | tf_op jit(solution)/shard_map/ppermute | solution.py:75
  827.9 27.5 %collective-permute-start.30 = (bf16[1,96,192]{1,2,0:T(8,128)(2,1)S(1)}, bf16[1,96,192]{1,2,0:T(8,128)(2,1)S(1)}, u32[]{:S(2)}, u32[]{:S(2)}) collective-permute-start(bf16[1,96,192]{1,2,0:T(8,128)(2,1)S(1)} %fusion.54), channel_id=1, source_target_pairs={{0,4},{8,0},{16,8},{24,16},{28,24},{20,28},{12,20},{4,12},{1,5},{9... | collective-permute-start | bytes 110600 | tf_op jit(solution)/shard_map/ppermute | solution.py:75
  832.2 24.0 %collective-permute-start.23 = (bf16[3,96,192]{1,2,0:T(8,128)(2,1)S(1)}, bf16[3,96,192]{1,2,0:T(8,128)(2,1)S(1)}, u32[]{:S(2)}, u32[]{:S(2)}) collective-permute-start(bf16[3,96,192]{1,2,0:T(8,128)(2,1)S(1)} %fusion.46), channel_id=1, source_target_pairs={{0,8},{8,16},{16,24},{24,28},{28,20},{20,12},{12,4},{4,0},{1,9},{9... | collective-permute-start | bytes 331784 | tf_op jit(solution)/shard_map/ppermute | solution.py:75
  860.1 28.7 %collective-permute-start.37 = (bf16[8,96,768]{2,1,0:T(8,128)(2,1)}, bf16[8,96,768]{2,1,0:T(8,128)(2,1)}, u32[]{:S(2)}, u32[]{:S(2)}) collective-permute-start(bf16[8,96,768]{2,1,0:T(8,128)(2,1)} %add_convert_fusion.17), channel_id=1, source_target_pairs={{0,8},{8,16},{16,24},{24,28},{28,20},{20,12},{12,4},{4,0},{1,9},{9... | collective-permute-start | bytes 3538952 | tf_op jit(solution)/shard_map/ppermute | solution.py:75
  874.1 18.0 %collective-permute-start.14 = (f32[31,768]{1,0:T(8,128)S(1)}, f32[31,768]{1,0:T(8,128)S(1)}, u32[]{:S(2)}, u32[]{:S(2)}) collective-permute-start(f32[31,768]{1,0:T(8,128)S(1)} %concatenate.33), channel_id=1, source_target_pairs={{0,4},{4,0},{8,12},{12,8},{16,20},{20,16},{24,28},{28,24},{1,5},{5... | collective-permute-start | bytes 285704 | tf_op jit(solution)/shard_map/ppermute | solution.py:54
  892.1 4.7 collective-permute-start.15
  896.8 11.0 %collective-permute-start.16 = (f32[31,768]{1,0:T(8,128)S(1)}, f32[31,768]{1,0:T(8,128)S(1)}, u32[]{:S(2)}, u32[]{:S(2)}) collective-permute-start(f32[31,768]{1,0:T(8,128)S(1)} %add.682), channel_id=1, source_target_pairs={{0,16},{4,20},{8,24},{12,28},{16,0},{20,4},{24,8},{28,12},{1,17},{... | collective-permute-start | bytes 285704 | tf_op jit(solution)/shard_map/ppermute | solution.py:54
  (88 other events, 674.7 us)

commit v2 on v1

--- a/solution.py
+++ b/solution.py
@@ -1,12 +1,12 @@
 import jax
 import jax.numpy as jnp
 from jax import lax
+from jax.experimental import pallas as pl
+from jax.experimental.pallas import tpu as pltpu
 from jax.sharding import PartitionSpec as P
 
-TOP = 2
 SEQ = 197
 HD = 64
-CAP = 768
 
 
 EPSILON = 1e-06
@@ -76,6 +76,281 @@
         total = got.astype(jnp.float32) + local(step).astype(jnp.float32)
         moving = total.astype(jnp.bfloat16) if step < count - 1 else total
     return moving
+
+
+BLOCK = 512
+GROUPS = 2
+LOCAL = 1152
+ROOM = 1024
+TILE = 256
+VMEM = 56 * 1024 * 1024
+
+
+def route_plan(routes, expert_count):
+    tokens = routes.shape[0]
+    blocks = -(-tokens // BLOCK)
+    padded = jnp.pad(routes.T, ((0, 0), (0, blocks * BLOCK - tokens)), constant_values=-1)
+    experts = jnp.arange(expert_count, dtype=jnp.int32)[:, None]
+    first = padded[0][None, :] == experts
+    second = padded[1][None, :] == experts
+    named = (first | second).reshape(expert_count * blocks, BLOCK)
+    ahead = jnp.arange(BLOCK)[:, None] < jnp.arange(BLOCK)[None, :]
+    rank = jnp.dot(
+        named.astype(jnp.bfloat16), ahead.astype(jnp.bfloat16), preferred_element_type=jnp.float32
+    )
+    rank = rank.astype(jnp.int32).reshape(expert_count, blocks, BLOCK)
+    chunks = (jnp.sum(named.astype(jnp.int32), axis=1).reshape(expert_count, blocks) + 15) // 16
+    inside = jnp.cumsum(chunks, axis=0) - chunks
+    offset = jnp.cumsum(chunks, axis=1) - chunks
+    place = (rank + 16 * inside[:, :, None]).reshape(expert_count, blocks * BLOCK)
+    target = jnp.stack(
+        [jnp.sum(jnp.where(hot, place + 1, 0), axis=0) - 1 for hot in (first, second)]
+    )
+    tiles = (jnp.sum(chunks, axis=1) * 16 + TILE - 1) // TILE
+    plan = jnp.concatenate([chunks.T.reshape(-1), inside.T.reshape(-1), offset.T.reshape(-1)])
+    rows = target.reshape(2, blocks, BLOCK).transpose(1, 0, 2)
+    return rows, target.T, plan, tiles
+
+
+def spread(source, rows, plan, expert_count):
+    blocks, cols = rows.shape[0], source.shape[1]
+
+    def kernel(plan_ref, rows_ref, source_ref, out_ref, local):
+        block = pl.program_id(0)
+
+        @pl.when(block == 0)
+        def _():
+            out_ref[...] = jnp.zeros_like(out_ref)
+
+        part = LOCAL // 3
+        for i in range(3):
+            slot = lax.broadcasted_iota(jnp.int32, (part, BLOCK), 0) + i * part
+            hot = (slot == rows_ref[0, 0:1, :]) | (slot == rows_ref[0, 1:2, :])
+            local[pl.ds(i * part, part), :] = jnp.dot(
+                jnp.where(hot, 1.0, 0.0).astype(jnp.bfloat16),
+                source_ref[...],
+                preferred_element_type=jnp.float32,
+            ).astype(jnp.bfloat16)
+        for e in range(expert_count):
+            at = block * expert_count + e
+            size = blocks * expert_count
+            begin, goal = plan_ref[size + at], plan_ref[2 * size + at]
+
+            def move(j, carry):
+                here = pl.ds(pl.multiple_of((begin + j) * 16, 16), 16)
+                there = pl.ds(pl.multiple_of((goal + j) * 16, 16), 16)
+                out_ref[e, there, :] = local[here, :]
+                return carry
+
+            lax.fori_loop(0, plan_ref[at], move, 0)
+
+    return pl.pallas_call(
+        kernel,
+        grid_spec=pltpu.PrefetchScalarGridSpec(
+            num_scalar_prefetch=1,
+            grid=(blocks,),
+            in_specs=[
+                pl.BlockSpec((1, 2, BLOCK), lambda b, plan: (b, 0, 0)),
+                pl.BlockSpec((BLOCK, cols), lambda b, plan: (b, 0)),
+            ],
+            out_specs=pl.BlockSpec((expert_count, ROOM, cols), lambda b, plan: (0, 0, 0)),
+            scratch_shapes=[pltpu.VMEM((LOCAL, cols), jnp.bfloat16)],
+        ),
+        out_shape=jax.ShapeDtypeStruct((expert_count, ROOM, cols), jnp.bfloat16),
+        compiler_params=pltpu.CompilerParams(vmem_limit_bytes=VMEM),
+        cost_estimate=pl.CostEstimate(
+            flops=2 * blocks * LOCAL * BLOCK * cols,
+            bytes_accessed=2 * cols * (blocks * BLOCK + expert_count * ROOM),
+            transcendentals=0,
+        ),
+        name="spread",
+    )(plan, rows, source)
+
+
+def collect(buffers, columns, plan, kept):
+    each, room, cols = buffers[0].shape
+    expert_count = each * len(buffers)
+    blocks = columns.shape[0] // BLOCK
+    extra = cols - kept
+
+    def kernel(plan_ref, columns_ref, *refs):
+        held, refs = refs[: len(buffers)], refs[len(buffers) :]
+        out_ref, local = refs[0], refs[-1]
+        block = pl.program_id(0)
+
+        @pl.when(block == 0)
+        def _():
+            local[...] = jnp.zeros_like(local)
+
+        for e in range(expert_count):
+            at = block * expert_count + e
+            size = blocks * expert_count
+            begin, goal = plan_ref[size + at], plan_ref[2 * size + at]
+
+            def move(j, carry):
+                here = pl.ds(pl.multiple_of((begin + j) * 16, 16), 16)
+                there = pl.ds(pl.multiple_of((goal + j) * 16, 16), 16)
+                local[here, :] = held[e // each][e % each, there, :]
+                return carry
+
+            lax.fori_loop(0, plan_ref[at], move, 0)
+        part = BLOCK // 2
+        for i in range(2):
+            rows = pl.ds(i * part, part)
+            slot = lax.broadcasted_iota(jnp.int32, (part, LOCAL), 1)
+            hot = (slot == columns_ref[rows, 0:1]) | (slot == columns_ref[rows, 1:2])
+            total = jnp.dot(
+                jnp.where(hot, 1.0, 0.0).astype(jnp.bfloat16),
+                local[...],
+                preferred_element_type=jnp.float32,
+            )
+            out_ref[rows, :] = total[:, :kept].astype(jnp.bfloat16)
+            if extra:
+                refs[1][rows, :] = total[:, kept:]
+
+    out_specs = [pl.BlockSpec((BLOCK, kept), lambda b, plan: (b, 0))]
+    out_shape = [jax.ShapeDtypeStruct((blocks * BLOCK, kept), jnp.bfloat16)]
+    if extra:
+        out_specs.append(pl.BlockSpec((BLOCK, extra), lambda b, plan: (b, 0)))
+        out_shape.append(jax.ShapeDtypeStruct((blocks * BLOCK, extra), jnp.float32))
+    return pl.pallas_call(
+        kernel,
+        grid_spec=pltpu.PrefetchScalarGridSpec(
+            num_scalar_prefetch=1,
+            grid=(blocks,),
+            in_specs=[
+                pl.BlockSpec((BLOCK, 2), lambda b, plan: (b, 0)),
+            ]
+            + [pl.BlockSpec((each, room, cols), lambda b, plan: (0, 0, 0))] * len(buffers),
+            out_specs=out_specs,
+            scratch_shapes=[pltpu.VMEM((LOCAL, cols), jnp.bfloat16)],
+        ),
+        out_shape=out_shape,
+        compiler_params=pltpu.CompilerParams(vmem_limit_bytes=VMEM),
+        cost_estimate=pl.CostEstimate(
+            flops=2 * blocks * LOCAL * BLOCK * cols,
+            bytes_accessed=2 * cols * (blocks * BLOCK + expert_count * room),
+            transcendentals=0,
+        ),
+        name="collect",
+    )(plan, columns, *buffers)
+
+
+GELU_A = 0.7978845608028654
+GELU_B = 0.044715
+
+
+def expert_pass(inputs, grads, up_weight, up_bias, down_weight, tiles, first, count):
+    expert_count, room, cols = inputs.shape
+    width, hidden = up_weight.shape[1:]
+
+    def kernel(
+        tiles_ref, x_ref, g_ref, up_ref, bias_ref, down_ref,
+        y_ref, dx_ref, dup_ref, ddown_ref, dbias_ref, mixed, dpre,
+    ):
+        step = pl.program_id(0)
+        expert = step + first
+
+        @pl.when(step == 0)
+        def _():
+            mixed[...] = jnp.zeros_like(mixed)
+            dpre[...] = jnp.zeros_like(dpre)
+
+        dbias_ref[...] = jnp.zeros_like(dbias_ref)
+        lane = lax.broadcasted_iota(jnp.int32, (TILE, cols - width), 1)
+
+        def tile(r, carry):
+            rows = pl.ds(pl.multiple_of(r * TILE, TILE), TILE)
+            x = x_ref[0, rows, :width]
+            g = g_ref[0, rows, :]
+            gates = x_ref[0, rows, width:].astype(jnp.float32)
+            own = (lane == expert) | (lane == expert + expert_count)
+            mix = jnp.sum(jnp.where(own, gates, 0.0), axis=1, keepdims=True)
+            pre = jnp.dot(x, up_ref[0], preferred_element_type=jnp.float32)
+            pre = pre + bias_ref[0].astype(jnp.float32)
+            back = lax.dot_general(
+                g, down_ref[0], (((1,), (1,)), ((), ())), preferred_element_type=jnp.float32
+            )
+            square = pre * pre
+            bend = jnp.tanh(pre * (GELU_A + GELU_A * GELU_B * square))
+            upper = 0.5 + 0.5 * bend
+            act = pre * upper
+            slope = upper + 0.5 * pre * (1.0 - bend * bend) * (
+                GELU_A + 3.0 * GELU_A * GELU_B * square
+            )
+            dot = jnp.sum(act * back, axis=1, keepdims=True)
+            act_low = (mix * act).astype(jnp.bfloat16)
+            down = (mix * back * slope).astype(jnp.bfloat16)
+            mixed[rows, :] = act_low
+            dpre[rows, :] = down
+            dbias_ref[0] += jnp.sum(down.astype(jnp.float32), axis=0, keepdims=True)
+            y_ref[0, rows, :] = jnp.dot(
+                act_low, down_ref[0], preferred_element_type=jnp.float32
+            ).astype(jnp.bfloat16)
+            dx_ref[0, rows, :width] = lax.dot_general(
+                down, up_ref[0], (((1,), (1,)), ((), ())), preferred_element_type=jnp.float32
+            ).astype(jnp.bfloat16)
+            high = dot.astype(jnp.bfloat16).astype(jnp.float32)
+            dx_ref[0, rows, width:] = jnp.where(
+                lane == expert, high, jnp.where(lane == expert + expert_count, dot - high, 0.0)
+            ).astype(jnp.bfloat16)
+            return carry
+
+        lax.fori_loop(0, tiles_ref[expert], tile, 0)
+
+        def weights(depth):
+            rows = pl.ds(0, depth)
+            for i in range(width // TILE):
+                part = pl.ds(i * TILE, TILE)
+                dup_ref[0, part, :] = lax.dot_general(
+                    x_ref[0, rows, part], dpre[rows, :], (((0,), (0,)), ((), ())),
+                    preferred_element_type=jnp.float32,
+                ).astype(jnp.bfloat16)
+                ddown_ref[0, part, :] = lax.dot_general(
+                    g_ref[0, rows, part], mixed[rows, :], (((0,), (0,)), ((), ())),
+                    preferred_element_type=jnp.float32,
+                ).astype(jnp.bfloat16)
+
+        pl.when(tiles_ref[expert] <= 3)(lambda: weights(3 * TILE))
+        pl.when(tiles_ref[expert] > 3)(lambda: weights(room))
+
+    def whole(*dims):
+        return pl.BlockSpec((1, *dims), lambda e, tiles: (e + first, 0, 0))
+
+    def own(*dims):
+        return pl.BlockSpec((1, *dims), lambda e, tiles: (e, 0, 0))
+
+    shapes = [
+        ((room, width), jnp.bfloat16),
+        ((room, cols), jnp.bfloat16),
+        ((width, hidden), jnp.bfloat16),
+        ((width, hidden), jnp.bfloat16),
+        ((1, hidden), jnp.float32),
+    ]
+    return pl.pallas_call(
+        kernel,
+        grid_spec=pltpu.PrefetchScalarGridSpec(
+            num_scalar_prefetch=1,
+            grid=(count,),
+            in_specs=[
+                whole(room, cols),
+                whole(room, width),
+                whole(width, hidden),
+                whole(1, hidden),
+                whole(hidden, width),
+            ],
+            out_specs=[own(*dims) for dims, _ in shapes],
+            scratch_shapes=[pltpu.VMEM((room, hidden), jnp.bfloat16)] * 2,
+        ),
+        out_shape=[jax.ShapeDtypeStruct((count, *dims), kind) for dims, kind in shapes],
+        compiler_params=pltpu.CompilerParams(vmem_limit_bytes=VMEM),
+        cost_estimate=pl.CostEstimate(
+            flops=count * 12 * 768 * width * hidden,
+            bytes_accessed=count * (4 * room * (cols + width) + 8 * width * hidden),
+            transcendentals=count * 768 * hidden,
+        ),
+        name="experts",
+    )(tiles, inputs, grads, up_weight, up_bias[:, None, :], down_weight)
 
 
 def on_device(
@@ -134,48 +409,40 @@
     moe_normed = moe_norm.astype(jnp.bfloat16)
     logits = jnp.dot(moe_normed, router_weight, preferred_element_type=jnp.float32)
     gate_probs = jax.nn.softmax(logits, axis=-1)
-    choose = (
-        routes[:, :, None] == jnp.arange(expert_count, dtype=jnp.int32)[None, None, :]
-    ).astype(jnp.float32)
-    mixing = gate_probs * jnp.sum(choose, axis=1)
-    picked = jnp.sum(gate_probs[:, None, :] * choose, axis=-1)
-    flat_expert = routes.reshape(-1)
-    route_hot = choose.reshape(-1, expert_count).astype(jnp.int32)
-    before = jnp.cumsum(route_hot, axis=0) - route_hot
-    slot_index = jnp.sum(before * route_hot, axis=1)
-    target = flat_expert * CAP + slot_index
-    route_count = flat_expert.shape[0]
-    route_of_slot = (
-        jnp.full((expert_count * CAP,), route_count, jnp.int32)
-        .at[target]
-        .set(jnp.arange(route_count, dtype=jnp.int32))
-    )
-    token_of_slot = route_of_slot // TOP
-    padded = jnp.concatenate(
-        [moe_normed, jnp.zeros((1, moe_normed.shape[1]), jnp.bfloat16)], axis=0
-    )
-    buffers = padded[token_of_slot].reshape(expert_count, CAP, moe_normed.shape[1])
-    pre_act = (
-        jnp.einsum("ecd,edf->ecf", buffers, up_weight, preferred_element_type=jnp.float32)
-        + up_bias.astype(jnp.float32)[:, None, :]
-    )
-    activated, gelu_back = jax.vjp(jax.nn.gelu, pre_act)
-    activated_low = activated.astype(jnp.bfloat16)
-    expert_out = jnp.einsum(
-        "ecf,efd->ecd", activated_low, down_weight, preferred_element_type=jnp.float32
-    )
-    route_out = expert_out.reshape(expert_count * CAP, -1)[target].reshape(tok_rows, TOP, -1)
-    moe_part = jnp.sum(picked[:, :, None] * route_out, axis=1)
-    moe_total = tensor_sum(moe_part.astype(jnp.bfloat16))
+    experts = jnp.arange(expert_count, dtype=jnp.int32)[None, :]
+    mask = ((routes[:, :1] == experts) | (routes[:, 1:] == experts)).astype(jnp.float32)
+    mixing = gate_probs * mask
+    rows, columns, plan, tiles = route_plan(routes, expert_count)
+    blank = rows.shape[0] * BLOCK - tok_rows
+    grad_buffers = spread(jnp.pad(cotangent, ((0, blank), (0, 0))), rows, plan, expert_count)
+    mix_high = mixing.astype(jnp.bfloat16)
+    mix_low = (mixing - mix_high.astype(jnp.float32)).astype(jnp.bfloat16)
+    wide = jnp.concatenate([moe_normed, mix_high, mix_low], axis=1)
+    wide = jnp.pad(wide, ((0, blank), (0, 128 - 2 * expert_count)))
+    buffers = spread(wide, rows, plan, expert_count)
+    group = expert_count // GROUPS
+    outs = []
+    for i in range(GROUPS):
+        outs.append(
+            expert_pass(
+                buffers, grad_buffers, up_weight, up_bias, down_weight, tiles, i * group, group
+            )
+        )
+    y_buffers, back_buffers, up_parts, down_parts, bias_parts = zip(*outs)
+    back_part, dots = collect(back_buffers, columns, plan, moe_normed.shape[1])
+    back_part = back_part[:tok_rows]
+    (moe_part,) = collect(y_buffers, columns, plan, moe_normed.shape[1])
+    moe_part = moe_part[:tok_rows]
+    grad_up_bias = jnp.concatenate(bias_parts)[:, 0]
+    moe_total = tensor_sum(moe_part)
     down_bias_f = down_bias.astype(jnp.float32)
     layer_out = middle + moe_total + jnp.dot(mixing, down_bias_f, precision=HIGHEST)
     upstream = cotangent.astype(jnp.float32)
     grad_down_bias = jnp.dot(mixing.T, upstream, precision=HIGHEST)
     bias_dot = jnp.dot(cotangent, down_bias.T, preferred_element_type=jnp.float32)
-    route_dot_part = jnp.sum(route_out * upstream[:, None, :], axis=-1)
-    route_dot = small_sum(route_dot_part, "tensor")
-    grad_picked = route_dot + jnp.sum(bias_dot[:, None, :] * choose, axis=-1)
-    grad_gates = jnp.sum(choose * grad_picked[:, :, None], axis=1)
+    dots = dots[:tok_rows, : 2 * expert_count].T
+    route_dot = small_sum(dots[:expert_count] + dots[expert_count:], "tensor").T
+    grad_gates = route_dot + bias_dot * mask
     grad_logits = gate_probs * (
         grad_gates - jnp.sum(gate_probs * grad_gates, axis=-1, keepdims=True)
     )
@@ -186,27 +453,7 @@
     router_back = lax.dot_general(
         grad_logits_low, router_weight, (((1,), (1,)), ((), ())), preferred_element_type=jnp.float32
     )
-    route_grad = (
-        (picked[:, :, None] * upstream[:, None, :]).astype(jnp.bfloat16).reshape(route_count, -1)
-    )
-    route_grad_pad = jnp.concatenate(
-        [route_grad, jnp.zeros((1, route_grad.shape[1]), jnp.bfloat16)], axis=0
-    )
-    slot_grad = route_grad_pad[route_of_slot].reshape(expert_count, CAP, -1)
-    grad_down = jnp.einsum(
-        "ecf,ecd->edf", activated_low, slot_grad, preferred_element_type=jnp.float32
-    )
-    hidden_grad = jnp.einsum(
-        "ecd,efd->ecf", slot_grad, down_weight, preferred_element_type=jnp.float32
-    )
-    pre_grad = gelu_back(hidden_grad)[0].astype(jnp.bfloat16)
-    grad_up_bias = jnp.sum(pre_grad, axis=1, dtype=jnp.float32)
-    grad_up = jnp.einsum("ecd,ecf->edf", buffers, pre_grad, preferred_element_type=jnp.float32)
-    slot_back = jnp.einsum("ecf,edf->ecd", pre_grad, up_weight, preferred_element_type=jnp.float32)
-    back_part = jnp.sum(
-        slot_back.reshape(expert_count * CAP, -1)[target].reshape(tok_rows, TOP, -1), axis=1
-    )
-    back_total = tensor_sum(back_part.astype(jnp.bfloat16))
+    back_total = tensor_sum(back_part)
     normed2_grad = back_total + router_back
     middle_grad_ln, grad_moe_gain, grad_moe_shift = moe_norm_back(normed2_grad)
     middle_grad = upstream + middle_grad_ln
@@ -252,12 +499,13 @@
         "cth,cdh->td", grad_proj, qkv_weight, preferred_element_type=jnp.float32
     )
     normed_grad = tensor_sum(normed_back.astype(jnp.bfloat16))
-    embed_grad_ln, grad_attn_gain, grad_attn_shift = attn_norm_back(normed_grad)
+    embed_grad_ln = attn_norm_back(normed_grad)[0]
+    _, grad_attn_gain, grad_attn_shift = attn_norm_back(normed_back)
+    norm_parts = small_sum(jnp.stack([grad_attn_gain, grad_attn_shift]), "tensor")
     grad_embedded = middle_grad + embed_grad_ln
     width = embedded.shape[1]
     pieces = (
-        grad_attn_gain[None],
-        grad_attn_shift[None],
+        norm_parts,
         grad_out_bias[None],
         grad_moe_gain[None],
         grad_moe_shift[None],
@@ -272,8 +520,9 @@
     grad_router = packed[7 : 7 + expert_count].T
     grad_up_bias = packed[7 + expert_count : 7 + 2 * expert_count]
     grad_down_bias = packed[7 + 2 * expert_count :]
-    grad_up = ring_scatter(grad_up.astype(jnp.bfloat16), 1)
-    grad_down = ring_scatter(grad_down.astype(jnp.bfloat16), -1).transpose(0, 2, 1)
+    grad_up = jnp.concatenate([ring_scatter(part, 1) for part in up_parts])
+    grad_down = jnp.concatenate([ring_scatter(part, -1) for part in down_parts])
+    grad_down = grad_down.transpose(0, 2, 1)
     grad_qkv = ring_scatter(grad_qkv.astype(jnp.bfloat16), 1)
     grad_out = ring_scatter(grad_out.T[None].astype(jnp.bfloat16), -1)[0].T
     return (

time: 917 us -> 720 us (0.79)
  local copies, waits for them, and re-layouts: 293 us -> 104 us
  Pallas kernels: 0 us -> 136 us
  matrix products: 173 us -> 70.3 us
  other arithmetic: 208 us -> 114 us
  waiting for transfers between devices: 165 us -> 197 us
  starting transfers between devices: 46.3 us -> 69 us
    pallas_call x0 -> x6, Pallas kernels: none -> 136 us  [the longest x2 70.1 us: expert_pass(): pl.pallas_call(kernel, grid_spec=pltpu.PrefetchScalarGridSpec(num_scalar_...]
    dot_general x6 -> x1, matrix products: 113 us -> 0.24 us  [route_plan(): jnp.dot(named.astype(jnp.bfloat16), ahead.astype(jnp.bfloat16), preferred...]
    gather x4 -> x0, local copies, waits for them, and re-layouts: 112 us -> none  [the longest x1 32 us: on_device(): slot_grad = route_grad_pad[route_of_slot].reshape(expert_count, CAP, -1)]
    reduce_sum x6 -> x3, other arithmetic: 98.8 us -> 0.4 us  [the longest x1 0.22 us: route_plan(): jnp.sum(named.astype(jnp.int32), axis=1).reshape(expert_count, blocks) + 15]
    mul x5 -> x1, local copies, waits for them, and re-layouts: 37.1 us -> 0.08 us  [route_plan(): 16 * inside[:, :, None]]
    reshape x4, local copies, waits for them, and re-layouts: 34.6 us -> 0.28 us  [the longest x1 0.08 us: route_plan(): inside.T.reshape(-1)]
    ppermute x28 -> x42, waiting for transfers between devices: 89.7 us -> 121 us  [ring_scatter(): got = lax.ppermute(moving, 'dp', path)]
    ppermute x28 -> x42, starting transfers between devices: 32 us -> 55 us  [ring_scatter(): got = lax.ppermute(moving, 'dp', path)]
  transfers between devices with their start and end apart: 45 -> 61, of which waited for: 18 -> 29; matrix products, arithmetic and copies ran while one was open for 45% -> 27% of each run, Pallas kernels for 0% -> 7%
where the time goes in v2:
time: 720 us; the launch traced here: 713 us
  waiting for transfers between devices  197 us (27%)
  Pallas kernels  136 us (19%)
  other arithmetic  114 us (16%)
  local copies, waits for them, and re-layouts  104 us (14%)
  matrix products  70.3 us (10%)
  starting transfers between devices  69 us (10%)
  between operations  23.7 us (3%)
    ppermute x42, waiting for transfers between devices, ring_scatter(): got = lax.ppermute(moving, 'dp', path)  121 us
    pallas_call x2, Pallas kernels, expert_pass(): pl.pallas_call(kernel, grid_spec=pltpu.PrefetchScalarGridSpec(num_scalar_...  70.1 us
    ppermute x4, waiting for transfers between devices, tensor_sum(): far = lax.ppermute(both, 'tensor', pairs(4, 2))  63.8 us
    ppermute x42, starting transfers between devices, ring_scatter(): got = lax.ppermute(moving, 'dp', path)  55 us
    pallas_call x2, Pallas kernels, spread(): pl.pallas_call(kernel, grid_spec=pltpu.PrefetchScalarGridSpec(num_scalar_...  33.1 us
    pallas_call x2, Pallas kernels, collect(): pl.pallas_call(kernel, grid_spec=pltpu.PrefetchScalarGridSpec(num_scalar_...  33 us
    unnamed x182, local copies, waits for them, and re-layouts  20.5 us
    convert_element_type x36, other arithmetic, ring_scatter(): moving = total.astype(jnp.bfloat16) if step < count - 1 else total  17.6 us
  transfers between devices with their start and end apart: 61, of which 29 were waited for; matrix products, arithmetic and copies ran while one was open for 27% of the time, Pallas kernels for 7%

profile of v2, /device:TPU:0, one launch (start us, length us, event | category | flops | bytes accessed | tf_op | source)
XLA Modules:
  0.0 713.5 jit_solution(12687215688028643915)
XLA Ops:
  9.9 4.8 unstack.51
  14.7 5.7 unstack.53
  20.4 4.0 multiply_reduce_fusion.4
  27.5 3.6 unstack.49
  31.1 5.5 fusion.34
  46.6 3.7 collective-permute-done
  56.8 39.0 %collective-permute-done.1 = bf16[2364,384]{1,0:T(8,128)(2,1)} collective-permute-done((bf16[2364,384]{1,0:T(8,128)(2,1)S(1)}, bf16[2364,384]{1,0:T(8,128)(2,1)}, u32[]{:S(2)}, u32[]{:S(2)}) %collective-permute-start.1) | collective-permute-done | bytes 1815584 | tf_op jit(solution)/shard_map/ppermute | solution.py:40
  121.9 4.2 pad.18.source_ref
  130.1 15.5 %spread.3.g_ref = bf16[8,1024,768]{2,1,0:T(8,128)(2,1)} custom-call(s32[120]{0:T(128)} %pad_add_fusion.1.plan_ref, s32[5,2,512]{2,1,0:T(2,128)} %add_bitcast_fusion.rows_ref, bf16[2560,768]{1,0:T(8,128)(2,1)} %pad.18.source_ref), custom_call_target="tpu_custom_call" | custom-call | flops 4529848320 | bytes 16515072 | tf_op jit(solution)/shard_map/spread/pallas_call | solution.py:147
  165.5 8.2 %fusion.25.source_ref = bf16[2560,896]{1,0:T(8,128)(2,1)} fusion(bf16[2364,8]{1,0:T(8,128)(2,1)S(1)} %get-tuple-element.134, bf16[2364,8]{1,0:T(8,128)(2,1)S(1)} %get-tuple-element.133, bf16[2364,768]{1,0:T(8,128)(2,1)S(1)} %copy-done.7), kind=kLoop, calls=%fused_computation.51 | loop fusion | flops 34406400 | bytes 8294272 | tf_op jit(solution)/shard_map/concatenate | solution.py:420
  173.7 17.6 %spread.2.x_ref = bf16[8,1024,896]{2,1,0:T(8,128)(2,1)} custom-call(s32[120]{0:T(128)} %pad_add_fusion.1.plan_ref, s32[5,2,512]{2,1,0:T(2,128)} %add_bitcast_fusion.rows_ref, bf16[2560,896]{1,0:T(8,128)(2,1)} %fusion.25.source_ref), custom_call_target="tpu_custom_call" | custom-call | flops 5284823040 | bytes 19267584 | tf_op jit(solution)/shard_map/spread/pallas_call | solution.py:147
  191.3 31.3 %experts.2 = (bf16[4,1024,768]{2,1,0:T(8,128)(2,1)}, bf16[4,1024,896]{2,1,0:T(8,128)(2,1)}, bf16[4,768,768]{2,1,0:T(8,128)(2,1)}, bf16[4,768,768]{2,1,0:T(8,128)(2,1)}, f32[4,1,768]{2,1,0:T(1,128)}) custom-call(s32[8]{0:T(128)} %and_select_fusion.tiles_ref, bf16[8,1024,896]{2,1,0:T(8,128)(2,1)} %spread.2.x_ref, bf16[8,1024,768]{2,1,0:T(8,128)(2,1)} %spread.3.g_ref, ...), custom_call_target="tpu_custom_call" | custom-call | flops 21743271936 | bytes 46137344 | tf_op jit(solution)/shard_map/experts/pallas_call | solution.py:330
  222.6 38.8 %experts.3 = (bf16[4,1024,768]{2,1,0:T(8,128)(2,1)}, bf16[4,1024,896]{2,1,0:T(8,128)(2,1)}, bf16[4,768,768]{2,1,0:T(8,128)(2,1)}, bf16[4,768,768]{2,1,0:T(8,128)(2,1)}, f32[4,1,768]{2,1,0:T(1,128)}) custom-call(s32[8]{0:T(128)} %and_select_fusion.tiles_ref, bf16[8,1024,896]{2,1,0:T(8,128)(2,1)} %spread.2.x_ref, bf16[8,1024,768]{2,1,0:T(8,128)(2,1)} %spread.3.g_ref, ...), custom_call_target="tpu_custom_call" | custom-call | flops 21743271936 | bytes 46137344 | tf_op jit(solution)/shard_map/experts/pallas_call | solution.py:330
  261.4 5.0 fusion.82
  268.4 3.4 collective-permute-start.47
  278.8 17.9 %collect.3 = (bf16[2560,768]{1,0:T(8,128)(2,1)}, f32[2560,128]{1,0:T(8,128)}) custom-call(s32[120]{0:T(128)} %pad_add_fusion.1.plan_ref, s32[2560,2]{1,0:T(8,128)} %bitcast.198, bf16[4,1024,896]{2,1,0:T(8,128)(2,1)} %get-tuple-element.29.refs_0_, bf16[4,1024,896]{2,1,0:T(8,128)(2,1)} %get-tuple-element.30.refs_1_), custom_call_target="tpu_custom_call" | custom-call | flops 5284823040 | bytes 19267584 | tf_op jit(solution)/shard_map/collect/pallas_call | solution.py:216
  307.7 15.1 %collect.2 = bf16[2560,768]{1,0:T(8,128)(2,1)} custom-call(s32[120]{0:T(128)} %pad_add_fusion.1.plan_ref, s32[2560,2]{1,0:T(8,128)} %bitcast.199, bf16[4,1024,768]{2,1,0:T(8,128)(2,1)} %get-tuple-element.27.refs_0_, bf16[4,1024,768]{2,1,0:T(8,128)(2,1)} %get-tuple-element.28.refs_1_), custom_call_target="tpu_custom_call" | custom-call | flops 4529848320 | bytes 16515072 | tf_op jit(solution)/shard_map/collect/pallas_call | solution.py:216
  330.6 3.4 fusion.127
  337.8 3.4 collective-permute-done.10
  342.7 5.4 multiply_reduce_fusion.5
  361.8 8.0 %collective-permute-done.48 = bf16[4,96,768]{2,1,0:T(8,128)(2,1)S(1)} collective-permute-done((bf16[4,96,768]{2,1,0:T(8,128)(2,1)S(1)}, bf16[4,96,768]{2,1,0:T(8,128)(2,1)S(1)}, u32[]{:S(2)}, u32[]{:S(2)}) %collective-permute-start.48) | collective-permute-done | bytes 589856 | tf_op jit(solution)/shard_map/ppermute | solution.py:75
  372.5 9.1 %collective-permute-done.55 = bf16[4,96,768]{2,1,0:T(8,128)(2,1)S(1)} collective-permute-done((bf16[4,96,768]{2,1,0:T(8,128)(2,1)S(1)}, bf16[4,96,768]{2,1,0:T(8,128)(2,1)S(1)}, u32[]{:S(2)}, u32[]{:S(2)}) %collective-permute-start.55) | collective-permute-done | bytes 589856 | tf_op jit(solution)/shard_map/ppermute | solution.py:75
  388.1 9.7 %collective-permute-done.49 = bf16[4,96,768]{2,1,0:T(8,128)(2,1)S(1)} collective-permute-done((bf16[4,96,768]{2,1,0:T(8,128)(2,1)S(1)}, bf16[4,96,768]{2,1,0:T(8,128)(2,1)S(1)}, u32[]{:S(2)}, u32[]{:S(2)}) %collective-permute-start.49) | collective-permute-done | bytes 589856 | tf_op jit(solution)/shard_map/ppermute | solution.py:75
  400.6 8.1 %collective-permute-done.56 = bf16[4,96,768]{2,1,0:T(8,128)(2,1)S(1)} collective-permute-done((bf16[4,96,768]{2,1,0:T(8,128)(2,1)S(1)}, bf16[4,96,768]{2,1,0:T(8,128)(2,1)S(1)}, u32[]{:S(2)}, u32[]{:S(2)}) %collective-permute-start.56) | collective-permute-done | bytes 589856 | tf_op jit(solution)/shard_map/ppermute | solution.py:75
  419.6 5.3 collective-permute-done.50
  426.6 8.8 %collective-permute-done.57 = bf16[4,96,768]{2,1,0:T(8,128)(2,1)S(1)} collective-permute-done((bf16[4,96,768]{2,1,0:T(8,128)(2,1)S(1)}, bf16[4,96,768]{2,1,0:T(8,128)(2,1)S(1)}, u32[]{:S(2)}, u32[]{:S(2)}) %collective-permute-start.57) | collective-permute-done | bytes 589856 | tf_op jit(solution)/shard_map/ppermute | solution.py:75
  440.7 11.0 %collective-permute-done.51 = bf16[4,96,768]{2,1,0:T(8,128)(2,1)S(1)} collective-permute-done((bf16[4,96,768]{2,1,0:T(8,128)(2,1)S(1)}, bf16[4,96,768]{2,1,0:T(8,128)(2,1)S(1)}, u32[]{:S(2)}, u32[]{:S(2)}) %collective-permute-start.51) | collective-permute-done | bytes 589856 | tf_op jit(solution)/shard_map/ppermute | solution.py:75
  453.6 8.0 %collective-permute-done.58 = bf16[4,96,768]{2,1,0:T(8,128)(2,1)S(1)} collective-permute-done((bf16[4,96,768]{2,1,0:T(8,128)(2,1)S(1)}, bf16[4,96,768]{2,1,0:T(8,128)(2,1)S(1)}, u32[]{:S(2)}, u32[]{:S(2)}) %collective-permute-start.58) | collective-permute-done | bytes 589856 | tf_op jit(solution)/shard_map/ppermute | solution.py:75
  467.1 10.7 %collective-permute-done.52 = bf16[4,96,768]{2,1,0:T(8,128)(2,1)S(1)} collective-permute-done((bf16[4,96,768]{2,1,0:T(8,128)(2,1)S(1)}, bf16[4,96,768]{2,1,0:T(8,128)(2,1)S(1)}, u32[]{:S(2)}, u32[]{:S(2)}) %collective-permute-start.52) | collective-permute-done | bytes 589856 | tf_op jit(solution)/shard_map/ppermute | solution.py:75
  479.7 8.0 %collective-permute-done.59 = bf16[4,96,768]{2,1,0:T(8,128)(2,1)S(1)} collective-permute-done((bf16[4,96,768]{2,1,0:T(8,128)(2,1)S(1)}, bf16[4,96,768]{2,1,0:T(8,128)(2,1)S(1)}, u32[]{:S(2)}, u32[]{:S(2)}) %collective-permute-start.59) | collective-permute-done | bytes 589856 | tf_op jit(solution)/shard_map/ppermute | solution.py:75
  498.5 5.4 collective-permute-done.53
  505.1 6.7 collective-permute-done.60
  517.3 9.0 %multiply_reduce_fusion.1 = (f32[768]{0:T(1024)S(1)}, f32[2364]{0:T(1024)S(1)}, f32[768]{0:T(1024)S(1)}, f32[2364,768]{1,0:T(8,128)}) fusion(f32[2364]{0:T(1024)S(1)} %fusion.71, bf16[2364,384]{1,0:T(8,128)(2,1)S(1)} %get-tuple-element.125, bf16[2364,384]{1,0:T(8,128)(2,1)S(1)} %get-tuple-element.124, f32[2364]{0:T(1024)S(1)} %broadcast_multiply_fusion, ...), kind=kOutput, calls=%fused_computation.29 | convolution fusion | flops 65355972 | bytes 18246288 | tf_op jit(solution)/shard_map/dot_general | solution.py:453
  526.3 7.8 %fusion.96 = (f32[2364]{0:T(1024)S(1)}, f32[2364,768]{1,0:T(8,128)S(1)}) fusion(f32[2364]{0:T(1024)S(1)} %multiply_multiply_fusion.1, f32[2364]{0:T(1024)S(1)} %broadcast_multiply_fusion, f32[768]{0:T(1024)S(1)} %convert_element_type.617, bf16[2364,384]{1,0:T(8,128)(2,1)S(1)} %copy-done.11, bf16[2364,384]{1,0:T(8,128)(2,1)S(1)} %get-tuple-element.128, ...), kind=kLoop, calls=%fused_computation.257 | loop fusion | flops 34493124 | bytes 25461696 | tf_op jit(solution)/shard_map/transpose(jvp())/reduce_sum | solution.py:18
  534.1 5.5 convert_reduce_fusion.1
  543.8 5.3 reshape.488
  549.1 5.4 fusion.35
  554.6 5.6 multiply_reduce_fusion
  568.7 3.8 stack.39
  575.5 3.8 stack.38
  582.4 3.9 stack.37
  589.2 5.9 bitcast_convert_fusion
  612.7 8.5 %add_convert_fusion = bf16[2364,768]{1,0:T(8,128)(2,1)} fusion(bf16[2364,768]{1,0:T(8,128)(2,1)S(1)} %copy-done.4, bf16[2364,384]{1,0:T(8,128)(2,1)S(1)} %get-tuple-element.127, bf16[2364,384]{1,0:T(8,128)(2,1)S(1)} %get-tuple-element.126, f32[768]{0:T(1024)S(1)} %convert_element_type.617, bf16[2364,384]{1,0:T(8,128)(2,1)S(1)} %copy-done.12, ...), kind=kOutput, calls=%fused_computation.36 | convolution fusion | flops 199824192 | bytes 14653248 | tf_op jit(solution)/shard_map/dot_general | solution.py:439
  626.7 22.8 %collective-permute-done.12 = bf16[2364,384]{1,0:T(8,128)(2,1)S(1)} collective-permute-done((bf16[2364,384]{1,0:T(8,128)(2,1)S(1)}, bf16[2364,384]{1,0:T(8,128)(2,1)S(1)}, u32[]{:S(2)}, u32[]{:S(2)}) %collective-permute-start.12) | collective-permute-done | bytes 1815584 | tf_op jit(solution)/shard_map/ppermute | solution.py:40
  671.8 6.9 fusion.12
  689.9 4.0 collective-permute-done.25
  696.2 4.3 collective-permute-done.17
  701.5 9.9 %add_add_fusion.2 = f32[2364,768]{1,0:T(8,128)} fusion(bf16[2364,768]{1,0:T(8,128)(2,1)} %param.28, f32[2364,768]{1,0:T(8,128)} %copy-done.9, bf16[2364,768]{1,0:T(8,128)(2,1)} %param.43, f32[2364]{0:T(1024)S(1)} %negate_multiply_fusion, f32[2364]{0:T(1024)S(1)} %multiply_multiply_fusion, f32[2364]{0:T(1024)S(1)} %negate_multiply_fusion.1, ...), kind=kLoop, calls=%fused_computation.31 | loop fusion | flops 29048832 | bytes 25468080 | tf_op jit(solution)/shard_map/add | solution.py:505
  (468 shorter events, 243.0 us)
Async XLA Ops:
  52.8 43.0 %collective-permute-start.1 = (bf16[2364,384]{1,0:T(8,128)(2,1)S(1)}, bf16[2364,384]{1,0:T(8,128)(2,1)}, u32[]{:S(2)}, u32[]{:S(2)}) collective-permute-start(bf16[2364,384]{1,0:T(8,128)(2,1)S(1)} %add_convert_fusion.10), channel_id=1, source_target_pairs={{0,2},{1,3},{2,0},{3,1},{4,6},{5,7},{6,4},{7,5},{8,10},{9,11},{10,... | collective-permute-start | bytes 5446664 | tf_op jit(solution)/shard_map/ppermute | solution.py:40
  98.3 47.2 %collective-permute-start.2 = (bf16[2364,384]{1,0:T(8,128)(2,1)S(1)}, bf16[2364,384]{1,0:T(8,128)(2,1)}, u32[]{:S(2)}, u32[]{:S(2)}) collective-permute-start(bf16[2364,384]{1,0:T(8,128)(2,1)S(1)} %add_convert_fusion.9), channel_id=1, source_target_pairs={{0,1},{1,0},{2,3},{3,2},{4,5},{5,4},{6,7},{7,6},{8,9},{9,8},{10,11... | collective-permute-start | bytes 5446664 | tf_op jit(solution)/shard_map/ppermute | solution.py:42
  268.4 82.5 %collective-permute-start.47 = (bf16[4,96,768]{2,1,0:T(8,128)(2,1)}, bf16[4,96,768]{2,1,0:T(8,128)(2,1)}, u32[]{:S(2)}, u32[]{:S(2)}) collective-permute-start(bf16[4,96,768]{2,1,0:T(8,128)(2,1)} %constant_dynamic-slice_fusion.2), channel_id=1, source_target_pairs={{0,4},{8,0},{16,8},{24,16},{28,24},{20,28},{12,20},{4,12},{1,5},{9... | collective-permute-start | bytes 1769480 | tf_op jit(solution)/shard_map/ppermute | solution.py:75
  273.7 79.9 %collective-permute-start.54 = (bf16[4,96,768]{2,1,0:T(8,128)(2,1)}, bf16[4,96,768]{2,1,0:T(8,128)(2,1)}, u32[]{:S(2)}, u32[]{:S(2)}) collective-permute-start(bf16[4,96,768]{2,1,0:T(8,128)(2,1)} %constant_dynamic-slice_fusion.1), channel_id=1, source_target_pairs={{0,4},{8,0},{16,8},{24,16},{28,24},{20,28},{12,20},{4,12},{1,5},{9... | collective-permute-start | bytes 1769480 | tf_op jit(solution)/shard_map/ppermute | solution.py:75
  275.6 81.4 %collective-permute-start.33 = (bf16[4,96,768]{2,1,0:T(8,128)(2,1)}, bf16[4,96,768]{2,1,0:T(8,128)(2,1)}, u32[]{:S(2)}, u32[]{:S(2)}) collective-permute-start(bf16[4,96,768]{2,1,0:T(8,128)(2,1)} %constant_dynamic-slice_fusion.3), channel_id=1, source_target_pairs={{0,8},{8,16},{16,24},{24,28},{28,20},{20,12},{12,4},{4,0},{1,9},{9... | collective-permute-start | bytes 1769480 | tf_op jit(solution)/shard_map/ppermute | solution.py:75
  278.7 79.8 %collective-permute-start.40 = (bf16[4,96,768]{2,1,0:T(8,128)(2,1)S(1)}, bf16[4,96,768]{2,1,0:T(8,128)(2,1)}, u32[]{:S(2)}, u32[]{:S(2)}) collective-permute-start(bf16[4,96,768]{2,1,0:T(8,128)(2,1)S(1)} %constant_dynamic-slice_fusion), channel_id=1, source_target_pairs={{0,8},{8,16},{16,24},{24,28},{28,20},{20,12},{12,4},{4,0},{1,9},{9... | collective-permute-start | bytes 1769480 | tf_op jit(solution)/shard_map/ppermute | solution.py:75
  302.1 26.1 %collective-permute-start.9 = (f32[8,2364]{1,0:T(8,128)S(1)}, f32[8,2364]{1,0:T(8,128)}, u32[]{:S(2)}, u32[]{:S(2)}) collective-permute-start(f32[8,2364]{1,0:T(8,128)S(1)} %copy.124), channel_id=1, source_target_pairs={{0,1},{1,0},{2,3},{3,2},{4,5},{5,4},{6,7},{7,6},{8,9},{9,8},{10,11... | collective-permute-start | bytes 226952 | tf_op jit(solution)/shard_map/ppermute | solution.py:54
  341.3 73.3 %collective-permute-start.6 = (bf16[2364,384]{1,0:T(8,128)(2,1)}, bf16[2364,384]{1,0:T(8,128)(2,1)}, u32[]{:S(2)}, u32[]{:S(2)}) collective-permute-start(bf16[2364,384]{1,0:T(8,128)(2,1)} %constant_dynamic-slice_fusion.5), channel_id=1, source_target_pairs={{0,1},{1,0},{2,3},{3,2},{4,5},{5,4},{6,7},{7,6},{8,9},{9,8},{10,11... | collective-permute-start | bytes 5446664 | tf_op jit(solution)/shard_map/ppermute | solution.py:38
  350.8 66.7 %collective-permute-start.3 = (bf16[2364,384]{1,0:T(8,128)(2,1)S(1)}, bf16[2364,384]{1,0:T(8,128)(2,1)S(1)}, u32[]{:S(2)}, u32[]{:S(2)}) collective-permute-start(bf16[2364,384]{1,0:T(8,128)(2,1)S(1)} %copy-done.44), channel_id=1, source_target_pairs={{0,1},{1,0},{2,3},{3,2},{4,5},{5,4},{6,7},{7,6},{8,9},{9,8},{10,11... | collective-permute-start | bytes 5446664 | tf_op jit(solution)/shard_map/ppermute | solution.py:38
  353.6 16.2 %collective-permute-start.48 = (bf16[4,96,768]{2,1,0:T(8,128)(2,1)S(1)}, bf16[4,96,768]{2,1,0:T(8,128)(2,1)S(1)}, u32[]{:S(2)}, u32[]{:S(2)}) collective-permute-start(bf16[4,96,768]{2,1,0:T(8,128)(2,1)S(1)} %add_convert_fusion.22), channel_id=1, source_target_pairs={{0,4},{8,0},{16,8},{24,16},{28,24},{20,28},{12,20},{4,12},{1,5},{9... | collective-permute-start | bytes 1769480 | tf_op jit(solution)/shard_map/ppermute | solution.py:75
  357.0 24.5 %collective-permute-start.55 = (bf16[4,96,768]{2,1,0:T(8,128)(2,1)S(1)}, bf16[4,96,768]{2,1,0:T(8,128)(2,1)S(1)}, u32[]{:S(2)}, u32[]{:S(2)}) collective-permute-start(bf16[4,96,768]{2,1,0:T(8,128)(2,1)S(1)} %add_convert_fusion.16), channel_id=1, source_target_pairs={{0,4},{8,0},{16,8},{24,16},{28,24},{20,28},{12,20},{4,12},{1,5},{9... | collective-permute-start | bytes 1769480 | tf_op jit(solution)/shard_map/ppermute | solution.py:75
  358.6 26.4 %collective-permute-start.34 = (bf16[4,96,768]{2,1,0:T(8,128)(2,1)S(1)}, bf16[4,96,768]{2,1,0:T(8,128)(2,1)S(1)}, u32[]{:S(2)}, u32[]{:S(2)}) collective-permute-start(bf16[4,96,768]{2,1,0:T(8,128)(2,1)S(1)} %add_convert_fusion.34), channel_id=1, source_target_pairs={{0,8},{8,16},{16,24},{24,28},{28,20},{20,12},{12,4},{4,0},{1,9},{9... | collective-permute-start | bytes 1769480 | tf_op jit(solution)/shard_map/ppermute | solution.py:75
  369.8 16.5 %collective-permute-start.41 = (bf16[4,96,768]{2,1,0:T(8,128)(2,1)S(1)}, bf16[4,96,768]{2,1,0:T(8,128)(2,1)S(1)}, u32[]{:S(2)}, u32[]{:S(2)}) collective-permute-start(bf16[4,96,768]{2,1,0:T(8,128)(2,1)S(1)} %add_convert_fusion.28), channel_id=1, source_target_pairs={{0,8},{8,16},{16,24},{24,28},{28,20},{20,12},{12,4},{4,0},{1,9},{9... | collective-permute-start | bytes 1769480 | tf_op jit(solution)/shard_map/ppermute | solution.py:75
  381.5 16.3 %collective-permute-start.49 = (bf16[4,96,768]{2,1,0:T(8,128)(2,1)S(1)}, bf16[4,96,768]{2,1,0:T(8,128)(2,1)S(1)}, u32[]{:S(2)}, u32[]{:S(2)}) collective-permute-start(bf16[4,96,768]{2,1,0:T(8,128)(2,1)S(1)} %add_convert_fusion.21), channel_id=1, source_target_pairs={{0,4},{8,0},{16,8},{24,16},{28,24},{20,28},{12,20},{4,12},{1,5},{9... | collective-permute-start | bytes 1769480 | tf_op jit(solution)/shard_map/ppermute | solution.py:75
  385.0 23.7 %collective-permute-start.56 = (bf16[4,96,768]{2,1,0:T(8,128)(2,1)S(1)}, bf16[4,96,768]{2,1,0:T(8,128)(2,1)S(1)}, u32[]{:S(2)}, u32[]{:S(2)}) collective-permute-start(bf16[4,96,768]{2,1,0:T(8,128)(2,1)S(1)} %add_convert_fusion.15), channel_id=1, source_target_pairs={{0,4},{8,0},{16,8},{24,16},{28,24},{20,28},{12,20},{4,12},{1,5},{9... | collective-permute-start | bytes 1769480 | tf_op jit(solution)/shard_map/ppermute | solution.py:75
  386.3 25.6 %collective-permute-start.35 = (bf16[4,96,768]{2,1,0:T(8,128)(2,1)S(1)}, bf16[4,96,768]{2,1,0:T(8,128)(2,1)S(1)}, u32[]{:S(2)}, u32[]{:S(2)}) collective-permute-start(bf16[4,96,768]{2,1,0:T(8,128)(2,1)S(1)} %add_convert_fusion.33), channel_id=1, source_target_pairs={{0,8},{8,16},{16,24},{24,28},{28,20},{20,12},{12,4},{4,0},{1,9},{9... | collective-permute-start | bytes 1769480 | tf_op jit(solution)/shard_map/ppermute | solution.py:75
  397.8 15.2 %collective-permute-start.42 = (bf16[4,96,768]{2,1,0:T(8,128)(2,1)S(1)}, bf16[4,96,768]{2,1,0:T(8,128)(2,1)S(1)}, u32[]{:S(2)}, u32[]{:S(2)}) collective-permute-start(bf16[4,96,768]{2,1,0:T(8,128)(2,1)S(1)} %add_convert_fusion.27), channel_id=1, source_target_pairs={{0,8},{8,16},{16,24},{24,28},{28,20},{20,12},{12,4},{4,0},{1,9},{9... | collective-permute-start | bytes 1769480 | tf_op jit(solution)/shard_map/ppermute | solution.py:75
  408.6 16.3 %collective-permute-start.50 = (bf16[4,96,768]{2,1,0:T(8,128)(2,1)S(1)}, bf16[4,96,768]{2,1,0:T(8,128)(2,1)S(1)}, u32[]{:S(2)}, u32[]{:S(2)}) collective-permute-start(bf16[4,96,768]{2,1,0:T(8,128)(2,1)S(1)} %add_convert_fusion.20), channel_id=1, source_target_pairs={{0,4},{8,0},{16,8},{24,16},{28,24},{20,28},{12,20},{4,12},{1,5},{9... | collective-permute-start | bytes 1769480 | tf_op jit(solution)/shard_map/ppermute | solution.py:75
  411.9 23.5 %collective-permute-start.57 = (bf16[4,96,768]{2,1,0:T(8,128)(2,1)S(1)}, bf16[4,96,768]{2,1,0:T(8,128)(2,1)S(1)}, u32[]{:S(2)}, u32[]{:S(2)}) collective-permute-start(bf16[4,96,768]{2,1,0:T(8,128)(2,1)S(1)} %add_convert_fusion.14), channel_id=1, source_target_pairs={{0,4},{8,0},{16,8},{24,16},{28,24},{20,28},{12,20},{4,12},{1,5},{9... | collective-permute-start | bytes 1769480 | tf_op jit(solution)/shard_map/ppermute | solution.py:75
  413.0 24.0 %collective-permute-start.36 = (bf16[4,96,768]{2,1,0:T(8,128)(2,1)S(1)}, bf16[4,96,768]{2,1,0:T(8,128)(2,1)S(1)}, u32[]{:S(2)}, u32[]{:S(2)}) collective-permute-start(bf16[4,96,768]{2,1,0:T(8,128)(2,1)S(1)} %add_convert_fusion.32), channel_id=1, source_target_pairs={{0,8},{8,16},{16,24},{24,28},{28,20},{20,12},{12,4},{4,0},{1,9},{9... | collective-permute-start | bytes 1769480 | tf_op jit(solution)/shard_map/ppermute | solution.py:75
  414.6 24.5 %collective-permute-start.43 = (bf16[4,96,768]{2,1,0:T(8,128)(2,1)S(1)}, bf16[4,96,768]{2,1,0:T(8,128)(2,1)S(1)}, u32[]{:S(2)}, u32[]{:S(2)}) collective-permute-start(bf16[4,96,768]{2,1,0:T(8,128)(2,1)S(1)} %add_convert_fusion.26), channel_id=1, source_target_pairs={{0,8},{8,16},{16,24},{24,28},{28,20},{20,12},{12,4},{4,0},{1,9},{9... | collective-permute-start | bytes 1769480 | tf_op jit(solution)/shard_map/ppermute | solution.py:75
  417.5 72.9 %collective-permute-start.7 = (bf16[2364,384]{1,0:T(8,128)(2,1)S(1)}, bf16[2364,384]{1,0:T(8,128)(2,1)S(1)}, u32[]{:S(2)}, u32[]{:S(2)}) collective-permute-start(bf16[2364,384]{1,0:T(8,128)(2,1)S(1)} %add_convert_fusion.6), channel_id=1, source_target_pairs={{0,2},{1,3},{2,0},{3,1},{4,6},{5,7},{6,4},{7,5},{8,10},{9,11},{10,... | collective-permute-start | bytes 5446664 | tf_op jit(solution)/shard_map/ppermute | solution.py:40
  424.9 70.3 %collective-permute-start.4 = (bf16[2364,384]{1,0:T(8,128)(2,1)S(1)}, bf16[2364,384]{1,0:T(8,128)(2,1)S(1)}, u32[]{:S(2)}, u32[]{:S(2)}) collective-permute-start(bf16[2364,384]{1,0:T(8,128)(2,1)S(1)} %add_convert_fusion.8), channel_id=1, source_target_pairs={{0,2},{1,3},{2,0},{3,1},{4,6},{5,7},{6,4},{7,5},{8,10},{9,11},{10,... | collective-permute-start | bytes 5446664 | tf_op jit(solution)/shard_map/ppermute | solution.py:40
  435.4 16.3 %collective-permute-start.51 = (bf16[4,96,768]{2,1,0:T(8,128)(2,1)S(1)}, bf16[4,96,768]{2,1,0:T(8,128)(2,1)S(1)}, u32[]{:S(2)}, u32[]{:S(2)}) collective-permute-start(bf16[4,96,768]{2,1,0:T(8,128)(2,1)S(1)} %add_convert_fusion.19), channel_id=1, source_target_pairs={{0,4},{8,0},{16,8},{24,16},{28,24},{20,28},{12,20},{4,12},{1,5},{9... | collective-permute-start | bytes 1769480 | tf_op jit(solution)/shard_map/ppermute | solution.py:75
  437.0 24.5 %collective-permute-start.58 = (bf16[4,96,768]{2,1,0:T(8,128)(2,1)S(1)}, bf16[4,96,768]{2,1,0:T(8,128)(2,1)S(1)}, u32[]{:S(2)}, u32[]{:S(2)}) collective-permute-start(bf16[4,96,768]{2,1,0:T(8,128)(2,1)S(1)} %add_convert_fusion.13), channel_id=1, source_target_pairs={{0,4},{8,0},{16,8},{24,16},{28,24},{20,28},{12,20},{4,12},{1,5},{9... | collective-permute-start | bytes 1769480 | tf_op jit(solution)/shard_map/ppermute | solution.py:75
  439.1 24.1 %collective-permute-start.37 = (bf16[4,96,768]{2,1,0:T(8,128)(2,1)S(1)}, bf16[4,96,768]{2,1,0:T(8,128)(2,1)S(1)}, u32[]{:S(2)}, u32[]{:S(2)}) collective-permute-start(bf16[4,96,768]{2,1,0:T(8,128)(2,1)S(1)} %add_convert_fusion.31), channel_id=1, source_target_pairs={{0,8},{8,16},{16,24},{24,28},{28,20},{20,12},{12,4},{4,0},{1,9},{9... | collective-permute-start | bytes 1769480 | tf_op jit(solution)/shard_map/ppermute | solution.py:75
  451.7 13.5 %collective-permute-start.44 = (bf16[4,96,768]{2,1,0:T(8,128)(2,1)S(1)}, bf16[4,96,768]{2,1,0:T(8,128)(2,1)S(1)}, u32[]{:S(2)}, u32[]{:S(2)}) collective-permute-start(bf16[4,96,768]{2,1,0:T(8,128)(2,1)S(1)} %add_convert_fusion.25), channel_id=1, source_target_pairs={{0,8},{8,16},{16,24},{24,28},{28,20},{20,12},{12,4},{4,0},{1,9},{9... | collective-permute-start | bytes 1769480 | tf_op jit(solution)/shard_map/ppermute | solution.py:75
  461.5 16.3 %collective-permute-start.52 = (bf16[4,96,768]{2,1,0:T(8,128)(2,1)S(1)}, bf16[4,96,768]{2,1,0:T(8,128)(2,1)S(1)}, u32[]{:S(2)}, u32[]{:S(2)}) collective-permute-start(bf16[4,96,768]{2,1,0:T(8,128)(2,1)S(1)} %add_convert_fusion.18), channel_id=1, source_target_pairs={{0,4},{8,0},{16,8},{24,16},{28,24},{20,28},{12,20},{4,12},{1,5},{9... | collective-permute-start | bytes 1769480 | tf_op jit(solution)/shard_map/ppermute | solution.py:75
  463.2 24.5 %collective-permute-start.59 = (bf16[4,96,768]{2,1,0:T(8,128)(2,1)S(1)}, bf16[4,96,768]{2,1,0:T(8,128)(2,1)S(1)}, u32[]{:S(2)}, u32[]{:S(2)}) collective-permute-start(bf16[4,96,768]{2,1,0:T(8,128)(2,1)S(1)} %add_convert_fusion.12), channel_id=1, source_target_pairs={{0,4},{8,0},{16,8},{24,16},{28,24},{20,28},{12,20},{4,12},{1,5},{9... | collective-permute-start | bytes 1769480 | tf_op jit(solution)/shard_map/ppermute | solution.py:75
  465.2 24.1 %collective-permute-start.38 = (bf16[4,96,768]{2,1,0:T(8,128)(2,1)S(1)}, bf16[4,96,768]{2,1,0:T(8,128)(2,1)S(1)}, u32[]{:S(2)}, u32[]{:S(2)}) collective-permute-start(bf16[4,96,768]{2,1,0:T(8,128)(2,1)S(1)} %add_convert_fusion.30), channel_id=1, source_target_pairs={{0,8},{8,16},{16,24},{24,28},{28,20},{20,12},{12,4},{4,0},{1,9},{9... | collective-permute-start | bytes 1769480 | tf_op jit(solution)/shard_map/ppermute | solution.py:75
  477.8 14.3 %collective-permute-start.45 = (bf16[4,96,768]{2,1,0:T(8,128)(2,1)S(1)}, bf16[4,96,768]{2,1,0:T(8,128)(2,1)S(1)}, u32[]{:S(2)}, u32[]{:S(2)}) collective-permute-start(bf16[4,96,768]{2,1,0:T(8,128)(2,1)S(1)} %add_convert_fusion.24), channel_id=1, source_target_pairs={{0,8},{8,16},{16,24},{24,28},{28,20},{20,12},{12,4},{4,0},{1,9},{9... | collective-permute-start | bytes 1769480 | tf_op jit(solution)/shard_map/ppermute | solution.py:75
  487.7 16.3 %collective-permute-start.53 = (bf16[4,96,768]{2,1,0:T(8,128)(2,1)S(1)}, bf16[4,96,768]{2,1,0:T(8,128)(2,1)S(1)}, u32[]{:S(2)}, u32[]{:S(2)}) collective-permute-start(bf16[4,96,768]{2,1,0:T(8,128)(2,1)S(1)} %add_convert_fusion.17), channel_id=1, source_target_pairs={{0,4},{8,0},{16,8},{24,16},{28,24},{20,28},{12,20},{4,12},{1,5},{9... | collective-permute-start | bytes 1769480 | tf_op jit(solution)/shard_map/ppermute | solution.py:75
  489.3 22.5 %collective-permute-start.60 = (bf16[4,96,768]{2,1,0:T(8,128)(2,1)S(1)}, bf16[4,96,768]{2,1,0:T(8,128)(2,1)S(1)}, u32[]{:S(2)}, u32[]{:S(2)}) collective-permute-start(bf16[4,96,768]{2,1,0:T(8,128)(2,1)S(1)} %add_convert_fusion.11), channel_id=1, source_target_pairs={{0,4},{8,0},{16,8},{24,16},{28,24},{20,28},{12,20},{4,12},{1,5},{9... | collective-permute-start | bytes 1769480 | tf_op jit(solution)/shard_map/ppermute | solution.py:75
  490.4 22.5 %collective-permute-start.39 = (bf16[4,96,768]{2,1,0:T(8,128)(2,1)S(1)}, bf16[4,96,768]{2,1,0:T(8,128)(2,1)S(1)}, u32[]{:S(2)}, u32[]{:S(2)}) collective-permute-start(bf16[4,96,768]{2,1,0:T(8,128)(2,1)S(1)} %add_convert_fusion.29), channel_id=1, source_target_pairs={{0,8},{8,16},{16,24},{24,28},{28,20},{20,12},{12,4},{4,0},{1,9},{9... | collective-permute-start | bytes 1769480 | tf_op jit(solution)/shard_map/ppermute | solution.py:75
  492.1 21.9 %collective-permute-start.8 = (bf16[2364,384]{1,0:T(8,128)(2,1)S(1)}, bf16[2364,384]{1,0:T(8,128)(2,1)S(1)}, u32[]{:S(2)}, u32[]{:S(2)}) collective-permute-start(bf16[2364,384]{1,0:T(8,128)(2,1)S(1)} %add_convert_fusion.5), channel_id=1, source_target_pairs={{0,1},{1,0},{2,3},{3,2},{4,5},{5,4},{6,7},{7,6},{8,9},{9,8},{10,11... | collective-permute-start | bytes 5446664 | tf_op jit(solution)/shard_map/ppermute | solution.py:42
  495.2 100.2 %collective-permute-start.46 = (bf16[4,96,768]{2,1,0:T(8,128)(2,1)}, bf16[4,96,768]{2,1,0:T(8,128)(2,1)S(1)}, u32[]{:S(2)}, u32[]{:S(2)}) collective-permute-start(bf16[4,96,768]{2,1,0:T(8,128)(2,1)} %add_convert_fusion.23), channel_id=1, source_target_pairs={{0,8},{8,16},{16,24},{24,28},{28,20},{20,12},{12,4},{4,0},{1,9},{9... | collective-permute-start | bytes 1769480 | tf_op jit(solution)/shard_map/ppermute | solution.py:75
  503.9 105.6 %collective-permute-start.5 = (bf16[2364,384]{1,0:T(8,128)(2,1)}, bf16[2364,384]{1,0:T(8,128)(2,1)}, u32[]{:S(2)}, u32[]{:S(2)}) collective-permute-start(bf16[2364,384]{1,0:T(8,128)(2,1)} %add_convert_fusion.7), channel_id=1, source_target_pairs={{0,1},{1,0},{2,3},{3,2},{4,5},{5,4},{6,7},{7,6},{8,9},{9,8},{10,11... | collective-permute-start | bytes 5446664 | tf_op jit(solution)/shard_map/ppermute | solution.py:42
  595.3 12.2 %collective-permute-start.11 = (bf16[2364,384]{1,0:T(8,128)(2,1)S(1)}, bf16[2364,384]{1,0:T(8,128)(2,1)S(1)}, u32[]{:S(2)}, u32[]{:S(2)}) collective-permute-start(bf16[2364,384]{1,0:T(8,128)(2,1)S(1)} %constant_dynamic-slice_fusion.4), channel_id=1, source_target_pairs={{0,1},{1,0},{2,3},{3,2},{4,5},{5,4},{6,7},{7,6},{8,9},{9,8},{10,11... | collective-permute-start | bytes 5446664 | tf_op jit(solution)/shard_map/ppermute | solution.py:38
  602.0 9.9 %collective-permute-start.26 = (bf16[1,96,192]{1,2,0:T(8,128)(2,1)S(1)}, bf16[1,96,192]{1,2,0:T(8,128)(2,1)S(1)}, u32[]{:S(2)}, u32[]{:S(2)}) collective-permute-start(bf16[1,96,192]{1,2,0:T(8,128)(2,1)S(1)} %dynamic-slice_bitcast_fusion.1), channel_id=1, source_target_pairs={{0,4},{8,0},{16,8},{24,16},{28,24},{20,28},{12,20},{4,12},{1,5},{9... | collective-permute-start | bytes 110600 | tf_op jit(solution)/shard_map/ppermute | solution.py:75
  605.9 44.8 %collective-permute-start.19 = (bf16[3,96,192]{1,2,0:T(8,128)(2,1)S(1)}, bf16[3,96,192]{1,2,0:T(8,128)(2,1)S(1)}, u32[]{:S(2)}, u32[]{:S(2)}) collective-permute-start(bf16[3,96,192]{1,2,0:T(8,128)(2,1)S(1)} %dynamic-slice_bitcast_fusion), channel_id=1, source_target_pairs={{0,8},{8,16},{16,24},{24,28},{28,20},{20,12},{12,4},{4,0},{1,9},{9... | collective-permute-start | bytes 331784 | tf_op jit(solution)/shard_map/ppermute | solution.py:75
  608.0 41.6 %collective-permute-start.12 = (bf16[2364,384]{1,0:T(8,128)(2,1)S(1)}, bf16[2364,384]{1,0:T(8,128)(2,1)S(1)}, u32[]{:S(2)}, u32[]{:S(2)}) collective-permute-start(bf16[2364,384]{1,0:T(8,128)(2,1)S(1)} %add_convert_fusion.4), channel_id=1, source_target_pairs={{0,2},{1,3},{2,0},{3,1},{4,6},{5,7},{6,4},{7,5},{8,10},{9,11},{10,... | collective-permute-start | bytes 5446664 | tf_op jit(solution)/shard_map/ppermute | solution.py:40
  612.1 9.1 %collective-permute-start.27 = (bf16[1,96,192]{1,2,0:T(8,128)(2,1)S(1)}, bf16[1,96,192]{1,2,0:T(8,128)(2,1)S(1)}, u32[]{:S(2)}, u32[]{:S(2)}) collective-permute-start(bf16[1,96,192]{1,2,0:T(8,128)(2,1)S(1)} %fusion.65), channel_id=1, source_target_pairs={{0,4},{8,0},{16,8},{24,16},{28,24},{20,28},{12,20},{4,12},{1,5},{9... | collective-permute-start | bytes 110600 | tf_op jit(solution)/shard_map/ppermute | solution.py:75
  625.5 24.6 %collective-permute-start.29 = (bf16[1,96,192]{1,2,0:T(8,128)(2,1)S(1)}, bf16[1,96,192]{1,2,0:T(8,128)(2,1)S(1)}, u32[]{:S(2)}, u32[]{:S(2)}) collective-permute-start(bf16[1,96,192]{1,2,0:T(8,128)(2,1)S(1)} %fusion.63), channel_id=1, source_target_pairs={{0,4},{8,0},{16,8},{24,16},{28,24},{20,28},{12,20},{4,12},{1,5},{9... | collective-permute-start | bytes 110600 | tf_op jit(solution)/shard_map/ppermute | solution.py:75
  650.0 19.5 %collective-permute-start.13 = (bf16[2364,384]{1,0:T(8,128)(2,1)S(1)}, bf16[2364,384]{1,0:T(8,128)(2,1)S(1)}, u32[]{:S(2)}, u32[]{:S(2)}) collective-permute-start(bf16[2364,384]{1,0:T(8,128)(2,1)S(1)} %add_convert_fusion.3), channel_id=1, source_target_pairs={{0,1},{1,0},{2,3},{3,2},{4,5},{5,4},{6,7},{7,6},{8,9},{9,8},{10,11... | collective-permute-start | bytes 5446664 | tf_op jit(solution)/shard_map/ppermute | solution.py:42
  667.9 11.0 %collective-permute-start.23 = (bf16[3,96,192]{1,2,0:T(8,128)(2,1)S(1)}, bf16[3,96,192]{1,2,0:T(8,128)(2,1)S(1)}, u32[]{:S(2)}, u32[]{:S(2)}) collective-permute-start(bf16[3,96,192]{1,2,0:T(8,128)(2,1)S(1)} %fusion.54), channel_id=1, source_target_pairs={{0,8},{8,16},{16,24},{24,28},{28,20},{20,12},{12,4},{4,0},{1,9},{9... | collective-permute-start | bytes 331784 | tf_op jit(solution)/shard_map/ppermute | solution.py:75
  681.4 7.3 %collective-permute-start.15 = (f32[2,768]{1,0:T(2,128)S(1)}, f32[2,768]{1,0:T(2,128)S(1)}, u32[]{:S(2)}, u32[]{:S(2)}) collective-permute-start(f32[2,768]{1,0:T(2,128)S(1)} %fusion.81), channel_id=1, source_target_pairs={{0,2},{1,3},{2,0},{3,1},{4,6},{5,7},{6,4},{7,5},{8,10},{9,11},{10,... | collective-permute-start | bytes 18440 | tf_op jit(solution)/shard_map/ppermute | solution.py:54
  689.1 6.7 collective-permute-start.16
  700.6 10.8 %collective-permute-start.18 = (f32[31,768]{1,0:T(8,128)S(1)}, f32[31,768]{1,0:T(8,128)S(1)}, u32[]{:S(2)}, u32[]{:S(2)}) collective-permute-start(f32[31,768]{1,0:T(8,128)S(1)} %add.942), channel_id=1, source_target_pairs={{0,16},{4,20},{8,24},{12,28},{16,0},{20,4},{24,8},{28,12},{1,17},{... | collective-permute-start | bytes 285704 | tf_op jit(solution)/shard_map/ppermute | solution.py:54
  (102 other events, 1385.2 us)

commit v3 on v2

v3 whole, which is shorter than its diff:
```python
import jax
import jax.numpy as jnp
from jax import lax
from jax.experimental import pallas as pl
from jax.experimental.pallas import tpu as pltpu
from jax.sharding import PartitionSpec as P

SEQ = 197
HD = 64
EPSILON = 1e-06
RING = (0, 2, 4, 6, 7, 5, 3, 1)


def pairs(count, bit):
    return [(i, i ^ bit) for i in range(count)]


def small_sum(values, axis):
    count = lax.axis_size(axis)
    if count not in (4, 8):
        return lax.psum(values, axis)
    bit = 1
    while bit < count:
        values = values + lax.ppermute(values, axis, pairs(count, bit))
        bit *= 2
    return values


ROWS = 208
PAIR = 2
BLOCK = 416
GROUPS = 2
LOCAL = 960
ROOM = 1024
TILE = 256
VMEM = 56 * 1024 * 1024


def route_plan(routes, expert_count):
    tokens = routes.shape[0]
    blocks = -(-tokens // BLOCK)
    padded = jnp.pad(routes.T, ((0, 0), (0, blocks * BLOCK - tokens)), constant_values=-1)
    experts = jnp.arange(expert_count, dtype=jnp.int32)[:, None]
    first = padded[0][None, :] == experts
    second = padded[1][None, :] == experts
    named = (first | second).reshape(expert_count * blocks, BLOCK)
    ahead = jnp.arange(BLOCK)[:, None] < jnp.arange(BLOCK)[None, :]
    rank = jnp.dot(
        named.astype(jnp.bfloat16), ahead.astype(jnp.bfloat16), preferred_element_type=jnp.float32
    )
    rank = rank.astype(jnp.int32).reshape(expert_count, blocks, BLOCK)
    chunks = (jnp.sum(named.astype(jnp.int32), axis=1).reshape(expert_count, blocks) + 15) // 16
    inside = jnp.cumsum(chunks, axis=0) - chunks
    offset = jnp.cumsum(chunks, axis=1) - chunks
    place = (rank + 16 * inside[:, :, None]).reshape(expert_count, blocks * BLOCK)
    target = jnp.stack(
        [jnp.sum(jnp.where(hot, place + 1, 0), axis=0) - 1 for hot in (first, second)]
    )
    tiles = (jnp.sum(chunks, axis=1) * 16 + TILE - 1) // TILE
    plan = jnp.concatenate([chunks.T.reshape(-1), inside.T.reshape(-1), offset.T.reshape(-1)])
    rows = target.reshape(2, blocks, BLOCK).transpose(1, 0, 2)
    return rows, target.T, plan, tiles


def spread(source, rows, plan, expert_count):
    blocks, cols = rows.shape[0], source.shape[1]

    def kernel(plan_ref, rows_ref, source_ref, out_ref, local):
        block = pl.program_id(0)

        @pl.when(block == 0)
        def _():
            out_ref[...] = jnp.zeros_like(out_ref)

        part = LOCAL // 3
        for i in range(3):
            slot = lax.broadcasted_iota(jnp.int32, (part, BLOCK), 0) + i * part
            hot = (slot == rows_ref[0, 0:1, :]) | (slot == rows_ref[0, 1:2, :])
            local[pl.ds(i * part, part), :] = jnp.dot(
                jnp.where(hot, 1.0, 0.0).astype(jnp.bfloat16),
                source_ref[...],
                preferred_element_type=jnp.float32,
            ).astype(jnp.bfloat16)
        for e in range(expert_count):
            at = block * expert_count + e
            size = blocks * expert_count
            begin, goal = plan_ref[size + at], plan_ref[2 * size + at]

            def move(j, carry):
                here = pl.ds(pl.multiple_of((begin + j) * 16, 16), 16)
                there = pl.ds(pl.multiple_of((goal + j) * 16, 16), 16)
                out_ref[e, there, :] = local[here, :]
                return carry

            lax.fori_loop(0, plan_ref[at], move, 0)

    return pl.pallas_call(
        kernel,
        grid_spec=pltpu.PrefetchScalarGridSpec(
            num_scalar_prefetch=1,
            grid=(blocks,),
            in_specs=[
                pl.BlockSpec((1, 2, BLOCK), lambda b, plan: (b, 0, 0)),
                pl.BlockSpec((BLOCK, cols), lambda b, plan: (b, 0)),
            ],
            out_specs=pl.BlockSpec((expert_count, ROOM, cols), lambda b, plan: (0, 0, 0)),
            scratch_shapes=[pltpu.VMEM((LOCAL, cols), jnp.bfloat16)],
        ),
        out_shape=jax.ShapeDtypeStruct((expert_count, ROOM, cols), jnp.bfloat16),
        compiler_params=pltpu.CompilerParams(vmem_limit_bytes=VMEM),
        cost_estimate=pl.CostEstimate(
            flops=2 * blocks * LOCAL * BLOCK * cols,
            bytes_accessed=2 * cols * (blocks * BLOCK + expert_count * ROOM),
            transcendentals=0,
        ),
        name="spread",
    )(plan, rows, source)


def gated_spread(source, rows, plan, chosen, router, expert_count, extra):
    blocks, cols = rows.shape[0], source.shape[1]
    both = cols + extra

    def kernel(
        plan_ref, rows_ref, source_ref, chosen_ref, router_ref, out_ref, gate_ref, pair_ref, local
    ):
        block = pl.program_id(0)

        @pl.when(block == 0)
        def _():
            out_ref[...] = jnp.zeros_like(out_ref)

        logits = jnp.dot(source_ref[...], router_ref[...], preferred_element_type=jnp.float32)
        lane = lax.broadcasted_iota(jnp.int32, logits.shape, 1)
        first, second = lane < expert_count, lane < 2 * expert_count
        expert = jnp.where(first, lane, lane - expert_count)
        top = jnp.max(jnp.where(first, logits, -jnp.inf), axis=-1, keepdims=True)
        raised = jnp.where(second, jnp.exp(logits - top), 0.0)
        gate = raised / jnp.sum(jnp.where(first, raised, 0.0), axis=-1, keepdims=True)
        named = (expert == chosen_ref[:, 0:1]) | (expert == chosen_ref[:, 1:2])
        mixing = jnp.where(named & second, gate, 0.0)
        high = mixing.astype(jnp.bfloat16).astype(jnp.float32)
        pair = jnp.where(first, high, mixing - high).astype(jnp.bfloat16)
        gate_ref[...] = gate
        pair_ref[...] = pair
        part = LOCAL // 3
        for i in range(3):
            slot = lax.broadcasted_iota(jnp.int32, (part, BLOCK), 0) + i * part
            hot = (slot == rows_ref[0, 0:1, :]) | (slot == rows_ref[0, 1:2, :])
            hot = jnp.where(hot, 1.0, 0.0).astype(jnp.bfloat16)
            for begin, end, value in ((0, cols, source_ref[...]), (cols, both, pair)):
                local[pl.ds(i * part, part), begin:end] = jnp.dot(
                    hot, value, preferred_element_type=jnp.float32
                ).astype(jnp.bfloat16)
        for e in range(expert_count):
            at = block * expert_count + e
            size = blocks * expert_count
            begin, goal = plan_ref[size + at], plan_ref[2 * size + at]

            def move(j, carry):
                here = pl.ds(pl.multiple_of((begin + j) * 16, 16), 16)
                there = pl.ds(pl.multiple_of((goal + j) * 16, 16), 16)
                out_ref[e, there, :] = local[here, :]
                return carry

            lax.fori_loop(0, plan_ref[at], move, 0)

    return pl.pallas_call(
        kernel,
        grid_spec=pltpu.PrefetchScalarGridSpec(
            num_scalar_prefetch=1,
            grid=(blocks,),
            in_specs=[
                pl.BlockSpec((1, 2, BLOCK), lambda b, plan: (b, 0, 0)),
                pl.BlockSpec((BLOCK, cols), lambda b, plan: (b, 0)),
                pl.BlockSpec((BLOCK, 2), lambda b, plan: (b, 0)),
                pl.BlockSpec(router.shape, lambda b, plan: (0, 0)),
            ],
            out_specs=[
                pl.BlockSpec((expert_count, ROOM, both), lambda b, plan: (0, 0, 0)),
                pl.BlockSpec((BLOCK, extra), lambda b, plan: (b, 0)),
                pl.BlockSpec((BLOCK, extra), lambda b, plan: (b, 0)),
            ],
            scratch_shapes=[pltpu.VMEM((LOCAL, both), jnp.bfloat16)],
        ),
        out_shape=[
            jax.ShapeDtypeStruct((expert_count, ROOM, both), jnp.bfloat16),
            jax.ShapeDtypeStruct((blocks * BLOCK, extra), jnp.float32),
            jax.ShapeDtypeStruct((blocks * BLOCK, extra), jnp.bfloat16),
        ],
        compiler_params=pltpu.CompilerParams(vmem_limit_bytes=VMEM),
        cost_estimate=pl.CostEstimate(
            flops=2 * blocks * LOCAL * BLOCK * cols,
            bytes_accessed=2 * cols * (blocks * BLOCK + expert_count * ROOM),
            transcendentals=0,
        ),
        name="gated_spread",
    )(plan, rows, source, chosen, router)


def collect(buffers, columns, plan, kept, after):
    each, room, cols = buffers[0].shape
    expert_count = each * len(buffers)
    blocks = columns.shape[0] // BLOCK
    extra = cols - kept

    def kernel(plan_ref, columns_ref, *refs):
        held, refs = refs[: len(buffers)], refs[len(buffers) + len(after) :]
        out_ref, local = refs[0], refs[-1]
        block = pl.program_id(0)

        @pl.when(block == 0)
        def _():
            local[...] = jnp.zeros_like(local)

        for e in range(expert_count):
            at = block * expert_count + e
            size = blocks * expert_count
            begin, goal = plan_ref[size + at], plan_ref[2 * size + at]

            def move(j, carry):
                here = pl.ds(pl.multiple_of((begin + j) * 16, 16), 16)
                there = pl.ds(pl.multiple_of((goal + j) * 16, 16), 16)
                local[here, :] = held[e // each][e % each, there, :]
                return carry

            lax.fori_loop(0, plan_ref[at], move, 0)
        part = BLOCK // 2
        for i in range(2):
            rows = pl.ds(i * part, part)
            slot = lax.broadcasted_iota(jnp.int32, (part, LOCAL), 1)
            hot = (slot == columns_ref[rows, 0:1]) | (slot == columns_ref[rows, 1:2])
            total = jnp.dot(
                jnp.where(hot, 1.0, 0.0).astype(jnp.bfloat16),
                local[...],
                preferred_element_type=jnp.float32,
            )
            out_ref[rows, :] = total[:, :kept].astype(jnp.bfloat16)
            if extra:
                refs[1][rows, :] = total[:, kept:]

    out_specs = [pl.BlockSpec((BLOCK, kept), lambda b, plan: (b, 0))]
    out_shape = [jax.ShapeDtypeStruct((blocks * BLOCK, kept), jnp.bfloat16)]
    if extra:
        out_specs.append(pl.BlockSpec((BLOCK, extra), lambda b, plan: (b, 0)))
        out_shape.append(jax.ShapeDtypeStruct((blocks * BLOCK, extra), jnp.float32))
    return pl.pallas_call(
        kernel,
        grid_spec=pltpu.PrefetchScalarGridSpec(
            num_scalar_prefetch=1,
            grid=(blocks,),
            in_specs=[
                pl.BlockSpec((BLOCK, 2), lambda b, plan: (b, 0)),
            ]
            + [pl.BlockSpec((each, room, cols), lambda b, plan: (0, 0, 0))] * len(buffers)
            + [pl.BlockSpec(memory_space=pl.ANY)] * len(after),
            out_specs=out_specs,
            scratch_shapes=[pltpu.VMEM((LOCAL, cols), jnp.bfloat16)],
        ),
        out_shape=out_shape,
        compiler_params=pltpu.CompilerParams(vmem_limit_bytes=VMEM),
        cost_estimate=pl.CostEstimate(
            flops=2 * blocks * LOCAL * BLOCK * cols,
            bytes_accessed=2 * cols * (blocks * BLOCK + expert_count * room),
            transcendentals=0,
        ),
        name="collect",
    )(plan, columns, *buffers, *after)


GELU_A = 0.7978845608028654
GELU_B = 0.044715


def expert_pass(inputs, grads, up_weight, up_bias, down_weight, tiles, first, count, after):
    expert_count, room, cols = inputs.shape
    width, hidden = up_weight.shape[1:]

    def kernel(
        tiles_ref, x_ref, g_ref, up_ref, bias_ref, down_ref, *refs
    ):
        y_ref, dx_ref, dup_ref, ddown_ref, dbias_ref, mixed, dpre = refs[len(after) :]
        step = pl.program_id(0)
        expert = step + first

        @pl.when(step == 0)
        def _():
            mixed[...] = jnp.zeros_like(mixed)
            dpre[...] = jnp.zeros_like(dpre)

        dbias_ref[...] = jnp.zeros_like(dbias_ref)
        lane = lax.broadcasted_iota(jnp.int32, (TILE, cols - width), 1)

        def tile(r, carry):
            rows = pl.ds(pl.multiple_of(r * TILE, TILE), TILE)
            x = x_ref[0, rows, :width]
            g = g_ref[0, rows, :]
            gates = x_ref[0, rows, width:].astype(jnp.float32)
            own = (lane == expert) | (lane == expert + expert_count)
            mix = jnp.sum(jnp.where(own, gates, 0.0), axis=1, keepdims=True)
            pre = jnp.dot(x, up_ref[0], preferred_element_type=jnp.float32)
            pre = pre + bias_ref[0].astype(jnp.float32)
            back = lax.dot_general(
                g, down_ref[0], (((1,), (1,)), ((), ())), preferred_element_type=jnp.float32
            )
            square = pre * pre
            bend = jnp.tanh(pre * (GELU_A + GELU_A * GELU_B * square))
            upper = 0.5 + 0.5 * bend
            act = pre * upper
            slope = upper + 0.5 * pre * (1.0 - bend * bend) * (
                GELU_A + 3.0 * GELU_A * GELU_B * square
            )
            dot = jnp.sum(act * back, axis=1, keepdims=True)
            act_low = (mix * act).astype(jnp.bfloat16)
            down = (mix * back * slope).astype(jnp.bfloat16)
            mixed[rows, :] = act_low
            dpre[rows, :] = down
            dbias_ref[0] += jnp.sum(down.astype(jnp.float32), axis=0, keepdims=True)
            y_ref[0, rows, :] = jnp.dot(
                act_low, down_ref[0], preferred_element_type=jnp.float32
            ).astype(jnp.bfloat16)
            dx_ref[0, rows, :width] = lax.dot_general(
                down, up_ref[0], (((1,), (1,)), ((), ())), preferred_element_type=jnp.float32
            ).astype(jnp.bfloat16)
            high = dot.astype(jnp.bfloat16).astype(jnp.float32)
            dx_ref[0, rows, width:] = jnp.where(
                lane == expert, high, jnp.where(lane == expert + expert_count, dot - high, 0.0)
            ).astype(jnp.bfloat16)
            return carry

        lax.fori_loop(0, tiles_ref[expert], tile, 0)

        def weights(depth):
            rows = pl.ds(0, depth)
            for i in range(width // TILE):
                part = pl.ds(i * TILE, TILE)
                dup_ref[0, part, :] = lax.dot_general(
                    x_ref[0, rows, part], dpre[rows, :], (((0,), (0,)), ((), ())),
                    preferred_element_type=jnp.float32,
                ).astype(jnp.bfloat16)
                ddown_ref[0, part, :] = lax.dot_general(
                    g_ref[0, rows, part], mixed[rows, :], (((0,), (0,)), ((), ())),
                    preferred_element_type=jnp.float32,
                ).astype(jnp.bfloat16)

        pl.when(tiles_ref[expert] <= 3)(lambda: weights(3 * TILE))
        pl.when(tiles_ref[expert] > 3)(lambda: weights(room))

    def whole(*dims):
        return pl.BlockSpec((1, *dims), lambda e, tiles: (e + first, 0, 0))

    def own(*dims):
        return pl.BlockSpec((1, *dims), lambda e, tiles: (e, 0, 0))

    shapes = [
        ((room, width), jnp.bfloat16),
        ((room, cols), jnp.bfloat16),
        ((width, hidden), jnp.bfloat16),
        ((width, hidden), jnp.bfloat16),
        ((1, hidden), jnp.float32),
    ]
    return pl.pallas_call(
        kernel,
        grid_spec=pltpu.PrefetchScalarGridSpec(
            num_scalar_prefetch=1,
            grid=(count,),
            in_specs=[
                whole(room, cols),
                whole(room, width),
                whole(width, hidden),
                whole(1, hidden),
                whole(hidden, width),
            ]
            + [pl.BlockSpec(memory_space=pl.ANY)] * len(after),
            out_specs=[own(*dims) for dims, _ in shapes],
            scratch_shapes=[pltpu.VMEM((room, hidden), jnp.bfloat16)] * 2,
        ),
        out_shape=[jax.ShapeDtypeStruct((count, *dims), kind) for dims, kind in shapes],
        compiler_params=pltpu.CompilerParams(vmem_limit_bytes=VMEM),
        cost_estimate=pl.CostEstimate(
            flops=count * 12 * 768 * width * hidden,
            bytes_accessed=count * (4 * room * (cols + width) + 8 * width * hidden),
            transcendentals=count * 768 * hidden,
        ),
        name="experts",
    )(tiles, inputs, grads, up_weight, up_bias[:, None, :], down_weight, *after)


def call(kernel, name, grid, ins, outs, after=(), scratch=(), flops=0, traffic=0, each=1, turn=None):
    turn = jnp.zeros((1,), jnp.int32) if turn is None else turn

    def spec(shape, split):
        zeros = (0,) * (len(shape) - 1)
        if split == "turned":
            return pl.BlockSpec((each, *shape[1:]), lambda i, t: ((i + t[0]) % grid, *zeros))
        if split:
            return pl.BlockSpec((each, *shape[1:]), lambda i, t: (i, *zeros))
        return pl.BlockSpec(tuple(shape), lambda i, t: (0, *zeros))

    count, late = len(ins), len(after)

    def body(turn_ref, *refs):
        kernel(*refs[:count], *refs[count + late :])

    return pl.pallas_call(
        body,
        grid_spec=pltpu.PrefetchScalarGridSpec(
            num_scalar_prefetch=1,
            grid=(grid,),
            in_specs=[spec(a.shape, split) for a, split in ins]
            + [pl.BlockSpec(memory_space=pl.ANY)] * late,
            out_specs=[spec(a.shape, split) for a, split in outs],
            scratch_shapes=list(scratch),
        ),
        out_shape=[a for a, _ in outs],
        compiler_params=pltpu.CompilerParams(vmem_limit_bytes=VMEM),
        cost_estimate=pl.CostEstimate(flops=flops, bytes_accessed=traffic, transcendentals=0),
        name=name,
    )(turn, *[a for a, _ in ins], *after)


def shape_of(dims, kind):
    return jax.ShapeDtypeStruct(tuple(dims), kind)


def normal(x):
    centered = x - jnp.mean(x, axis=-1, keepdims=True)
    spread_of = lax.rsqrt(jnp.mean(centered * centered, axis=-1, keepdims=True) + EPSILON)
    return centered * spread_of, spread_of


def contract(left, right, left_dim, right_dim):
    return lax.dot_general(
        left, right, (((left_dim,), (right_dim,)), ((), ())), preferred_element_type=jnp.float32
    )


def head_masks(width):
    lane = lax.broadcasted_iota(jnp.int32, (1, width), 1)
    return [(lane >= h * HD) & (lane < (h + 1) * HD) for h in range(width // HD)]


def head_probs(q, k, mask):
    own = jnp.where(mask, q, jnp.zeros_like(q)) * jnp.bfloat16(HD ** (-0.5))
    scores = contract(own, k, 1, 1)
    column = lax.broadcasted_iota(jnp.int32, scores.shape, 1)
    scores = jnp.where(column < SEQ, scores, -1e30)
    raised = jnp.exp(scores - jnp.max(scores, axis=-1, keepdims=True))
    return raised / jnp.sum(raised, axis=-1, keepdims=True)


def attention_forward(x, turn, gain, shift, weight, bias, out_weight):
    images, seq, width = x.shape
    rows, inner = ROWS, weight.shape[2]

    def kernel(
        x_ref, gain_ref, shift_ref, w_ref, b_ref, wo_ref,
        part_ref, pad_ref, n_ref, q_ref, k_ref, v_ref, o_ref, held,
    ):
        held[...] = jnp.zeros_like(held)
        for i in range(PAIR):
            held[i, :seq, :] = x_ref[i].astype(jnp.float32)
        for i in range(PAIR):
            value = held[i]
            pad_ref[i] = value.astype(jnp.bfloat16)
            n = (normal(value)[0] * gain_ref[...] + shift_ref[...]).astype(jnp.bfloat16)
            n_ref[i] = n
            q, k, v = [
                (
                    jnp.dot(n, w_ref[j], preferred_element_type=jnp.float32) + b_ref[j : j + 1, :]
                ).astype(jnp.bfloat16)
                for j in range(3)
            ]
            q_ref[i], k_ref[i], v_ref[i] = q, k, v
            mixed = jnp.zeros((rows, inner), jnp.float32)
            for mask in head_masks(inner):
                probs = head_probs(q, k, mask).astype(jnp.bfloat16)
                head = jnp.dot(probs, v, preferred_element_type=jnp.float32)
                mixed = jnp.where(mask, head, mixed)
            mixed = mixed.astype(jnp.bfloat16)
            o_ref[i] = mixed
            part_ref[i] = jnp.dot(mixed, wo_ref[...], preferred_element_type=jnp.float32).astype(
                jnp.bfloat16
            )

    wide = shape_of((images, rows, width), jnp.bfloat16)
    slim = shape_of((images, rows, inner), jnp.bfloat16)
    return call(
        kernel, "attention_forward", images // PAIR,
        [(x, "turned"), (gain, False), (shift, False), (weight, False), (bias, False), (out_weight, False)],
        [(wide, True)] * 3 + [(slim, True)] * 4,
        scratch=[pltpu.VMEM((PAIR, rows, width), jnp.float32)], each=PAIR, turn=turn,
        flops=images * rows * width * inner * 8, traffic=images * rows * (width * 8 + inner * 8),
    )


def attention_backward(da, x, n, q, k, v, o, weight, out_weight, after):
    images, rows, width = x.shape
    inner = weight.shape[2]

    def kernel(
        da_ref, x_ref, n_ref, q_ref, k_ref, v_ref, o_ref, w_ref, wo_ref,
        back_ref, dw_ref, dwo_ref, dbias_ref, sums_ref,
    ):
        @pl.when(pl.program_id(0) == 0)
        def _():
            dw_ref[...] = jnp.zeros_like(dw_ref)
            dwo_ref[...] = jnp.zeros_like(dwo_ref)
            dbias_ref[...] = jnp.zeros_like(dbias_ref)
            sums_ref[...] = jnp.zeros_like(sums_ref)

        for i in range(PAIR):
            da, q, k, v = da_ref[i], q_ref[i], k_ref[i], v_ref[i]
            do = contract(da, wo_ref[...], 1, 1).astype(jnp.bfloat16)
            dq = dk = dv = jnp.zeros((rows, inner), jnp.float32)
            for mask in head_masks(inner):
                probs = head_probs(q, k, mask)
                dv = jnp.where(mask, contract(probs.astype(jnp.bfloat16), do, 0, 0), dv)
                dp = contract(jnp.where(mask, do, jnp.zeros_like(do)), v, 1, 1)
                ds = probs * (dp - jnp.sum(probs * dp, axis=-1, keepdims=True))
                ds = ds.astype(jnp.bfloat16)
                dq = jnp.where(mask, jnp.dot(ds, k, preferred_element_type=jnp.float32), dq)
                dk = jnp.where(mask, contract(ds, q, 0, 0), dk)
            scale = HD ** (-0.5)
            grads = [(dq * scale).astype(jnp.bfloat16), (dk * scale).astype(jnp.bfloat16), dv.astype(jnp.bfloat16)]
            n = n_ref[i]
            back = jnp.zeros((rows, width), jnp.float32)
            for j in range(3):
                dw_ref[j] += contract(n, grads[j], 0, 0)
                back += contract(grads[j], w_ref[j], 1, 1)
            dwo_ref[0] += contract(da, o_ref[i], 0, 0)
            back_ref[i] = back.astype(jnp.bfloat16)
            dbias_ref[0:1, :] += jnp.sum(grads[0].astype(jnp.float32), axis=0, keepdims=True)
            dbias_ref[1:2, :] += jnp.sum(grads[2].astype(jnp.float32), axis=0, keepdims=True)
            unit, _ = normal(x_ref[i].astype(jnp.float32))
            sums_ref[0:1, :] += jnp.sum(back * unit, axis=0, keepdims=True)
            sums_ref[1:2, :] += jnp.sum(back, axis=0, keepdims=True)
            sums_ref[2:3, :] += jnp.sum(da.astype(jnp.float32), axis=0, keepdims=True)

    return call(
        kernel, "attention_backward", images // PAIR,
        [(a, True) for a in (da, x, n, q, k, v, o)] + [(weight, False), (out_weight, False)],
        [
            (shape_of((images, rows, width), jnp.bfloat16), True),
            (shape_of((3, width, inner), jnp.float32), False),
            (shape_of((1, width, inner), jnp.float32), False),
            (shape_of((2, inner), jnp.float32), False),
            (shape_of((3, width), jnp.float32), False),
        ],
        after=after, each=PAIR, flops=images * rows * width * inner * 18,
        traffic=images * rows * (width * 8 + inner * 8),
    )


def middle_norm(near, far, x, out_bias, gain, shift, after):
    def kernel(near_ref, far_ref, x_ref, bias_ref, gain_ref, shift_ref, middle_ref, n_ref):
        total = near_ref[0].astype(jnp.float32) + far_ref[0].astype(jnp.float32)
        middle = x_ref[0].astype(jnp.float32) + total + bias_ref[...]
        middle_ref[0] = middle
        n_ref[0] = (normal(middle)[0] * gain_ref[...] + shift_ref[...]).astype(jnp.bfloat16)

    return call(
        kernel, "middle_norm", near.shape[0],
        [(near, True), (far, True), (x, True), (out_bias, False), (gain, False), (shift, False)],
        [(shape_of(near.shape, jnp.float32), True), (shape_of(near.shape, jnp.bfloat16), True)],
        after=after, traffic=12 * near.size,
    )


def norm_back(dn, unit, spread_of, gain):
    dz = dn * gain
    mean = jnp.mean(dz, axis=-1, keepdims=True)
    return spread_of * (dz - mean - unit * jnp.mean(dz * unit, axis=-1, keepdims=True))


def middle_back(near, far, dots, gates, chosen, pair, n, router_weight, down_bias, middle, upstream, gain, after):
    count, wide = down_bias.shape[0], pair.shape[2]

    def kernel(
        near_ref, far_ref, dots_ref, gates_ref, chosen_ref, pair_ref, n_ref, router_ref, bias_ref,
        middle_ref, g_ref, gain_ref, grad_ref, da_ref, sums_ref, drouter_ref, dbias_ref,
    ):
        @pl.when(pl.program_id(0) == 0)
        def _():
            sums_ref[...] = jnp.zeros_like(sums_ref)
            drouter_ref[...] = jnp.zeros_like(drouter_ref)
            dbias_ref[...] = jnp.zeros_like(dbias_ref)

        g = g_ref[0]
        lane = lax.broadcasted_iota(jnp.int32, (g.shape[0], count), 1)
        named = (lane == chosen_ref[0, :, 0:1]) | (lane == chosen_ref[0, :, 1:2])
        dmix = dots_ref[0] + jnp.where(named, contract(g, bias_ref[...], 1, 1), 0.0)
        gate = gates_ref[0, :, :count]
        dlogits = gate * (dmix - jnp.sum(gate * dmix, axis=-1, keepdims=True))
        dlogits = dlogits.astype(jnp.bfloat16)
        drouter_ref[...] += contract(dlogits, n_ref[0], 0, 0)
        dbias_ref[...] += contract(pair_ref[0], g, 0, 0)
        dn = near_ref[0].astype(jnp.float32) + far_ref[0].astype(jnp.float32)
        dn = dn + contract(dlogits, router_ref[...], 1, 1)
        unit, spread_of = normal(middle_ref[0])
        grad = g.astype(jnp.float32) + norm_back(dn, unit, spread_of, gain_ref[...])
        grad_ref[0] = grad
        da_ref[0] = grad.astype(jnp.bfloat16)
        sums_ref[0:1, :] += jnp.sum(dn * unit, axis=0, keepdims=True)
        sums_ref[1:2, :] += jnp.sum(dn, axis=0, keepdims=True)

    width = middle.shape[2]
    return call(
        kernel, "middle_back", middle.shape[0],
        [(a, True) for a in (near, far, dots, gates, chosen, pair, n)]
        + [(router_weight, False), (down_bias, False), (middle, True), (upstream, True), (gain, False)],
        [
            (shape_of(middle.shape, jnp.float32), True),
            (shape_of(middle.shape, jnp.bfloat16), True),
            (shape_of((2, width), jnp.float32), False),
            (shape_of((count, width), jnp.float32), False),
            (shape_of((wide, width), jnp.float32), False),
        ],
        after=after, traffic=18 * middle.size,
    )


def finish(near, far, middle, pair, down_bias, after):
    def kernel(near_ref, far_ref, middle_ref, pair_ref, bias_ref, out_ref):
        total = near_ref[0].astype(jnp.float32) + far_ref[0].astype(jnp.float32)
        total = total + jnp.dot(pair_ref[0], bias_ref[...], preferred_element_type=jnp.float32)
        out_ref[0] = (middle_ref[0] + total).astype(jnp.bfloat16)

    return call(
        kernel, "finish", middle.shape[0],
        [(near, True), (far, True), (middle, True), (pair, True), (down_bias, False)],
        [(shape_of(middle.shape, jnp.bfloat16), True)],
        after=after, traffic=10 * middle.size,
    )[0]


def input_back(own, other, x, own_grad, other_grad, gain, turn, after):
    images, _, width = x.shape
    half = images // 2

    def kernel(turn_ref, own_ref, other_ref, x_ref, own_grad_ref, other_grad_ref, gain_ref, *refs):
        out_ref = refs[-1]
        step = pl.program_id(0)
        place = (step + turn_ref[0]) % images
        mine = step < half
        dn = jnp.where(mine, own_ref[0], other_ref[0]).astype(jnp.float32)
        unit, spread_of = normal(x_ref[0].astype(jnp.float32))
        grad = jnp.where(mine, own_grad_ref[0], other_grad_ref[0])
        grad = grad + norm_back(dn, unit, spread_of, gain_ref[...])
        for j in range(images):

            @pl.when(place == j)
            def _():
                out_ref[j * SEQ : (j + 1) * SEQ, :] = grad[:SEQ]

    def low(shape):
        return pl.BlockSpec((1, *shape[1:]), lambda i, t: (jnp.minimum(i, half - 1), 0, 0))

    def high(shape):
        return pl.BlockSpec((1, *shape[1:]), lambda i, t: (jnp.maximum(i - half, 0), 0, 0))

    return pl.pallas_call(
        kernel,
        grid_spec=pltpu.PrefetchScalarGridSpec(
            num_scalar_prefetch=1,
            grid=(images,),
            in_specs=[
                low(own.shape),
                high(other.shape),
                pl.BlockSpec((1, *x.shape[1:]), lambda i, t: (i, 0, 0)),
                low(own_grad.shape),
                high(other_grad.shape),
                pl.BlockSpec(gain.shape, lambda i, t: (0, 0)),
            ]
            + [pl.BlockSpec(memory_space=pl.ANY)] * len(after),
            out_specs=pl.BlockSpec((images * SEQ, width), lambda i, t: (0, 0)),
        ),
        out_shape=jax.ShapeDtypeStruct((images * SEQ, width), jnp.float32),
        compiler_params=pltpu.CompilerParams(vmem_limit_bytes=VMEM),
        cost_estimate=pl.CostEstimate(flops=0, bytes_accessed=14 * x.size, transcendentals=0),
        name="input_back",
    )(turn, own, other, x, own_grad, other_grad, gain, *after)


def to_core(value):
    return lax.ppermute(value, "tensor", pairs(lax.axis_size("tensor"), 1))


def across(value):
    return lax.ppermute(value, "tensor", pairs(lax.axis_size("tensor"), 2))


def core_sum(part, zero):
    half = part.shape[0] // 2
    got = to_core(part[half:])
    return (part[:half].astype(jnp.float32) + got.astype(jnp.float32) + zero).astype(jnp.bfloat16)


def zero_of(value):
    return value[(0,) * value.ndim].astype(jnp.float32) * 0.0


class Ring:
    def __init__(self, values, way):
        self.values, self.way, self.step, self.count = values, way, 0, lax.axis_size("dp")
        self.ring = self.count == len(RING)
        self.moving = self.local(0) if self.ring else values.astype(jnp.bfloat16)

    def local(self, step):
        count = self.count
        chunk = self.values.shape[1] // count
        order = jnp.array(RING, jnp.int32)
        place = jnp.array([RING.index(i) for i in range(count)], jnp.int32)
        owner = order[(place[lax.axis_index("dp")] - self.way * (step + 1)) % count]
        size = (self.values.shape[0], chunk, self.values.shape[2])
        return lax.dynamic_slice(self.values, (0, owner * chunk, 0), size).astype(jnp.bfloat16)

    def hop(self, zero):
        if not self.ring or self.step == self.count - 1:
            return
        path = [(RING[i], RING[(i + self.way) % self.count]) for i in range(self.count)]
        got = lax.ppermute(self.moving, "dp", path)
        self.step += 1
        total = got.astype(jnp.float32) + self.local(self.step).astype(jnp.float32) + zero
        self.moving = total.astype(jnp.bfloat16) if self.step < self.count - 1 else total

    def result(self):
        if not self.ring:
            return lax.psum_scatter(self.moving, "dp", scatter_dimension=1, tiled=True).astype(jnp.float32)
        while self.step < self.count - 1:
            self.hop(0.0)
        return self.moving


def halving_scatter(values):
    if lax.axis_size("dp") != 8:
        return lax.psum_scatter(values.astype(jnp.bfloat16), "dp", scatter_dimension=1, tiled=True).astype(jnp.float32)
    index = lax.axis_index("dp")
    many, rows, cols = values.shape
    values = values.reshape(many, 2, 2, 2, rows // 8, cols)
    for bit, axis in ((0, 3), (1, 2), (2, 1)):
        mine = (index >> bit) % 2
        keep = lax.dynamic_index_in_dim(values, mine, axis, keepdims=True)
        give = lax.dynamic_index_in_dim(values, 1 - mine, axis, keepdims=True)
        got = lax.ppermute(give.astype(jnp.bfloat16), "dp", pairs(8, 1 << bit))
        values = keep.astype(jnp.float32) + got.astype(jnp.float32)
    return values.reshape(many, rows // 8, cols)


def on_device(
    embedded,
    attn_gain,
    attn_shift,
    qkv_weight,
    qv_bias,
    out_weight,
    out_bias,
    moe_gain,
    moe_shift,
    router_weight,
    up_weight,
    up_bias,
    down_weight,
    down_bias,
    routes,
    cotangent,
):
    tok_rows, width = embedded.shape
    images = tok_rows // SEQ
    half = images // 2
    head_width = qkv_weight.shape[2]
    expert_count = up_weight.shape[0]
    core = lax.axis_index("tensor") % 2
    f32 = jnp.float32

    def own_first(value, fill):
        value = value.reshape(images, SEQ, value.shape[1])
        value = jnp.pad(value, ((0, 0), (0, ROWS - SEQ), (0, 0)), constant_values=fill)
        return jnp.where(core == 0, value, jnp.roll(value, half, axis=0))

    def in_order(own, other):
        low = jnp.where(core == 0, own, other)
        high = jnp.where(core == 0, other, own)
        return jnp.concatenate([low, high])[:, :SEQ].reshape(tok_rows, width)

    def row(value):
        return value.astype(f32)[None]

    def imaged(value):
        return value.reshape(images, ROWS, value.shape[1])

    turn = (half * core).astype(jnp.int32)[None]
    bias_rows = jnp.stack([qv_bias[0], jnp.zeros_like(qv_bias[0]), qv_bias[1]]).astype(f32)
    part, x, normed, queries, keys, values, mixed = attention_forward(
        embedded.reshape(images, SEQ, width), turn // PAIR, row(attn_gain), row(attn_shift),
        qkv_weight, bias_rows, out_weight,
    )
    near = core_sum(part, 0.0)
    far = across(near)

    chosen = own_first(routes, -1).reshape(images * ROWS, 2)
    rows, columns, plan, tiles = route_plan(chosen, expert_count)
    upstream = own_first(cotangent, 0)
    grad_buffers = spread(upstream.reshape(images * ROWS, width), rows, plan, expert_count)

    middle, own_normed = middle_norm(
        near, far, x, row(out_bias), row(moe_gain), row(moe_shift), (grad_buffers,)
    )
    moe_normed = jnp.concatenate([own_normed, to_core(own_normed)]).reshape(images * ROWS, width)
    extra = 128
    router_twice = jnp.pad(
        jnp.concatenate([router_weight, router_weight], axis=1),
        ((0, 0), (0, extra - 2 * expert_count)),
    )
    bias_twice = jnp.pad(
        jnp.concatenate([down_bias, down_bias]), ((0, extra - 2 * expert_count), (0, 0))
    )
    buffers, gates, mix_pair = gated_spread(
        moe_normed, rows, plan, chosen, router_twice, expert_count, extra
    )
    gates, mix_pair, chosen = imaged(gates), imaged(mix_pair), imaged(chosen)
    group = expert_count // GROUPS

    def experts_of(i, after):
        return expert_pass(
            buffers, grad_buffers, up_weight, up_bias, down_weight, tiles, i * group, group, after
        )

    def tokens(*some):
        return tuple(ring.moving for ring in some)

    def hops(value, *some):
        for ring in some:
            ring.hop(zero_of(value))

    y_first, back_first, up_grad, down_grad, bias_first = experts_of(0, ())
    first = (Ring(up_grad, 1), Ring(down_grad, -1))
    y_second, back_second, up_grad, down_grad, bias_second = experts_of(1, tokens(*first))
    hops(bias_second, *first)
    back_part, dots = collect((back_first, back_second), columns, plan, width, tokens(*first))
    second = (Ring(up_grad, 1), Ring(down_grad, -1))
    back_near = core_sum(imaged(back_part), 0.0)
    back_far = across(back_near)
    dots = dots[:, : 2 * expert_count].T
    dots = dots[:expert_count] + dots[expert_count:]
    own_rows = half * ROWS
    dots = dots[:, :own_rows] + to_core(dots[:, own_rows:])
    dots = (dots + across(dots)).T.reshape(half, ROWS, expert_count)
    hops(back_near, *first)
    (moe_part,) = collect(
        (y_first, y_second), columns, plan, width, (back_near, *tokens(*first, *second))
    )
    hops(moe_part, *second)
    hops(second[1].moving, *first)
    hops(first[1].moving, *second)
    middle_grad, own_da, moe_sums, router_sums, bias_sums = middle_back(
        back_near, back_far, dots, gates, chosen, mix_pair, imaged(moe_normed), router_weight,
        down_bias, middle, upstream, row(moe_gain), tokens(*second),
    )
    da = jnp.concatenate([own_da, to_core(own_da)])
    y_near = core_sum(imaged(moe_part), zero_of(own_da))
    y_far = across(y_near)
    other_grad = to_core(middle_grad)
    hops(own_da, *first)
    normed_back, grad_qkv, grad_out, grad_qv_bias, sums = attention_backward(
        da, x, normed, queries, keys, values, mixed, qkv_weight, out_weight, tokens(*first)
    )
    last_near = core_sum(normed_back, 0.0)
    last_far = across(last_near)
    hops(normed_back, *second)
    hops(last_near, *first)
    own_out = finish(y_near, y_far, middle, mix_pair, bias_twice, (last_near,))
    layer_out = in_order(own_out, to_core(own_out))
    router_bias = [router_sums, bias_sums[:expert_count] + bias_sums[expert_count : 2 * expert_count]]
    tensor_parts = jnp.concatenate([sums[:2]] + [0.5 * part for part in (moe_sums, *router_bias)])
    packed = jnp.concatenate(
        [
            small_sum(tensor_parts, "tensor"),
            sums[2:],
            jnp.pad(grad_qv_bias, ((0, 0), (0, width - head_width))),
            bias_first[:, 0],
            bias_second[:, 0],
        ]
    )
    packed = small_sum(packed, "dp")
    slim = halving_scatter(jnp.concatenate([grad_qkv, grad_out]))
    up_first, down_first, up_second, down_second = [ring.result() for ring in first + second]
    last = (last_near.astype(f32) + last_far.astype(f32)).astype(jnp.bfloat16)
    grad_embedded = input_back(
        last, to_core(last), x, middle_grad, other_grad, row(attn_gain), turn,
        (layer_out, packed, slim),
    )
    base = 4 + 2 * expert_count
    return (
        layer_out,
        grad_embedded,
        packed[0],
        packed[1],
        slim[:3],
        packed[base + 1 : base + 3, :head_width],
        slim[3].T,
        packed[base],
        packed[2],
        packed[3],
        packed[4 : 4 + expert_count].T,
        jnp.concatenate([up_first, up_second]),
        packed[base + 3 :],
        jnp.concatenate([down_first, down_second]).transpose(0, 2, 1),
        packed[4 + expert_count : base],
    )


def solution(mesh):
    return jax.shard_map(
        on_device,
        mesh=mesh,
        in_specs=(
            P("dp", None),
            P(),
            P(),
            P(None, None, "tensor"),
            P(None, "tensor"),
            P("tensor", None),
            P(),
            P(),
            P(),
            P(),
            P(None, None, "tensor"),
            P(None, "tensor"),
            P(None, "tensor", None),
            P(),
            P("dp", None),
            P("dp", None),
        ),
        out_specs=(
            P("dp", None),
            P("dp", None),
            P(),
            P(),
            P(None, "dp", "tensor"),
            P(None, "tensor"),
            P("tensor", "dp"),
            P(),
            P(),
            P(),
            P(),
            P(None, "dp", "tensor"),
            P(None, "tensor"),
            P(None, "tensor", "dp"),
            P(),
        ),
        check_vma=False,
    )
```

time: 720 us -> 636 us (0.88)
  Pallas kernels: 136 us -> 239 us
  matrix products: 70.3 us -> 0.23 us
  other arithmetic: 114 us -> 72.8 us
  local copies, waits for them, and re-layouts: 104 us -> 63.1 us
  starting transfers between devices: 69 us -> 42.8 us
  waiting for transfers between devices: 197 us -> 179 us
    pallas_call x0 -> x7, Pallas kernels: none -> 121 us  [the longest x5 84.6 us: call(): pl.pallas_call(body, grid_spec=pltpu.PrefetchScalarGridSpec(num_scalar_pr...]
    dot_general x17 -> x0, matrix products: 67.4 us -> none  [the longest x1 8.95 us: on_device(): lax.dot_general(grad_logits_low, router_weight, (((1,), (1,)), ((), ())),...]
    ppermute x54 -> x46, waiting for transfers between devices: 189 us -> 127 us  [the longest x28 88.6 us: hop(): got = lax.ppermute(self.moving, 'dp', path)]
    ppermute x7 -> x5, waiting for transfers between devices: 7.75 us -> 52.7 us  [small_sum(): values = values + lax.ppermute(values, axis, pairs(count, bit))]
    reduce_sum x11 -> x0, other arithmetic: 34.2 us -> none  [the longest x2 8.79 us: layer_norm(): return centered * lax.rsqrt(row_var + EPSILON) * gain_vec + shift_vec]
    another operation x12 -> x1, local copies, waits for them, and re-layouts: 32.8 us -> 0.07 us  [on_device(): jnp.stack([qv_bias[0], jnp.zeros_like(qv_bias[0]), qv_bias[1]]).astype(f32)]
    ppermute x54 -> x46, starting transfers between devices: 63.9 us -> 38.9 us  [the longest x28 27.1 us: hop(): got = lax.ppermute(self.moving, 'dp', path)]
    pallas_call x2 -> x1, Pallas kernels: 33.1 us -> 15.4 us  [spread(): pl.pallas_call(kernel, grid_spec=pltpu.PrefetchScalarGridSpec(num_scalar_...]
  transfers between devices with their start and end apart: 61 -> 51, of which waited for: 29 -> 19; matrix products, arithmetic and copies ran while one was open for 27% -> 17% of each run, Pallas kernels for 7% -> 19%
where the time goes in v3:
time: 636 us; the launch traced here: 626 us
  Pallas kernels  239 us (38%)
  waiting for transfers between devices  179 us (28%)
  other arithmetic  72.8 us (11%)
  local copies, waits for them, and re-layouts  63.1 us (10%)
  starting transfers between devices  42.8 us (7%)
  between operations  28.6 us (4%)
    ppermute x28, waiting for transfers between devices, hop(): got = lax.ppermute(self.moving, 'dp', path)  88.6 us
    pallas_call x5, Pallas kernels, call(): pl.pallas_call(body, grid_spec=pltpu.PrefetchScalarGridSpec(num_scalar_pr...  84.6 us
    pallas_call x2, Pallas kernels, expert_pass(): pl.pallas_call(kernel, grid_spec=pltpu.PrefetchScalarGridSpec(num_scalar_...  71.4 us
    ppermute x5, waiting for transfers between devices, small_sum(): values = values + lax.ppermute(values, axis, pairs(count, bit))  52.7 us
    convert_element_type x24, other arithmetic, hop(): total.astype(jnp.bfloat16)  41.5 us
    pallas_call x2, Pallas kernels, collect(): pl.pallas_call(kernel, grid_spec=pltpu.PrefetchScalarGridSpec(num_scalar_...  30.9 us
    ppermute x28, starting transfers between devices, hop(): got = lax.ppermute(self.moving, 'dp', path)  27.1 us
    ppermute x3, waiting for transfers between devices, halving_scatter(): got = lax.ppermute(give.astype(jnp.bfloat16), 'dp', pairs(8, 1 << bit))  24.4 us
  transfers between devices with their start and end apart: 51, of which 19 were waited for; matrix products, arithmetic and copies ran while one was open for 17% of the time, Pallas kernels for 19%

profile of v3, /device:TPU:0, one launch (start us, length us, event | category | flops | bytes accessed | tf_op | source)
XLA Modules:
  0.0 625.8 jit_solution(16523973501063279612)
XLA Ops:
  1.4 2.3 copy.164.refs_3_.refs_7_
  4.4 4.2 reshape.346.refs_0_
  9.9 21.2 %attention_forward.1 = (bf16[12,208,768]{2,1,0:T(8,128)(2,1)}, bf16[12,208,768]{2,1,0:T(8,128)(2,1)}, bf16[12,208,768]{2,1,0:T(8,128)(2,1)}, bf16[12,208,192]{2,...) custom-call(s32[1]{0:T(128)S(6)} %select_n.462.turn_ref, ...), custom_call_target="tpu_custom_call" | custom-call | flops 2944401408 | bytes 19169280 | tf_op jit(solution)/shard_map/attention_forward/pallas_call | solution.py:405
  31.1 2.9 slice.167
  38.4 2.6 add_convert_fusion.2.refs_0_
  41.0 2.9 collective-permute-start.1
  45.5 4.3 reshape.347
  52.8 2.5 pad_slice_fusion.1
  56.0 2.4 maximum_select_fusion.refs_10_
  58.4 15.4 %spread.1.refs_6_.g_ref = bf16[8,1024,768]{2,1,0:T(8,128)(2,1)} custom-call(s32[144]{0:T(256)} %pad_add_fusion.1.plan_ref, s32[6,2,416]{2,1,0:T(2,128)} %add_bitcast_fusion.rows_ref, bf16[2496,768]{1,0:T(8,128)(2,1)} %bitcast.108), custom_call_target="tpu_custom_call" | custom-call | flops 3680501760 | bytes 16416768 | tf_op jit(solution)/shard_map/spread/pallas_call | solution.py:97
  73.8 12.3 %collective-permute-done.1.refs_1_ = bf16[6,208,768]{2,1,0:T(8,128)(2,1)} collective-permute-done((bf16[6,208,768]{2,1,0:T(8,128)(2,1)S(1)}, bf16[6,208,768]{2,1,0:T(8,128)(2,1)}, u32[]{:S(2)}, u32[]{:S(2)}) %collective-permute-start.1) | collective-permute-done | bytes 1916960 | tf_op jit(solution)/shard_map/ppermute | solution.py:690
  86.1 7.1 %middle_norm.1 = (f32[6,208,768]{2,1,0:T(8,128)}, bf16[6,208,768]{2,1,0:T(8,128)(2,1)}) custom-call(s32[1]{0:T(128)} %constant.372.clone.1.turn_ref, bf16[6,208,768]{2,1,0:T(8,128)(2,1)} %copy-done.8, bf16[6,208,768]{2,1,0:T(8,128)(2,1)} %collective-permute-done.1.refs_1_, bf16[12,208,768]{2,1,0:T(8,128)(2,1)} %get-tuple-element.50.refs_2_.refs_1_.x_ref, ...), custom_call_target="tpu_custom_call" | custom-call | bytes 11501568 | tf_op jit(solution)/shard_map/middle_norm/pallas_call | solution.py:405
  116.5 21.0 %gated_spread.1 = (bf16[8,1024,896]{2,1,0:T(8,128)(2,1)}, f32[2496,128]{1,0:T(8,128)}, bf16[2496,128]{1,0:T(8,128)(2,1)}) custom-call(s32[144]{0:T(256)} %pad_add_fusion.1.plan_ref, s32[6,2,416]{2,1,0:T(2,128)} %add_bitcast_fusion.rows_ref, bf16[2496,768]{1,0:T(8,128)(2,1)} %bitcast.115, s32[2496,2]{1,0:T(8,128)} %bitcast.110, bf16[768,128]{1,0:T(8,128)(2,1)} %pad.22.router_ref), custom_call_target="tpu_custom_call" | custom-call | flops 3680501760 | bytes 16416768 | tf_op jit(solution)/shard_map/gated_spread/pallas_call | solution.py:168
  137.5 39.0 %experts.2 = (bf16[4,1024,768]{2,1,0:T(8,128)(2,1)}, bf16[4,1024,896]{2,1,0:T(8,128)(2,1)}, bf16[4,768,768]{2,1,0:T(8,128)(2,1)}, bf16[4,768,768]{2,1,0:T(8,128)(2,1)}, f32[4,1,768]{2,1,0:T(1,128)}) custom-call(s32[8]{0:T(128)} %and_select_fusion.tiles_ref, bf16[8,1024,896]{2,1,0:T(8,128)(2,1)} %get-tuple-element.52.x_ref, ...), custom_call_target="tpu_custom_call" | custom-call | flops 21743271936 | bytes 46137344 | tf_op jit(solution)/shard_map/experts/pallas_call | solution.py:362
  177.6 3.4 collective-permute-start.4
  183.0 32.4 %experts.3 = (bf16[4,1024,768]{2,1,0:T(8,128)(2,1)}, bf16[4,1024,896]{2,1,0:T(8,128)(2,1)}, bf16[4,768,768]{2,1,0:T(8,128)(2,1)}, bf16[4,768,768]{2,1,0:T(8,128)(2,1)}, f32[4,1,768]{2,1,0:T(1,128)}) custom-call(s32[8]{0:T(128)} %and_select_fusion.tiles_ref, bf16[8,1024,896]{2,1,0:T(8,128)(2,1)} %get-tuple-element.52.x_ref, ...), custom_call_target="tpu_custom_call" | custom-call | flops 21743271936 | bytes 46137344 | tf_op jit(solution)/shard_map/experts/pallas_call | solution.py:362
  223.3 16.5 %collect.2 = (bf16[2496,768]{1,0:T(8,128)(2,1)}, f32[2496,128]{1,0:T(8,128)}) custom-call(s32[144]{0:T(256)} %pad_add_fusion.1.plan_ref, s32[2496,2]{1,0:T(8,128)} %bitcast.111, bf16[4,1024,896]{2,1,0:T(8,128)(2,1)} %get-tuple-element.57.refs_0_, bf16[4,1024,896]{2,1,0:T(8,128)(2,1)} %get-tuple-element.58.refs_1_, ...), custom_call_target="tpu_custom_call" | custom-call | flops 4293918720 | bytes 19152896 | tf_op jit(solution)/shard_map/collect/pallas_call | solution.py:247
  239.9 4.3 fusion.19
  249.5 2.3 collective-permute-start.6
  253.8 2.6 fusion.2.refs_2_.refs_0_
  257.7 18.1 %collective-permute-done.7 = bf16[4,96,768]{2,1,0:T(8,128)(2,1)} collective-permute-done((bf16[4,96,768]{2,1,0:T(8,128)(2,1)}, bf16[4,96,768]{2,1,0:T(8,128)(2,1)}, u32[]{:S(2)}, u32[]{:S(2)}) %collective-permute-start.7) | collective-permute-done | bytes 589856 | tf_op jit(solution)/shard_map/ppermute | solution.py:722
  277.4 2.2 add_convert_fusion.23.refs_4_
  279.9 2.2 add_convert_fusion.24.refs_3_
  282.1 14.4 %collect.3 = bf16[2496,768]{1,0:T(8,128)(2,1)} custom-call(s32[144]{0:T(256)} %pad_add_fusion.1.plan_ref, s32[2496,2]{1,0:T(8,128)} %bitcast.112, bf16[4,1024,768]{2,1,0:T(8,128)(2,1)} %get-tuple-element.53.refs_0_, bf16[4,1024,768]{2,1,0:T(8,128)(2,1)} %get-tuple-element.56.refs_1_, bf16[6,208,768]{2,1,0:T(8,128)(2,1)} %copy-done.2, ...), custom_call_target="tpu_custom_call" | custom-call | flops 3680501760 | bytes 16416768 | tf_op jit(solution)/shard_map/collect/pallas_call | solution.py:247
  298.4 2.3 add_convert_fusion.21
  301.4 2.2 add_convert_fusion.22
  321.2 2.3 add_convert_fusion.18.refs_13_
  323.4 2.2 add_convert_fusion.19.refs_12_
  325.7 11.4 %middle_back.1 = (f32[6,208,768]{2,1,0:T(8,128)}, bf16[6,208,768]{2,1,0:T(8,128)(2,1)}, f32[2,768]{1,0:T(2,128)}, f32[8,768]{1,0:T(8,128)}, f32[128,768]{1,0:T(8,128)}) custom-call(s32[1]{0:T(128)} %constant.372.clone.1.turn_ref, bf16[6,208,768]{2,1,0:T(8,128)(2,1)} %copy-done.2, bf16[6,208,768]{2,1,0:T(8,128)(2,1)} %collective-permute-done.9.refs_1_, ...), custom_call_target="tpu_custom_call" | custom-call | bytes 17252352 | tf_op jit(solution)/shard_map/middle_back/pallas_call | solution.py:405
  344.2 10.1 %collective-permute-done.21 = bf16[4,96,768]{2,1,0:T(8,128)(2,1)S(1)} collective-permute-done((bf16[4,96,768]{2,1,0:T(8,128)(2,1)S(1)}, bf16[4,96,768]{2,1,0:T(8,128)(2,1)S(1)}, u32[]{:S(2)}, u32[]{:S(2)}) %collective-permute-start.21) | collective-permute-done | bytes 589856 | tf_op jit(solution)/shard_map/ppermute | solution.py:722
  364.5 38.3 %attention_backward.1 = (bf16[12,208,768]{2,1,0:T(8,128)(2,1)}, f32[3,768,192]{2,1,0:T(8,128)}, f32[1,768,192]{2,1,0:T(8,128)}, f32[2,192]{1,0:T(2,128)}, f32[3,768]{1,0:T(4,128)}) custom-call(s32[1]{0:T(128)} %constant.372.clone.1.turn_ref, bf16[12,208,768]{2,1,0:T(8,128)(2,1)} %pad_maximum_fusion.refs_0_, ...), custom_call_target="tpu_custom_call" | custom-call | flops 6624903168 | bytes 19169280 | tf_op jit(solution)/shard_map/attention_backward/pallas_call | solution.py:405
  410.4 41.0 %collective-permute-done.28 = f32[20,768]{1,0:T(8,128)S(1)} collective-permute-done((f32[20,768]{1,0:T(8,128)S(1)}, f32[20,768]{1,0:T(8,128)S(1)}, u32[]{:S(2)}, u32[]{:S(2)}) %collective-permute-start.28) | collective-permute-done | bytes 61472 | tf_op jit(solution)/shard_map/ppermute | solution.py:24
  453.8 2.5 collective-permute-done.29
  459.9 3.0 collective-permute-done.30
  464.5 6.2 collective-permute-done.31
  471.9 4.2 collective-permute-done.32
  477.6 9.6 %collective-permute-done.47 = bf16[4,96,768]{2,1,0:T(8,128)(2,1)S(1)} collective-permute-done((bf16[4,96,768]{2,1,0:T(8,128)(2,1)S(1)}, bf16[4,96,768]{2,1,0:T(8,128)(2,1)S(1)}, u32[]{:S(2)}, u32[]{:S(2)}) %collective-permute-start.47) | collective-permute-done | bytes 589856 | tf_op jit(solution)/shard_map/ppermute | solution.py:722
  488.4 6.3 %collective-permute-done.33 = bf16[4,2,1,1,96,192]{5,4,0,3,2,1:T(8,128)(2,1)S(1)} collective-permute-done((bf16[4,2,1,1,96,192]{5,4,0,3,2,1:T(8,128)(2,1)S(1)}, bf16[4,2,1,1,96,192]{5,4,0,3,2,1:T(8,128)(2,1)S(1)}, u32[]{:S(2)}, u32[]{:S(2)}) %collective-permute-start.33) | collective-permute-done | bytes 294944 | tf_op jit(solution)/shard_map/ppermute | solution.py:745
  494.8 5.9 collective-permute-done.39
  502.8 13.9 %collective-permute-done.34 = bf16[4,1,1,1,96,192]{5,4,0,3,2,1:T(8,128)(2,1)S(1)} collective-permute-done((bf16[4,1,1,1,96,192]{5,4,0,3,2,1:T(8,128)(2,1)S(1)}, bf16[4,1,1,1,96,192]{5,4,0,3,2,1:T(8,128)(2,1)S(1)}, u32[]{:S(2)}, u32[]{:S(2)}) %collective-permute-start.34) | collective-permute-done | bytes 147488 | tf_op jit(solution)/shard_map/ppermute | solution.py:745
  522.8 7.6 %collective-permute-done.40 = bf16[4,96,768]{2,1,0:T(8,128)(2,1)S(1)} collective-permute-done((bf16[4,96,768]{2,1,0:T(8,128)(2,1)S(1)}, bf16[4,96,768]{2,1,0:T(8,128)(2,1)S(1)}, u32[]{:S(2)}, u32[]{:S(2)}) %collective-permute-start.40) | collective-permute-done | bytes 589856 | tf_op jit(solution)/shard_map/ppermute | solution.py:722
  541.1 7.8 %collective-permute-done.41 = bf16[4,96,768]{2,1,0:T(8,128)(2,1)S(1)} collective-permute-done((bf16[4,96,768]{2,1,0:T(8,128)(2,1)}, bf16[4,96,768]{2,1,0:T(8,128)(2,1)S(1)}, u32[]{:S(2)}, u32[]{:S(2)}) %collective-permute-start.41) | collective-permute-done | bytes 589856 | tf_op jit(solution)/shard_map/ppermute | solution.py:722
  550.1 6.6 %finish.1 = bf16[6,208,768]{2,1,0:T(8,128)(2,1)} custom-call(s32[1]{0:T(128)} %constant.372.clone.1.turn_ref, bf16[6,208,768]{2,1,0:T(8,128)(2,1)} %fusion.1.refs_0_, bf16[6,208,768]{2,1,0:T(8,128)(2,1)} %collective-permute-done.17.refs_1_, f32[6,208,768]{2,1,0:T(8,128)} %get-tuple-element.66.refs_9_.refs_2_, bf16[12,208,128]{2,1,0:T(8,128)(2,1)} %bitcast.120, ...), custom_call_target="tpu_custom_call" | custom-call | bytes 9584640 | tf_op jit(solution)/shard_map/finish/pallas_call | solution.py:405
  561.9 4.2 collective-permute-done.44
  571.4 12.0 %collective-permute-done.36 = bf16[4,96,768]{2,1,0:T(8,128)(2,1)S(1)} collective-permute-done((bf16[4,96,768]{2,1,0:T(8,128)(2,1)S(1)}, bf16[4,96,768]{2,1,0:T(8,128)(2,1)S(1)}, u32[]{:S(2)}, u32[]{:S(2)}) %collective-permute-start.36) | collective-permute-done | bytes 589856 | tf_op jit(solution)/shard_map/ppermute | solution.py:722
  589.3 11.2 %collective-permute-done.37 = bf16[4,96,768]{2,1,0:T(8,128)(2,1)S(1)} collective-permute-done((bf16[4,96,768]{2,1,0:T(8,128)(2,1)S(1)}, bf16[4,96,768]{2,1,0:T(8,128)(2,1)S(1)}, u32[]{:S(2)}, u32[]{:S(2)}) %collective-permute-start.37) | collective-permute-done | bytes 589856 | tf_op jit(solution)/shard_map/ppermute | solution.py:722
  605.6 4.2 reshape.353.refs_0_
  609.8 15.5 %input_back.1 = f32[2364,768]{1,0:T(8,128)} custom-call(s32[1]{0:T(128)} %bitcast.8.turn_ref, bf16[6,208,768]{2,1,0:T(8,128)(2,1)} %copy-done.9, bf16[6,208,768]{2,1,0:T(8,128)(2,1)} %collective-permute-done.25.other_ref, bf16[12,208,768]{2,1,0:T(8,128)(2,1)} %get-tuple-element.50.refs_2_.refs_1_.x_ref, f32[6,208,768]{2,1,0:T(8,128)} %get-tuple-element.74.own_grad_ref, ...), custom_call_target="tpu_custom_call" | custom-call | bytes 26836992 | tf_op jit(solution)/shard_map/input_back/pallas_call | solution.py:662
  (302 shorter events, 128.0 us)
Async XLA Ops:
  41.0 45.1 %collective-permute-start.1 = (bf16[6,208,768]{2,1,0:T(8,128)(2,1)S(1)}, bf16[6,208,768]{2,1,0:T(8,128)(2,1)}, u32[]{:S(2)}, u32[]{:S(2)}) collective-permute-start(bf16[6,208,768]{2,1,0:T(8,128)(2,1)S(1)} %add_convert_fusion.2.refs_0_), channel_id=1, source_target_pairs={{0,2},{1,3},{2,0},{3,1},{4,6},{5,7},{6,4},{7,5},{8,10},{9,11},{10,... | collective-permute-start | bytes 5750792 | tf_op jit(solution)/shard_map/ppermute | solution.py:690
  93.2 19.8 %collective-permute-start.2 = (bf16[6,208,768]{2,1,0:T(8,128)(2,1)}, bf16[6,208,768]{2,1,0:T(8,128)(2,1)}, u32[]{:S(2)}, u32[]{:S(2)}) collective-permute-start(bf16[6,208,768]{2,1,0:T(8,128)(2,1)} %get-tuple-element.51), channel_id=1, source_target_pairs={{0,1},{1,0},{2,3},{3,2},{4,5},{5,4},{6,7},{7,6},{8,9},{9,8},{10,11... | collective-permute-start | bytes 5750792 | tf_op jit(solution)/shard_map/ppermute | solution.py:686
  177.6 41.5 %collective-permute-start.4 = (bf16[4,96,768]{2,1,0:T(8,128)(2,1)S(1)}, bf16[4,96,768]{2,1,0:T(8,128)(2,1)S(1)}, u32[]{:S(2)}, u32[]{:S(2)}) collective-permute-start(bf16[4,96,768]{2,1,0:T(8,128)(2,1)S(1)} %constant_dynamic-slice_fusion.4.refs_1_), channel_id=1, source_target_pairs={{0,4},{8,0},{16,8},{24,16},{28,24},{20,28},{12,20},{4,12},{1,5},{9... | collective-permute-start | bytes 1769480 | tf_op jit(solution)/shard_map/ppermute | solution.py:722
  182.2 39.1 %collective-permute-start.3 = (bf16[4,96,768]{2,1,0:T(8,128)(2,1)S(1)}, bf16[4,96,768]{2,1,0:T(8,128)(2,1)S(1)}, u32[]{:S(2)}, u32[]{:S(2)}) collective-permute-start(bf16[4,96,768]{2,1,0:T(8,128)(2,1)S(1)} %constant_dynamic-slice_fusion.5.refs_0_), channel_id=1, source_target_pairs={{0,8},{8,16},{16,24},{24,28},{28,20},{20,12},{12,4},{4,0},{1,9},{9... | collective-permute-start | bytes 1769480 | tf_op jit(solution)/shard_map/ppermute | solution.py:722
  244.2 8.1 %collective-permute-start.5 = (bf16[6,208,768]{2,1,0:T(8,128)(2,1)}, bf16[6,208,768]{2,1,0:T(8,128)(2,1)}, u32[]{:S(2)}, u32[]{:S(2)}) collective-permute-start(bf16[6,208,768]{2,1,0:T(8,128)(2,1)} %bitcast.22), channel_id=1, source_target_pairs={{0,1},{1,0},{2,3},{3,2},{4,5},{5,4},{6,7},{7,6},{8,9},{9,8},{10,11... | collective-permute-start | bytes 5750792 | tf_op jit(solution)/shard_map/ppermute | solution.py:686
  247.4 50.9 %collective-permute-start.15 = (bf16[4,96,768]{2,1,0:T(8,128)(2,1)}, bf16[4,96,768]{2,1,0:T(8,128)(2,1)}, u32[]{:S(2)}, u32[]{:S(2)}) collective-permute-start(bf16[4,96,768]{2,1,0:T(8,128)(2,1)} %constant_dynamic-slice_fusion.2.refs_6_), channel_id=1, source_target_pairs={{0,4},{8,0},{16,8},{24,16},{28,24},{20,28},{12,20},{4,12},{1,5},{9... | collective-permute-start | bytes 1769480 | tf_op jit(solution)/shard_map/ppermute | solution.py:722
  247.4 54.0 %collective-permute-start.12 = (bf16[4,96,768]{2,1,0:T(8,128)(2,1)}, bf16[4,96,768]{2,1,0:T(8,128)(2,1)}, u32[]{:S(2)}, u32[]{:S(2)}) collective-permute-start(bf16[4,96,768]{2,1,0:T(8,128)(2,1)} %constant_dynamic-slice_fusion.3.refs_5_), channel_id=1, source_target_pairs={{0,8},{8,16},{16,24},{24,28},{28,20},{20,12},{12,4},{4,0},{1,9},{9... | collective-permute-start | bytes 1769480 | tf_op jit(solution)/shard_map/ppermute | solution.py:722
  249.4 26.4 %collective-permute-start.7 = (bf16[4,96,768]{2,1,0:T(8,128)(2,1)}, bf16[4,96,768]{2,1,0:T(8,128)(2,1)}, u32[]{:S(2)}, u32[]{:S(2)}) collective-permute-start(bf16[4,96,768]{2,1,0:T(8,128)(2,1)} %add_convert_fusion.25.refs_3_), channel_id=1, source_target_pairs={{0,4},{8,0},{16,8},{24,16},{28,24},{20,28},{12,20},{4,12},{1,5},{9... | collective-permute-start | bytes 1769480 | tf_op jit(solution)/shard_map/ppermute | solution.py:722
  249.5 30.1 %collective-permute-start.6 = (bf16[4,96,768]{2,1,0:T(8,128)(2,1)S(1)}, bf16[4,96,768]{2,1,0:T(8,128)(2,1)}, u32[]{:S(2)}, u32[]{:S(2)}) collective-permute-start(bf16[4,96,768]{2,1,0:T(8,128)(2,1)S(1)} %copy-done.12), channel_id=1, source_target_pairs={{0,8},{8,16},{16,24},{24,28},{28,20},{20,12},{12,4},{4,0},{1,9},{9... | collective-permute-start | bytes 1769480 | tf_op jit(solution)/shard_map/ppermute | solution.py:722
  252.3 61.2 %collective-permute-start.11 = (f32[8,1248]{1,0:T(8,128)S(1)}, f32[8,1248]{1,0:T(8,128)S(1)}, u32[]{:S(2)}, u32[]{:S(2)}) collective-permute-start(f32[8,1248]{1,0:T(8,128)S(1)} %copy.170), channel_id=1, source_target_pairs={{0,2},{1,3},{2,0},{3,1},{4,6},{5,7},{6,4},{7,5},{8,10},{9,11},{10,... | collective-permute-start | bytes 119816 | tf_op jit(solution)/shard_map/ppermute | solution.py:690
  275.8 49.8 %collective-permute-start.9 = (bf16[6,208,768]{2,1,0:T(8,128)(2,1)S(1)}, bf16[6,208,768]{2,1,0:T(8,128)(2,1)}, u32[]{:S(2)}, u32[]{:S(2)}) collective-permute-start(bf16[6,208,768]{2,1,0:T(8,128)(2,1)S(1)} %fusion.2.refs_2_.refs_0_), channel_id=1, source_target_pairs={{0,2},{1,3},{2,0},{3,1},{4,6},{5,7},{6,4},{7,5},{8,10},{9,11},{10,... | collective-permute-start | bytes 5750792 | tf_op jit(solution)/shard_map/ppermute | solution.py:690
  279.6 38.9 %collective-permute-start.14 = (bf16[4,96,768]{2,1,0:T(8,128)(2,1)}, bf16[4,96,768]{2,1,0:T(8,128)(2,1)}, u32[]{:S(2)}, u32[]{:S(2)}) collective-permute-start(bf16[4,96,768]{2,1,0:T(8,128)(2,1)} %add_convert_fusion.23.refs_4_), channel_id=1, source_target_pairs={{0,4},{8,0},{16,8},{24,16},{28,24},{20,28},{12,20},{4,12},{1,5},{9... | collective-permute-start | bytes 1769480 | tf_op jit(solution)/shard_map/ppermute | solution.py:722
  300.6 20.5 %collective-permute-start.16 = (bf16[4,96,768]{2,1,0:T(8,128)(2,1)}, bf16[4,96,768]{2,1,0:T(8,128)(2,1)}, u32[]{:S(2)}, u32[]{:S(2)}) collective-permute-start(bf16[4,96,768]{2,1,0:T(8,128)(2,1)} %add_convert_fusion.21), channel_id=1, source_target_pairs={{0,4},{8,0},{16,8},{24,16},{28,24},{20,28},{12,20},{4,12},{1,5},{9... | collective-permute-start | bytes 1769480 | tf_op jit(solution)/shard_map/ppermute | solution.py:722
  303.7 19.8 %collective-permute-start.13 = (bf16[4,96,768]{2,1,0:T(8,128)(2,1)}, bf16[4,96,768]{2,1,0:T(8,128)(2,1)}, u32[]{:S(2)}, u32[]{:S(2)}) collective-permute-start(bf16[4,96,768]{2,1,0:T(8,128)(2,1)} %add_convert_fusion.22), channel_id=1, source_target_pairs={{0,8},{8,16},{16,24},{24,28},{28,20},{20,12},{12,4},{4,0},{1,9},{9... | collective-permute-start | bytes 1769480 | tf_op jit(solution)/shard_map/ppermute | solution.py:722
  315.8 24.6 %collective-permute-start.19 = (bf16[4,96,768]{2,1,0:T(8,128)(2,1)}, bf16[4,96,768]{2,1,0:T(8,128)(2,1)}, u32[]{:S(2)}, u32[]{:S(2)}) collective-permute-start(bf16[4,96,768]{2,1,0:T(8,128)(2,1)} %add_convert_fusion.24.refs_3_), channel_id=1, source_target_pairs={{0,8},{8,16},{16,24},{24,28},{28,20},{20,12},{12,4},{4,0},{1,9},{9... | collective-permute-start | bytes 1769480 | tf_op jit(solution)/shard_map/ppermute | solution.py:722
  337.1 25.1 %collective-permute-start.18 = (bf16[6,208,768]{2,1,0:T(8,128)(2,1)}, bf16[6,208,768]{2,1,0:T(8,128)(2,1)S(1)}, u32[]{:S(2)}, u32[]{:S(2)}) collective-permute-start(bf16[6,208,768]{2,1,0:T(8,128)(2,1)} %get-tuple-element.67), channel_id=1, source_target_pairs={{0,1},{1,0},{2,3},{3,2},{4,5},{5,4},{6,7},{7,6},{8,9},{9,8},{10,11... | collective-permute-start | bytes 5750792 | tf_op jit(solution)/shard_map/ppermute | solution.py:686
  337.5 66.1 %collective-permute-start.8 = (bf16[6,208,768]{2,1,0:T(8,128)(2,1)S(1)}, bf16[6,208,768]{2,1,0:T(8,128)(2,1)S(1)}, u32[]{:S(2)}, u32[]{:S(2)}) collective-permute-start(bf16[6,208,768]{2,1,0:T(8,128)(2,1)S(1)} %bitcast.122), channel_id=1, source_target_pairs={{0,1},{1,0},{2,3},{3,2},{4,5},{5,4},{6,7},{7,6},{8,9},{9,8},{10,11... | collective-permute-start | bytes 5750792 | tf_op jit(solution)/shard_map/ppermute | solution.py:686
  338.1 16.2 %collective-permute-start.21 = (bf16[4,96,768]{2,1,0:T(8,128)(2,1)S(1)}, bf16[4,96,768]{2,1,0:T(8,128)(2,1)S(1)}, u32[]{:S(2)}, u32[]{:S(2)}) collective-permute-start(bf16[4,96,768]{2,1,0:T(8,128)(2,1)S(1)} %copy-done.21), channel_id=1, source_target_pairs={{0,4},{8,0},{16,8},{24,16},{28,24},{20,28},{12,20},{4,12},{1,5},{9... | collective-permute-start | bytes 1769480 | tf_op jit(solution)/shard_map/ppermute | solution.py:722
  338.7 119.6 %collective-permute-start.46 = (bf16[4,96,768]{2,1,0:T(8,128)(2,1)}, bf16[4,96,768]{2,1,0:T(8,128)(2,1)}, u32[]{:S(2)}, u32[]{:S(2)}) collective-permute-start(bf16[4,96,768]{2,1,0:T(8,128)(2,1)} %add_convert_fusion.18.refs_13_), channel_id=1, source_target_pairs={{0,4},{8,0},{16,8},{24,16},{28,24},{20,28},{12,20},{4,12},{1,5},{9... | collective-permute-start | bytes 1769480 | tf_op jit(solution)/shard_map/ppermute | solution.py:722
  341.9 16.6 %collective-permute-start.20 = (bf16[4,96,768]{2,1,0:T(8,128)(2,1)S(1)}, bf16[4,96,768]{2,1,0:T(8,128)(2,1)S(1)}, u32[]{:S(2)}, u32[]{:S(2)}) collective-permute-start(bf16[4,96,768]{2,1,0:T(8,128)(2,1)S(1)} %add_convert_fusion.17), channel_id=1, source_target_pairs={{0,8},{8,16},{16,24},{24,28},{28,20},{20,12},{12,4},{4,0},{1,9},{9... | collective-permute-start | bytes 1769480 | tf_op jit(solution)/shard_map/ppermute | solution.py:722
  354.3 108.7 %collective-permute-start.38 = (bf16[4,96,768]{2,1,0:T(8,128)(2,1)}, bf16[4,96,768]{2,1,0:T(8,128)(2,1)}, u32[]{:S(2)}, u32[]{:S(2)}) collective-permute-start(bf16[4,96,768]{2,1,0:T(8,128)(2,1)} %add_convert_fusion.19.refs_12_), channel_id=1, source_target_pairs={{0,8},{8,16},{16,24},{24,28},{28,20},{20,12},{12,4},{4,0},{1,9},{9... | collective-permute-start | bytes 1769480 | tf_op jit(solution)/shard_map/ppermute | solution.py:722
  358.4 176.6 %collective-permute-start.43 = (bf16[4,96,768]{2,1,0:T(8,128)(2,1)}, bf16[4,96,768]{2,1,0:T(8,128)(2,1)}, u32[]{:S(2)}, u32[]{:S(2)}) collective-permute-start(bf16[4,96,768]{2,1,0:T(8,128)(2,1)} %add_convert_fusion.15.refs_10_), channel_id=1, source_target_pairs={{0,4},{8,0},{16,8},{24,16},{28,24},{20,28},{12,20},{4,12},{1,5},{9... | collective-permute-start | bytes 1769480 | tf_op jit(solution)/shard_map/ppermute | solution.py:722
  405.5 132.2 %collective-permute-start.17 = (bf16[6,208,768]{2,1,0:T(8,128)(2,1)}, bf16[6,208,768]{2,1,0:T(8,128)(2,1)}, u32[]{:S(2)}, u32[]{:S(2)}) collective-permute-start(bf16[6,208,768]{2,1,0:T(8,128)(2,1)} %fusion.1.refs_0_), channel_id=1, source_target_pairs={{0,2},{1,3},{2,0},{3,1},{4,6},{5,7},{6,4},{7,5},{8,10},{9,11},{10,... | collective-permute-start | bytes 5750792 | tf_op jit(solution)/shard_map/ppermute | solution.py:690
  406.0 45.4 %collective-permute-start.28 = (f32[20,768]{1,0:T(8,128)S(1)}, f32[20,768]{1,0:T(8,128)S(1)}, u32[]{:S(2)}, u32[]{:S(2)}) collective-permute-start(f32[20,768]{1,0:T(8,128)S(1)} %fusion.16), channel_id=1, source_target_pairs={{0,2},{1,3},{2,0},{3,1},{4,6},{5,7},{6,4},{7,5},{8,10},{9,11},{10,... | collective-permute-start | bytes 184328 | tf_op jit(solution)/shard_map/ppermute | solution.py:24
  451.6 4.7 collective-permute-start.29
  456.3 19.7 %collective-permute-start.32 = (bf16[4,2,2,1,96,192]{5,4,0,3,2,1:T(8,128)(2,1)S(1)}, bf16[4,2,2,1,96,192]{5,4,0,3,2,1:T(8,128)(2,1)S(1)}, u32[]{:S(2)}, u32[]{:S(2)}) collective-permute-start(bf16[4,2,2,1,96,192]{5,4,0,3,2,1:T(8,128)(2,1)S(1)} %copy.190), channel_id=1, source_target_pairs={{0,4},{4,0},{8,12},{12,8},{16,20},{20,16},{24,28},{28,24},{1,5},{5... | collective-permute-start | bytes 1769480 | tf_op jit(solution)/shard_map/ppermute | solution.py:745
  458.3 4.7 collective-permute-start.30
  463.0 58.7 %collective-permute-start.22 = (bf16[6,208,768]{2,1,0:T(8,128)(2,1)S(1)}, bf16[6,208,768]{2,1,0:T(8,128)(2,1)S(1)}, u32[]{:S(2)}, u32[]{:S(2)}) collective-permute-start(bf16[6,208,768]{2,1,0:T(8,128)(2,1)S(1)} %slice.188), channel_id=1, source_target_pairs={{0,1},{1,0},{2,3},{3,2},{4,5},{5,4},{6,7},{7,6},{8,9},{9,8},{10,11... | collective-permute-start | bytes 5750792 | tf_op jit(solution)/shard_map/ppermute | solution.py:686
  463.0 7.7 %collective-permute-start.31 = (f32[31,768]{1,0:T(8,128)S(1)}, f32[31,768]{1,0:T(8,128)S(1)}, u32[]{:S(2)}, u32[]{:S(2)}) collective-permute-start(f32[31,768]{1,0:T(8,128)S(1)} %add.837), channel_id=1, source_target_pairs={{0,16},{4,20},{8,24},{12,28},{16,0},{20,4},{24,8},{28,12},{1,17},{... | collective-permute-start | bytes 285704 | tf_op jit(solution)/shard_map/ppermute | solution.py:24
  470.7 16.4 %collective-permute-start.47 = (bf16[4,96,768]{2,1,0:T(8,128)(2,1)S(1)}, bf16[4,96,768]{2,1,0:T(8,128)(2,1)S(1)}, u32[]{:S(2)}, u32[]{:S(2)}) collective-permute-start(bf16[4,96,768]{2,1,0:T(8,128)(2,1)S(1)} %add_convert_fusion.6), channel_id=1, source_target_pairs={{0,4},{8,0},{16,8},{24,16},{28,24},{20,28},{12,20},{4,12},{1,5},{9... | collective-permute-start | bytes 1769480 | tf_op jit(solution)/shard_map/ppermute | solution.py:722
  476.3 18.4 %collective-permute-start.33 = (bf16[4,2,1,1,96,192]{5,4,0,3,2,1:T(8,128)(2,1)S(1)}, bf16[4,2,1,1,96,192]{5,4,0,3,2,1:T(8,128)(2,1)S(1)}, u32[]{:S(2)}, u32[]{:S(2)}) collective-permute-start(bf16[4,2,1,1,96,192]{5,4,0,3,2,1:T(8,128)(2,1)S(1)} %dynamic-slice_convert_fusion), channel_id=1, source_target_pairs={{0,8},{4,12},{8,0},{12,4},{16,24},{20,28},{24,16},{28,20},{1,9},{5... | collective-permute-start | bytes 884744 | tf_op jit(solution)/shard_map/ppermute | solution.py:745
  487.1 13.6 %collective-permute-start.39 = (bf16[4,96,768]{2,1,0:T(8,128)(2,1)S(1)}, bf16[4,96,768]{2,1,0:T(8,128)(2,1)S(1)}, u32[]{:S(2)}, u32[]{:S(2)}) collective-permute-start(bf16[4,96,768]{2,1,0:T(8,128)(2,1)S(1)} %add_convert_fusion.12), channel_id=1, source_target_pairs={{0,8},{8,16},{16,24},{24,28},{28,20},{20,12},{12,4},{4,0},{1,9},{9... | collective-permute-start | bytes 1769480 | tf_op jit(solution)/shard_map/ppermute | solution.py:722
  494.7 22.9 %collective-permute-start.48 = (bf16[4,96,768]{2,1,0:T(8,128)(2,1)S(1)}, bf16[4,96,768]{2,1,0:T(8,128)(2,1)S(1)}, u32[]{:S(2)}, u32[]{:S(2)}) collective-permute-start(bf16[4,96,768]{2,1,0:T(8,128)(2,1)S(1)} %add_convert_fusion.5), channel_id=1, source_target_pairs={{0,4},{8,0},{16,8},{24,16},{28,24},{20,28},{12,20},{4,12},{1,5},{9... | collective-permute-start | bytes 1769480 | tf_op jit(solution)/shard_map/ppermute | solution.py:722
  500.7 16.0 %collective-permute-start.34 = (bf16[4,1,1,1,96,192]{5,4,0,3,2,1:T(8,128)(2,1)S(1)}, bf16[4,1,1,1,96,192]{5,4,0,3,2,1:T(8,128)(2,1)S(1)}, u32[]{:S(2)}, u32[]{:S(2)}) collective-permute-start(bf16[4,1,1,1,96,192]{5,4,0,3,2,1:T(8,128)(2,1)S(1)} %dynamic-slice_convert_fusion.1), channel_id=1, source_target_pairs={{0,16},{4,20},{8,24},{12,28},{16,0},{20,4},{24,8},{28,12},{1,17},{... | collective-permute-start | bytes 442376 | tf_op jit(solution)/shard_map/ppermute | solution.py:745
  516.7 13.7 %collective-permute-start.40 = (bf16[4,96,768]{2,1,0:T(8,128)(2,1)S(1)}, bf16[4,96,768]{2,1,0:T(8,128)(2,1)S(1)}, u32[]{:S(2)}, u32[]{:S(2)}) collective-permute-start(bf16[4,96,768]{2,1,0:T(8,128)(2,1)S(1)} %add_convert_fusion.11), channel_id=1, source_target_pairs={{0,8},{8,16},{16,24},{24,28},{28,20},{20,12},{12,4},{4,0},{1,9},{9... | collective-permute-start | bytes 1769480 | tf_op jit(solution)/shard_map/ppermute | solution.py:722
  519.6 15.4 %collective-permute-start.49 = (bf16[4,96,768]{2,1,0:T(8,128)(2,1)}, bf16[4,96,768]{2,1,0:T(8,128)(2,1)}, u32[]{:S(2)}, u32[]{:S(2)}) collective-permute-start(bf16[4,96,768]{2,1,0:T(8,128)(2,1)} %add_convert_fusion.4), channel_id=1, source_target_pairs={{0,4},{8,0},{16,8},{24,16},{28,24},{20,28},{12,20},{4,12},{1,5},{9... | collective-permute-start | bytes 1769480 | tf_op jit(solution)/shard_map/ppermute | solution.py:722
  522.2 45.1 %collective-permute-start.24 = (bf16[6,208,768]{2,1,0:T(8,128)(2,1)S(1)}, bf16[6,208,768]{2,1,0:T(8,128)(2,1)}, u32[]{:S(2)}, u32[]{:S(2)}) collective-permute-start(bf16[6,208,768]{2,1,0:T(8,128)(2,1)S(1)} %add_convert_fusion.1.refs_5_), channel_id=1, source_target_pairs={{0,2},{1,3},{2,0},{3,1},{4,6},{5,7},{6,4},{7,5},{8,10},{9,11},{10,... | collective-permute-start | bytes 5750792 | tf_op jit(solution)/shard_map/ppermute | solution.py:690
  532.5 16.5 %collective-permute-start.41 = (bf16[4,96,768]{2,1,0:T(8,128)(2,1)}, bf16[4,96,768]{2,1,0:T(8,128)(2,1)S(1)}, u32[]{:S(2)}, u32[]{:S(2)}) collective-permute-start(bf16[4,96,768]{2,1,0:T(8,128)(2,1)} %add_convert_fusion.10), channel_id=1, source_target_pairs={{0,8},{8,16},{16,24},{24,28},{28,20},{20,12},{12,4},{4,0},{1,9},{9... | collective-permute-start | bytes 1769480 | tf_op jit(solution)/shard_map/ppermute | solution.py:722
  535.0 23.7 %collective-permute-start.35 = (bf16[4,96,768]{2,1,0:T(8,128)(2,1)S(1)}, bf16[4,96,768]{2,1,0:T(8,128)(2,1)S(1)}, u32[]{:S(2)}, u32[]{:S(2)}) collective-permute-start(bf16[4,96,768]{2,1,0:T(8,128)(2,1)S(1)} %copy-done.19), channel_id=1, source_target_pairs={{0,8},{8,16},{16,24},{24,28},{28,20},{20,12},{12,4},{4,0},{1,9},{9... | collective-permute-start | bytes 1769480 | tf_op jit(solution)/shard_map/ppermute | solution.py:722
  535.0 74.8 %collective-permute-start.26 = (f32[6,208,768]{2,1,0:T(8,128)}, f32[6,208,768]{2,1,0:T(8,128)}, u32[]{:S(2)}, u32[]{:S(2)}) collective-permute-start(f32[6,208,768]{2,1,0:T(8,128)} %get-tuple-element.74.own_grad_ref), channel_id=1, source_target_pairs={{0,1},{1,0},{2,3},{3,2},{4,5},{5,4},{6,7},{7,6},{8,9},{9,8},{10,11... | collective-permute-start | bytes 11501576 | tf_op jit(solution)/shard_map/ppermute | solution.py:686
  537.7 22.5 %collective-permute-start.50 = (bf16[4,96,768]{2,1,0:T(8,128)(2,1)S(1)}, bf16[4,96,768]{2,1,0:T(8,128)(2,1)S(1)}, u32[]{:S(2)}, u32[]{:S(2)}) collective-permute-start(bf16[4,96,768]{2,1,0:T(8,128)(2,1)S(1)} %add_convert_fusion.3), channel_id=1, source_target_pairs={{0,4},{8,0},{16,8},{24,16},{28,24},{20,28},{12,20},{4,12},{1,5},{9... | collective-permute-start | bytes 1769480 | tf_op jit(solution)/shard_map/ppermute | solution.py:722
  548.9 17.2 %collective-permute-start.44 = (bf16[4,96,768]{2,1,0:T(8,128)(2,1)S(1)}, bf16[4,96,768]{2,1,0:T(8,128)(2,1)S(1)}, u32[]{:S(2)}, u32[]{:S(2)}) collective-permute-start(bf16[4,96,768]{2,1,0:T(8,128)(2,1)S(1)} %add_convert_fusion.8), channel_id=1, source_target_pairs={{0,4},{8,0},{16,8},{24,16},{28,24},{20,28},{12,20},{4,12},{1,5},{9... | collective-permute-start | bytes 1769480 | tf_op jit(solution)/shard_map/ppermute | solution.py:722
  558.7 26.0 %collective-permute-start.42 = (bf16[4,96,768]{2,1,0:T(8,128)(2,1)S(1)}, bf16[4,96,768]{2,1,0:T(8,128)(2,1)S(1)}, u32[]{:S(2)}, u32[]{:S(2)}) collective-permute-start(bf16[4,96,768]{2,1,0:T(8,128)(2,1)S(1)} %add_convert_fusion.9), channel_id=1, source_target_pairs={{0,8},{8,16},{16,24},{24,28},{28,20},{20,12},{12,4},{4,0},{1,9},{9... | collective-permute-start | bytes 1769480 | tf_op jit(solution)/shard_map/ppermute | solution.py:722
  560.2 23.2 %collective-permute-start.36 = (bf16[4,96,768]{2,1,0:T(8,128)(2,1)S(1)}, bf16[4,96,768]{2,1,0:T(8,128)(2,1)S(1)}, u32[]{:S(2)}, u32[]{:S(2)}) collective-permute-start(bf16[4,96,768]{2,1,0:T(8,128)(2,1)S(1)} %add_convert_fusion.14), channel_id=1, source_target_pairs={{0,8},{8,16},{16,24},{24,28},{28,20},{20,12},{12,4},{4,0},{1,9},{9... | collective-permute-start | bytes 1769480 | tf_op jit(solution)/shard_map/ppermute | solution.py:722
  566.1 37.1 %collective-permute-start.23 = (bf16[6,208,768]{2,1,0:T(8,128)(2,1)S(1)}, bf16[6,208,768]{2,1,0:T(8,128)(2,1)S(1)}, u32[]{:S(2)}, u32[]{:S(2)}) collective-permute-start(bf16[6,208,768]{2,1,0:T(8,128)(2,1)S(1)} %copy-done.7), channel_id=1, source_target_pairs={{0,1},{1,0},{2,3},{3,2},{4,5},{5,4},{6,7},{7,6},{8,9},{9,8},{10,11... | collective-permute-start | bytes 5750792 | tf_op jit(solution)/shard_map/ppermute | solution.py:686
  567.3 19.2 %collective-permute-start.45 = (bf16[4,96,768]{2,1,0:T(8,128)(2,1)S(1)}, bf16[4,96,768]{2,1,0:T(8,128)(2,1)S(1)}, u32[]{:S(2)}, u32[]{:S(2)}) collective-permute-start(bf16[4,96,768]{2,1,0:T(8,128)(2,1)S(1)} %add_convert_fusion.7), channel_id=1, source_target_pairs={{0,4},{8,0},{16,8},{24,16},{28,24},{20,28},{12,20},{4,12},{1,5},{9... | collective-permute-start | bytes 1769480 | tf_op jit(solution)/shard_map/ppermute | solution.py:722
  583.5 26.3 %collective-permute-start.25 = (bf16[6,208,768]{2,1,0:T(8,128)(2,1)S(1)}, bf16[6,208,768]{2,1,0:T(8,128)(2,1)}, u32[]{:S(2)}, u32[]{:S(2)}) collective-permute-start(bf16[6,208,768]{2,1,0:T(8,128)(2,1)S(1)} %add_convert_fusion.own_ref), channel_id=1, source_target_pairs={{0,1},{1,0},{2,3},{3,2},{4,5},{5,4},{6,7},{7,6},{8,9},{9,8},{10,11... | collective-permute-start | bytes 5750792 | tf_op jit(solution)/shard_map/ppermute | solution.py:686
  584.7 15.8 %collective-permute-start.37 = (bf16[4,96,768]{2,1,0:T(8,128)(2,1)S(1)}, bf16[4,96,768]{2,1,0:T(8,128)(2,1)S(1)}, u32[]{:S(2)}, u32[]{:S(2)}) collective-permute-start(bf16[4,96,768]{2,1,0:T(8,128)(2,1)S(1)} %add_convert_fusion.13), channel_id=1, source_target_pairs={{0,8},{8,16},{16,24},{24,28},{28,20},{20,12},{12,4},{4,0},{1,9},{9... | collective-permute-start | bytes 1769480 | tf_op jit(solution)/shard_map/ppermute | solution.py:722
  (43 other events, 364.5 us)

commit v4 on v3

--- a/solution.py
+++ b/solution.py
@@ -34,6 +34,10 @@
 ROOM = 1024
 TILE = 256
 VMEM = 56 * 1024 * 1024
+
+
+def cost(us):
+    return pl.CostEstimate(flops=int(us * 1.1e9), bytes_accessed=0, transcendentals=0)
 
 
 def route_plan(routes, expert_count):
@@ -108,11 +112,7 @@
         ),
         out_shape=jax.ShapeDtypeStruct((expert_count, ROOM, cols), jnp.bfloat16),
         compiler_params=pltpu.CompilerParams(vmem_limit_bytes=VMEM),
-        cost_estimate=pl.CostEstimate(
-            flops=2 * blocks * LOCAL * BLOCK * cols,
-            bytes_accessed=2 * cols * (blocks * BLOCK + expert_count * ROOM),
-            transcendentals=0,
-        ),
+        cost_estimate=cost(15),
         name="spread",
     )(plan, rows, source)
 
@@ -189,11 +189,7 @@
             jax.ShapeDtypeStruct((blocks * BLOCK, extra), jnp.bfloat16),
         ],
         compiler_params=pltpu.CompilerParams(vmem_limit_bytes=VMEM),
-        cost_estimate=pl.CostEstimate(
-            flops=2 * blocks * LOCAL * BLOCK * cols,
-            bytes_accessed=2 * cols * (blocks * BLOCK + expert_count * ROOM),
-            transcendentals=0,
-        ),
+        cost_estimate=cost(20),
         name="gated_spread",
     )(plan, rows, source, chosen, router)
 
@@ -259,11 +255,7 @@
         ),
         out_shape=out_shape,
         compiler_params=pltpu.CompilerParams(vmem_limit_bytes=VMEM),
-        cost_estimate=pl.CostEstimate(
-            flops=2 * blocks * LOCAL * BLOCK * cols,
-            bytes_accessed=2 * cols * (blocks * BLOCK + expert_count * room),
-            transcendentals=0,
-        ),
+        cost_estimate=cost(16),
         name="collect",
     )(plan, columns, *buffers, *after)
 
@@ -386,7 +378,7 @@
     )(tiles, inputs, grads, up_weight, up_bias[:, None, :], down_weight, *after)
 
 
-def call(kernel, name, grid, ins, outs, after=(), scratch=(), flops=0, traffic=0, each=1, turn=None):
+def call(kernel, name, grid, ins, outs, after=(), scratch=(), us=5, each=1, turn=None):
     turn = jnp.zeros((1,), jnp.int32) if turn is None else turn
 
     def spec(shape, split):
@@ -414,7 +406,7 @@
         ),
         out_shape=[a for a, _ in outs],
         compiler_params=pltpu.CompilerParams(vmem_limit_bytes=VMEM),
-        cost_estimate=pl.CostEstimate(flops=flops, bytes_accessed=traffic, transcendentals=0),
+        cost_estimate=cost(us),
         name=name,
     )(turn, *[a for a, _ in ins], *after)
 
@@ -446,7 +438,7 @@
     column = lax.broadcasted_iota(jnp.int32, scores.shape, 1)
     scores = jnp.where(column < SEQ, scores, -1e30)
     raised = jnp.exp(scores - jnp.max(scores, axis=-1, keepdims=True))
-    return raised / jnp.sum(raised, axis=-1, keepdims=True)
+    return raised * (1.0 / jnp.sum(raised, axis=-1, keepdims=True))
 
 
 def attention_forward(x, turn, gain, shift, weight, bias, out_weight):
@@ -460,28 +452,24 @@
         held[...] = jnp.zeros_like(held)
         for i in range(PAIR):
             held[i, :seq, :] = x_ref[i].astype(jnp.float32)
+        value = held[...].reshape(PAIR * rows, width)
+        pad_ref[...] = value.astype(jnp.bfloat16).reshape(PAIR, rows, width)
+        n = (normal(value)[0] * gain_ref[...] + shift_ref[...]).astype(jnp.bfloat16)
+        n_ref[...] = n.reshape(PAIR, rows, width)
+        for j, ref in enumerate((q_ref, k_ref, v_ref)):
+            made = jnp.dot(n, w_ref[j], preferred_element_type=jnp.float32) + b_ref[j : j + 1, :]
+            ref[...] = made.astype(jnp.bfloat16).reshape(PAIR, rows, inner)
         for i in range(PAIR):
-            value = held[i]
-            pad_ref[i] = value.astype(jnp.bfloat16)
-            n = (normal(value)[0] * gain_ref[...] + shift_ref[...]).astype(jnp.bfloat16)
-            n_ref[i] = n
-            q, k, v = [
-                (
-                    jnp.dot(n, w_ref[j], preferred_element_type=jnp.float32) + b_ref[j : j + 1, :]
-                ).astype(jnp.bfloat16)
-                for j in range(3)
-            ]
-            q_ref[i], k_ref[i], v_ref[i] = q, k, v
+            q, k, v = q_ref[i], k_ref[i], v_ref[i]
             mixed = jnp.zeros((rows, inner), jnp.float32)
             for mask in head_masks(inner):
                 probs = head_probs(q, k, mask).astype(jnp.bfloat16)
                 head = jnp.dot(probs, v, preferred_element_type=jnp.float32)
                 mixed = jnp.where(mask, head, mixed)
-            mixed = mixed.astype(jnp.bfloat16)
-            o_ref[i] = mixed
-            part_ref[i] = jnp.dot(mixed, wo_ref[...], preferred_element_type=jnp.float32).astype(
-                jnp.bfloat16
-            )
+            o_ref[i] = mixed.astype(jnp.bfloat16)
+        mixed = o_ref[...].reshape(PAIR * rows, inner)
+        part = jnp.dot(mixed, wo_ref[...], preferred_element_type=jnp.float32)
+        part_ref[...] = part.astype(jnp.bfloat16).reshape(PAIR, rows, width)
 
     wide = shape_of((images, rows, width), jnp.bfloat16)
     slim = shape_of((images, rows, inner), jnp.bfloat16)
@@ -490,7 +478,7 @@
         [(x, "turned"), (gain, False), (shift, False), (weight, False), (bias, False), (out_weight, False)],
         [(wide, True)] * 3 + [(slim, True)] * 4,
         scratch=[pltpu.VMEM((PAIR, rows, width), jnp.float32)], each=PAIR, turn=turn,
-        flops=images * rows * width * inner * 8, traffic=images * rows * (width * 8 + inner * 8),
+        us=20,
     )
 
 
@@ -500,7 +488,7 @@
 
     def kernel(
         da_ref, x_ref, n_ref, q_ref, k_ref, v_ref, o_ref, w_ref, wo_ref,
-        back_ref, dw_ref, dwo_ref, dbias_ref, sums_ref,
+        back_ref, dw_ref, dwo_ref, dbias_ref, sums_ref, held,
     ):
         @pl.when(pl.program_id(0) == 0)
         def _():
@@ -509,9 +497,12 @@
             dbias_ref[...] = jnp.zeros_like(dbias_ref)
             sums_ref[...] = jnp.zeros_like(sums_ref)
 
+        joined = PAIR * rows
+        da = da_ref[...].reshape(joined, width)
+        do_all = contract(da, wo_ref[...], 1, 1).astype(jnp.bfloat16).reshape(PAIR, rows, inner)
+        scale = HD ** (-0.5)
         for i in range(PAIR):
-            da, q, k, v = da_ref[i], q_ref[i], k_ref[i], v_ref[i]
-            do = contract(da, wo_ref[...], 1, 1).astype(jnp.bfloat16)
+            q, k, v, do = q_ref[i], k_ref[i], v_ref[i], do_all[i]
             dq = dk = dv = jnp.zeros((rows, inner), jnp.float32)
             for mask in head_masks(inner):
                 probs = head_probs(q, k, mask)
@@ -521,21 +512,25 @@
                 ds = ds.astype(jnp.bfloat16)
                 dq = jnp.where(mask, jnp.dot(ds, k, preferred_element_type=jnp.float32), dq)
                 dk = jnp.where(mask, contract(ds, q, 0, 0), dk)
-            scale = HD ** (-0.5)
-            grads = [(dq * scale).astype(jnp.bfloat16), (dk * scale).astype(jnp.bfloat16), dv.astype(jnp.bfloat16)]
-            n = n_ref[i]
-            back = jnp.zeros((rows, width), jnp.float32)
-            for j in range(3):
-                dw_ref[j] += contract(n, grads[j], 0, 0)
-                back += contract(grads[j], w_ref[j], 1, 1)
-            dwo_ref[0] += contract(da, o_ref[i], 0, 0)
-            back_ref[i] = back.astype(jnp.bfloat16)
-            dbias_ref[0:1, :] += jnp.sum(grads[0].astype(jnp.float32), axis=0, keepdims=True)
-            dbias_ref[1:2, :] += jnp.sum(grads[2].astype(jnp.float32), axis=0, keepdims=True)
-            unit, _ = normal(x_ref[i].astype(jnp.float32))
-            sums_ref[0:1, :] += jnp.sum(back * unit, axis=0, keepdims=True)
-            sums_ref[1:2, :] += jnp.sum(back, axis=0, keepdims=True)
-            sums_ref[2:3, :] += jnp.sum(da.astype(jnp.float32), axis=0, keepdims=True)
+            held[0, i] = (dq * scale).astype(jnp.bfloat16)
+            held[1, i] = (dk * scale).astype(jnp.bfloat16)
+            held[2, i] = dv.astype(jnp.bfloat16)
+        n = n_ref[...].reshape(joined, width)
+        back = jnp.zeros((joined, width), jnp.float32)
+        for j in range(3):
+            grad = held[j].reshape(joined, inner)
+            dw_ref[j] += contract(n, grad, 0, 0)
+            back += contract(grad, w_ref[j], 1, 1)
+            if j != 1:
+                dbias_ref[j // 2 : j // 2 + 1, :] += jnp.sum(
+                    grad.astype(jnp.float32), axis=0, keepdims=True
+                )
+        dwo_ref[0] += contract(da, o_ref[...].reshape(joined, inner), 0, 0)
+        back_ref[...] = back.astype(jnp.bfloat16).reshape(PAIR, rows, width)
+        unit, _ = normal(x_ref[...].reshape(joined, width).astype(jnp.float32))
+        sums_ref[0:1, :] += jnp.sum(back * unit, axis=0, keepdims=True)
+        sums_ref[1:2, :] += jnp.sum(back, axis=0, keepdims=True)
+        sums_ref[2:3, :] += jnp.sum(da.astype(jnp.float32), axis=0, keepdims=True)
 
     return call(
         kernel, "attention_backward", images // PAIR,
@@ -547,8 +542,8 @@
             (shape_of((2, inner), jnp.float32), False),
             (shape_of((3, width), jnp.float32), False),
         ],
-        after=after, each=PAIR, flops=images * rows * width * inner * 18,
-        traffic=images * rows * (width * 8 + inner * 8),
+        after=after, each=PAIR, us=30,
+        scratch=[pltpu.VMEM((3, PAIR, rows, inner), jnp.bfloat16)],
     )
 
 
@@ -563,7 +558,7 @@
         kernel, "middle_norm", near.shape[0],
         [(near, True), (far, True), (x, True), (out_bias, False), (gain, False), (shift, False)],
         [(shape_of(near.shape, jnp.float32), True), (shape_of(near.shape, jnp.bfloat16), True)],
-        after=after, traffic=12 * near.size,
+        after=after, us=8,
     )
 
 
@@ -616,7 +611,7 @@
             (shape_of((count, width), jnp.float32), False),
             (shape_of((wide, width), jnp.float32), False),
         ],
-        after=after, traffic=18 * middle.size,
+        after=after, us=8,
     )
 
 
@@ -630,7 +625,7 @@
         kernel, "finish", middle.shape[0],
         [(near, True), (far, True), (middle, True), (pair, True), (down_bias, False)],
         [(shape_of(middle.shape, jnp.bfloat16), True)],
-        after=after, traffic=10 * middle.size,
+        after=after, us=8,
     )[0]
 
 
@@ -677,7 +672,7 @@
         ),
         out_shape=jax.ShapeDtypeStruct((images * SEQ, width), jnp.float32),
         compiler_params=pltpu.CompilerParams(vmem_limit_bytes=VMEM),
-        cost_estimate=pl.CostEstimate(flops=0, bytes_accessed=14 * x.size, transcendentals=0),
+        cost_estimate=cost(15),
         name="input_back",
     )(turn, own, other, x, own_grad, other_grad, gain, *after)
 
@@ -700,36 +695,62 @@
     return value[(0,) * value.ndim].astype(jnp.float32) * 0.0
 
 
-class Ring:
-    def __init__(self, values, way):
-        self.values, self.way, self.step, self.count = values, way, 0, lax.axis_size("dp")
-        self.ring = self.count == len(RING)
-        self.moving = self.local(0) if self.ring else values.astype(jnp.bfloat16)
-
-    def local(self, step):
-        count = self.count
-        chunk = self.values.shape[1] // count
-        order = jnp.array(RING, jnp.int32)
-        place = jnp.array([RING.index(i) for i in range(count)], jnp.int32)
-        owner = order[(place[lax.axis_index("dp")] - self.way * (step + 1)) % count]
-        size = (self.values.shape[0], chunk, self.values.shape[2])
-        return lax.dynamic_slice(self.values, (0, owner * chunk, 0), size).astype(jnp.bfloat16)
-
-    def hop(self, zero):
-        if not self.ring or self.step == self.count - 1:
-            return
-        path = [(RING[i], RING[(i + self.way) % self.count]) for i in range(self.count)]
-        got = lax.ppermute(self.moving, "dp", path)
-        self.step += 1
-        total = got.astype(jnp.float32) + self.local(self.step).astype(jnp.float32) + zero
-        self.moving = total.astype(jnp.bfloat16) if self.step < self.count - 1 else total
-
-    def result(self):
-        if not self.ring:
-            return lax.psum_scatter(self.moving, "dp", scatter_dimension=1, tiled=True).astype(jnp.float32)
-        while self.step < self.count - 1:
-            self.hop(0.0)
-        return self.moving
+def ring_owner(way, step):
+    index = lax.axis_index("dp")
+    place = jnp.where(index % 2 == 0, index // 2, 7 - index // 2)
+    place = (place - way * (step + 1)) % 8
+    return jnp.where(place < 4, 2 * place, 15 - 2 * place).astype(jnp.int32)
+
+
+def ring_hop(value, way):
+    path = [(RING[i], RING[(i + way) % len(RING)]) for i in range(len(RING))]
+    return lax.ppermute(value, "dp", path)
+
+
+def ring_add(got, sources, steps, kinds, after):
+    groups, came = len(sources), got[0].shape[0]
+    many, total, cols = sources[0][0].shape
+    rows, part = total // 8, 2
+    owners = jnp.stack([ring_owner(way, step) for step in steps for way in (1, -1)])
+    joint = all(kind == kinds[0] for kind in kinds)
+
+    def kernel(owners_ref, *refs):
+        held, locals_, outs = refs[:2], refs[2 : 2 + 2 * groups], refs[2 + 2 * groups + len(after) :]
+        for g in range(groups):
+            for d in range(2):
+                value = locals_[2 * g + d][...]
+                if g < came:
+                    value = value.astype(jnp.float32) + held[d][g].astype(jnp.float32)
+                if joint:
+                    outs[d][g] = value.astype(kinds[g])
+                else:
+                    outs[2 * g + d][0] = value.astype(kinds[g])
+
+    def source(slot):
+        return pl.BlockSpec((part, rows, cols), lambda i, own: (i, own[slot], 0))
+
+    def stack(count):
+        return pl.BlockSpec((count, part, rows, cols), lambda i, own: (0, i, 0, 0))
+
+    if joint:
+        outs = [((groups, many, rows, cols), kinds[0])] * 2
+    else:
+        outs = [((1, many, rows, cols), kind) for kind in kinds for _ in range(2)]
+    return pl.pallas_call(
+        kernel,
+        grid_spec=pltpu.PrefetchScalarGridSpec(
+            num_scalar_prefetch=1,
+            grid=(many // part,),
+            in_specs=[stack(came)] * 2
+            + [source(i) for i in range(2 * groups)]
+            + [pl.BlockSpec(memory_space=pl.ANY)] * len(after),
+            out_specs=[stack(dims[0]) for dims, _ in outs],
+        ),
+        out_shape=[jax.ShapeDtypeStruct(dims, kind) for dims, kind in outs],
+        compiler_params=pltpu.CompilerParams(vmem_limit_bytes=VMEM),
+        cost_estimate=cost(5),
+        name="ring_add",
+    )(owners, *got, *[piece for pair in sources for piece in pair], *after)
 
 
 def halving_scatter(values):
@@ -826,19 +847,28 @@
             buffers, grad_buffers, up_weight, up_bias, down_weight, tiles, i * group, group, after
         )
 
-    def tokens(*some):
-        return tuple(ring.moving for ring in some)
-
-    def hops(value, *some):
-        for ring in some:
-            ring.hop(zero_of(value))
-
-    y_first, back_first, up_grad, down_grad, bias_first = experts_of(0, ())
-    first = (Ring(up_grad, 1), Ring(down_grad, -1))
-    y_second, back_second, up_grad, down_grad, bias_second = experts_of(1, tokens(*first))
-    hops(bias_second, *first)
-    back_part, dots = collect((back_first, back_second), columns, plan, width, tokens(*first))
-    second = (Ring(up_grad, 1), Ring(down_grad, -1))
+    ringed = lax.axis_size("dp") == len(RING)
+    low = jnp.bfloat16
+    y_first, back_first, *first, bias_first = experts_of(0, ())
+    moving = ()
+    if ringed:
+        rows_each = width // 8
+        moving = [
+            lax.dynamic_slice_in_dim(grad, ring_owner(way, 0) * rows_each, rows_each, 1)[None]
+            for grad, way in zip(first, (1, -1))
+        ]
+    y_second, back_second, *second, bias_second = experts_of(1, tuple(moving))
+
+    def round_trip(step, kinds, *after):
+        if not ringed:
+            return ()
+        got = [ring_hop(value, way) for value, way in zip(moving, (1, -1))]
+        if step < 8:
+            return ring_add(got, [first, second], [step, step - 1], kinds, after)
+        return ring_add(got, [second], [step - 1], kinds, after)
+
+    moving = round_trip(1, [low, low])
+    back_part, dots = collect((back_first, back_second), columns, plan, width, tuple(moving))
     back_near = core_sum(imaged(back_part), 0.0)
     back_far = across(back_near)
     dots = dots[:, : 2 * expert_count].T
@@ -846,36 +876,32 @@
     own_rows = half * ROWS
     dots = dots[:, :own_rows] + to_core(dots[:, own_rows:])
     dots = (dots + across(dots)).T.reshape(half, ROWS, expert_count)
-    hops(back_near, *first)
-    (moe_part,) = collect(
-        (y_first, y_second), columns, plan, width, (back_near, *tokens(*first, *second))
-    )
-    hops(moe_part, *second)
-    hops(second[1].moving, *first)
-    hops(first[1].moving, *second)
+    moving = round_trip(2, [low, low], back_near)
+    (moe_part,) = collect((y_first, y_second), columns, plan, width, (back_near, *moving))
+    moving = round_trip(3, [low, low], moe_part)
     middle_grad, own_da, moe_sums, router_sums, bias_sums = middle_back(
         back_near, back_far, dots, gates, chosen, mix_pair, imaged(moe_normed), router_weight,
-        down_bias, middle, upstream, row(moe_gain), tokens(*second),
+        down_bias, middle, upstream, row(moe_gain), tuple(moving),
     )
     da = jnp.concatenate([own_da, to_core(own_da)])
     y_near = core_sum(imaged(moe_part), zero_of(own_da))
     y_far = across(y_near)
     other_grad = to_core(middle_grad)
-    hops(own_da, *first)
+    moving = round_trip(4, [low, low], own_da)
     normed_back, grad_qkv, grad_out, grad_qv_bias, sums = attention_backward(
-        da, x, normed, queries, keys, values, mixed, qkv_weight, out_weight, tokens(*first)
+        da, x, normed, queries, keys, values, mixed, qkv_weight, out_weight, (y_near, *moving)
     )
     last_near = core_sum(normed_back, 0.0)
     last_far = across(last_near)
-    hops(normed_back, *second)
-    hops(last_near, *first)
+    moving = round_trip(5, [low, low], last_near)
+    near_zero = zero_of(last_near)
     own_out = finish(y_near, y_far, middle, mix_pair, bias_twice, (last_near,))
     layer_out = in_order(own_out, to_core(own_out))
     router_bias = [router_sums, bias_sums[:expert_count] + bias_sums[expert_count : 2 * expert_count]]
     tensor_parts = jnp.concatenate([sums[:2]] + [0.5 * part for part in (moe_sums, *router_bias)])
     packed = jnp.concatenate(
         [
-            small_sum(tensor_parts, "tensor"),
+            small_sum(tensor_parts + near_zero, "tensor"),
             sums[2:],
             jnp.pad(grad_qv_bias, ((0, 0), (0, width - head_width))),
             bias_first[:, 0],
@@ -883,8 +909,18 @@
         ]
     )
     packed = small_sum(packed, "dp")
-    slim = halving_scatter(jnp.concatenate([grad_qkv, grad_out]))
-    up_first, down_first, up_second, down_second = [ring.result() for ring in first + second]
+    slim = halving_scatter(jnp.concatenate([grad_qkv, grad_out]) + near_zero)
+    if ringed:
+        moving = round_trip(6, [low, low])
+        up_first, down_first, *moving = round_trip(7, [f32, low])
+        up_second, down_second = round_trip(8, [f32])
+    else:
+        up_first, down_first, up_second, down_second = [
+            lax.psum_scatter(grad, "dp", scatter_dimension=1, tiled=True).astype(f32)[None]
+            for grad in (*first, *second)
+        ]
+    grad_up = jnp.concatenate([up_first[0], up_second[0]])
+    grad_down = jnp.concatenate([down_first[0], down_second[0]]).transpose(0, 2, 1)
     last = (last_near.astype(f32) + last_far.astype(f32)).astype(jnp.bfloat16)
     grad_embedded = input_back(
         last, to_core(last), x, middle_grad, other_grad, row(attn_gain), turn,
@@ -903,9 +939,9 @@
         packed[2],
         packed[3],
         packed[4 : 4 + expert_count].T,
-        jnp.concatenate([up_first, up_second]),
+        grad_up,
         packed[base + 3 :],
-        jnp.concatenate([down_first, down_second]).transpose(0, 2, 1),
+        grad_down,
         packed[4 + expert_count : base],
     )
 

time: 636 us -> 578 us (0.909)
  other arithmetic: 72.8 us -> 41.6 us
  Pallas kernels: 239 us -> 269 us
  waiting for transfers between devices: 179 us -> 151 us
  between operations: 28.6 us -> 3.44 us
  starting transfers between devices: 42.8 us -> 34.5 us
    ppermute x28 -> x16, waiting for transfers between devices: 88.6 us -> 34.6 us  [ring_hop(): return lax.ppermute(value, 'dp', path)]
    convert_element_type x24 -> x0, other arithmetic: 41.5 us -> none  [hop(): total.astype(jnp.bfloat16)]
    ppermute x5, waiting for transfers between devices: 12.3 us -> 49.4 us  [across(): return lax.ppermute(value, 'tensor', pairs(lax.axis_size('tensor'), 2))]
    pallas_call x0 -> x8, Pallas kernels: none -> 33.4 us  [ring_add(): pl.pallas_call(kernel, grid_spec=pltpu.PrefetchScalarGridSpec(num_scalar_...]
    ppermute x3, waiting for transfers between devices: 24.4 us -> 6.16 us  [halving_scatter(): got = lax.ppermute(give.astype(jnp.bfloat16), 'dp', pairs(8, 1 << bit))]
    ppermute x28 -> x16, starting transfers between devices: 27.1 us -> 15.3 us  [ring_hop(): return lax.ppermute(value, 'dp', path)]
    unnamed x88 -> x105, local copies, waits for them, and re-layouts: 8.74 us -> 18.1 us
    dynamic_slice x7 -> x0, local copies, waits for them, and re-layouts: 7.51 us -> none  [the longest x4 6.05 us: local(): lax.dynamic_slice(self.values, (0, owner * chunk, 0), size)]
  transfers between devices with their start and end apart: 51 -> 39, of which waited for: 19 -> 17; matrix products, arithmetic and copies ran while one was open for 17% -> 13% of each run, Pallas kernels for 19% -> 23%
where the time goes in v4:
time: 578 us; the launch traced here: 568 us
  Pallas kernels  269 us (47%)
  waiting for transfers between devices  151 us (26%)
  local copies, waits for them, and re-layouts  68.3 us (12%)
  other arithmetic  41.6 us (7%)
  starting transfers between devices  34.5 us (6%)
    pallas_call x5, Pallas kernels, call(): pl.pallas_call(body, grid_spec=pltpu.PrefetchScalarGridSpec(num_scalar_pr...  79 us
    pallas_call x2, Pallas kernels, expert_pass(): pl.pallas_call(kernel, grid_spec=pltpu.PrefetchScalarGridSpec(num_scalar_...  73.2 us
    ppermute x5, waiting for transfers between devices, small_sum(): values = values + lax.ppermute(values, axis, pairs(count, bit))  59.9 us
    ppermute x5, waiting for transfers between devices, across(): return lax.ppermute(value, 'tensor', pairs(lax.axis_size('tensor'), 2))  49.4 us
    ppermute x16, waiting for transfers between devices, ring_hop(): return lax.ppermute(value, 'dp', path)  34.6 us
    pallas_call x8, Pallas kernels, ring_add(): pl.pallas_call(kernel, grid_spec=pltpu.PrefetchScalarGridSpec(num_scalar_...  33.4 us
    pallas_call x2, Pallas kernels, collect(): pl.pallas_call(kernel, grid_spec=pltpu.PrefetchScalarGridSpec(num_scalar_...  31 us
    pallas_call x1, Pallas kernels, gated_spread(): pl.pallas_call(kernel, grid_spec=pltpu.PrefetchScalarGridSpec(num_scalar_...  21.4 us
  transfers between devices with their start and end apart: 39, of which 17 were waited for; matrix products, arithmetic and copies ran while one was open for 13% of the time, Pallas kernels for 23%

profile of v4, /device:TPU:0, one launch (start us, length us, event | category | flops | bytes accessed | tf_op | source)
XLA Modules:
  0.0 568.0 jit_solution(5572062466613183480)
XLA Ops:
  1.4 2.3 copy.97.refs_3_.refs_7_
  4.4 4.2 reshape.201.refs_0_
  9.9 18.6 %attention_forward.1 = (bf16[12,208,768]{2,1,0:T(8,128)(2,1)}, bf16[12,208,768]{2,1,0:T(8,128)(2,1)}, bf16[12,208,768]{2,1,0:T(8,128)(2,1)}, bf16[12,208,192]{2,...) custom-call(s32[1]{0:T(128)S(6)} %select_n.441.turn_ref, ...), custom_call_target="tpu_custom_call" | custom-call | flops 22000001024 | tf_op jit(solution)/shard_map/attention_forward/pallas_call | solution.py:397
  28.5 2.9 slice.140
  36.0 4.3 reshape.202
  42.7 2.5 pad_slice_fusion.1
  45.8 2.3 add_convert_fusion.2.refs_0_
  48.2 2.6 collective-permute-start.1
  51.4 2.4 maximum_select_fusion.refs_10_
  53.7 15.4 %spread.1.refs_6_.g_ref = bf16[8,1024,768]{2,1,0:T(8,128)(2,1)} custom-call(s32[144]{0:T(256)} %pad_add_fusion.1.plan_ref, s32[6,2,416]{2,1,0:T(2,128)} %add_bitcast_fusion.rows_ref, bf16[2496,768]{1,0:T(8,128)(2,1)} %bitcast.99), custom_call_target="tpu_custom_call" | custom-call | flops 16499999744 | tf_op jit(solution)/shard_map/spread/pallas_call | solution.py:101
  69.1 24.0 %collective-permute-done.1.refs_1_ = bf16[6,208,768]{2,1,0:T(8,128)(2,1)S(1)} collective-permute-done((bf16[6,208,768]{2,1,0:T(8,128)(2,1)S(1)}, bf16[6,208,768]{2,1,0:T(8,128)(2,1)S(1)}, u32[]{:S(2)}, u32[]{:S(2)}) %collective-permute-start.1) | collective-permute-done | bytes 1916960 | tf_op jit(solution)/shard_map/ppermute | solution.py:685
  94.4 6.6 %middle_norm.1 = (f32[6,208,768]{2,1,0:T(8,128)}, bf16[6,208,768]{2,1,0:T(8,128)(2,1)}) custom-call(s32[1]{0:T(128)} %constant.452.clone.1.turn_ref, bf16[6,208,768]{2,1,0:T(8,128)(2,1)} %copy-done.9, bf16[6,208,768]{2,1,0:T(8,128)(2,1)} %copy-done.44, bf16[12,208,768]{2,1,0:T(8,128)(2,1)} %get-tuple-element.68.refs_2_.refs_1_.x_ref, ...), custom_call_target="tpu_custom_call" | custom-call | flops 8800000000 | tf_op jit(solution)/shard_map/middle_norm/pallas_call | solution.py:397
  109.1 21.4 %gated_spread.1 = (bf16[8,1024,896]{2,1,0:T(8,128)(2,1)}, f32[2496,128]{1,0:T(8,128)}, bf16[2496,128]{1,0:T(8,128)(2,1)}) custom-call(s32[144]{0:T(256)} %pad_add_fusion.1.plan_ref, s32[6,2,416]{2,1,0:T(2,128)} %add_bitcast_fusion.rows_ref, bf16[2496,768]{1,0:T(8,128)(2,1)} %bitcast.108, s32[2496,2]{1,0:T(8,128)} %bitcast.96, bf16[768,128]{1,0:T(8,128)(2,1)} %pad.22.router_ref), custom_call_target="tpu_custom_call" | custom-call | flops 22000001024 | tf_op jit(solution)/shard_map/gated_spread/pallas_call | solution.py:168
  130.5 38.4 %experts.2 = (bf16[4,1024,768]{2,1,0:T(8,128)(2,1)}, bf16[4,1024,896]{2,1,0:T(8,128)(2,1)}, bf16[4,768,768]{2,1,0:T(8,128)(2,1)}, bf16[4,768,768]{2,1,0:T(8,128)(2,1)}, f32[4,1,768]{2,1,0:T(1,128)}) custom-call(s32[8]{0:T(128)} %and_select_fusion.tiles_ref, bf16[8,1024,896]{2,1,0:T(8,128)(2,1)} %get-tuple-element.70.x_ref, ...), custom_call_target="tpu_custom_call" | custom-call | flops 21743271936 | bytes 46137344 | tf_op jit(solution)/shard_map/experts/pallas_call | solution.py:354
  173.8 34.8 %experts.3 = (bf16[4,1024,768]{2,1,0:T(8,128)(2,1)}, bf16[4,1024,896]{2,1,0:T(8,128)(2,1)}, bf16[4,768,768]{2,1,0:T(8,128)(2,1)}, bf16[4,768,768]{2,1,0:T(8,128)(2,1)}, f32[4,1,768]{2,1,0:T(1,128)}) custom-call(s32[8]{0:T(128)} %and_select_fusion.tiles_ref, bf16[8,1024,896]{2,1,0:T(8,128)(2,1)} %get-tuple-element.70.x_ref, ...), custom_call_target="tpu_custom_call" | custom-call | flops 21743271936 | bytes 46137344 | tf_op jit(solution)/shard_map/experts/pallas_call | solution.py:354
  209.6 3.9 ring_add.8
  215.5 16.5 %collect.2 = (bf16[2496,768]{1,0:T(8,128)(2,1)}, f32[2496,128]{1,0:T(8,128)}) custom-call(s32[144]{0:T(256)} %pad_add_fusion.1.plan_ref, s32[2496,2]{1,0:T(8,128)} %bitcast.102, bf16[4,1024,896]{2,1,0:T(8,128)(2,1)} %get-tuple-element.75.refs_0_, bf16[4,1024,896]{2,1,0:T(8,128)(2,1)} %get-tuple-element.76.refs_1_, ...), custom_call_target="tpu_custom_call" | custom-call | flops 17600000000 | tf_op jit(solution)/shard_map/collect/pallas_call | solution.py:243
  232.0 3.7 fusion.19
  250.1 4.3 ring_add.9
  256.4 14.5 %collect.3.refs_6_ = bf16[2496,768]{1,0:T(8,128)(2,1)} custom-call(s32[144]{0:T(256)} %pad_add_fusion.1.plan_ref, s32[2496,2]{1,0:T(8,128)} %bitcast.103, bf16[4,1024,768]{2,1,0:T(8,128)(2,1)} %get-tuple-element.71.refs_0_, bf16[4,1024,768]{2,1,0:T(8,128)(2,1)} %get-tuple-element.74.refs_1_, bf16[6,208,768]{2,1,0:T(8,128)(2,1)} %copy-done.4, ...), custom_call_target="tpu_custom_call" | custom-call | flops 17600000000 | tf_op jit(solution)/shard_map/collect/pallas_call | solution.py:243
  270.9 3.6 fusion.18
  274.5 6.6 %collective-permute-done.12.refs_0_ = bf16[2,4,96,768]{3,2,1,0:T(8,128)(2,1)S(1)} collective-permute-done((bf16[2,4,96,768]{3,2,1,0:T(8,128)(2,1)}, bf16[2,4,96,768]{3,2,1,0:T(8,128)(2,1)S(1)}, u32[]{:S(2)}, u32[]{:S(2)}) %collective-permute-start.12) | collective-permute-done | bytes 1179680 | tf_op jit(solution)/shard_map/ppermute | solution.py:707
  283.2 4.4 ring_add.10
  287.5 3.8 collective-permute-done.9.refs_1_
  291.3 11.2 %middle_back.1 = (f32[6,208,768]{2,1,0:T(8,128)}, bf16[6,208,768]{2,1,0:T(8,128)(2,1)}, f32[2,768]{1,0:T(2,128)}, f32[8,768]{1,0:T(8,128)}, f32[128,768]{1,0:T(8,128)}) custom-call(s32[1]{0:T(128)} %constant.452.clone.1.turn_ref, bf16[6,208,768]{2,1,0:T(8,128)(2,1)} %copy-done.4, bf16[6,208,768]{2,1,0:T(8,128)(2,1)} %collective-permute-done.9.refs_1_, ...), custom_call_target="tpu_custom_call" | custom-call | flops 8800000000 | tf_op jit(solution)/shard_map/middle_back/pallas_call | solution.py:397
  307.2 3.4 fusion.1.refs_9_.refs_0_
  310.6 20.7 %collective-permute-done.16.refs_0_ = bf16[2,4,96,768]{3,2,1,0:T(8,128)(2,1)S(1)} collective-permute-done((bf16[2,4,96,768]{3,2,1,0:T(8,128)(2,1)}, bf16[2,4,96,768]{3,2,1,0:T(8,128)(2,1)S(1)}, u32[]{:S(2)}, u32[]{:S(2)}) %collective-permute-start.16) | collective-permute-done | bytes 1179680 | tf_op jit(solution)/shard_map/ppermute | solution.py:707
  332.3 4.4 ring_add.11
  336.6 3.8 pad_maximum_fusion.refs_0_
  340.4 36.0 %attention_backward.1 = (bf16[12,208,768]{2,1,0:T(8,128)(2,1)}, f32[3,768,192]{2,1,0:T(8,128)}, f32[1,768,192]{2,1,0:T(8,128)}, f32[2,192]{1,0:T(2,128)}, f32[3,768]{1,0:T(4,128)}) custom-call(s32[1]{0:T(128)} %constant.452.clone.1.turn_ref, bf16[12,208,768]{2,1,0:T(8,128)(2,1)} %pad_maximum_fusion.refs_0_, ...), custom_call_target="tpu_custom_call" | custom-call | flops 32999999488 | tf_op jit(solution)/shard_map/attention_backward/pallas_call | solution.py:397
  376.5 2.9 slice.156
  393.7 34.4 %collective-permute-done.24 = f32[20,768]{1,0:T(8,128)S(1)} collective-permute-done((f32[20,768]{1,0:T(8,128)S(1)}, f32[20,768]{1,0:T(8,128)S(1)}, u32[]{:S(2)}, u32[]{:S(2)}) %collective-permute-start.24) | collective-permute-done | bytes 61472 | tf_op jit(solution)/shard_map/ppermute | solution.py:24
  429.9 3.2 collective-permute-done.25
  434.8 4.3 ring_add.12
  441.2 2.4 collective-permute-start.27
  445.9 6.6 %finish.1 = bf16[6,208,768]{2,1,0:T(8,128)(2,1)} custom-call(s32[1]{0:T(128)} %constant.452.clone.1.turn_ref, bf16[6,208,768]{2,1,0:T(8,128)(2,1)} %fusion.1.refs_9_.refs_0_, bf16[6,208,768]{2,1,0:T(8,128)(2,1)} %collective-permute-done.14.refs_1_, f32[6,208,768]{2,1,0:T(8,128)} %get-tuple-element.87.refs_9_.refs_2_, bf16[12,208,128]{2,1,0:T(8,128)(2,1)} %bitcast.116, ...), custom_call_target="tpu_custom_call" | custom-call | flops 8800000000 | tf_op jit(solution)/shard_map/finish/pallas_call | solution.py:397
  452.5 21.3 %collective-permute-done.27 = f32[31,768]{1,0:T(8,128)S(1)} collective-permute-done((f32[31,768]{1,0:T(8,128)S(1)}, f32[31,768]{1,0:T(8,128)S(1)}, u32[]{:S(2)}, u32[]{:S(2)}) %collective-permute-start.27) | collective-permute-done | bytes 95264 | tf_op jit(solution)/shard_map/ppermute | solution.py:24
  476.6 2.3 collective-permute-done.29
  482.1 4.3 ring_add.13
  486.7 3.9 collective-permute-done.30
  495.9 20.5 %collective-permute-done.20 = bf16[6,208,768]{2,1,0:T(8,128)(2,1)} collective-permute-done((bf16[6,208,768]{2,1,0:T(8,128)(2,1)S(1)}, bf16[6,208,768]{2,1,0:T(8,128)(2,1)}, u32[]{:S(2)}, u32[]{:S(2)}) %collective-permute-start.20) | collective-permute-done | bytes 1916960 | tf_op jit(solution)/shard_map/ppermute | solution.py:685
  516.4 3.3 add_convert_fusion.own_ref
  520.7 4.5 ring_add.14
  531.1 4.2 reshape.208.refs_0_
  535.3 5.8 %collective-permute-done.37.refs_0_ = bf16[1,4,96,768]{3,2,1,0:T(8,128)(2,1)S(1)} collective-permute-done((bf16[1,4,96,768]{3,2,1,0:T(8,128)(2,1)}, bf16[1,4,96,768]{3,2,1,0:T(8,128)(2,1)S(1)}, u32[]{:S(2)}, u32[]{:S(2)}) %collective-permute-start.37) | collective-permute-done | bytes 589856 | tf_op jit(solution)/shard_map/ppermute | solution.py:707
  542.8 3.4 ring_add.15
  546.2 3.0 maximum_bitcast_fusion
  552.1 15.5 %input_back.1 = f32[2364,768]{1,0:T(8,128)} custom-call(s32[1]{0:T(128)} %bitcast.8.turn_ref, bf16[6,208,768]{2,1,0:T(8,128)(2,1)} %add_convert_fusion.own_ref, bf16[6,208,768]{2,1,0:T(8,128)(2,1)} %copy-done.43, bf16[12,208,768]{2,1,0:T(8,128)(2,1)} %get-tuple-element.68.refs_2_.refs_1_.x_ref, f32[6,208,768]{2,1,0:T(8,128)} %get-tuple-element.99.own_grad_ref, ...), custom_call_target="tpu_custom_call" | custom-call | flops 16499999744 | tf_op jit(solution)/shard_map/input_back/pallas_call | solution.py:657
  (273 shorter events, 95.5 us)
Async XLA Ops:
  31.4 13.7 %collective-permute-start = (bf16[6,208,768]{2,1,0:T(8,128)(2,1)}, bf16[6,208,768]{2,1,0:T(8,128)(2,1)}, u32[]{:S(2)}, u32[]{:S(2)}) collective-permute-start(bf16[6,208,768]{2,1,0:T(8,128)(2,1)} %slice.140), channel_id=1, source_target_pairs={{0,1},{1,0},{2,3},{3,2},{4,5},{5,4},{6,7},{7,6},{8,9},{9,8},{10,11... | collective-permute-start | bytes 5750792 | tf_op jit(solution)/shard_map/ppermute | solution.py:681
  48.2 45.0 %collective-permute-start.1 = (bf16[6,208,768]{2,1,0:T(8,128)(2,1)S(1)}, bf16[6,208,768]{2,1,0:T(8,128)(2,1)S(1)}, u32[]{:S(2)}, u32[]{:S(2)}) collective-permute-start(bf16[6,208,768]{2,1,0:T(8,128)(2,1)S(1)} %add_convert_fusion.2.refs_0_), channel_id=1, source_target_pairs={{0,2},{1,3},{2,0},{3,1},{4,6},{5,7},{6,4},{7,5},{8,10},{9,11},{10,... | collective-permute-start | bytes 5750792 | tf_op jit(solution)/shard_map/ppermute | solution.py:685
  94.4 7.8 %copy-start.34 = (bf16[8,768]{1,0:T(8,128)(2,1)S(1)}, bf16[8,768]{1,0:T(8,128)(2,1)}, u32[]{:S(2)}) copy-start(bf16[8,768]{1,0:T(8,128)(2,1)} %param.27) | copy-start | bytes 36868
  101.0 4.5 collective-permute-start.2
  170.1 38.5 %collective-permute-start.4 = (bf16[1,4,96,768]{3,2,1,0:T(8,128)(2,1)S(1)}, bf16[1,4,96,768]{3,2,1,0:T(8,128)(2,1)S(1)}, u32[]{:S(2)}, u32[]{:S(2)}) collective-permute-start(bf16[1,4,96,768]{3,2,1,0:T(8,128)(2,1)S(1)} %dynamic-slice_bitcast_fusion.refs_1_), channel_id=1, source_target_pairs={{0,4},{8,0},{16,8},{24,16},{28,24},{20,28},{12,20},{4,12},{1,5},{9... | collective-permute-start | bytes 1769480 | tf_op jit(solution)/shard_map/ppermute | solution.py:707
  173.0 35.6 %collective-permute-start.3 = (bf16[1,4,96,768]{3,2,1,0:T(8,128)(2,1)S(1)}, bf16[1,4,96,768]{3,2,1,0:T(8,128)(2,1)S(1)}, u32[]{:S(2)}, u32[]{:S(2)}) collective-permute-start(bf16[1,4,96,768]{3,2,1,0:T(8,128)(2,1)S(1)} %dynamic-slice_bitcast_fusion.1.refs_0_), channel_id=1, source_target_pairs={{0,8},{8,16},{16,24},{24,28},{28,20},{20,12},{12,4},{4,0},{1,9},{9... | collective-permute-start | bytes 1769480 | tf_op jit(solution)/shard_map/ppermute | solution.py:707
  213.5 36.6 %collective-permute-start.6 = (bf16[2,4,96,768]{3,2,1,0:T(8,128)(2,1)}, bf16[2,4,96,768]{3,2,1,0:T(8,128)(2,1)}, u32[]{:S(2)}, u32[]{:S(2)}) collective-permute-start(bf16[2,4,96,768]{3,2,1,0:T(8,128)(2,1)} %get-tuple-element.79.refs_2_), channel_id=1, source_target_pairs={{0,8},{8,16},{16,24},{24,28},{28,20},{20,12},{12,4},{4,0},{1,9},{9... | collective-permute-start | bytes 3538952 | tf_op jit(solution)/shard_map/ppermute | solution.py:707
  213.7 36.3 %collective-permute-start.7 = (bf16[2,4,96,768]{3,2,1,0:T(8,128)(2,1)}, bf16[2,4,96,768]{3,2,1,0:T(8,128)(2,1)}, u32[]{:S(2)}, u32[]{:S(2)}) collective-permute-start(bf16[2,4,96,768]{3,2,1,0:T(8,128)(2,1)} %get-tuple-element.80.refs_3_), channel_id=1, source_target_pairs={{0,4},{8,0},{16,8},{24,16},{28,24},{20,28},{12,20},{4,12},{1,5},{9... | collective-permute-start | bytes 3538952 | tf_op jit(solution)/shard_map/ppermute | solution.py:707
  235.7 10.8 %collective-permute-start.5 = (bf16[6,208,768]{2,1,0:T(8,128)(2,1)}, bf16[6,208,768]{2,1,0:T(8,128)(2,1)}, u32[]{:S(2)}, u32[]{:S(2)}) collective-permute-start(bf16[6,208,768]{2,1,0:T(8,128)(2,1)} %bitcast.19), channel_id=1, source_target_pairs={{0,1},{1,0},{2,3},{3,2},{4,5},{5,4},{6,7},{7,6},{8,9},{9,8},{10,11... | collective-permute-start | bytes 5750792 | tf_op jit(solution)/shard_map/ppermute | solution.py:681
  237.5 2.2 collective-permute-start.10
  241.2 4.0 collective-permute-start.11
  248.5 42.8 %collective-permute-start.9 = (bf16[6,208,768]{2,1,0:T(8,128)(2,1)S(1)}, bf16[6,208,768]{2,1,0:T(8,128)(2,1)}, u32[]{:S(2)}, u32[]{:S(2)}) collective-permute-start(bf16[6,208,768]{2,1,0:T(8,128)(2,1)S(1)} %fusion.2.refs_6_.refs_2_.refs_0_), channel_id=1, source_target_pairs={{0,2},{1,3},{2,0},{3,1},{4,6},{5,7},{6,4},{7,5},{8,10},{9,11},{10,... | collective-permute-start | bytes 5750792 | tf_op jit(solution)/shard_map/ppermute | solution.py:685
  254.4 26.8 %collective-permute-start.12 = (bf16[2,4,96,768]{3,2,1,0:T(8,128)(2,1)}, bf16[2,4,96,768]{3,2,1,0:T(8,128)(2,1)S(1)}, u32[]{:S(2)}, u32[]{:S(2)}) collective-permute-start(bf16[2,4,96,768]{3,2,1,0:T(8,128)(2,1)} %get-tuple-element.82.refs_3_), channel_id=1, source_target_pairs={{0,8},{8,16},{16,24},{24,28},{28,20},{20,12},{12,4},{4,0},{1,9},{9... | collective-permute-start | bytes 3538952 | tf_op jit(solution)/shard_map/ppermute | solution.py:707
  255.0 26.8 %collective-permute-start.13 = (bf16[2,4,96,768]{3,2,1,0:T(8,128)(2,1)}, bf16[2,4,96,768]{3,2,1,0:T(8,128)(2,1)S(1)}, u32[]{:S(2)}, u32[]{:S(2)}) collective-permute-start(bf16[2,4,96,768]{3,2,1,0:T(8,128)(2,1)} %get-tuple-element.83.refs_4_), channel_id=1, source_target_pairs={{0,4},{8,0},{16,8},{24,16},{28,24},{20,28},{12,20},{4,12},{1,5},{9... | collective-permute-start | bytes 3538952 | tf_op jit(solution)/shard_map/ppermute | solution.py:707
  274.5 32.7 %collective-permute-start.8 = (bf16[6,208,768]{2,1,0:T(8,128)(2,1)}, bf16[6,208,768]{2,1,0:T(8,128)(2,1)}, u32[]{:S(2)}, u32[]{:S(2)}) collective-permute-start(bf16[6,208,768]{2,1,0:T(8,128)(2,1)} %bitcast.23), channel_id=1, source_target_pairs={{0,1},{1,0},{2,3},{3,2},{4,5},{5,4},{6,7},{7,6},{8,9},{9,8},{10,11... | collective-permute-start | bytes 5750792 | tf_op jit(solution)/shard_map/ppermute | solution.py:681
  302.6 34.1 %collective-permute-start.15 = (bf16[6,208,768]{2,1,0:T(8,128)(2,1)}, bf16[6,208,768]{2,1,0:T(8,128)(2,1)}, u32[]{:S(2)}, u32[]{:S(2)}) collective-permute-start(bf16[6,208,768]{2,1,0:T(8,128)(2,1)} %get-tuple-element.90.refs_6_), channel_id=1, source_target_pairs={{0,1},{1,0},{2,3},{3,2},{4,5},{5,4},{6,7},{7,6},{8,9},{9,8},{10,11... | collective-permute-start | bytes 5750792 | tf_op jit(solution)/shard_map/ppermute | solution.py:681
  302.7 28.6 %collective-permute-start.16 = (bf16[2,4,96,768]{3,2,1,0:T(8,128)(2,1)}, bf16[2,4,96,768]{3,2,1,0:T(8,128)(2,1)S(1)}, u32[]{:S(2)}, u32[]{:S(2)}) collective-permute-start(bf16[2,4,96,768]{3,2,1,0:T(8,128)(2,1)} %get-tuple-element.88.refs_12_), channel_id=1, source_target_pairs={{0,8},{8,16},{16,24},{24,28},{28,20},{20,12},{12,4},{4,0},{1,9},{9... | collective-permute-start | bytes 3538952 | tf_op jit(solution)/shard_map/ppermute | solution.py:707
  303.3 28.6 %collective-permute-start.17 = (bf16[2,4,96,768]{3,2,1,0:T(8,128)(2,1)}, bf16[2,4,96,768]{3,2,1,0:T(8,128)(2,1)}, u32[]{:S(2)}, u32[]{:S(2)}) collective-permute-start(bf16[2,4,96,768]{3,2,1,0:T(8,128)(2,1)} %get-tuple-element.89.refs_13_), channel_id=1, source_target_pairs={{0,4},{8,0},{16,8},{24,16},{28,24},{20,28},{12,20},{4,12},{1,5},{9... | collective-permute-start | bytes 3538952 | tf_op jit(solution)/shard_map/ppermute | solution.py:707
  310.6 26.1 %copy-start.5 = (bf16[6,208,768]{2,1,0:T(8,128)(2,1)S(1)}, bf16[6,208,768]{2,1,0:T(8,128)(2,1)}, u32[]{:S(2)}) copy-start(bf16[6,208,768]{2,1,0:T(8,128)(2,1)} %get-tuple-element.90.refs_6_) | copy-start | bytes 5750788
  376.5 7.9 %copy-start.29 = (f32[8,768]{1,0:T(8,128)S(1)}, f32[8,768]{1,0:T(8,128)}, u32[]{:S(2)}) copy-start(f32[8,768]{1,0:T(8,128)} %get-tuple-element.102) | copy-start | bytes 73732
  376.5 9.9 %copy-start.35 = (f32[3,768]{1,0:T(4,128)S(1)}, f32[3,768]{1,0:T(4,128)}, u32[]{:S(2)}) copy-start(f32[3,768]{1,0:T(4,128)} %get-tuple-element.100) | copy-start | bytes 27652
  376.5 9.9 %copy-start.37 = (f32[2,192]{1,0:T(2,128)S(1)}, f32[2,192]{1,0:T(2,128)}, u32[]{:S(2)}) copy-start(f32[2,192]{1,0:T(2,128)} %get-tuple-element.104) | copy-start | bytes 4612
  379.4 7.0 %collective-permute-start.18 = (bf16[6,208,768]{2,1,0:T(8,128)(2,1)}, bf16[6,208,768]{2,1,0:T(8,128)(2,1)S(1)}, u32[]{:S(2)}, u32[]{:S(2)}) collective-permute-start(bf16[6,208,768]{2,1,0:T(8,128)(2,1)} %slice.156), channel_id=1, source_target_pairs={{0,1},{1,0},{2,3},{3,2},{4,5},{5,4},{6,7},{7,6},{8,9},{9,8},{10,11... | collective-permute-start | bytes 5750792 | tf_op jit(solution)/shard_map/ppermute | solution.py:681
  382.0 63.0 %collective-permute-start.14 = (bf16[6,208,768]{2,1,0:T(8,128)(2,1)}, bf16[6,208,768]{2,1,0:T(8,128)(2,1)}, u32[]{:S(2)}, u32[]{:S(2)}) collective-permute-start(bf16[6,208,768]{2,1,0:T(8,128)(2,1)} %fusion.1.refs_9_.refs_0_), channel_id=1, source_target_pairs={{0,2},{1,3},{2,0},{3,1},{4,6},{5,7},{6,4},{7,5},{8,10},{9,11},{10,... | collective-permute-start | bytes 5750792 | tf_op jit(solution)/shard_map/ppermute | solution.py:685
  384.3 48.8 %collective-permute-start.31 = (bf16[2,4,96,768]{3,2,1,0:T(8,128)(2,1)}, bf16[2,4,96,768]{3,2,1,0:T(8,128)(2,1)}, u32[]{:S(2)}, u32[]{:S(2)}) collective-permute-start(bf16[2,4,96,768]{3,2,1,0:T(8,128)(2,1)} %get-tuple-element.96.refs_10_), channel_id=1, source_target_pairs={{0,8},{8,16},{16,24},{24,28},{28,20},{20,12},{12,4},{4,0},{1,9},{9... | collective-permute-start | bytes 3538952 | tf_op jit(solution)/shard_map/ppermute | solution.py:707
  385.9 48.9 %collective-permute-start.32 = (bf16[2,4,96,768]{3,2,1,0:T(8,128)(2,1)}, bf16[2,4,96,768]{3,2,1,0:T(8,128)(2,1)}, u32[]{:S(2)}, u32[]{:S(2)}) collective-permute-start(bf16[2,4,96,768]{3,2,1,0:T(8,128)(2,1)} %get-tuple-element.97.refs_11_), channel_id=1, source_target_pairs={{0,4},{8,0},{16,8},{24,16},{28,24},{20,28},{12,20},{4,12},{1,5},{9... | collective-permute-start | bytes 3538952 | tf_op jit(solution)/shard_map/ppermute | solution.py:707
  389.9 1.3 collective-permute-start.23
  391.3 36.8 %collective-permute-start.24 = (f32[20,768]{1,0:T(8,128)S(1)}, f32[20,768]{1,0:T(8,128)S(1)}, u32[]{:S(2)}, u32[]{:S(2)}) collective-permute-start(f32[20,768]{1,0:T(8,128)S(1)} %fusion.16), channel_id=1, source_target_pairs={{0,2},{1,3},{2,0},{3,1},{4,6},{5,7},{6,4},{7,5},{8,10},{9,11},{10,... | collective-permute-start | bytes 184328 | tf_op jit(solution)/shard_map/ppermute | solution.py:24
  392.9 48.3 %collective-permute-start.28 = (bf16[4,2,2,1,96,192]{5,4,0,3,2,1:T(8,128)(2,1)}, bf16[4,2,2,1,96,192]{5,4,0,3,2,1:T(8,128)(2,1)}, u32[]{:S(2)}, u32[]{:S(2)}) collective-permute-start(bf16[4,2,2,1,96,192]{5,4,0,3,2,1:T(8,128)(2,1)} %dynamic-slice_convert_fusion), channel_id=1, source_target_pairs={{0,4},{4,0},{8,12},{12,8},{16,20},{20,16},{24,28},{28,24},{1,5},{5... | collective-permute-start | bytes 1769480 | tf_op jit(solution)/shard_map/ppermute | solution.py:766
  428.5 4.7 collective-permute-start.25
  433.1 117.7 %collective-permute-start.22 = (f32[6,208,768]{2,1,0:T(8,128)}, f32[6,208,768]{2,1,0:T(8,128)}, u32[]{:S(2)}, u32[]{:S(2)}) collective-permute-start(f32[6,208,768]{2,1,0:T(8,128)} %get-tuple-element.99.own_grad_ref), channel_id=1, source_target_pairs={{0,1},{1,0},{2,3},{3,2},{4,5},{5,4},{6,7},{7,6},{8,9},{9,8},{10,11... | collective-permute-start | bytes 11501576 | tf_op jit(solution)/shard_map/ppermute | solution.py:681
  433.2 6.4 %collective-permute-start.26 = (f32[31,768]{1,0:T(8,128)S(1)}, f32[31,768]{1,0:T(8,128)S(1)}, u32[]{:S(2)}, u32[]{:S(2)}) collective-permute-start(f32[31,768]{1,0:T(8,128)S(1)} %add.356), channel_id=1, source_target_pairs={{0,8},{4,12},{8,0},{12,4},{16,24},{20,28},{24,16},{28,20},{1,9},{5... | collective-permute-start | bytes 285704 | tf_op jit(solution)/shard_map/ppermute | solution.py:24
  439.1 39.9 %collective-permute-start.33 = (bf16[2,4,96,768]{3,2,1,0:T(8,128)(2,1)}, bf16[2,4,96,768]{3,2,1,0:T(8,128)(2,1)S(1)}, u32[]{:S(2)}, u32[]{:S(2)}) collective-permute-start(bf16[2,4,96,768]{3,2,1,0:T(8,128)(2,1)} %get-tuple-element.109), channel_id=1, source_target_pairs={{0,8},{8,16},{16,24},{24,28},{28,20},{20,12},{12,4},{4,0},{1,9},{9... | collective-permute-start | bytes 3538952 | tf_op jit(solution)/shard_map/ppermute | solution.py:707
  439.6 41.5 %collective-permute-start.34 = (bf16[2,4,96,768]{3,2,1,0:T(8,128)(2,1)}, bf16[2,4,96,768]{3,2,1,0:T(8,128)(2,1)S(1)}, u32[]{:S(2)}, u32[]{:S(2)}) collective-permute-start(bf16[2,4,96,768]{3,2,1,0:T(8,128)(2,1)} %get-tuple-element.110), channel_id=1, source_target_pairs={{0,4},{8,0},{16,8},{24,16},{28,24},{20,28},{12,20},{4,12},{1,5},{9... | collective-permute-start | bytes 3538952 | tf_op jit(solution)/shard_map/ppermute | solution.py:707
  441.2 32.7 %collective-permute-start.27 = (f32[31,768]{1,0:T(8,128)S(1)}, f32[31,768]{1,0:T(8,128)S(1)}, u32[]{:S(2)}, u32[]{:S(2)}) collective-permute-start(f32[31,768]{1,0:T(8,128)S(1)} %add.357), channel_id=1, source_target_pairs={{0,16},{4,20},{8,24},{12,28},{16,0},{20,4},{24,8},{28,12},{1,17},{... | collective-permute-start | bytes 285704 | tf_op jit(solution)/shard_map/ppermute | solution.py:24
  445.0 28.8 %copy-start.2 = (bf16[6,208,768]{2,1,0:T(8,128)(2,1)S(1)}, bf16[6,208,768]{2,1,0:T(8,128)(2,1)}, u32[]{:S(2)}) copy-start(bf16[6,208,768]{2,1,0:T(8,128)(2,1)} %copy-done.1) | copy-start | bytes 5750788
  445.0 33.8 %collective-permute-start.29 = (bf16[4,2,1,1,96,192]{5,4,0,3,2,1:T(8,128)(2,1)S(1)}, bf16[4,2,1,1,96,192]{5,4,0,3,2,1:T(8,128)(2,1)S(1)}, u32[]{:S(2)}, u32[]{:S(2)}) collective-permute-start(bf16[4,2,1,1,96,192]{5,4,0,3,2,1:T(8,128)(2,1)S(1)} %dynamic-slice_convert_fusion.1), channel_id=1, source_target_pairs={{0,8},{4,12},{8,0},{12,4},{16,24},{20,28},{24,16},{28,20},{1,9},{5... | collective-permute-start | bytes 884744 | tf_op jit(solution)/shard_map/ppermute | solution.py:766
  473.8 42.5 %collective-permute-start.20 = (bf16[6,208,768]{2,1,0:T(8,128)(2,1)S(1)}, bf16[6,208,768]{2,1,0:T(8,128)(2,1)}, u32[]{:S(2)}, u32[]{:S(2)}) collective-permute-start(bf16[6,208,768]{2,1,0:T(8,128)(2,1)S(1)} %copy-done.2), channel_id=1, source_target_pairs={{0,2},{1,3},{2,0},{3,1},{4,6},{5,7},{6,4},{7,5},{8,10},{9,11},{10,... | collective-permute-start | bytes 5750792 | tf_op jit(solution)/shard_map/ppermute | solution.py:685
  478.9 48.3 %collective-permute-start.19 = (bf16[6,208,768]{2,1,0:T(8,128)(2,1)}, bf16[6,208,768]{2,1,0:T(8,128)(2,1)}, u32[]{:S(2)}, u32[]{:S(2)}) collective-permute-start(bf16[6,208,768]{2,1,0:T(8,128)(2,1)} %finish.1), channel_id=1, source_target_pairs={{0,1},{1,0},{2,3},{3,2},{4,5},{5,4},{6,7},{7,6},{8,9},{9,8},{10,11... | collective-permute-start | bytes 5750792 | tf_op jit(solution)/shard_map/ppermute | solution.py:681
  479.0 11.6 %collective-permute-start.30 = (bf16[4,1,1,1,96,192]{5,4,0,3,2,1:T(8,128)(2,1)S(1)}, bf16[4,1,1,1,96,192]{5,4,0,3,2,1:T(8,128)(2,1)S(1)}, u32[]{:S(2)}, u32[]{:S(2)}) collective-permute-start(bf16[4,1,1,1,96,192]{5,4,0,3,2,1:T(8,128)(2,1)S(1)} %dynamic-slice_convert_fusion.2), channel_id=1, source_target_pairs={{0,16},{4,20},{8,24},{12,28},{16,0},{20,4},{24,8},{28,12},{1,17},{... | collective-permute-start | bytes 442376 | tf_op jit(solution)/shard_map/ppermute | solution.py:766
  486.5 33.2 %collective-permute-start.35 = (bf16[2,4,96,768]{3,2,1,0:T(8,128)(2,1)}, bf16[2,4,96,768]{3,2,1,0:T(8,128)(2,1)S(1)}, u32[]{:S(2)}, u32[]{:S(2)}) collective-permute-start(bf16[2,4,96,768]{3,2,1,0:T(8,128)(2,1)} %get-tuple-element.111), channel_id=1, source_target_pairs={{0,8},{8,16},{16,24},{24,28},{28,20},{20,12},{12,4},{4,0},{1,9},{9... | collective-permute-start | bytes 3538952 | tf_op jit(solution)/shard_map/ppermute | solution.py:707
  490.6 29.1 %collective-permute-start.36 = (bf16[2,4,96,768]{3,2,1,0:T(8,128)(2,1)}, bf16[2,4,96,768]{3,2,1,0:T(8,128)(2,1)}, u32[]{:S(2)}, u32[]{:S(2)}) collective-permute-start(bf16[2,4,96,768]{3,2,1,0:T(8,128)(2,1)} %get-tuple-element.112), channel_id=1, source_target_pairs={{0,4},{8,0},{16,8},{24,16},{28,24},{20,28},{12,20},{4,12},{1,5},{9... | collective-permute-start | bytes 3538952 | tf_op jit(solution)/shard_map/ppermute | solution.py:707
  492.8 26.9 %copy-start.12 = (f32[4,1,1,1,96,192]{5,4,0,3,2,1:T(8,128)}, f32[4,1,1,1,96,192]{5,4,0,3,2,1:T(8,128)S(1)}, u32[]{:S(2)}) copy-start(f32[4,1,1,1,96,192]{5,4,0,3,2,1:T(8,128)S(1)} %convert_add_fusion.4) | copy-start | bytes 884740
  519.7 7.5 %copy-start.11 = (bf16[6,208,768]{2,1,0:T(8,128)(2,1)S(1)}, bf16[6,208,768]{2,1,0:T(8,128)(2,1)}, u32[]{:S(2)}) copy-start(bf16[6,208,768]{2,1,0:T(8,128)(2,1)} %finish.1) | copy-start | bytes 5750788
  519.7 31.1 %collective-permute-start.21 = (bf16[6,208,768]{2,1,0:T(8,128)(2,1)}, bf16[6,208,768]{2,1,0:T(8,128)(2,1)S(1)}, u32[]{:S(2)}, u32[]{:S(2)}) collective-permute-start(bf16[6,208,768]{2,1,0:T(8,128)(2,1)} %add_convert_fusion.own_ref), channel_id=1, source_target_pairs={{0,1},{1,0},{2,3},{3,2},{4,5},{5,4},{6,7},{7,6},{8,9},{9,8},{10,11... | collective-permute-start | bytes 5750792 | tf_op jit(solution)/shard_map/ppermute | solution.py:681
  525.2 15.9 %collective-permute-start.37 = (bf16[1,4,96,768]{3,2,1,0:T(8,128)(2,1)}, bf16[1,4,96,768]{3,2,1,0:T(8,128)(2,1)S(1)}, u32[]{:S(2)}, u32[]{:S(2)}) collective-permute-start(bf16[1,4,96,768]{3,2,1,0:T(8,128)(2,1)} %get-tuple-element.114), channel_id=1, source_target_pairs={{0,8},{8,16},{16,24},{24,28},{28,20},{20,12},{12,4},{4,0},{1,9},{9... | collective-permute-start | bytes 1769480 | tf_op jit(solution)/shard_map/ppermute | solution.py:707
  525.2 16.0 %collective-permute-start.38 = (bf16[1,4,96,768]{3,2,1,0:T(8,128)(2,1)}, bf16[1,4,96,768]{3,2,1,0:T(8,128)(2,1)S(1)}, u32[]{:S(2)}, u32[]{:S(2)}) collective-permute-start(bf16[1,4,96,768]{3,2,1,0:T(8,128)(2,1)} %get-tuple-element.115), channel_id=1, source_target_pairs={{0,4},{8,0},{16,8},{24,16},{28,24},{20,28},{12,20},{4,12},{1,5},{9... | collective-permute-start | bytes 1769480 | tf_op jit(solution)/shard_map/ppermute | solution.py:707
  535.3 10.8 %copy-start.19 = (f32[1,4,96,768]{3,2,1,0:T(8,128)S(1)}, f32[1,4,96,768]{3,2,1,0:T(8,128)}, u32[]{:S(2)}) copy-start(f32[1,4,96,768]{3,2,1,0:T(8,128)} %get-tuple-element.117) | copy-start | bytes 3538948
  (40 other events, 120.9 us)

commit v5 on v4

--- a/solution.py
+++ b/solution.py
@@ -28,6 +28,7 @@
 
 ROWS = 208
 PAIR = 2
+TRIO = 3
 BLOCK = 416
 GROUPS = 2
 LOCAL = 960
@@ -441,25 +442,26 @@
     return raised * (1.0 / jnp.sum(raised, axis=-1, keepdims=True))
 
 
-def attention_forward(x, turn, gain, shift, weight, bias, out_weight):
+def attention_forward(x, turn, gain, shift, weight, bias, out_weight, half, kept):
     images, seq, width = x.shape
     rows, inner = ROWS, weight.shape[2]
 
     def kernel(
-        x_ref, gain_ref, shift_ref, w_ref, b_ref, wo_ref,
-        part_ref, pad_ref, n_ref, q_ref, k_ref, v_ref, o_ref, held,
+        turn_ref, x_ref, gain_ref, shift_ref, w_ref, b_ref, wo_ref,
+        *refs
     ):
+        part_ref, pad_ref, n_ref, q_ref, k_ref, v_ref, o_ref, held = refs[len(kept) :]
         held[...] = jnp.zeros_like(held)
-        for i in range(PAIR):
+        for i in range(TRIO):
             held[i, :seq, :] = x_ref[i].astype(jnp.float32)
-        value = held[...].reshape(PAIR * rows, width)
-        pad_ref[...] = value.astype(jnp.bfloat16).reshape(PAIR, rows, width)
+        value = held[...].reshape(TRIO * rows, width)
+        pad_ref[...] = value.astype(jnp.bfloat16).reshape(TRIO, rows, width)
         n = (normal(value)[0] * gain_ref[...] + shift_ref[...]).astype(jnp.bfloat16)
-        n_ref[...] = n.reshape(PAIR, rows, width)
+        n_ref[...] = n.reshape(TRIO, rows, width)
         for j, ref in enumerate((q_ref, k_ref, v_ref)):
             made = jnp.dot(n, w_ref[j], preferred_element_type=jnp.float32) + b_ref[j : j + 1, :]
-            ref[...] = made.astype(jnp.bfloat16).reshape(PAIR, rows, inner)
-        for i in range(PAIR):
+            ref[...] = made.astype(jnp.bfloat16).reshape(TRIO, rows, inner)
+        for i in range(TRIO):
             q, k, v = q_ref[i], k_ref[i], v_ref[i]
             mixed = jnp.zeros((rows, inner), jnp.float32)
             for mask in head_masks(inner):
@@ -467,19 +469,43 @@
                 head = jnp.dot(probs, v, preferred_element_type=jnp.float32)
                 mixed = jnp.where(mask, head, mixed)
             o_ref[i] = mixed.astype(jnp.bfloat16)
-        mixed = o_ref[...].reshape(PAIR * rows, inner)
+        mixed = o_ref[...].reshape(TRIO * rows, inner)
         part = jnp.dot(mixed, wo_ref[...], preferred_element_type=jnp.float32)
-        part_ref[...] = part.astype(jnp.bfloat16).reshape(PAIR, rows, width)
+        part_ref[...] = part.astype(jnp.bfloat16).reshape(TRIO, rows, width)
 
     wide = shape_of((images, rows, width), jnp.bfloat16)
     slim = shape_of((images, rows, inner), jnp.bfloat16)
-    return call(
-        kernel, "attention_forward", images // PAIR,
-        [(x, "turned"), (gain, False), (shift, False), (weight, False), (bias, False), (out_weight, False)],
-        [(wide, True)] * 3 + [(slim, True)] * 4,
-        scratch=[pltpu.VMEM((PAIR, rows, width), jnp.float32)], each=PAIR, turn=turn,
-        us=20,
-    )
+    blocks = images // TRIO
+
+    def place(i, turn):
+        return (2 * i + half, 0, 0)
+
+    def whole(array):
+        return pl.BlockSpec(array.shape, lambda i, turn: (0,) * array.ndim)
+
+    small = (gain, shift, weight, bias, out_weight)
+    return pl.pallas_call(
+        kernel,
+        grid_spec=pltpu.PrefetchScalarGridSpec(
+            num_scalar_prefetch=1,
+            grid=(blocks // 2,),
+            in_specs=[
+                pl.BlockSpec(
+                    (TRIO, seq, width), lambda i, turn: ((2 * i + half + turn[0]) % blocks, 0, 0)
+                )
+            ]
+            + [whole(array) for array in small]
+            + [pl.BlockSpec(memory_space=pl.ANY)] * len(kept),
+            out_specs=[pl.BlockSpec((TRIO, rows, width), lambda i, turn: (i, 0, 0))]
+            + [pl.BlockSpec((TRIO, *a.shape[1:]), place) for a in [wide] * 2 + [slim] * 4],
+            scratch_shapes=[pltpu.VMEM((TRIO, rows, width), jnp.float32)],
+        ),
+        out_shape=[shape_of((images // 2, rows, width), jnp.bfloat16)] + [wide] * 2 + [slim] * 4,
+        input_output_aliases={7 + i: 1 + i for i in range(len(kept))},
+        compiler_params=pltpu.CompilerParams(vmem_limit_bytes=VMEM),
+        cost_estimate=cost(9),
+        name="attention_forward",
+    )(turn, x, *small, *kept)
 
 
 def attention_backward(da, x, n, q, k, v, o, weight, out_weight, after):
@@ -548,18 +574,34 @@
 
 
 def middle_norm(near, far, x, out_bias, gain, shift, after):
-    def kernel(near_ref, far_ref, x_ref, bias_ref, gain_ref, shift_ref, middle_ref, n_ref):
-        total = near_ref[0].astype(jnp.float32) + far_ref[0].astype(jnp.float32)
+    each = near[0].shape[0]
+    count, (_, rows, width) = 2 * each, x.shape
+
+    def kernel(near_a, near_b, far_a, far_b, x_ref, bias_ref, gain_ref, shift_ref, *refs):
+        middle_ref, n_ref = refs[len(after) :]
+        early = pl.program_id(0) < each
+        total = jnp.where(early, near_a[0], near_b[0]).astype(jnp.float32)
+        total = total + jnp.where(early, far_a[0], far_b[0]).astype(jnp.float32)
         middle = x_ref[0].astype(jnp.float32) + total + bias_ref[...]
         middle_ref[0] = middle
         n_ref[0] = (normal(middle)[0] * gain_ref[...] + shift_ref[...]).astype(jnp.bfloat16)
 
-    return call(
-        kernel, "middle_norm", near.shape[0],
-        [(near, True), (far, True), (x, True), (out_bias, False), (gain, False), (shift, False)],
-        [(shape_of(near.shape, jnp.float32), True), (shape_of(near.shape, jnp.bfloat16), True)],
-        after=after, us=8,
-    )
+    block = (1, rows, width)
+    low = pl.BlockSpec(block, lambda i: (jnp.minimum(i, each - 1), 0, 0))
+    high = pl.BlockSpec(block, lambda i: (jnp.maximum(i - each, 0), 0, 0))
+    one = pl.BlockSpec(block, lambda i: (i, 0, 0))
+    flat = pl.BlockSpec((1, width), lambda i: (0, 0))
+    return pl.pallas_call(
+        kernel,
+        grid=(count,),
+        in_specs=[low, high, low, high, one, flat, flat, flat]
+        + [pl.BlockSpec(memory_space=pl.ANY)] * len(after),
+        out_specs=[one, one],
+        out_shape=[shape_of((count, rows, width), kind) for kind in (jnp.float32, jnp.bfloat16)],
+        compiler_params=pltpu.CompilerParams(vmem_limit_bytes=VMEM),
+        cost_estimate=cost(7),
+        name="middle_norm",
+    )(*near, *far, x, out_bias, gain, shift, *after)
 
 
 def norm_back(dn, unit, spread_of, gain):
@@ -707,24 +749,23 @@
     return lax.ppermute(value, "dp", path)
 
 
-def ring_add(got, sources, steps, kinds, after):
-    groups, came = len(sources), got[0].shape[0]
-    many, total, cols = sources[0][0].shape
+def ring_add(got, sources, way, steps, kinds, after):
+    groups, came = len(sources), got.shape[0]
+    many, total, cols = sources[0].shape
     rows, part = total // 8, 2
-    owners = jnp.stack([ring_owner(way, step) for step in steps for way in (1, -1)])
+    owners = jnp.stack([ring_owner(way, step) for step in steps])
     joint = all(kind == kinds[0] for kind in kinds)
 
-    def kernel(owners_ref, *refs):
-        held, locals_, outs = refs[:2], refs[2 : 2 + 2 * groups], refs[2 + 2 * groups + len(after) :]
+    def kernel(owners_ref, held, *refs):
+        outs = refs[groups + len(after) :]
         for g in range(groups):
-            for d in range(2):
-                value = locals_[2 * g + d][...]
-                if g < came:
-                    value = value.astype(jnp.float32) + held[d][g].astype(jnp.float32)
-                if joint:
-                    outs[d][g] = value.astype(kinds[g])
-                else:
-                    outs[2 * g + d][0] = value.astype(kinds[g])
+            value = refs[g][...]
+            if g < came:
+                value = value.astype(jnp.float32) + held[g].astype(jnp.float32)
+            if joint:
+                outs[0][g] = value.astype(kinds[g])
+            else:
+                outs[g][0] = value.astype(kinds[g])
 
     def source(slot):
         return pl.BlockSpec((part, rows, cols), lambda i, own: (i, own[slot], 0))
@@ -733,24 +774,24 @@
         return pl.BlockSpec((count, part, rows, cols), lambda i, own: (0, i, 0, 0))
 
     if joint:
-        outs = [((groups, many, rows, cols), kinds[0])] * 2
+        outs = [((groups, many, rows, cols), kinds[0])]
     else:
-        outs = [((1, many, rows, cols), kind) for kind in kinds for _ in range(2)]
+        outs = [((1, many, rows, cols), kind) for kind in kinds]
     return pl.pallas_call(
         kernel,
         grid_spec=pltpu.PrefetchScalarGridSpec(
             num_scalar_prefetch=1,
             grid=(many // part,),
-            in_specs=[stack(came)] * 2
-            + [source(i) for i in range(2 * groups)]
+            in_specs=[stack(came)]
+            + [source(i) for i in range(groups)]
             + [pl.BlockSpec(memory_space=pl.ANY)] * len(after),
             out_specs=[stack(dims[0]) for dims, _ in outs],
         ),
         out_shape=[jax.ShapeDtypeStruct(dims, kind) for dims, kind in outs],
         compiler_params=pltpu.CompilerParams(vmem_limit_bytes=VMEM),
-        cost_estimate=cost(5),
+        cost_estimate=cost(3),
         name="ring_add",
-    )(owners, *got, *[piece for pair in sources for piece in pair], *after)
+    )(owners, got, *sources, *after)
 
 
 def halving_scatter(values):
@@ -812,12 +853,16 @@
 
     turn = (half * core).astype(jnp.int32)[None]
     bias_rows = jnp.stack([qv_bias[0], jnp.zeros_like(qv_bias[0]), qv_bias[1]]).astype(f32)
-    part, x, normed, queries, keys, values, mixed = attention_forward(
-        embedded.reshape(images, SEQ, width), turn // PAIR, row(attn_gain), row(attn_shift),
-        qkv_weight, bias_rows, out_weight,
-    )
-    near = core_sum(part, 0.0)
-    far = across(near)
+    images_in = embedded.reshape(images, SEQ, width)
+    kept, near, far = (), [], []
+    for i in range(2):
+        part, *kept = attention_forward(
+            images_in, turn // TRIO, row(attn_gain), row(attn_shift),
+            qkv_weight, bias_rows, out_weight, i, tuple(kept),
+        )
+        near.append(core_sum(part, 0.0))
+        far.append(across(near[i]))
+    x, normed, queries, keys, values, mixed = kept
 
     chosen = own_first(routes, -1).reshape(images * ROWS, 2)
     rows, columns, plan, tiles = route_plan(chosen, expert_count)
@@ -862,10 +907,14 @@
     def round_trip(step, kinds, *after):
         if not ringed:
             return ()
-        got = [ring_hop(value, way) for value, way in zip(moving, (1, -1))]
-        if step < 8:
-            return ring_add(got, [first, second], [step, step - 1], kinds, after)
-        return ring_add(got, [second], [step - 1], kinds, after)
+        made = []
+        for d, way in enumerate((1, -1)):
+            got = ring_hop(moving[d], way)
+            if step < 8:
+                made.append(ring_add(got, [first[d], second[d]], way, [step, step - 1], kinds, after))
+            else:
+                made.append(ring_add(got, [second[d]], way, [step - 1], kinds, after))
+        return [piece for pieces in zip(*made) for piece in pieces]
 
     moving = round_trip(1, [low, low])
     back_part, dots = collect((back_first, back_second), columns, plan, width, tuple(moving))
@@ -884,24 +933,24 @@
         down_bias, middle, upstream, row(moe_gain), tuple(moving),
     )
     da = jnp.concatenate([own_da, to_core(own_da)])
-    y_near = core_sum(imaged(moe_part), zero_of(own_da))
+    y_near = core_sum(imaged(moe_part), zero_of(back_far))
     y_far = across(y_near)
     other_grad = to_core(middle_grad)
     moving = round_trip(4, [low, low], own_da)
     normed_back, grad_qkv, grad_out, grad_qv_bias, sums = attention_backward(
-        da, x, normed, queries, keys, values, mixed, qkv_weight, out_weight, (y_near, *moving)
+        da, x, normed, queries, keys, values, mixed, qkv_weight, out_weight, (y_far, *moving)
     )
     last_near = core_sum(normed_back, 0.0)
     last_far = across(last_near)
     moving = round_trip(5, [low, low], last_near)
-    near_zero = zero_of(last_near)
+    near_zero, far_zero = zero_of(last_near), zero_of(last_far)
     own_out = finish(y_near, y_far, middle, mix_pair, bias_twice, (last_near,))
     layer_out = in_order(own_out, to_core(own_out))
     router_bias = [router_sums, bias_sums[:expert_count] + bias_sums[expert_count : 2 * expert_count]]
     tensor_parts = jnp.concatenate([sums[:2]] + [0.5 * part for part in (moe_sums, *router_bias)])
     packed = jnp.concatenate(
         [
-            small_sum(tensor_parts + near_zero, "tensor"),
+            small_sum(tensor_parts + far_zero, "tensor"),
             sums[2:],
             jnp.pad(grad_qv_bias, ((0, 0), (0, width - head_width))),
             bias_first[:, 0],
@@ -911,7 +960,7 @@
     packed = small_sum(packed, "dp")
     slim = halving_scatter(jnp.concatenate([grad_qkv, grad_out]) + near_zero)
     if ringed:
-        moving = round_trip(6, [low, low])
+        moving = round_trip(6, [low, low], own_out)
         up_first, down_first, *moving = round_trip(7, [f32, low])
         up_second, down_second = round_trip(8, [f32])
     else:

time: 578 us -> 619 us (1.071)
  Pallas kernels: 269 us -> 288 us
  waiting for transfers between devices: 151 us -> 163 us
    ppermute x5, waiting for transfers between devices: 59.9 us -> 28.2 us  [small_sum(): values = values + lax.ppermute(values, axis, pairs(count, bit))]
    ppermute x16, waiting for transfers between devices: 34.6 us -> 64.8 us  [ring_hop(): return lax.ppermute(value, 'dp', path)]
    ppermute x3, waiting for transfers between devices: 6.16 us -> 35.5 us  [halving_scatter(): got = lax.ppermute(give.astype(jnp.bfloat16), 'dp', pairs(8, 1 << bit))]
    pallas_call x0 -> x3, Pallas kernels: none -> 28.3 us  [the longest x2 21.3 us: attention_forward(): pl.pallas_call(kernel, grid_spec=pltpu.PrefetchScalarGridSpec(num_scalar_...]
    pallas_call x5 -> x3, Pallas kernels: 79 us -> 53.9 us  [call(): pl.pallas_call(body, grid_spec=pltpu.PrefetchScalarGridSpec(num_scalar_pr...]
    pallas_call x8 -> x16, Pallas kernels: 33.4 us -> 49.8 us  [ring_add(): pl.pallas_call(kernel, grid_spec=pltpu.PrefetchScalarGridSpec(num_scalar_...]
    ppermute x5 -> x6, waiting for transfers between devices: 49.4 us -> 34.3 us  [across(): return lax.ppermute(value, 'tensor', pairs(lax.axis_size('tensor'), 2))]
    unnamed x105 -> x121, local copies, waits for them, and re-layouts: 18.1 us -> 19.1 us
  transfers between devices with their start and end apart: 39 -> 41, of which waited for: 17 -> 16; matrix products, arithmetic and copies ran while one was open for 13% -> 13% of each run, Pallas kernels for 23% -> 21%
where the time goes in v5:
time: 619 us; the launch traced here: 609 us
  Pallas kernels  288 us (47%)
  waiting for transfers between devices  163 us (26%)
  local copies, waits for them, and re-layouts  72.6 us (12%)
  other arithmetic  42.2 us (7%)
  starting transfers between devices  38.5 us (6%)
    pallas_call x2, Pallas kernels, expert_pass(): pl.pallas_call(kernel, grid_spec=pltpu.PrefetchScalarGridSpec(num_scalar_...  73.1 us
    ppermute x16, waiting for transfers between devices, ring_hop(): return lax.ppermute(value, 'dp', path)  64.8 us
    pallas_call x3, Pallas kernels, call(): pl.pallas_call(body, grid_spec=pltpu.PrefetchScalarGridSpec(num_scalar_pr...  53.9 us
    pallas_call x16, Pallas kernels, ring_add(): pl.pallas_call(kernel, grid_spec=pltpu.PrefetchScalarGridSpec(num_scalar_...  49.8 us
    ppermute x3, waiting for transfers between devices, halving_scatter(): got = lax.ppermute(give.astype(jnp.bfloat16), 'dp', pairs(8, 1 << bit))  35.5 us
    ppermute x6, waiting for transfers between devices, across(): return lax.ppermute(value, 'tensor', pairs(lax.axis_size('tensor'), 2))  34.3 us
    pallas_call x2, Pallas kernels, collect(): pl.pallas_call(kernel, grid_spec=pltpu.PrefetchScalarGridSpec(num_scalar_...  30.8 us
    ppermute x5, waiting for transfers between devices, small_sum(): values = values + lax.ppermute(values, axis, pairs(count, bit))  28.2 us
  transfers between devices with their start and end apart: 41, of which 16 were waited for; matrix products, arithmetic and copies ran while one was open for 13% of the time, Pallas kernels for 21%

profile of v5, /device:TPU:0, one launch (start us, length us, event | category | flops | bytes accessed | tf_op | source)
XLA Modules:
  0.0 609.2 jit_solution(1696917717159889356)
XLA Ops:
  4.4 4.3 reshape.200.x_ref
  10.0 10.6 %attention_forward.2 = (bf16[6,208,768]{2,1,0:T(8,128)(2,1)}, bf16[12,208,768]{2,1,0:T(8,128)(2,1)}, bf16[12,208,768]{2,1,0:T(8,128)(2,1)}, bf16[12,208,192]{2,1...) custom-call(s32[1]{0:T(128)S(6)} %select_n.442.turn_ref, ...), custom_call_target="tpu_custom_call" | custom-call | flops 9900000256 | tf_op jit(solution)/shard_map/attention_forward/pallas_call | solution.py:487
  20.6 10.7 %attention_forward.3 = (bf16[6,208,768]{2,1,0:T(8,128)(2,1)}, bf16[12,208,768]{2,1,0:T(8,128)(2,1)}, bf16[12,208,768]{2,1,0:T(8,128)(2,1)}, bf16[12,208,192]{2,1...) custom-call(s32[1]{0:T(128)S(6)} %select_n.442.turn_ref, ...), custom_call_target="tpu_custom_call", output_to_operand_aliasing={{1}: (7, {}), {2}: (8, {}), {3}: (9, {}), {4}: (10, {}), {5... | custom-call | flops 9900000256 | tf_op jit(solution)/shard_map/attention_forward/pallas_call | solution.py:487
  40.0 4.6 reshape.201
  54.1 3.0 collective-permute-start.3
  57.6 15.4 %spread.1.refs_0_.g_ref = bf16[8,1024,768]{2,1,0:T(8,128)(2,1)} custom-call(s32[144]{0:T(256)} %pad_add_fusion.1.plan_ref, s32[6,2,416]{2,1,0:T(2,128)} %add_bitcast_fusion.rows_ref, bf16[2496,768]{1,0:T(8,128)(2,1)} %bitcast.100), custom_call_target="tpu_custom_call" | custom-call | flops 16499999744 | tf_op jit(solution)/shard_map/spread/pallas_call | solution.py:102
  73.1 6.1 collective-permute-done.3.far_b
  79.2 19.9 %collective-permute-done.2.far_a = bf16[3,208,768]{2,1,0:T(8,128)(2,1)S(1)} collective-permute-done((bf16[3,208,768]{2,1,0:T(8,128)(2,1)S(1)}, bf16[3,208,768]{2,1,0:T(8,128)(2,1)S(1)}, u32[]{:S(2)}, u32[]{:S(2)}) %collective-permute-start.2) | collective-permute-done | bytes 958496 | tf_op jit(solution)/shard_map/ppermute | solution.py:727
  100.0 7.0 %middle_norm.1 = (f32[6,208,768]{2,1,0:T(8,128)}, bf16[6,208,768]{2,1,0:T(8,128)(2,1)}) custom-call(bf16[3,208,768]{2,1,0:T(8,128)(2,1)} %copy-done.25, bf16[3,208,768]{2,1,0:T(8,128)(2,1)} %copy-done.24, bf16[3,208,768]{2,1,0:T(8,128)(2,1)} %copy-done.52, bf16[3,208,768]{2,1,0:T(8,128)(2,1)} %copy-done.51, ...), custom_call_target="tpu_custom_call" | custom-call | flops 7699999744 | tf_op jit(solution)/shard_map/middle_norm/pallas_call | solution.py:594
  115.1 21.0 %gated_spread.1 = (bf16[8,1024,896]{2,1,0:T(8,128)(2,1)}, f32[2496,128]{1,0:T(8,128)}, bf16[2496,128]{1,0:T(8,128)(2,1)}) custom-call(s32[144]{0:T(256)} %pad_add_fusion.1.plan_ref, s32[6,2,416]{2,1,0:T(2,128)} %add_bitcast_fusion.rows_ref, bf16[2496,768]{1,0:T(8,128)(2,1)} %bitcast.109, s32[2496,2]{1,0:T(8,128)} %bitcast.97, bf16[768,128]{1,0:T(8,128)(2,1)} %pad.22.router_ref), custom_call_target="tpu_custom_call" | custom-call | flops 22000001024 | tf_op jit(solution)/shard_map/gated_spread/pallas_call | solution.py:169
  136.1 38.5 %experts.2 = (bf16[4,1024,768]{2,1,0:T(8,128)(2,1)}, bf16[4,1024,896]{2,1,0:T(8,128)(2,1)}, bf16[4,768,768]{2,1,0:T(8,128)(2,1)}, bf16[4,768,768]{2,1,0:T(8,128)(2,1)}, f32[4,1,768]{2,1,0:T(1,128)}) custom-call(s32[8]{0:T(128)} %and_select_fusion.tiles_ref, bf16[8,1024,896]{2,1,0:T(8,128)(2,1)} %get-tuple-element.70.x_ref, ...), custom_call_target="tpu_custom_call" | custom-call | flops 21743271936 | bytes 46137344 | tf_op jit(solution)/shard_map/experts/pallas_call | solution.py:355
  179.4 34.6 %experts.3 = (bf16[4,1024,768]{2,1,0:T(8,128)(2,1)}, bf16[4,1024,896]{2,1,0:T(8,128)(2,1)}, bf16[4,768,768]{2,1,0:T(8,128)(2,1)}, bf16[4,768,768]{2,1,0:T(8,128)(2,1)}, f32[4,1,768]{2,1,0:T(1,128)}) custom-call(s32[8]{0:T(128)} %and_select_fusion.tiles_ref, bf16[8,1024,896]{2,1,0:T(8,128)(2,1)} %get-tuple-element.70.x_ref, ...), custom_call_target="tpu_custom_call" | custom-call | flops 21743271936 | bytes 46137344 | tf_op jit(solution)/shard_map/experts/pallas_call | solution.py:355
  214.8 3.0 ring_add.17.refs_3_
  221.7 16.5 %collect.2 = (bf16[2496,768]{1,0:T(8,128)(2,1)}, f32[2496,128]{1,0:T(8,128)}) custom-call(s32[144]{0:T(256)} %pad_add_fusion.1.plan_ref, s32[2496,2]{1,0:T(8,128)} %bitcast.103, bf16[4,1024,896]{2,1,0:T(8,128)(2,1)} %get-tuple-element.75.refs_0_, bf16[4,1024,896]{2,1,0:T(8,128)(2,1)} %get-tuple-element.76.refs_1_, bf16[2,4,96,768]{3,2,1,0:T(8,128)(2,1)} %ring_add.16.refs_2_, ...), custom_call_target="tpu_custom_call" | custom-call | flops 17600000000 | tf_op jit(solution)/shard_map/collect/pallas_call | solution.py:244
  238.2 4.2 fusion.19
  254.5 16.6 %collective-permute-done.9.held = bf16[2,4,96,768]{3,2,1,0:T(8,128)(2,1)} collective-permute-done((bf16[2,4,96,768]{3,2,1,0:T(8,128)(2,1)}, bf16[2,4,96,768]{3,2,1,0:T(8,128)(2,1)}, u32[]{:S(2)}, u32[]{:S(2)}) %collective-permute-start.9) | collective-permute-done | bytes 1179680 | tf_op jit(solution)/shard_map/ppermute | solution.py:749
  271.1 3.3 ring_add.19.refs_4_
  275.0 3.2 ring_add.18.refs_3_
  279.7 14.3 %collect.3.refs_2_ = bf16[2496,768]{1,0:T(8,128)(2,1)} custom-call(s32[144]{0:T(256)} %pad_add_fusion.1.plan_ref, s32[2496,2]{1,0:T(8,128)} %bitcast.104, bf16[4,1024,768]{2,1,0:T(8,128)(2,1)} %get-tuple-element.71.refs_0_, bf16[4,1024,768]{2,1,0:T(8,128)(2,1)} %get-tuple-element.74.refs_1_, bf16[6,208,768]{2,1,0:T(8,128)(2,1)} %copy-done.3, ...), custom_call_target="tpu_custom_call" | custom-call | flops 17600000000 | tf_op jit(solution)/shard_map/collect/pallas_call | solution.py:244
  294.0 4.3 fusion.18
  303.8 3.2 ring_add.21.refs_13_
  308.1 3.5 ring_add.20.refs_12_
  311.6 11.4 %middle_back.1 = (f32[6,208,768]{2,1,0:T(8,128)}, bf16[6,208,768]{2,1,0:T(8,128)(2,1)}, f32[2,768]{1,0:T(2,128)}, f32[8,768]{1,0:T(8,128)}, f32[128,768]{1,0:T(8,128)}) custom-call(s32[1]{0:T(128)} %constant.448.clone.1.turn_ref, bf16[6,208,768]{2,1,0:T(8,128)(2,1)} %copy-done.3, bf16[6,208,768]{2,1,0:T(8,128)(2,1)} %collective-permute-done.11.refs_1_, ...), custom_call_target="tpu_custom_call" | custom-call | flops 8800000000 | tf_op jit(solution)/shard_map/middle_back/pallas_call | solution.py:398
  330.3 4.7 collective-permute-done.19.held
  335.0 3.2 ring_add.23.refs_11_
  338.3 18.9 %collective-permute-done.18.held = bf16[2,4,96,768]{3,2,1,0:T(8,128)(2,1)} collective-permute-done((bf16[2,4,96,768]{3,2,1,0:T(8,128)(2,1)S(1)}, bf16[2,4,96,768]{3,2,1,0:T(8,128)(2,1)}, u32[]{:S(2)}, u32[]{:S(2)}) %collective-permute-start.18) | collective-permute-done | bytes 1179680 | tf_op jit(solution)/shard_map/ppermute | solution.py:749
  357.2 3.4 ring_add.22.refs_10_
  360.5 3.8 pad_maximum_fusion.refs_0_
  364.3 7.2 %collective-permute-done.12.refs_9_.refs_1_ = bf16[6,208,768]{2,1,0:T(8,128)(2,1)} collective-permute-done((bf16[6,208,768]{2,1,0:T(8,128)(2,1)S(1)}, bf16[6,208,768]{2,1,0:T(8,128)(2,1)}, u32[]{:S(2)}, u32[]{:S(2)}) %collective-permute-start.12) | collective-permute-done | bytes 1916960 | tf_op jit(solution)/shard_map/ppermute | solution.py:727
  371.5 36.0 %attention_backward.1 = (bf16[12,208,768]{2,1,0:T(8,128)(2,1)}, f32[3,768,192]{2,1,0:T(8,128)}, f32[1,768,192]{2,1,0:T(8,128)}, f32[2,192]{1,0:T(2,128)}, f32[3,768]{1,0:T(4,128)}) custom-call(s32[1]{0:T(128)} %constant.448.clone.1.turn_ref, bf16[12,208,768]{2,1,0:T(8,128)(2,1)} %pad_maximum_fusion.refs_0_, ...), custom_call_target="tpu_custom_call" | custom-call | flops 32999999488 | tf_op jit(solution)/shard_map/attention_backward/pallas_call | solution.py:398
  427.7 16.7 %collective-permute-done.37.held = bf16[2,4,96,768]{3,2,1,0:T(8,128)(2,1)S(1)} collective-permute-done((bf16[2,4,96,768]{3,2,1,0:T(8,128)(2,1)}, bf16[2,4,96,768]{3,2,1,0:T(8,128)(2,1)S(1)}, u32[]{:S(2)}, u32[]{:S(2)}) %collective-permute-start.37) | collective-permute-done | bytes 1179680 | tf_op jit(solution)/shard_map/ppermute | solution.py:749
  445.4 3.2 ring_add.28
  451.0 11.6 %collective-permute-done.30 = bf16[4,2,2,1,96,192]{5,4,0,3,2,1:T(8,128)(2,1)} collective-permute-done((bf16[4,2,2,1,96,192]{5,4,0,3,2,1:T(8,128)(2,1)}, bf16[4,2,2,1,96,192]{5,4,0,3,2,1:T(8,128)(2,1)}, u32[]{:S(2)}, u32[]{:S(2)}) %collective-permute-start.30) | collective-permute-done | bytes 589856 | tf_op jit(solution)/shard_map/ppermute | solution.py:807
  464.1 3.2 ring_add.24
  469.3 15.2 %collective-permute-done.31 = bf16[4,2,1,1,96,192]{5,4,0,3,2,1:T(8,128)(2,1)S(1)} collective-permute-done((bf16[4,2,1,1,96,192]{5,4,0,3,2,1:T(8,128)(2,1)S(1)}, bf16[4,2,1,1,96,192]{5,4,0,3,2,1:T(8,128)(2,1)S(1)}, u32[]{:S(2)}, u32[]{:S(2)}) %collective-permute-start.31) | collective-permute-done | bytes 294944 | tf_op jit(solution)/shard_map/ppermute | solution.py:807
  486.4 6.6 %finish.1.refs_2_ = bf16[6,208,768]{2,1,0:T(8,128)(2,1)} custom-call(s32[1]{0:T(128)} %constant.448.clone.1.turn_ref, bf16[6,208,768]{2,1,0:T(8,128)(2,1)} %copy-done.11, bf16[6,208,768]{2,1,0:T(8,128)(2,1)} %collective-permute-done.12.refs_9_.refs_1_, f32[6,208,768]{2,1,0:T(8,128)} %get-tuple-element.80.refs_9_.refs_2_, bf16[12,208,128]{2,1,0:T(8,128)(2,1)} %bitcast.117, ...), custom_call_target="tpu_custom_call" | custom-call | flops 8800000000 | tf_op jit(solution)/shard_map/finish/pallas_call | solution.py:398
  492.9 8.7 %collective-permute-done.32 = bf16[4,1,1,1,96,192]{5,4,0,3,2,1:T(8,128)(2,1)S(1)} collective-permute-done((bf16[4,1,1,1,96,192]{5,4,0,3,2,1:T(8,128)(2,1)S(1)}, bf16[4,1,1,1,96,192]{5,4,0,3,2,1:T(8,128)(2,1)S(1)}, u32[]{:S(2)}, u32[]{:S(2)}) %collective-permute-start.32) | collective-permute-done | bytes 147488 | tf_op jit(solution)/shard_map/ppermute | solution.py:807
  507.1 3.2 ring_add.29
  510.4 3.4 collective-permute-start.39
  516.5 3.5 ring_add.25
  522.3 3.3 add_convert_fusion.own_ref
  525.6 24.1 %collective-permute-done.27 = f32[31,768]{1,0:T(8,128)S(1)} collective-permute-done((f32[31,768]{1,0:T(8,128)S(1)}, f32[31,768]{1,0:T(8,128)S(1)}, u32[]{:S(2)}, u32[]{:S(2)}) %collective-permute-start.27) | collective-permute-done | bytes 95264 | tf_op jit(solution)/shard_map/ppermute | solution.py:24
  551.8 3.2 collective-permute-done.28
  557.1 4.2 reshape.207.refs_0_
  563.0 3.3 ring_add.30
  567.9 3.3 ring_add.26
  573.8 7.9 %collective-permute-done.40.held = bf16[1,4,96,768]{3,2,1,0:T(8,128)(2,1)S(1)} collective-permute-done((bf16[1,4,96,768]{3,2,1,0:T(8,128)(2,1)}, bf16[1,4,96,768]{3,2,1,0:T(8,128)(2,1)S(1)}, u32[]{:S(2)}, u32[]{:S(2)}) %collective-permute-start.40) | collective-permute-done | bytes 589856 | tf_op jit(solution)/shard_map/ppermute | solution.py:749
  593.3 15.5 %input_back.1 = f32[2364,768]{1,0:T(8,128)} custom-call(s32[1]{0:T(128)} %bitcast.8.turn_ref, bf16[6,208,768]{2,1,0:T(8,128)(2,1)} %add_convert_fusion.own_ref, bf16[6,208,768]{2,1,0:T(8,128)(2,1)} %collective-permute-done.23.other_ref, bf16[12,208,768]{2,1,0:T(8,128)(2,1)} %get-tuple-element.68.x_ref.refs_1_, ...), custom_call_target="tpu_custom_call" | custom-call | flops 16499999744 | tf_op jit(solution)/shard_map/input_back/pallas_call | solution.py:699
  (307 shorter events, 128.5 us)
Async XLA Ops:
  33.7 18.8 %collective-permute-start.1 = (bf16[3,208,768]{2,1,0:T(8,128)(2,1)}, bf16[3,208,768]{2,1,0:T(8,128)(2,1)}, u32[]{:S(2)}, u32[]{:S(2)}) collective-permute-start(bf16[3,208,768]{2,1,0:T(8,128)(2,1)} %slice.151), channel_id=1, source_target_pairs={{0,1},{1,0},{2,3},{3,2},{4,5},{5,4},{6,7},{7,6},{8,9},{9,8},{10,11... | collective-permute-start | bytes 2875400 | tf_op jit(solution)/shard_map/ppermute | solution.py:723
  35.1 22.0 %collective-permute-start = (bf16[3,208,768]{2,1,0:T(8,128)(2,1)}, bf16[3,208,768]{2,1,0:T(8,128)(2,1)S(1)}, u32[]{:S(2)}, u32[]{:S(2)}) collective-permute-start(bf16[3,208,768]{2,1,0:T(8,128)(2,1)} %slice.149), channel_id=1, source_target_pairs={{0,1},{1,0},{2,3},{3,2},{4,5},{5,4},{6,7},{7,6},{8,9},{9,8},{10,11... | collective-permute-start | bytes 2875400 | tf_op jit(solution)/shard_map/ppermute | solution.py:723
  54.1 19.0 %copy-start.24 = (bf16[3,208,768]{2,1,0:T(8,128)(2,1)}, bf16[3,208,768]{2,1,0:T(8,128)(2,1)S(1)}, u32[]{:S(2)}) copy-start(bf16[3,208,768]{2,1,0:T(8,128)(2,1)S(1)} %add_convert_fusion.2.near_b) | copy-start | bytes 2875396
  54.1 25.0 %collective-permute-start.3 = (bf16[3,208,768]{2,1,0:T(8,128)(2,1)S(1)}, bf16[3,208,768]{2,1,0:T(8,128)(2,1)S(1)}, u32[]{:S(2)}, u32[]{:S(2)}) collective-permute-start(bf16[3,208,768]{2,1,0:T(8,128)(2,1)S(1)} %add_convert_fusion.2.near_b), channel_id=1, source_target_pairs={{0,2},{1,3},{2,0},{3,1},{4,6},{5,7},{6,4},{7,5},{8,10},{9,11},{10,... | collective-permute-start | bytes 2875400 | tf_op jit(solution)/shard_map/ppermute | solution.py:727
  57.4 15.7 %copy-start.25 = (bf16[3,208,768]{2,1,0:T(8,128)(2,1)}, bf16[3,208,768]{2,1,0:T(8,128)(2,1)S(1)}, u32[]{:S(2)}) copy-start(bf16[3,208,768]{2,1,0:T(8,128)(2,1)S(1)} %add_convert_fusion.3.near_a) | copy-start | bytes 2875396
  57.4 41.7 %collective-permute-start.2 = (bf16[3,208,768]{2,1,0:T(8,128)(2,1)S(1)}, bf16[3,208,768]{2,1,0:T(8,128)(2,1)S(1)}, u32[]{:S(2)}, u32[]{:S(2)}) collective-permute-start(bf16[3,208,768]{2,1,0:T(8,128)(2,1)S(1)} %add_convert_fusion.3.near_a), channel_id=1, source_target_pairs={{0,2},{1,3},{2,0},{3,1},{4,6},{5,7},{6,4},{7,5},{8,10},{9,11},{10,... | collective-permute-start | bytes 2875400 | tf_op jit(solution)/shard_map/ppermute | solution.py:727
  79.2 19.9 %copy-start.51 = (bf16[3,208,768]{2,1,0:T(8,128)(2,1)}, bf16[3,208,768]{2,1,0:T(8,128)(2,1)S(1)}, u32[]{:S(2)}) copy-start(bf16[3,208,768]{2,1,0:T(8,128)(2,1)S(1)} %collective-permute-done.3.far_b) | copy-start | bytes 2875396
  107.0 4.6 collective-permute-start.4
  175.6 38.4 %collective-permute-start.6 = (bf16[1,4,96,768]{3,2,1,0:T(8,128)(2,1)S(1)}, bf16[1,4,96,768]{3,2,1,0:T(8,128)(2,1)S(1)}, u32[]{:S(2)}, u32[]{:S(2)}) collective-permute-start(bf16[1,4,96,768]{3,2,1,0:T(8,128)(2,1)S(1)} %dynamic-slice_bitcast_fusion.refs_1_), channel_id=1, source_target_pairs={{0,4},{8,0},{16,8},{24,16},{28,24},{20,28},{12,20},{4,12},{1,5},{9... | collective-permute-start | bytes 1769480 | tf_op jit(solution)/shard_map/ppermute | solution.py:749
  178.6 39.3 %collective-permute-start.5 = (bf16[1,4,96,768]{3,2,1,0:T(8,128)(2,1)S(1)}, bf16[1,4,96,768]{3,2,1,0:T(8,128)(2,1)S(1)}, u32[]{:S(2)}, u32[]{:S(2)}) collective-permute-start(bf16[1,4,96,768]{3,2,1,0:T(8,128)(2,1)S(1)} %dynamic-slice_bitcast_fusion.1.refs_0_), channel_id=1, source_target_pairs={{0,8},{8,16},{16,24},{24,28},{28,20},{20,12},{12,4},{4,0},{1,9},{9... | collective-permute-start | bytes 1769480 | tf_op jit(solution)/shard_map/ppermute | solution.py:749
  242.4 6.7 %collective-permute-start.7 = (bf16[6,208,768]{2,1,0:T(8,128)(2,1)}, bf16[6,208,768]{2,1,0:T(8,128)(2,1)S(1)}, u32[]{:S(2)}, u32[]{:S(2)}) collective-permute-start(bf16[6,208,768]{2,1,0:T(8,128)(2,1)} %bitcast.19), channel_id=1, source_target_pairs={{0,1},{1,0},{2,3},{3,2},{4,5},{5,4},{6,7},{7,6},{8,9},{9,8},{10,11... | collective-permute-start | bytes 5750792 | tf_op jit(solution)/shard_map/ppermute | solution.py:723
  242.5 28.6 %collective-permute-start.9 = (bf16[2,4,96,768]{3,2,1,0:T(8,128)(2,1)}, bf16[2,4,96,768]{3,2,1,0:T(8,128)(2,1)}, u32[]{:S(2)}, u32[]{:S(2)}) collective-permute-start(bf16[2,4,96,768]{3,2,1,0:T(8,128)(2,1)} %ring_add.17.refs_3_), channel_id=1, source_target_pairs={{0,4},{8,0},{16,8},{24,16},{28,24},{20,28},{12,20},{4,12},{1,5},{9... | collective-permute-start | bytes 3538952 | tf_op jit(solution)/shard_map/ppermute | solution.py:749
  242.5 32.5 %collective-permute-start.8 = (bf16[2,4,96,768]{3,2,1,0:T(8,128)(2,1)}, bf16[2,4,96,768]{3,2,1,0:T(8,128)(2,1)}, u32[]{:S(2)}, u32[]{:S(2)}) collective-permute-start(bf16[2,4,96,768]{3,2,1,0:T(8,128)(2,1)} %ring_add.16.refs_2_), channel_id=1, source_target_pairs={{0,8},{8,16},{16,24},{24,28},{28,20},{20,12},{12,4},{4,0},{1,9},{9... | collective-permute-start | bytes 3538952 | tf_op jit(solution)/shard_map/ppermute | solution.py:749
  247.6 1.3 collective-permute-start.13
  252.9 18.2 %copy-start.3 = (bf16[6,208,768]{2,1,0:T(8,128)(2,1)}, bf16[6,208,768]{2,1,0:T(8,128)(2,1)S(1)}, u32[]{:S(2)}) copy-start(bf16[6,208,768]{2,1,0:T(8,128)(2,1)S(1)} %fusion.2.refs_2_.refs_0_) | copy-start | bytes 5750788
  252.9 58.6 %collective-permute-start.11 = (bf16[6,208,768]{2,1,0:T(8,128)(2,1)S(1)}, bf16[6,208,768]{2,1,0:T(8,128)(2,1)}, u32[]{:S(2)}, u32[]{:S(2)}) collective-permute-start(bf16[6,208,768]{2,1,0:T(8,128)(2,1)S(1)} %fusion.2.refs_2_.refs_0_), channel_id=1, source_target_pairs={{0,2},{1,3},{2,0},{3,1},{4,6},{5,7},{6,4},{7,5},{8,10},{9,11},{10,... | collective-permute-start | bytes 5750792 | tf_op jit(solution)/shard_map/ppermute | solution.py:727
  274.4 29.5 %collective-permute-start.16 = (bf16[2,4,96,768]{3,2,1,0:T(8,128)(2,1)}, bf16[2,4,96,768]{3,2,1,0:T(8,128)(2,1)}, u32[]{:S(2)}, u32[]{:S(2)}) collective-permute-start(bf16[2,4,96,768]{3,2,1,0:T(8,128)(2,1)} %ring_add.19.refs_4_), channel_id=1, source_target_pairs={{0,4},{8,0},{16,8},{24,16},{28,24},{20,28},{12,20},{4,12},{1,5},{9... | collective-permute-start | bytes 3538952 | tf_op jit(solution)/shard_map/ppermute | solution.py:749
  278.2 29.9 %collective-permute-start.15 = (bf16[2,4,96,768]{3,2,1,0:T(8,128)(2,1)}, bf16[2,4,96,768]{3,2,1,0:T(8,128)(2,1)}, u32[]{:S(2)}, u32[]{:S(2)}) collective-permute-start(bf16[2,4,96,768]{3,2,1,0:T(8,128)(2,1)} %ring_add.18.refs_3_), channel_id=1, source_target_pairs={{0,8},{8,16},{16,24},{24,28},{28,20},{20,12},{12,4},{4,0},{1,9},{9... | collective-permute-start | bytes 3538952 | tf_op jit(solution)/shard_map/ppermute | solution.py:749
  298.3 26.6 %collective-permute-start.10 = (bf16[6,208,768]{2,1,0:T(8,128)(2,1)}, bf16[6,208,768]{2,1,0:T(8,128)(2,1)}, u32[]{:S(2)}, u32[]{:S(2)}) collective-permute-start(bf16[6,208,768]{2,1,0:T(8,128)(2,1)} %bitcast.23), channel_id=1, source_target_pairs={{0,1},{1,0},{2,3},{3,2},{4,5},{5,4},{6,7},{7,6},{8,9},{9,8},{10,11... | collective-permute-start | bytes 5750792 | tf_op jit(solution)/shard_map/ppermute | solution.py:723
  298.6 4.0 collective-permute-start.14
  307.1 27.9 %collective-permute-start.19 = (bf16[2,4,96,768]{3,2,1,0:T(8,128)(2,1)}, bf16[2,4,96,768]{3,2,1,0:T(8,128)(2,1)}, u32[]{:S(2)}, u32[]{:S(2)}) collective-permute-start(bf16[2,4,96,768]{3,2,1,0:T(8,128)(2,1)} %ring_add.21.refs_13_), channel_id=1, source_target_pairs={{0,4},{8,0},{16,8},{24,16},{28,24},{20,28},{12,20},{4,12},{1,5},{9... | collective-permute-start | bytes 3538952 | tf_op jit(solution)/shard_map/ppermute | solution.py:749
  311.6 13.3 %copy-start.7 = (bf16[1248,768]{1,0:T(8,128)(2,1)S(1)}, bf16[1248,768]{1,0:T(8,128)(2,1)}, u32[]{:S(2)}) copy-start(bf16[1248,768]{1,0:T(8,128)(2,1)} %get-tuple-element.194) | copy-start | bytes 5750788
  323.0 37.6 %collective-permute-start.17 = (bf16[6,208,768]{2,1,0:T(8,128)(2,1)}, bf16[6,208,768]{2,1,0:T(8,128)(2,1)}, u32[]{:S(2)}, u32[]{:S(2)}) collective-permute-start(bf16[6,208,768]{2,1,0:T(8,128)(2,1)} %get-tuple-element.84.refs_2_), channel_id=1, source_target_pairs={{0,1},{1,0},{2,3},{3,2},{4,5},{5,4},{6,7},{7,6},{8,9},{9,8},{10,11... | collective-permute-start | bytes 5750792 | tf_op jit(solution)/shard_map/ppermute | solution.py:723
  327.1 11.1 %copy-start.11 = (bf16[6,208,768]{2,1,0:T(8,128)(2,1)}, bf16[6,208,768]{2,1,0:T(8,128)(2,1)S(1)}, u32[]{:S(2)}) copy-start(bf16[6,208,768]{2,1,0:T(8,128)(2,1)S(1)} %fusion.1.refs_0_) | copy-start | bytes 5750788
  327.2 44.3 %collective-permute-start.12 = (bf16[6,208,768]{2,1,0:T(8,128)(2,1)S(1)}, bf16[6,208,768]{2,1,0:T(8,128)(2,1)}, u32[]{:S(2)}, u32[]{:S(2)}) collective-permute-start(bf16[6,208,768]{2,1,0:T(8,128)(2,1)S(1)} %fusion.1.refs_0_), channel_id=1, source_target_pairs={{0,2},{1,3},{2,0},{3,1},{4,6},{5,7},{6,4},{7,5},{8,10},{9,11},{10,... | collective-permute-start | bytes 5750792 | tf_op jit(solution)/shard_map/ppermute | solution.py:727
  328.7 28.5 %collective-permute-start.18 = (bf16[2,4,96,768]{3,2,1,0:T(8,128)(2,1)S(1)}, bf16[2,4,96,768]{3,2,1,0:T(8,128)(2,1)}, u32[]{:S(2)}, u32[]{:S(2)}) collective-permute-start(bf16[2,4,96,768]{3,2,1,0:T(8,128)(2,1)S(1)} %copy-done.18), channel_id=1, source_target_pairs={{0,8},{8,16},{16,24},{24,28},{28,20},{20,12},{12,4},{4,0},{1,9},{9... | collective-permute-start | bytes 3538952 | tf_op jit(solution)/shard_map/ppermute | solution.py:749
  409.2 8.5 %collective-permute-start.20 = (bf16[6,208,768]{2,1,0:T(8,128)(2,1)S(1)}, bf16[6,208,768]{2,1,0:T(8,128)(2,1)}, u32[]{:S(2)}, u32[]{:S(2)}) collective-permute-start(bf16[6,208,768]{2,1,0:T(8,128)(2,1)S(1)} %slice.167), channel_id=1, source_target_pairs={{0,1},{1,0},{2,3},{3,2},{4,5},{5,4},{6,7},{7,6},{8,9},{9,8},{10,11... | collective-permute-start | bytes 5750792 | tf_op jit(solution)/shard_map/ppermute | solution.py:723
  415.7 28.7 %collective-permute-start.37 = (bf16[2,4,96,768]{3,2,1,0:T(8,128)(2,1)}, bf16[2,4,96,768]{3,2,1,0:T(8,128)(2,1)S(1)}, u32[]{:S(2)}, u32[]{:S(2)}) collective-permute-start(bf16[2,4,96,768]{3,2,1,0:T(8,128)(2,1)} %ring_add.23.refs_11_), channel_id=1, source_target_pairs={{0,4},{8,0},{16,8},{24,16},{28,24},{20,28},{12,20},{4,12},{1,5},{9... | collective-permute-start | bytes 3538952 | tf_op jit(solution)/shard_map/ppermute | solution.py:749
  417.8 46.3 %collective-permute-start.33 = (bf16[2,4,96,768]{3,2,1,0:T(8,128)(2,1)S(1)}, bf16[2,4,96,768]{3,2,1,0:T(8,128)(2,1)}, u32[]{:S(2)}, u32[]{:S(2)}) collective-permute-start(bf16[2,4,96,768]{3,2,1,0:T(8,128)(2,1)S(1)} %copy-done.19), channel_id=1, source_target_pairs={{0,8},{8,16},{16,24},{24,28},{28,20},{20,12},{12,4},{4,0},{1,9},{9... | collective-permute-start | bytes 3538952 | tf_op jit(solution)/shard_map/ppermute | solution.py:749
  423.0 39.7 %collective-permute-start.30 = (bf16[4,2,2,1,96,192]{5,4,0,3,2,1:T(8,128)(2,1)}, bf16[4,2,2,1,96,192]{5,4,0,3,2,1:T(8,128)(2,1)}, u32[]{:S(2)}, u32[]{:S(2)}) collective-permute-start(bf16[4,2,2,1,96,192]{5,4,0,3,2,1:T(8,128)(2,1)} %dynamic-slice_convert_fusion), channel_id=1, source_target_pairs={{0,4},{4,0},{8,12},{12,8},{16,20},{20,16},{24,28},{28,24},{1,5},{5... | collective-permute-start | bytes 1769480 | tf_op jit(solution)/shard_map/ppermute | solution.py:807
  425.0 168.3 %collective-permute-start.24 = (f32[6,208,768]{2,1,0:T(8,128)}, f32[6,208,768]{2,1,0:T(8,128)}, u32[]{:S(2)}, u32[]{:S(2)}) collective-permute-start(f32[6,208,768]{2,1,0:T(8,128)} %get-tuple-element.91.own_grad_ref), channel_id=1, source_target_pairs={{0,1},{1,0},{2,3},{3,2},{4,5},{5,4},{6,7},{7,6},{8,9},{9,8},{10,11... | collective-permute-start | bytes 11501576 | tf_op jit(solution)/shard_map/ppermute | solution.py:723
  426.2 78.5 %collective-permute-start.22 = (bf16[6,208,768]{2,1,0:T(8,128)(2,1)S(1)}, bf16[6,208,768]{2,1,0:T(8,128)(2,1)}, u32[]{:S(2)}, u32[]{:S(2)}) collective-permute-start(bf16[6,208,768]{2,1,0:T(8,128)(2,1)S(1)} %add_convert_fusion.1.refs_5_.refs_2_), channel_id=1, source_target_pairs={{0,2},{1,3},{2,0},{3,1},{4,6},{5,7},{6,4},{7,5},{8,10},{9,11},{10,... | collective-permute-start | bytes 5750792 | tf_op jit(solution)/shard_map/ppermute | solution.py:727
  448.6 58.5 %collective-permute-start.38 = (bf16[2,4,96,768]{3,2,1,0:T(8,128)(2,1)}, bf16[2,4,96,768]{3,2,1,0:T(8,128)(2,1)}, u32[]{:S(2)}, u32[]{:S(2)}) collective-permute-start(bf16[2,4,96,768]{3,2,1,0:T(8,128)(2,1)} %ring_add.28), channel_id=1, source_target_pairs={{0,4},{8,0},{16,8},{24,16},{28,24},{20,28},{12,20},{4,12},{1,5},{9... | collective-permute-start | bytes 3538952 | tf_op jit(solution)/shard_map/ppermute | solution.py:749
  464.0 20.5 %collective-permute-start.31 = (bf16[4,2,1,1,96,192]{5,4,0,3,2,1:T(8,128)(2,1)S(1)}, bf16[4,2,1,1,96,192]{5,4,0,3,2,1:T(8,128)(2,1)S(1)}, u32[]{:S(2)}, u32[]{:S(2)}) collective-permute-start(bf16[4,2,1,1,96,192]{5,4,0,3,2,1:T(8,128)(2,1)S(1)} %dynamic-slice_convert_fusion.1), channel_id=1, source_target_pairs={{0,8},{4,12},{8,0},{12,4},{16,24},{20,28},{24,16},{28,20},{1,9},{5... | collective-permute-start | bytes 884744 | tf_op jit(solution)/shard_map/ppermute | solution.py:807
  467.3 48.1 %collective-permute-start.34 = (bf16[2,4,96,768]{3,2,1,0:T(8,128)(2,1)}, bf16[2,4,96,768]{3,2,1,0:T(8,128)(2,1)S(1)}, u32[]{:S(2)}, u32[]{:S(2)}) collective-permute-start(bf16[2,4,96,768]{3,2,1,0:T(8,128)(2,1)} %ring_add.24), channel_id=1, source_target_pairs={{0,8},{8,16},{16,24},{24,28},{28,20},{20,12},{12,4},{4,0},{1,9},{9... | collective-permute-start | bytes 3538952 | tf_op jit(solution)/shard_map/ppermute | solution.py:749
  484.7 16.9 %collective-permute-start.32 = (bf16[4,1,1,1,96,192]{5,4,0,3,2,1:T(8,128)(2,1)S(1)}, bf16[4,1,1,1,96,192]{5,4,0,3,2,1:T(8,128)(2,1)S(1)}, u32[]{:S(2)}, u32[]{:S(2)}) collective-permute-start(bf16[4,1,1,1,96,192]{5,4,0,3,2,1:T(8,128)(2,1)S(1)} %dynamic-slice_convert_fusion.2), channel_id=1, source_target_pairs={{0,16},{4,20},{8,24},{12,28},{16,0},{20,4},{24,8},{28,12},{1,17},{... | collective-permute-start | bytes 442376 | tf_op jit(solution)/shard_map/ppermute | solution.py:807
  501.6 48.1 %collective-permute-start.21 = (bf16[6,208,768]{2,1,0:T(8,128)(2,1)}, bf16[6,208,768]{2,1,0:T(8,128)(2,1)}, u32[]{:S(2)}, u32[]{:S(2)}) collective-permute-start(bf16[6,208,768]{2,1,0:T(8,128)(2,1)} %finish.1.refs_2_), channel_id=1, source_target_pairs={{0,1},{1,0},{2,3},{3,2},{4,5},{5,4},{6,7},{7,6},{8,9},{9,8},{10,11... | collective-permute-start | bytes 5750792 | tf_op jit(solution)/shard_map/ppermute | solution.py:723
  506.6 7.2 %collective-permute-start.25 = (f32[20,768]{1,0:T(8,128)S(1)}, f32[20,768]{1,0:T(8,128)S(1)}, u32[]{:S(2)}, u32[]{:S(2)}) collective-permute-start(f32[20,768]{1,0:T(8,128)S(1)} %maximum_add_fusion.1), channel_id=1, source_target_pairs={{0,1},{1,0},{2,3},{3,2},{4,5},{5,4},{6,7},{7,6},{8,9},{9,8},{10,11... | collective-permute-start | bytes 184328 | tf_op jit(solution)/shard_map/ppermute | solution.py:24
  510.4 52.6 %collective-permute-start.39 = (bf16[2,4,96,768]{3,2,1,0:T(8,128)(2,1)}, bf16[2,4,96,768]{3,2,1,0:T(8,128)(2,1)}, u32[]{:S(2)}, u32[]{:S(2)}) collective-permute-start(bf16[2,4,96,768]{3,2,1,0:T(8,128)(2,1)} %ring_add.29), channel_id=1, source_target_pairs={{0,4},{8,0},{16,8},{24,16},{28,24},{20,28},{12,20},{4,12},{1,5},{9... | collective-permute-start | bytes 3538952 | tf_op jit(solution)/shard_map/ppermute | solution.py:749
  513.9 6.1 collective-permute-start.26
  520.0 46.9 %collective-permute-start.35 = (bf16[2,4,96,768]{3,2,1,0:T(8,128)(2,1)}, bf16[2,4,96,768]{3,2,1,0:T(8,128)(2,1)S(1)}, u32[]{:S(2)}, u32[]{:S(2)}) collective-permute-start(bf16[2,4,96,768]{3,2,1,0:T(8,128)(2,1)} %ring_add.25), channel_id=1, source_target_pairs={{0,8},{8,16},{16,24},{24,28},{28,20},{20,12},{12,4},{4,0},{1,9},{9... | collective-permute-start | bytes 3538952 | tf_op jit(solution)/shard_map/ppermute | solution.py:749
  520.2 29.5 %copy-start.5 = (bf16[6,208,768]{2,1,0:T(8,128)(2,1)S(1)}, bf16[6,208,768]{2,1,0:T(8,128)(2,1)}, u32[]{:S(2)}) copy-start(bf16[6,208,768]{2,1,0:T(8,128)(2,1)} %finish.1.refs_2_) | copy-start | bytes 5750788
  520.2 29.4 %collective-permute-start.27 = (f32[31,768]{1,0:T(8,128)S(1)}, f32[31,768]{1,0:T(8,128)S(1)}, u32[]{:S(2)}, u32[]{:S(2)}) collective-permute-start(f32[31,768]{1,0:T(8,128)S(1)} %concatenate.56), channel_id=1, source_target_pairs={{0,4},{4,0},{8,12},{12,8},{16,20},{20,16},{24,28},{28,24},{1,5},{5... | collective-permute-start | bytes 285704 | tf_op jit(solution)/shard_map/ppermute | solution.py:24
  549.6 43.6 %collective-permute-start.23 = (bf16[6,208,768]{2,1,0:T(8,128)(2,1)}, bf16[6,208,768]{2,1,0:T(8,128)(2,1)}, u32[]{:S(2)}, u32[]{:S(2)}) collective-permute-start(bf16[6,208,768]{2,1,0:T(8,128)(2,1)} %add_convert_fusion.own_ref), channel_id=1, source_target_pairs={{0,1},{1,0},{2,3},{3,2},{4,5},{5,4},{6,7},{7,6},{8,9},{9,8},{10,11... | collective-permute-start | bytes 5750792 | tf_op jit(solution)/shard_map/ppermute | solution.py:723
  549.7 5.3 collective-permute-start.28
  554.9 7.4 %collective-permute-start.29 = (f32[31,768]{1,0:T(8,128)S(1)}, f32[31,768]{1,0:T(8,128)S(1)}, u32[]{:S(2)}, u32[]{:S(2)}) collective-permute-start(f32[31,768]{1,0:T(8,128)S(1)} %add.361), channel_id=1, source_target_pairs={{0,16},{4,20},{8,24},{12,28},{16,0},{20,4},{24,8},{28,12},{1,17},{... | collective-permute-start | bytes 285704 | tf_op jit(solution)/shard_map/ppermute | solution.py:24
  566.3 15.5 %collective-permute-start.40 = (bf16[1,4,96,768]{3,2,1,0:T(8,128)(2,1)}, bf16[1,4,96,768]{3,2,1,0:T(8,128)(2,1)S(1)}, u32[]{:S(2)}, u32[]{:S(2)}) collective-permute-start(bf16[1,4,96,768]{3,2,1,0:T(8,128)(2,1)} %get-tuple-element.104), channel_id=1, source_target_pairs={{0,4},{8,0},{16,8},{24,16},{28,24},{20,28},{12,20},{4,12},{1,5},{9... | collective-permute-start | bytes 1769480 | tf_op jit(solution)/shard_map/ppermute | solution.py:749
  571.2 16.3 %collective-permute-start.36 = (bf16[1,4,96,768]{3,2,1,0:T(8,128)(2,1)}, bf16[1,4,96,768]{3,2,1,0:T(8,128)(2,1)S(1)}, u32[]{:S(2)}, u32[]{:S(2)}) collective-permute-start(bf16[1,4,96,768]{3,2,1,0:T(8,128)(2,1)} %get-tuple-element.102), channel_id=1, source_target_pairs={{0,8},{8,16},{16,24},{24,28},{28,20},{20,12},{12,4},{4,0},{1,9},{9... | collective-permute-start | bytes 1769480 | tf_op jit(solution)/shard_map/ppermute | solution.py:749
  (50 other events, 216.1 us)

commit v6 on v5

--- a/solution.py
+++ b/solution.py
@@ -13,17 +13,6 @@
 
 def pairs(count, bit):
     return [(i, i ^ bit) for i in range(count)]
-
-
-def small_sum(values, axis):
-    count = lax.axis_size(axis)
-    if count not in (4, 8):
-        return lax.psum(values, axis)
-    bit = 1
-    while bit < count:
-        values = values + lax.ppermute(values, axis, pairs(count, bit))
-        bit *= 2
-    return values
 
 
 ROWS = 208
@@ -38,7 +27,7 @@
 
 
 def cost(us):
-    return pl.CostEstimate(flops=int(us * 1.1e9), bytes_accessed=0, transcendentals=0)
+    return pl.CostEstimate(flops=int(us * 2e8), bytes_accessed=0, transcendentals=0)
 
 
 def route_plan(routes, expert_count):
@@ -118,20 +107,22 @@
     )(plan, rows, source)
 
 
-def gated_spread(source, rows, plan, chosen, router, expert_count, extra):
-    blocks, cols = rows.shape[0], source.shape[1]
+def gated_spread(own, other, rows, plan, chosen, router, expert_count, extra):
+    blocks, cols = rows.shape[0], own.shape[1]
     both = cols + extra
 
     def kernel(
-        plan_ref, rows_ref, source_ref, chosen_ref, router_ref, out_ref, gate_ref, pair_ref, local
+        plan_ref, rows_ref, own_ref, other_ref, chosen_ref, router_ref,
+        out_ref, gate_ref, pair_ref, local,
     ):
         block = pl.program_id(0)
+        source = jnp.where(block < blocks // 2, own_ref[...], other_ref[...])
 
         @pl.when(block == 0)
         def _():
             out_ref[...] = jnp.zeros_like(out_ref)
 
-        logits = jnp.dot(source_ref[...], router_ref[...], preferred_element_type=jnp.float32)
+        logits = jnp.dot(source, router_ref[...], preferred_element_type=jnp.float32)
         lane = lax.broadcasted_iota(jnp.int32, logits.shape, 1)
         first, second = lane < expert_count, lane < 2 * expert_count
         expert = jnp.where(first, lane, lane - expert_count)
@@ -149,7 +140,7 @@
             slot = lax.broadcasted_iota(jnp.int32, (part, BLOCK), 0) + i * part
             hot = (slot == rows_ref[0, 0:1, :]) | (slot == rows_ref[0, 1:2, :])
             hot = jnp.where(hot, 1.0, 0.0).astype(jnp.bfloat16)
-            for begin, end, value in ((0, cols, source_ref[...]), (cols, both, pair)):
+            for begin, end, value in ((0, cols, source), (cols, both, pair)):
                 local[pl.ds(i * part, part), begin:end] = jnp.dot(
                     hot, value, preferred_element_type=jnp.float32
                 ).astype(jnp.bfloat16)
@@ -173,7 +164,8 @@
             grid=(blocks,),
             in_specs=[
                 pl.BlockSpec((1, 2, BLOCK), lambda b, plan: (b, 0, 0)),
-                pl.BlockSpec((BLOCK, cols), lambda b, plan: (b, 0)),
+                pl.BlockSpec((BLOCK, cols), lambda b, plan: (jnp.minimum(b, blocks // 2 - 1), 0)),
+                pl.BlockSpec((BLOCK, cols), lambda b, plan: (jnp.maximum(b - blocks // 2, 0), 0)),
                 pl.BlockSpec((BLOCK, 2), lambda b, plan: (b, 0)),
                 pl.BlockSpec(router.shape, lambda b, plan: (0, 0)),
             ],
@@ -192,7 +184,7 @@
         compiler_params=pltpu.CompilerParams(vmem_limit_bytes=VMEM),
         cost_estimate=cost(20),
         name="gated_spread",
-    )(plan, rows, source, chosen, router)
+    )(plan, rows, own, other, chosen, router)
 
 
 def collect(buffers, columns, plan, kept, after):
@@ -203,8 +195,9 @@
 
     def kernel(plan_ref, columns_ref, *refs):
         held, refs = refs[: len(buffers)], refs[len(buffers) + len(after) :]
-        out_ref, local = refs[0], refs[-1]
+        own_ref, other_ref, local = refs[0], refs[1], refs[-1]
         block = pl.program_id(0)
+        mine = block < blocks // 2
 
         @pl.when(block == 0)
         def _():
@@ -232,12 +225,24 @@
                 local[...],
                 preferred_element_type=jnp.float32,
             )
-            out_ref[rows, :] = total[:, :kept].astype(jnp.bfloat16)
+            low = total[:, :kept].astype(jnp.bfloat16)
+
+            @pl.when(mine)
+            def _():
+                own_ref[rows, :] = low
+
+            @pl.when(jnp.logical_not(mine))
+            def _():
+                other_ref[rows, :] = low
+
             if extra:
-                refs[1][rows, :] = total[:, kept:]
-
-    out_specs = [pl.BlockSpec((BLOCK, kept), lambda b, plan: (b, 0))]
-    out_shape = [jax.ShapeDtypeStruct((blocks * BLOCK, kept), jnp.bfloat16)]
+                refs[2][rows, :] = total[:, kept:]
+
+    out_specs = [
+        pl.BlockSpec((BLOCK, kept), lambda b, plan: (jnp.minimum(b, blocks // 2 - 1), 0)),
+        pl.BlockSpec((BLOCK, kept), lambda b, plan: (jnp.maximum(b - blocks // 2, 0), 0)),
+    ]
+    out_shape = [jax.ShapeDtypeStruct((blocks // 2 * BLOCK, kept), jnp.bfloat16)] * 2
     if extra:
         out_specs.append(pl.BlockSpec((BLOCK, extra), lambda b, plan: (b, 0)))
         out_shape.append(jax.ShapeDtypeStruct((blocks * BLOCK, extra), jnp.float32))
@@ -386,6 +391,14 @@
         zeros = (0,) * (len(shape) - 1)
         if split == "turned":
             return pl.BlockSpec((each, *shape[1:]), lambda i, t: ((i + t[0]) % grid, *zeros))
+        if split == "low":
+            return pl.BlockSpec(
+                (each, *shape[1:]), lambda i, t: (jnp.minimum(i, grid // 2 - 1), *zeros)
+            )
+        if split == "high":
+            return pl.BlockSpec(
+                (each, *shape[1:]), lambda i, t: (jnp.maximum(i - grid // 2, 0), *zeros)
+            )
         if split:
             return pl.BlockSpec((each, *shape[1:]), lambda i, t: (i, *zeros))
         return pl.BlockSpec(tuple(shape), lambda i, t: (0, *zeros))
@@ -442,7 +455,7 @@
     return raised * (1.0 / jnp.sum(raised, axis=-1, keepdims=True))
 
 
-def attention_forward(x, turn, gain, shift, weight, bias, out_weight, half, kept):
+def attention_forward(x, turn, gain, shift, weight, bias, out_weight, half, kept, after):
     images, seq, width = x.shape
     rows, inner = ROWS, weight.shape[2]
 
@@ -450,7 +463,9 @@
         turn_ref, x_ref, gain_ref, shift_ref, w_ref, b_ref, wo_ref,
         *refs
     ):
-        part_ref, pad_ref, n_ref, q_ref, k_ref, v_ref, o_ref, held = refs[len(kept) :]
+        own_ref, other_ref, pad_ref, n_ref, q_ref, k_ref, v_ref, o_ref, held = refs[
+            len(kept) + len(after) :
+        ]
         held[...] = jnp.zeros_like(held)
         for i in range(TRIO):
             held[i, :seq, :] = x_ref[i].astype(jnp.float32)
@@ -471,14 +486,23 @@
             o_ref[i] = mixed.astype(jnp.bfloat16)
         mixed = o_ref[...].reshape(TRIO * rows, inner)
         part = jnp.dot(mixed, wo_ref[...], preferred_element_type=jnp.float32)
-        part_ref[...] = part.astype(jnp.bfloat16).reshape(TRIO, rows, width)
+        part = part.astype(jnp.bfloat16).reshape(TRIO, rows, width)
+
+        @pl.when(pl.program_id(0) == 0)
+        def _():
+            other_ref[...] = part
+
+        @pl.when(pl.program_id(0) == 1)
+        def _():
+            own_ref[...] = part
+
 
     wide = shape_of((images, rows, width), jnp.bfloat16)
     slim = shape_of((images, rows, inner), jnp.bfloat16)
     blocks = images // TRIO
 
     def place(i, turn):
-        return (2 * i + half, 0, 0)
+        return (2 * (1 - i) + half, 0, 0)
 
     def whole(array):
         return pl.BlockSpec(array.shape, lambda i, turn: (0,) * array.ndim)
@@ -491,30 +515,30 @@
             grid=(blocks // 2,),
             in_specs=[
                 pl.BlockSpec(
-                    (TRIO, seq, width), lambda i, turn: ((2 * i + half + turn[0]) % blocks, 0, 0)
+                    (TRIO, seq, width), lambda i, turn: ((2 * (1 - i) + half + turn[0]) % blocks, 0, 0)
                 )
             ]
             + [whole(array) for array in small]
-            + [pl.BlockSpec(memory_space=pl.ANY)] * len(kept),
-            out_specs=[pl.BlockSpec((TRIO, rows, width), lambda i, turn: (i, 0, 0))]
+            + [pl.BlockSpec(memory_space=pl.ANY)] * (len(kept) + len(after)),
+            out_specs=[pl.BlockSpec((TRIO, rows, width), lambda i, turn: (0, 0, 0))] * 2
             + [pl.BlockSpec((TRIO, *a.shape[1:]), place) for a in [wide] * 2 + [slim] * 4],
             scratch_shapes=[pltpu.VMEM((TRIO, rows, width), jnp.float32)],
         ),
-        out_shape=[shape_of((images // 2, rows, width), jnp.bfloat16)] + [wide] * 2 + [slim] * 4,
-        input_output_aliases={7 + i: 1 + i for i in range(len(kept))},
+        out_shape=[shape_of((TRIO, rows, width), jnp.bfloat16)] * 2 + [wide] * 2 + [slim] * 4,
+        input_output_aliases={7 + i: 2 + i for i in range(len(kept))},
         compiler_params=pltpu.CompilerParams(vmem_limit_bytes=VMEM),
         cost_estimate=cost(9),
         name="attention_forward",
-    )(turn, x, *small, *kept)
-
-
-def attention_backward(da, x, n, q, k, v, o, weight, out_weight, after):
+    )(turn, x, *small, *kept, *after)
+
+
+def attention_backward(own_da, other_da, x, n, q, k, v, o, weight, out_weight, after):
     images, rows, width = x.shape
     inner = weight.shape[2]
 
     def kernel(
-        da_ref, x_ref, n_ref, q_ref, k_ref, v_ref, o_ref, w_ref, wo_ref,
-        back_ref, dw_ref, dwo_ref, dbias_ref, sums_ref, held,
+        own_ref, other_ref, x_ref, n_ref, q_ref, k_ref, v_ref, o_ref, w_ref, wo_ref,
+        own_back_ref, other_back_ref, dw_ref, dwo_ref, dbias_ref, sums_ref, held,
     ):
         @pl.when(pl.program_id(0) == 0)
         def _():
@@ -524,7 +548,8 @@
             sums_ref[...] = jnp.zeros_like(sums_ref)
 
         joined = PAIR * rows
-        da = da_ref[...].reshape(joined, width)
+        mine = pl.program_id(0) < images // PAIR // 2
+        da = jnp.where(mine, own_ref[...], other_ref[...]).reshape(joined, width)
         do_all = contract(da, wo_ref[...], 1, 1).astype(jnp.bfloat16).reshape(PAIR, rows, inner)
         scale = HD ** (-0.5)
         for i in range(PAIR):
@@ -552,7 +577,16 @@
                     grad.astype(jnp.float32), axis=0, keepdims=True
                 )
         dwo_ref[0] += contract(da, o_ref[...].reshape(joined, inner), 0, 0)
-        back_ref[...] = back.astype(jnp.bfloat16).reshape(PAIR, rows, width)
+        back_low = back.astype(jnp.bfloat16).reshape(PAIR, rows, width)
+
+        @pl.when(mine)
+        def _():
+            own_back_ref[...] = back_low
+
+        @pl.when(jnp.logical_not(mine))
+        def _():
+            other_back_ref[...] = back_low
+
         unit, _ = normal(x_ref[...].reshape(joined, width).astype(jnp.float32))
         sums_ref[0:1, :] += jnp.sum(back * unit, axis=0, keepdims=True)
         sums_ref[1:2, :] += jnp.sum(back, axis=0, keepdims=True)
@@ -560,9 +594,11 @@
 
     return call(
         kernel, "attention_backward", images // PAIR,
-        [(a, True) for a in (da, x, n, q, k, v, o)] + [(weight, False), (out_weight, False)],
+        [(own_da, "low"), (other_da, "high")]
+        + [(a, True) for a in (x, n, q, k, v, o)] + [(weight, False), (out_weight, False)],
         [
-            (shape_of((images, rows, width), jnp.bfloat16), True),
+            (shape_of((images // 2, rows, width), jnp.bfloat16), "low"),
+            (shape_of((images // 2, rows, width), jnp.bfloat16), "high"),
             (shape_of((3, width, inner), jnp.float32), False),
             (shape_of((1, width, inner), jnp.float32), False),
             (shape_of((2, inner), jnp.float32), False),
@@ -727,10 +763,9 @@
     return lax.ppermute(value, "tensor", pairs(lax.axis_size("tensor"), 2))
 
 
-def core_sum(part, zero):
-    half = part.shape[0] // 2
-    got = to_core(part[half:])
-    return (part[:half].astype(jnp.float32) + got.astype(jnp.float32) + zero).astype(jnp.bfloat16)
+def core_sum(own, other, zero):
+    got = to_core(other)
+    return (own.astype(jnp.float32) + got.astype(jnp.float32) + zero).astype(jnp.bfloat16)
 
 
 def zero_of(value):
@@ -749,23 +784,24 @@
     return lax.ppermute(value, "dp", path)
 
 
-def ring_add(got, sources, way, steps, kinds, after):
-    groups, came = len(sources), got.shape[0]
-    many, total, cols = sources[0].shape
+def ring_add(got, sources, steps, kinds, after):
+    groups, came = len(sources), got[0].shape[0]
+    many, total, cols = sources[0][0].shape
     rows, part = total // 8, 2
-    owners = jnp.stack([ring_owner(way, step) for step in steps])
+    owners = jnp.stack([ring_owner(way, step) for step in steps for way in (1, -1)])
     joint = all(kind == kinds[0] for kind in kinds)
 
-    def kernel(owners_ref, held, *refs):
-        outs = refs[groups + len(after) :]
+    def kernel(owners_ref, *refs):
+        held, locals_, outs = refs[:2], refs[2 : 2 + 2 * groups], refs[2 + 2 * groups + len(after) :]
         for g in range(groups):
-            value = refs[g][...]
-            if g < came:
-                value = value.astype(jnp.float32) + held[g].astype(jnp.float32)
-            if joint:
-                outs[0][g] = value.astype(kinds[g])
-            else:
-                outs[g][0] = value.astype(kinds[g])
+            for d in range(2):
+                value = locals_[2 * g + d][...]
+                if g < came:
+                    value = value.astype(jnp.float32) + held[d][g].astype(jnp.float32)
+                if joint:
+                    outs[d][g] = value.astype(kinds[g])
+                else:
+                    outs[2 * g + d][0] = value.astype(kinds[g])
 
     def source(slot):
         return pl.BlockSpec((part, rows, cols), lambda i, own: (i, own[slot], 0))
@@ -774,39 +810,24 @@
         return pl.BlockSpec((count, part, rows, cols), lambda i, own: (0, i, 0, 0))
 
     if joint:
-        outs = [((groups, many, rows, cols), kinds[0])]
+        outs = [((groups, many, rows, cols), kinds[0])] * 2
     else:
-        outs = [((1, many, rows, cols), kind) for kind in kinds]
+        outs = [((1, many, rows, cols), kind) for kind in kinds for _ in range(2)]
     return pl.pallas_call(
         kernel,
         grid_spec=pltpu.PrefetchScalarGridSpec(
             num_scalar_prefetch=1,
             grid=(many // part,),
-            in_specs=[stack(came)]
-            + [source(i) for i in range(groups)]
+            in_specs=[stack(came)] * 2
+            + [source(i) for i in range(2 * groups)]
             + [pl.BlockSpec(memory_space=pl.ANY)] * len(after),
             out_specs=[stack(dims[0]) for dims, _ in outs],
         ),
         out_shape=[jax.ShapeDtypeStruct(dims, kind) for dims, kind in outs],
         compiler_params=pltpu.CompilerParams(vmem_limit_bytes=VMEM),
-        cost_estimate=cost(3),
+        cost_estimate=cost(5),
         name="ring_add",
-    )(owners, got, *sources, *after)
-
-
-def halving_scatter(values):
-    if lax.axis_size("dp") != 8:
-        return lax.psum_scatter(values.astype(jnp.bfloat16), "dp", scatter_dimension=1, tiled=True).astype(jnp.float32)
-    index = lax.axis_index("dp")
-    many, rows, cols = values.shape
-    values = values.reshape(many, 2, 2, 2, rows // 8, cols)
-    for bit, axis in ((0, 3), (1, 2), (2, 1)):
-        mine = (index >> bit) % 2
-        keep = lax.dynamic_index_in_dim(values, mine, axis, keepdims=True)
-        give = lax.dynamic_index_in_dim(values, 1 - mine, axis, keepdims=True)
-        got = lax.ppermute(give.astype(jnp.bfloat16), "dp", pairs(8, 1 << bit))
-        values = keep.astype(jnp.float32) + got.astype(jnp.float32)
-    return values.reshape(many, rows // 8, cols)
+    )(owners, *got, *[piece for pair in sources for piece in pair], *after)
 
 
 def on_device(
@@ -849,18 +870,18 @@
         return value.astype(f32)[None]
 
     def imaged(value):
-        return value.reshape(images, ROWS, value.shape[1])
+        return value.reshape(-1, ROWS, value.shape[1])
 
     turn = (half * core).astype(jnp.int32)[None]
     bias_rows = jnp.stack([qv_bias[0], jnp.zeros_like(qv_bias[0]), qv_bias[1]]).astype(f32)
     images_in = embedded.reshape(images, SEQ, width)
     kept, near, far = (), [], []
     for i in range(2):
-        part, *kept = attention_forward(
+        own, other, *kept = attention_forward(
             images_in, turn // TRIO, row(attn_gain), row(attn_shift),
-            qkv_weight, bias_rows, out_weight, i, tuple(kept),
+            qkv_weight, bias_rows, out_weight, i, tuple(kept), tuple(near),
         )
-        near.append(core_sum(part, 0.0))
+        near.append(core_sum(own, other, 0.0))
         far.append(across(near[i]))
     x, normed, queries, keys, values, mixed = kept
 
@@ -869,10 +890,6 @@
     upstream = own_first(cotangent, 0)
     grad_buffers = spread(upstream.reshape(images * ROWS, width), rows, plan, expert_count)
 
-    middle, own_normed = middle_norm(
-        near, far, x, row(out_bias), row(moe_gain), row(moe_shift), (grad_buffers,)
-    )
-    moe_normed = jnp.concatenate([own_normed, to_core(own_normed)]).reshape(images * ROWS, width)
     extra = 128
     router_twice = jnp.pad(
         jnp.concatenate([router_weight, router_weight], axis=1),
@@ -881,8 +898,14 @@
     bias_twice = jnp.pad(
         jnp.concatenate([down_bias, down_bias]), ((0, extra - 2 * expert_count), (0, 0))
     )
+    middle, own_normed = middle_norm(
+        near, far, x, row(out_bias), row(moe_gain), row(moe_shift),
+        (grad_buffers, router_twice, bias_twice, tiles),
+    )
+    own_rows = half * ROWS
     buffers, gates, mix_pair = gated_spread(
-        moe_normed, rows, plan, chosen, router_twice, expert_count, extra
+        own_normed.reshape(own_rows, width), to_core(own_normed).reshape(own_rows, width),
+        rows, plan, chosen, router_twice, expert_count, extra,
     )
     gates, mix_pair, chosen = imaged(gates), imaged(mix_pair), imaged(chosen)
     group = expert_count // GROUPS
@@ -907,74 +930,79 @@
     def round_trip(step, kinds, *after):
         if not ringed:
             return ()
-        made = []
-        for d, way in enumerate((1, -1)):
-            got = ring_hop(moving[d], way)
-            if step < 8:
-                made.append(ring_add(got, [first[d], second[d]], way, [step, step - 1], kinds, after))
-            else:
-                made.append(ring_add(got, [second[d]], way, [step - 1], kinds, after))
-        return [piece for pieces in zip(*made) for piece in pieces]
+        got = [ring_hop(value, way) for value, way in zip(moving, (1, -1))]
+        if step < 8:
+            return ring_add(got, [first, second], [step, step - 1], kinds, after)
+        return ring_add(got, [second], [step - 1], kinds, after)
 
     moving = round_trip(1, [low, low])
-    back_part, dots = collect((back_first, back_second), columns, plan, width, tuple(moving))
-    back_near = core_sum(imaged(back_part), 0.0)
+    own, other, dots = collect((back_first, back_second), columns, plan, width, tuple(moving))
+    back_near = core_sum(imaged(own), imaged(other), 0.0)
     back_far = across(back_near)
     dots = dots[:, : 2 * expert_count].T
     dots = dots[:expert_count] + dots[expert_count:]
-    own_rows = half * ROWS
     dots = dots[:, :own_rows] + to_core(dots[:, own_rows:])
     dots = (dots + across(dots)).T.reshape(half, ROWS, expert_count)
     moving = round_trip(2, [low, low], back_near)
-    (moe_part,) = collect((y_first, y_second), columns, plan, width, (back_near, *moving))
-    moving = round_trip(3, [low, low], moe_part)
+    own_y, other_y = collect((y_first, y_second), columns, plan, width, (back_near, *moving))
+    moving = round_trip(3, [low, low], other_y)
     middle_grad, own_da, moe_sums, router_sums, bias_sums = middle_back(
-        back_near, back_far, dots, gates, chosen, mix_pair, imaged(moe_normed), router_weight,
+        back_near, back_far, dots, gates, chosen, mix_pair, own_normed, router_weight,
         down_bias, middle, upstream, row(moe_gain), tuple(moving),
     )
-    da = jnp.concatenate([own_da, to_core(own_da)])
-    y_near = core_sum(imaged(moe_part), zero_of(back_far))
+    y_near = core_sum(imaged(own_y), imaged(other_y), zero_of(back_far))
     y_far = across(y_near)
-    other_grad = to_core(middle_grad)
+    other_da, other_grad = to_core(own_da), to_core(middle_grad)
     moving = round_trip(4, [low, low], own_da)
-    normed_back, grad_qkv, grad_out, grad_qv_bias, sums = attention_backward(
-        da, x, normed, queries, keys, values, mixed, qkv_weight, out_weight, (y_far, *moving)
-    )
-    last_near = core_sum(normed_back, 0.0)
+    own, other, grad_qkv, grad_out, grad_qv_bias, sums = attention_backward(
+        own_da, other_da, x, normed, queries, keys, values, mixed, qkv_weight, out_weight,
+        (y_far, *moving),
+    )
+    last_near = core_sum(own, other, 0.0)
     last_far = across(last_near)
+    slim = jnp.concatenate([grad_qkv, grad_out]).astype(low)
+    slim = lax.psum_scatter(slim, "dp", scatter_dimension=1, tiled=True).astype(f32)
     moving = round_trip(5, [low, low], last_near)
-    near_zero, far_zero = zero_of(last_near), zero_of(last_far)
-    own_out = finish(y_near, y_far, middle, mix_pair, bias_twice, (last_near,))
+
+    def after_round(value):
+        return value + zero_of(moving[1]) if ringed else value
+
+    def meet(value, axis, bit):
+        return value + lax.ppermute(value, axis, pairs(lax.axis_size(axis), bit))
+
+    own_out = finish(y_near, y_far, middle, mix_pair, bias_twice, (last_near, *moving))
     layer_out = in_order(own_out, to_core(own_out))
     router_bias = [router_sums, bias_sums[:expert_count] + bias_sums[expert_count : 2 * expert_count]]
     tensor_parts = jnp.concatenate([sums[:2]] + [0.5 * part for part in (moe_sums, *router_bias)])
+    tensor_parts = meet(meet(after_round(tensor_parts), "tensor", 1), "tensor", 2)
     packed = jnp.concatenate(
         [
-            small_sum(tensor_parts + far_zero, "tensor"),
+            tensor_parts,
             sums[2:],
             jnp.pad(grad_qv_bias, ((0, 0), (0, width - head_width))),
             bias_first[:, 0],
             bias_second[:, 0],
         ]
     )
-    packed = small_sum(packed, "dp")
-    slim = halving_scatter(jnp.concatenate([grad_qkv, grad_out]) + near_zero)
+    moving = round_trip(6, [low, low], layer_out)
+    last = (last_near.astype(f32) + last_far.astype(f32)).astype(low)
+    grad_embedded = input_back(
+        last, to_core(last), x, middle_grad, other_grad, row(attn_gain), turn, tuple(moving)
+    )
     if ringed:
-        moving = round_trip(6, [low, low], own_out)
-        up_first, down_first, *moving = round_trip(7, [f32, low])
-        up_second, down_second = round_trip(8, [f32])
+        packed = meet(after_round(packed), "dp", 1)
+        up_first, down_first, *moving = round_trip(7, [f32, low], grad_embedded, packed)
+        packed = meet(after_round(packed), "dp", 2)
+        up_second, down_second = round_trip(8, [f32], packed)
+        packed = meet(packed + zero_of(up_second), "dp", 4)
     else:
+        packed = lax.psum(packed, "dp")
         up_first, down_first, up_second, down_second = [
             lax.psum_scatter(grad, "dp", scatter_dimension=1, tiled=True).astype(f32)[None]
             for grad in (*first, *second)
         ]
     grad_up = jnp.concatenate([up_first[0], up_second[0]])
     grad_down = jnp.concatenate([down_first[0], down_second[0]]).transpose(0, 2, 1)
-    last = (last_near.astype(f32) + last_far.astype(f32)).astype(jnp.bfloat16)
-    grad_embedded = input_back(
-        last, to_core(last), x, middle_grad, other_grad, row(attn_gain), turn,
-        (layer_out, packed, slim),
-    )
     base = 4 + 2 * expert_count
     return (
         layer_out,

time: 619 us -> 626 us (1.011)
  local copies, waits for them, and re-layouts: 72.6 us -> 53 us
  between operations: 4.34 us -> 18.8 us
  waiting for transfers between devices: 163 us -> 174 us
    ppermute x8 -> x5, waiting for transfers between devices: 63.7 us -> 18 us  [meet(): return value + lax.ppermute(value, axis, pairs(lax.axis_size(axis), bit))]
    ppermute x16, waiting for transfers between devices: 64.8 us -> 105 us  [ring_hop(): return lax.ppermute(value, 'dp', path)]
    pallas_call x16 -> x8, Pallas kernels: 49.8 us -> 33.7 us  [ring_add(): pl.pallas_call(kernel, grid_spec=pltpu.PrefetchScalarGridSpec(num_scalar_...]
    reduce_scatter x0 -> x1, waiting for transfers between devices: none -> 14.8 us  [on_device(): lax.psum_scatter(slim, 'dp', scatter_dimension=1, tiled=True).astype(f32)]
    slice x5 -> x0, local copies, waits for them, and re-layouts: 13.7 us -> none  [core_sum(): got = to_core(part[half:])]
    unnamed x121 -> x104, local copies, waits for them, and re-layouts: 19.1 us -> 13.3 us
    convert_element_type x6 -> x7, other arithmetic: 12.5 us -> 15.2 us  [the longest x5 11.6 us: core_sum(): (own.astype(jnp.float32) + got.astype(jnp.float32) + zero).astype(jnp.bfl...]
  transfers between devices with their start and end apart: 41 -> 39, of which waited for: 16 -> 21; matrix products, arithmetic and copies ran while one was open for 13% -> 12% of each run, Pallas kernels for 21% -> 22%
where the time goes in v6:
time: 626 us; the launch traced here: 616 us
  Pallas kernels  291 us (46%)
  waiting for transfers between devices  174 us (28%)
  local copies, waits for them, and re-layouts  53 us (8%)
  other arithmetic  43.4 us (7%)
  starting transfers between devices  34 us (5%)
  between operations  18.8 us (3%)
    ppermute x16, waiting for transfers between devices, ring_hop(): return lax.ppermute(value, 'dp', path)  105 us
    pallas_call x2, Pallas kernels, expert_pass(): pl.pallas_call(kernel, grid_spec=pltpu.PrefetchScalarGridSpec(num_scalar_...  79.1 us
    pallas_call x3, Pallas kernels, call(): pl.pallas_call(body, grid_spec=pltpu.PrefetchScalarGridSpec(num_scalar_pr...  58.1 us
    pallas_call x2, Pallas kernels, collect(): pl.pallas_call(kernel, grid_spec=pltpu.PrefetchScalarGridSpec(num_scalar_...  36.5 us
    pallas_call x8, Pallas kernels, ring_add(): pl.pallas_call(kernel, grid_spec=pltpu.PrefetchScalarGridSpec(num_scalar_...  33.7 us
    ppermute x6, waiting for transfers between devices, across(): return lax.ppermute(value, 'tensor', pairs(lax.axis_size('tensor'), 2))  31.7 us
    pallas_call x2, Pallas kernels, attention_forward(): pl.pallas_call(kernel, grid_spec=pltpu.PrefetchScalarGridSpec(num_scalar_...  24.5 us
    pallas_call x1, Pallas kernels, gated_spread(): pl.pallas_call(kernel, grid_spec=pltpu.PrefetchScalarGridSpec(num_scalar_...  21.6 us
  transfers between devices with their start and end apart: 39, of which 21 were waited for; matrix products, arithmetic and copies ran while one was open for 12% of the time, Pallas kernels for 22%

profile of v6, /device:TPU:0, one launch (start us, length us, event | category | flops | bytes accessed | tf_op | source)
XLA Modules:
  0.0 616.2 jit_solution(11879313619000661861)
XLA Ops:
  8.0 2.3 copy.101.w_ref.refs_8_
  10.9 4.3 reshape.201.x_ref
  16.5 12.2 %attention_forward.2 = (bf16[3,208,768]{2,1,0:T(8,128)(2,1)}, bf16[3,208,768]{2,1,0:T(8,128)(2,1)}, bf16[12,208,768]{2,1,0:T(8,128)(2,1)}, bf16[12,208,768]{2,1,...) custom-call(s32[1]{0:T(128)S(6)} %select_n.409.turn_ref, ...), custom_call_target="tpu_custom_call" | custom-call | flops 1800000000 | tf_op jit(solution)/shard_map/attention_forward/pallas_call | solution.py:511
  37.5 12.3 %attention_forward.3 = (bf16[3,208,768]{2,1,0:T(8,128)(2,1)}, bf16[3,208,768]{2,1,0:T(8,128)(2,1)}, bf16[12,208,768]{2,1,0:T(8,128)(2,1)}, bf16[12,208,768]{2,1,...) custom-call(s32[1]{0:T(128)S(6)} %select_n.409.turn_ref, ...), custom_call_target="tpu_custom_call", output_to_operand_aliasing={{2}: (7, {}), {3}: (8, {}), {4}: (9, {}), {5}: (10, {}), {6... | custom-call | flops 1800000000 | tf_op jit(solution)/shard_map/attention_forward/pallas_call | solution.py:511
  50.6 4.5 reshape.202
  55.7 3.7 pad_slice_fusion.1
  59.5 3.0 collective-permute-start.2
  62.5 2.4 add_convert_fusion.2.near_b
  69.4 4.5 maximum_select_fusion.refs_10_
  73.8 15.4 %spread.1.refs_0_.g_ref = bf16[8,1024,768]{2,1,0:T(8,128)(2,1)} custom-call(s32[144]{0:T(256)} %pad_add_fusion.1.plan_ref, s32[6,2,416]{2,1,0:T(2,128)} %add_bitcast_fusion.rows_ref, bf16[2496,768]{1,0:T(8,128)(2,1)} %bitcast.94), custom_call_target="tpu_custom_call" | custom-call | flops 3000000000 | tf_op jit(solution)/shard_map/spread/pallas_call | solution.py:91
  89.2 15.3 %collective-permute-done.3.far_b = bf16[3,208,768]{2,1,0:T(8,128)(2,1)} collective-permute-done((bf16[3,208,768]{2,1,0:T(8,128)(2,1)}, bf16[3,208,768]{2,1,0:T(8,128)(2,1)}, u32[]{:S(2)}, u32[]{:S(2)}) %collective-permute-start.3) | collective-permute-done | bytes 958496 | tf_op jit(solution)/shard_map/ppermute | solution.py:763
  104.5 7.0 %middle_norm.1 = (f32[6,208,768]{2,1,0:T(8,128)}, bf16[6,208,768]{2,1,0:T(8,128)(2,1)}) custom-call(bf16[3,208,768]{2,1,0:T(8,128)(2,1)} %add_convert_fusion.3.refs_6_.near_a, bf16[3,208,768]{2,1,0:T(8,128)(2,1)} %add_convert_fusion.2.near_b, bf16[3,208,768]{2,1,0:T(8,128)(2,1)} %collective-permute-done.2.far_a, ...), custom_call_target="tpu_custom_call" | custom-call | flops 1400000000 | tf_op jit(solution)/shard_map/middle_norm/pallas_call | solution.py:630
  116.9 21.6 %gated_spread.1 = (bf16[8,1024,896]{2,1,0:T(8,128)(2,1)}, f32[2496,128]{1,0:T(8,128)}, bf16[2496,128]{1,0:T(8,128)(2,1)}) custom-call(s32[144]{0:T(256)} %pad_add_fusion.1.plan_ref, s32[6,2,416]{2,1,0:T(2,128)} %add_bitcast_fusion.rows_ref, bf16[1248,768]{1,0:T(8,128)(2,1)} %bitcast.104, bf16[1248,768]{1,0:T(8,128)(2,1)} %bitcast.114, s32[2496,2]{1,0:T(8,128)} %bitcast.96, ...), custom_call_target="tpu_custom_call" | custom-call | flops 4000000000 | tf_op jit(solution)/shard_map/gated_spread/pallas_call | solution.py:160
  138.5 32.3 %experts.2 = (bf16[4,1024,768]{2,1,0:T(8,128)(2,1)}, bf16[4,1024,896]{2,1,0:T(8,128)(2,1)}, bf16[4,768,768]{2,1,0:T(8,128)(2,1)}, bf16[4,768,768]{2,1,0:T(8,128)(2,1)}, f32[4,1,768]{2,1,0:T(1,128)}) custom-call(s32[8]{0:T(128)} %and_select_fusion.refs_3_.tiles_ref, bf16[8,1024,896]{2,1,0:T(8,128)(2,1)} %get-tuple-element.92.x_ref, ...), custom_call_target="tpu_custom_call" | custom-call | flops 21743271936 | bytes 46137344 | tf_op jit(solution)/shard_map/experts/pallas_call | solution.py:360
  171.9 3.5 collective-permute-start.6
  177.3 46.8 %experts.3 = (bf16[4,1024,768]{2,1,0:T(8,128)(2,1)}, bf16[4,1024,896]{2,1,0:T(8,128)(2,1)}, bf16[4,768,768]{2,1,0:T(8,128)(2,1)}, bf16[4,768,768]{2,1,0:T(8,128)(2,1)}, f32[4,1,768]{2,1,0:T(1,128)}) custom-call(s32[8]{0:T(128)} %and_select_fusion.refs_3_.tiles_ref, bf16[8,1024,896]{2,1,0:T(8,128)(2,1)} %get-tuple-element.92.x_ref, ...), custom_call_target="tpu_custom_call" | custom-call | flops 21743271936 | bytes 46137344 | tf_op jit(solution)/shard_map/experts/pallas_call | solution.py:360
  225.1 3.9 ring_add.8
  229.0 18.6 %collect.2 = (bf16[1248,768]{1,0:T(8,128)(2,1)}, bf16[1248,768]{1,0:T(8,128)(2,1)}, f32[2496,128]{1,0:T(8,128)}) custom-call(s32[144]{0:T(256)} %pad_add_fusion.1.plan_ref, s32[2496,2]{1,0:T(8,128)} %bitcast.97, bf16[4,1024,896]{2,1,0:T(8,128)(2,1)} %get-tuple-element.97.refs_0_, bf16[4,1024,896]{2,1,0:T(8,128)(2,1)} %get-tuple-element.98.refs_1_, ...), custom_call_target="tpu_custom_call" | custom-call | flops 3200000000 | tf_op jit(solution)/shard_map/collect/pallas_call | solution.py:249
  247.6 3.3 collective-permute-start.8
  252.9 2.6 fusion.2.refs_6_.refs_2_.refs_0_
  257.1 20.0 %collective-permute-done.8.refs_0_ = bf16[2,4,96,768]{3,2,1,0:T(8,128)(2,1)} collective-permute-done((bf16[2,4,96,768]{3,2,1,0:T(8,128)(2,1)}, bf16[2,4,96,768]{3,2,1,0:T(8,128)(2,1)}, u32[]{:S(2)}, u32[]{:S(2)}) %collective-permute-start.8) | collective-permute-done | bytes 1179680 | tf_op jit(solution)/shard_map/ppermute | solution.py:784
  279.1 4.3 ring_add.9
  283.5 17.9 %collect.3 = (bf16[1248,768]{1,0:T(8,128)(2,1)}, bf16[1248,768]{1,0:T(8,128)(2,1)}) custom-call(s32[144]{0:T(256)} %pad_add_fusion.1.plan_ref, s32[2496,2]{1,0:T(8,128)} %bitcast.98, bf16[4,1024,768]{2,1,0:T(8,128)(2,1)} %get-tuple-element.93.refs_0_, bf16[4,1024,768]{2,1,0:T(8,128)(2,1)} %get-tuple-element.96.refs_1_, bf16[6,208,768]{2,1,0:T(8,128)(2,1)} %copy-done, ...), custom_call_target="tpu_custom_call" | custom-call | flops 3200000000 | tf_op jit(solution)/shard_map/collect/pallas_call | solution.py:249
  313.3 16.9 %collective-permute-done.15.refs_0_ = bf16[2,4,96,768]{3,2,1,0:T(8,128)(2,1)} collective-permute-done((bf16[2,4,96,768]{3,2,1,0:T(8,128)(2,1)}, bf16[2,4,96,768]{3,2,1,0:T(8,128)(2,1)}, u32[]{:S(2)}, u32[]{:S(2)}) %collective-permute-start.15) | collective-permute-done | bytes 1179680 | tf_op jit(solution)/shard_map/ppermute | solution.py:784
  330.4 4.6 ring_add.10
  335.0 11.4 %middle_back.1 = (f32[6,208,768]{2,1,0:T(8,128)}, bf16[6,208,768]{2,1,0:T(8,128)(2,1)}, f32[2,768]{1,0:T(2,128)}, f32[8,768]{1,0:T(8,128)}, f32[128,768]{1,0:T(8,128)}) custom-call(s32[1]{0:T(128)} %constant.417.clone.1.turn_ref, bf16[6,208,768]{2,1,0:T(8,128)(2,1)} %copy-done, bf16[6,208,768]{2,1,0:T(8,128)(2,1)} %collective-permute-done.11.refs_1_, ...), custom_call_target="tpu_custom_call" | custom-call | flops 1600000000 | tf_op jit(solution)/shard_map/middle_back/pallas_call | solution.py:411
  354.7 25.8 %collective-permute-done.18.refs_0_ = bf16[2,4,96,768]{3,2,1,0:T(8,128)(2,1)} collective-permute-done((bf16[2,4,96,768]{3,2,1,0:T(8,128)(2,1)}, bf16[2,4,96,768]{3,2,1,0:T(8,128)(2,1)}, u32[]{:S(2)}, u32[]{:S(2)}) %collective-permute-start.18) | collective-permute-done | bytes 1179680 | tf_op jit(solution)/shard_map/ppermute | solution.py:784
  380.5 4.3 ring_add.11
  384.8 10.0 %collective-permute-done.12.refs_10_.refs_1_ = bf16[6,208,768]{2,1,0:T(8,128)(2,1)} collective-permute-done((bf16[6,208,768]{2,1,0:T(8,128)(2,1)S(1)}, bf16[6,208,768]{2,1,0:T(8,128)(2,1)}, u32[]{:S(2)}, u32[]{:S(2)}) %collective-permute-start.12) | collective-permute-done | bytes 1916960 | tf_op jit(solution)/shard_map/ppermute | solution.py:763
  394.9 40.0 %attention_backward.1 = (bf16[6,208,768]{2,1,0:T(8,128)(2,1)}, bf16[6,208,768]{2,1,0:T(8,128)(2,1)}, f32[3,768,192]{2,1,0:T(8,128)}, f32[1,768,192]{2,1,0:T(8,128)}, f32[2,192]{1,0:T(2,128)}, /*index=5*/f32[3,768]{1,0:T(4,128)}) custom-call(s32[1]{0:T(128)} %constant.417.clone.1.turn_ref, bf16[6,208,768]{2,1,0:T(8,128)(2,1)} %get-tuple-element.115.refs_6_.refs_0_, ...), custom_call_target="tpu_custom_call" | custom-call | flops 6000000000 | tf_op jit(solution)/shard_map/attention_backward/pallas_call | solution.py:411
  439.1 3.3 add_convert_fusion.1.refs_6_.refs_5_
  444.5 18.9 %collective-permute-done.21.refs_0_ = bf16[2,4,96,768]{3,2,1,0:T(8,128)(2,1)S(1)} collective-permute-done((bf16[2,4,96,768]{3,2,1,0:T(8,128)(2,1)S(1)}, bf16[2,4,96,768]{3,2,1,0:T(8,128)(2,1)S(1)}, u32[]{:S(2)}, u32[]{:S(2)}) %collective-permute-start.21) | collective-permute-done | bytes 1179680 | tf_op jit(solution)/shard_map/ppermute | solution.py:784
  464.3 4.4 ring_add.12
  468.7 6.7 %finish.1 = bf16[6,208,768]{2,1,0:T(8,128)(2,1)} custom-call(s32[1]{0:T(128)} %constant.417.clone.1.turn_ref, bf16[6,208,768]{2,1,0:T(8,128)(2,1)} %copy-done.3, bf16[6,208,768]{2,1,0:T(8,128)(2,1)} %collective-permute-done.12.refs_10_.refs_1_, f32[6,208,768]{2,1,0:T(8,128)} %get-tuple-element.109.refs_9_.refs_2_, bf16[12,208,128]{2,1,0:T(8,128)(2,1)} %bitcast.100, ...), custom_call_target="tpu_custom_call" | custom-call | flops 1600000000 | tf_op jit(solution)/shard_map/finish/pallas_call | solution.py:411
  481.2 5.3 collective-permute-done.24
  486.5 2.6 add_convert_fusion.own_ref
  495.1 4.3 reshape.211.refs_6_
  499.4 18.6 %collective-permute-done.27.refs_0_ = bf16[2,4,96,768]{3,2,1,0:T(8,128)(2,1)} collective-permute-done((bf16[2,4,96,768]{3,2,1,0:T(8,128)(2,1)}, bf16[2,4,96,768]{3,2,1,0:T(8,128)(2,1)}, u32[]{:S(2)}, u32[]{:S(2)}) %collective-permute-start.27) | collective-permute-done | bytes 1179680 | tf_op jit(solution)/shard_map/ppermute | solution.py:784
  518.0 2.2 collective-permute-done.28.refs_1_
  520.2 4.4 ring_add.13
  528.8 2.2 collective-permute-done.30
  534.9 14.8 %reduce-scatter.2.cloned.1.call-done = bf16[4,96,192]{2,1,0:T(8,128)(2,1)} async-done(((bf16[4,768,192]{2,1,0:T(8,128)(2,1)}), bf16[4,96,192]{2,1,0:T(8,128)(2,1)}) %reduce-scatter.2.cloned.1.call-update) | async-done | bytes 147472 | tf_op jit(solution)/shard_map/reduce_scatter | solution.py:964
  550.7 5.1 collective-permute-done.31
  556.5 15.5 %input_back.1.refs_6_ = f32[2364,768]{1,0:T(8,128)} custom-call(s32[1]{0:T(128)} %bitcast.8.turn_ref, bf16[6,208,768]{2,1,0:T(8,128)(2,1)} %copy-done.5, bf16[6,208,768]{2,1,0:T(8,128)(2,1)} %collective-permute-done.25.other_ref, bf16[12,208,768]{2,1,0:T(8,128)(2,1)} %get-tuple-element.90.x_ref.refs_2_, f32[6,208,768]{2,1,0:T(8,128)} %get-tuple-element.127.own_grad_ref, ...), custom_call_target="tpu_custom_call" | custom-call | flops 3000000000 | tf_op jit(solution)/shard_map/input_back/pallas_call | solution.py:735
  573.0 4.4 ring_add.14
  582.9 10.6 %collective-permute-done.34 = f32[31,768]{1,0:T(8,128)S(1)} collective-permute-done((f32[31,768]{1,0:T(8,128)S(1)}, f32[31,768]{1,0:T(8,128)S(1)}, u32[]{:S(2)}, u32[]{:S(2)}) %collective-permute-start.34) | collective-permute-done | bytes 95264 | tf_op jit(solution)/shard_map/ppermute | solution.py:971
  595.8 3.4 ring_add.15
  602.4 3.0 maximum_bitcast_fusion
  (272 shorter events, 93.1 us)
Async XLA Ops:
  7.2 542.5 %reduce-scatter.2.cloned.1.call-start = ((), (), s32[]{:S(2)}) async-start(), calls=%async_computation.1 | async-start | bytes 1769472 | tf_op jit(solution)/shard_map/reduce_scatter | solution.py:964
  28.7 7.6 %collective-permute-start = (bf16[3,208,768]{2,1,0:T(8,128)(2,1)}, bf16[3,208,768]{2,1,0:T(8,128)(2,1)S(1)}, u32[]{:S(2)}, u32[]{:S(2)}) collective-permute-start(bf16[3,208,768]{2,1,0:T(8,128)(2,1)} %get-tuple-element.81), channel_id=1, source_target_pairs={{0,1},{1,0},{2,3},{3,2},{4,5},{5,4},{6,7},{7,6},{8,9},{9,8},{10,11... | collective-permute-start | bytes 2875400 | tf_op jit(solution)/shard_map/ppermute | solution.py:759
  49.7 12.7 %collective-permute-start.1 = (bf16[3,208,768]{2,1,0:T(8,128)(2,1)}, bf16[3,208,768]{2,1,0:T(8,128)(2,1)}, u32[]{:S(2)}, u32[]{:S(2)}) collective-permute-start(bf16[3,208,768]{2,1,0:T(8,128)(2,1)} %get-tuple-element.89), channel_id=1, source_target_pairs={{0,1},{1,0},{2,3},{3,2},{4,5},{5,4},{6,7},{7,6},{8,9},{9,8},{10,11... | collective-permute-start | bytes 2875400 | tf_op jit(solution)/shard_map/ppermute | solution.py:759
  59.5 29.8 %collective-permute-start.2 = (bf16[3,208,768]{2,1,0:T(8,128)(2,1)S(1)}, bf16[3,208,768]{2,1,0:T(8,128)(2,1)}, u32[]{:S(2)}, u32[]{:S(2)}) collective-permute-start(bf16[3,208,768]{2,1,0:T(8,128)(2,1)S(1)} %copy-done.2), channel_id=1, source_target_pairs={{0,2},{1,3},{2,0},{3,1},{4,6},{5,7},{6,4},{7,5},{8,10},{9,11},{10,... | collective-permute-start | bytes 2875400 | tf_op jit(solution)/shard_map/ppermute | solution.py:763
  64.8 39.7 %collective-permute-start.3 = (bf16[3,208,768]{2,1,0:T(8,128)(2,1)}, bf16[3,208,768]{2,1,0:T(8,128)(2,1)}, u32[]{:S(2)}, u32[]{:S(2)}) collective-permute-start(bf16[3,208,768]{2,1,0:T(8,128)(2,1)} %add_convert_fusion.2.near_b), channel_id=1, source_target_pairs={{0,2},{1,3},{2,0},{3,1},{4,6},{5,7},{6,4},{7,5},{8,10},{9,11},{10,... | collective-permute-start | bytes 2875400 | tf_op jit(solution)/shard_map/ppermute | solution.py:763
  111.5 4.1 collective-permute-start.4
  171.9 52.2 %collective-permute-start.6 = (bf16[1,4,96,768]{3,2,1,0:T(8,128)(2,1)S(1)}, bf16[1,4,96,768]{3,2,1,0:T(8,128)(2,1)S(1)}, u32[]{:S(2)}, u32[]{:S(2)}) collective-permute-start(bf16[1,4,96,768]{3,2,1,0:T(8,128)(2,1)S(1)} %dynamic-slice_bitcast_fusion.refs_1_), channel_id=1, source_target_pairs={{0,4},{8,0},{16,8},{24,16},{28,24},{20,28},{12,20},{4,12},{1,5},{9... | collective-permute-start | bytes 1769480 | tf_op jit(solution)/shard_map/ppermute | solution.py:784
  176.5 47.6 %collective-permute-start.5 = (bf16[1,4,96,768]{3,2,1,0:T(8,128)(2,1)S(1)}, bf16[1,4,96,768]{3,2,1,0:T(8,128)(2,1)S(1)}, u32[]{:S(2)}, u32[]{:S(2)}) collective-permute-start(bf16[1,4,96,768]{3,2,1,0:T(8,128)(2,1)S(1)} %dynamic-slice_bitcast_fusion.1.refs_0_), channel_id=1, source_target_pairs={{0,8},{8,16},{16,24},{24,28},{28,20},{20,12},{12,4},{4,0},{1,9},{9... | collective-permute-start | bytes 1769480 | tf_op jit(solution)/shard_map/ppermute | solution.py:784
  229.0 22.0 %copy-start.18 = (bf16[2,4,96,768]{3,2,1,0:T(8,128)(2,1)S(1)}, bf16[2,4,96,768]{3,2,1,0:T(8,128)(2,1)}, u32[]{:S(2)}) copy-start(bf16[2,4,96,768]{3,2,1,0:T(8,128)(2,1)} %get-tuple-element.102.refs_3_) | copy-start | bytes 3538948
  247.6 4.1 collective-permute-start.7
  247.6 29.5 %collective-permute-start.8 = (bf16[2,4,96,768]{3,2,1,0:T(8,128)(2,1)}, bf16[2,4,96,768]{3,2,1,0:T(8,128)(2,1)}, u32[]{:S(2)}, u32[]{:S(2)}) collective-permute-start(bf16[2,4,96,768]{3,2,1,0:T(8,128)(2,1)} %get-tuple-element.101.refs_2_), channel_id=1, source_target_pairs={{0,8},{8,16},{16,24},{24,28},{28,20},{20,12},{12,4},{4,0},{1,9},{9... | collective-permute-start | bytes 3538952 | tf_op jit(solution)/shard_map/ppermute | solution.py:784
  250.9 28.2 %collective-permute-start.9 = (bf16[2,4,96,768]{3,2,1,0:T(8,128)(2,1)S(1)}, bf16[2,4,96,768]{3,2,1,0:T(8,128)(2,1)}, u32[]{:S(2)}, u32[]{:S(2)}) collective-permute-start(bf16[2,4,96,768]{3,2,1,0:T(8,128)(2,1)S(1)} %copy-done.18), channel_id=1, source_target_pairs={{0,4},{8,0},{16,8},{24,16},{28,24},{20,28},{12,20},{4,12},{1,5},{9... | collective-permute-start | bytes 3538952 | tf_op jit(solution)/shard_map/ppermute | solution.py:784
  255.5 23.6 %copy-start = (bf16[6,208,768]{2,1,0:T(8,128)(2,1)}, bf16[6,208,768]{2,1,0:T(8,128)(2,1)S(1)}, u32[]{:S(2)}) copy-start(bf16[6,208,768]{2,1,0:T(8,128)(2,1)S(1)} %fusion.2.refs_6_.refs_2_.refs_0_) | copy-start | bytes 5750788
  255.5 79.4 %collective-permute-start.11 = (bf16[6,208,768]{2,1,0:T(8,128)(2,1)S(1)}, bf16[6,208,768]{2,1,0:T(8,128)(2,1)}, u32[]{:S(2)}, u32[]{:S(2)}) collective-permute-start(bf16[6,208,768]{2,1,0:T(8,128)(2,1)S(1)} %fusion.2.refs_6_.refs_2_.refs_0_), channel_id=1, source_target_pairs={{0,2},{1,3},{2,0},{3,1},{4,6},{5,7},{6,4},{7,5},{8,10},{9,11},{10,... | collective-permute-start | bytes 5750792 | tf_op jit(solution)/shard_map/ppermute | solution.py:763
  283.5 17.9 %copy-start.12 = (f32[2496,128]{1,0:T(8,128)S(1)}, f32[2496,128]{1,0:T(8,128)}, u32[]{:S(2)}) copy-start(f32[2496,128]{1,0:T(8,128)} %get-tuple-element.111) | copy-start | bytes 3833860
  301.3 47.0 %collective-permute-start.10 = (bf16[6,208,768]{2,1,0:T(8,128)(2,1)}, bf16[6,208,768]{2,1,0:T(8,128)(2,1)}, u32[]{:S(2)}, u32[]{:S(2)}) collective-permute-start(bf16[6,208,768]{2,1,0:T(8,128)(2,1)} %bitcast.105), channel_id=1, source_target_pairs={{0,1},{1,0},{2,3},{3,2},{4,5},{5,4},{6,7},{7,6},{8,9},{9,8},{10,11... | collective-permute-start | bytes 5750792 | tf_op jit(solution)/shard_map/ppermute | solution.py:759
  301.4 28.7 %collective-permute-start.15 = (bf16[2,4,96,768]{3,2,1,0:T(8,128)(2,1)}, bf16[2,4,96,768]{3,2,1,0:T(8,128)(2,1)}, u32[]{:S(2)}, u32[]{:S(2)}) collective-permute-start(bf16[2,4,96,768]{3,2,1,0:T(8,128)(2,1)} %get-tuple-element.105.refs_3_), channel_id=1, source_target_pairs={{0,8},{8,16},{16,24},{24,28},{28,20},{20,12},{12,4},{4,0},{1,9},{9... | collective-permute-start | bytes 3538952 | tf_op jit(solution)/shard_map/ppermute | solution.py:784
  302.0 28.4 %collective-permute-start.16 = (bf16[2,4,96,768]{3,2,1,0:T(8,128)(2,1)}, bf16[2,4,96,768]{3,2,1,0:T(8,128)(2,1)}, u32[]{:S(2)}, u32[]{:S(2)}) collective-permute-start(bf16[2,4,96,768]{3,2,1,0:T(8,128)(2,1)} %get-tuple-element.106.refs_4_), channel_id=1, source_target_pairs={{0,4},{8,0},{16,8},{24,16},{28,24},{20,28},{12,20},{4,12},{1,5},{9... | collective-permute-start | bytes 3538952 | tf_op jit(solution)/shard_map/ppermute | solution.py:784
  305.2 1.3 collective-permute-start.13
  308.0 4.0 collective-permute-start.14
  346.4 38.5 %collective-permute-start.17 = (bf16[6,208,768]{2,1,0:T(8,128)(2,1)}, bf16[6,208,768]{2,1,0:T(8,128)(2,1)}, u32[]{:S(2)}, u32[]{:S(2)}) collective-permute-start(bf16[6,208,768]{2,1,0:T(8,128)(2,1)} %get-tuple-element.115.refs_6_.refs_0_), channel_id=1, source_target_pairs={{0,1},{1,0},{2,3},{3,2},{4,5},{5,4},{6,7},{7,6},{8,9},{9,8},{10,11... | collective-permute-start | bytes 5750792 | tf_op jit(solution)/shard_map/ppermute | solution.py:759
  350.5 34.3 %copy-start.3 = (bf16[6,208,768]{2,1,0:T(8,128)(2,1)}, bf16[6,208,768]{2,1,0:T(8,128)(2,1)S(1)}, u32[]{:S(2)}) copy-start(bf16[6,208,768]{2,1,0:T(8,128)(2,1)S(1)} %fusion.1.refs_0_) | copy-start | bytes 5750788
  350.5 44.3 %collective-permute-start.12 = (bf16[6,208,768]{2,1,0:T(8,128)(2,1)S(1)}, bf16[6,208,768]{2,1,0:T(8,128)(2,1)}, u32[]{:S(2)}, u32[]{:S(2)}) collective-permute-start(bf16[6,208,768]{2,1,0:T(8,128)(2,1)S(1)} %fusion.1.refs_0_), channel_id=1, source_target_pairs={{0,2},{1,3},{2,0},{3,1},{4,6},{5,7},{6,4},{7,5},{8,10},{9,11},{10,... | collective-permute-start | bytes 5750792 | tf_op jit(solution)/shard_map/ppermute | solution.py:763
  352.1 28.4 %collective-permute-start.18 = (bf16[2,4,96,768]{3,2,1,0:T(8,128)(2,1)}, bf16[2,4,96,768]{3,2,1,0:T(8,128)(2,1)}, u32[]{:S(2)}, u32[]{:S(2)}) collective-permute-start(bf16[2,4,96,768]{3,2,1,0:T(8,128)(2,1)} %get-tuple-element.113.refs_12_), channel_id=1, source_target_pairs={{0,8},{8,16},{16,24},{24,28},{28,20},{20,12},{12,4},{4,0},{1,9},{9... | collective-permute-start | bytes 3538952 | tf_op jit(solution)/shard_map/ppermute | solution.py:784
  352.4 28.1 %collective-permute-start.19 = (bf16[2,4,96,768]{3,2,1,0:T(8,128)(2,1)S(1)}, bf16[2,4,96,768]{3,2,1,0:T(8,128)(2,1)}, u32[]{:S(2)}, u32[]{:S(2)}) collective-permute-start(bf16[2,4,96,768]{3,2,1,0:T(8,128)(2,1)S(1)} %copy-done.15), channel_id=1, source_target_pairs={{0,4},{8,0},{16,8},{24,16},{28,24},{20,28},{12,20},{4,12},{1,5},{9... | collective-permute-start | bytes 3538952 | tf_op jit(solution)/shard_map/ppermute | solution.py:784
  394.9 40.1 %copy-start.17 = (bf16[2,4,96,768]{3,2,1,0:T(8,128)(2,1)S(1)}, bf16[2,4,96,768]{3,2,1,0:T(8,128)(2,1)}, u32[]{:S(2)}) copy-start(bf16[2,4,96,768]{3,2,1,0:T(8,128)(2,1)} %get-tuple-element.121.refs_11_) | copy-start | bytes 3538948
  394.9 40.5 %copy-start.16 = (bf16[2,4,96,768]{3,2,1,0:T(8,128)(2,1)S(1)}, bf16[2,4,96,768]{3,2,1,0:T(8,128)(2,1)}, u32[]{:S(2)}) copy-start(bf16[2,4,96,768]{3,2,1,0:T(8,128)(2,1)} %get-tuple-element.122.refs_12_) | copy-start | bytes 3538948
  434.9 4.2 collective-permute-start.20
  435.0 28.4 %collective-permute-start.21 = (bf16[2,4,96,768]{3,2,1,0:T(8,128)(2,1)S(1)}, bf16[2,4,96,768]{3,2,1,0:T(8,128)(2,1)S(1)}, u32[]{:S(2)}, u32[]{:S(2)}) collective-permute-start(bf16[2,4,96,768]{3,2,1,0:T(8,128)(2,1)S(1)} %copy-done.17), channel_id=1, source_target_pairs={{0,8},{8,16},{16,24},{24,28},{28,20},{20,12},{12,4},{4,0},{1,9},{9... | collective-permute-start | bytes 3538952 | tf_op jit(solution)/shard_map/ppermute | solution.py:784
  435.4 28.1 %collective-permute-start.22 = (bf16[2,4,96,768]{3,2,1,0:T(8,128)(2,1)S(1)}, bf16[2,4,96,768]{3,2,1,0:T(8,128)(2,1)}, u32[]{:S(2)}, u32[]{:S(2)}) collective-permute-start(bf16[2,4,96,768]{3,2,1,0:T(8,128)(2,1)S(1)} %copy-done.16), channel_id=1, source_target_pairs={{0,4},{8,0},{16,8},{24,16},{28,24},{20,28},{12,20},{4,12},{1,5},{9... | collective-permute-start | bytes 3538952 | tf_op jit(solution)/shard_map/ppermute | solution.py:784
  442.4 44.1 %collective-permute-start.24 = (bf16[6,208,768]{2,1,0:T(8,128)(2,1)}, bf16[6,208,768]{2,1,0:T(8,128)(2,1)}, u32[]{:S(2)}, u32[]{:S(2)}) collective-permute-start(bf16[6,208,768]{2,1,0:T(8,128)(2,1)} %add_convert_fusion.1.refs_6_.refs_5_), channel_id=1, source_target_pairs={{0,2},{1,3},{2,0},{3,1},{4,6},{5,7},{6,4},{7,5},{8,10},{9,11},{10,... | collective-permute-start | bytes 5750792 | tf_op jit(solution)/shard_map/ppermute | solution.py:763
  443.9 112.6 %collective-permute-start.26 = (f32[6,208,768]{2,1,0:T(8,128)}, f32[6,208,768]{2,1,0:T(8,128)}, u32[]{:S(2)}, u32[]{:S(2)}) collective-permute-start(f32[6,208,768]{2,1,0:T(8,128)} %get-tuple-element.127.own_grad_ref), channel_id=1, source_target_pairs={{0,1},{1,0},{2,3},{3,2},{4,5},{5,4},{6,7},{7,6},{8,9},{9,8},{10,11... | collective-permute-start | bytes 11501576 | tf_op jit(solution)/shard_map/ppermute | solution.py:759
  475.4 15.1 %collective-permute-start.23 = (bf16[6,208,768]{2,1,0:T(8,128)(2,1)}, bf16[6,208,768]{2,1,0:T(8,128)(2,1)}, u32[]{:S(2)}, u32[]{:S(2)}) collective-permute-start(bf16[6,208,768]{2,1,0:T(8,128)(2,1)} %finish.1), channel_id=1, source_target_pairs={{0,1},{1,0},{2,3},{3,2},{4,5},{5,4},{6,7},{7,6},{8,9},{9,8},{10,11... | collective-permute-start | bytes 5750792 | tf_op jit(solution)/shard_map/ppermute | solution.py:759
  478.9 39.1 %collective-permute-start.27 = (bf16[2,4,96,768]{3,2,1,0:T(8,128)(2,1)}, bf16[2,4,96,768]{3,2,1,0:T(8,128)(2,1)}, u32[]{:S(2)}, u32[]{:S(2)}) collective-permute-start(bf16[2,4,96,768]{3,2,1,0:T(8,128)(2,1)} %get-tuple-element.125.refs_6_), channel_id=1, source_target_pairs={{0,8},{8,16},{16,24},{24,28},{28,20},{20,12},{12,4},{4,0},{1,9},{9... | collective-permute-start | bytes 3538952 | tf_op jit(solution)/shard_map/ppermute | solution.py:784
  479.5 40.7 %collective-permute-start.28 = (bf16[2,4,96,768]{3,2,1,0:T(8,128)(2,1)S(1)}, bf16[2,4,96,768]{3,2,1,0:T(8,128)(2,1)}, u32[]{:S(2)}, u32[]{:S(2)}) collective-permute-start(bf16[2,4,96,768]{3,2,1,0:T(8,128)(2,1)S(1)} %copy-done.14), channel_id=1, source_target_pairs={{0,4},{8,0},{16,8},{24,16},{28,24},{20,28},{12,20},{4,12},{1,5},{9... | collective-permute-start | bytes 3538952 | tf_op jit(solution)/shard_map/ppermute | solution.py:784
  489.1 67.4 %collective-permute-start.25 = (bf16[6,208,768]{2,1,0:T(8,128)(2,1)S(1)}, bf16[6,208,768]{2,1,0:T(8,128)(2,1)}, u32[]{:S(2)}, u32[]{:S(2)}) collective-permute-start(bf16[6,208,768]{2,1,0:T(8,128)(2,1)S(1)} %add_convert_fusion.own_ref), channel_id=1, source_target_pairs={{0,1},{1,0},{2,3},{3,2},{4,5},{5,4},{6,7},{7,6},{8,9},{9,8},{10,11... | collective-permute-start | bytes 5750792 | tf_op jit(solution)/shard_map/ppermute | solution.py:759
  490.6 36.0 %collective-permute-start.29 = (f32[20,768]{1,0:T(8,128)S(1)}, f32[20,768]{1,0:T(8,128)S(1)}, u32[]{:S(2)}, u32[]{:S(2)}) collective-permute-start(f32[20,768]{1,0:T(8,128)S(1)} %maximum_add_fusion), channel_id=1, source_target_pairs={{0,1},{1,0},{2,3},{3,2},{4,5},{5,4},{6,7},{7,6},{8,9},{9,8},{10,11... | collective-permute-start | bytes 184328 | tf_op jit(solution)/shard_map/ppermute | solution.py:971
  499.4 29.4 %copy-start.38 = (f32[4,1,768]{2,1,0:T(1,128)S(1)}, f32[4,1,768]{2,1,0:T(1,128)}, u32[]{:S(2)}) copy-start(f32[4,1,768]{2,1,0:T(1,128)} %get-tuple-element.136) | copy-start | bytes 36868
  499.4 29.4 %copy-start.37 = (f32[4,1,768]{2,1,0:T(1,128)S(1)}, f32[4,1,768]{2,1,0:T(1,128)}, u32[]{:S(2)}) copy-start(f32[4,1,768]{2,1,0:T(1,128)} %get-tuple-element.135) | copy-start | bytes 36868
  499.4 29.5 %copy-start.42 = (f32[2,192]{1,0:T(2,128)S(1)}, f32[2,192]{1,0:T(2,128)}, u32[]{:S(2)}) copy-start(f32[2,192]{1,0:T(2,128)} %get-tuple-element.134) | copy-start | bytes 4612
  524.6 47.4 %collective-permute-start.32 = (bf16[2,4,96,768]{3,2,1,0:T(8,128)(2,1)}, bf16[2,4,96,768]{3,2,1,0:T(8,128)(2,1)S(1)}, u32[]{:S(2)}, u32[]{:S(2)}) collective-permute-start(bf16[2,4,96,768]{3,2,1,0:T(8,128)(2,1)} %get-tuple-element.128.refs_0_), channel_id=1, source_target_pairs={{0,8},{8,16},{16,24},{24,28},{28,20},{20,12},{12,4},{4,0},{1,9},{9... | collective-permute-start | bytes 3538952 | tf_op jit(solution)/shard_map/ppermute | solution.py:784
  526.3 45.7 %collective-permute-start.33 = (bf16[2,4,96,768]{3,2,1,0:T(8,128)(2,1)}, bf16[2,4,96,768]{3,2,1,0:T(8,128)(2,1)}, u32[]{:S(2)}, u32[]{:S(2)}) collective-permute-start(bf16[2,4,96,768]{3,2,1,0:T(8,128)(2,1)} %get-tuple-element.129.refs_1_), channel_id=1, source_target_pairs={{0,4},{8,0},{16,8},{24,16},{28,24},{20,28},{12,20},{4,12},{1,5},{9... | collective-permute-start | bytes 3538952 | tf_op jit(solution)/shard_map/ppermute | solution.py:784
  526.6 4.4 collective-permute-start.30
  533.1 22.7 %collective-permute-start.31 = (f32[31,768]{1,0:T(8,128)S(1)}, f32[31,768]{1,0:T(8,128)S(1)}, u32[]{:S(2)}, u32[]{:S(2)}) collective-permute-start(f32[31,768]{1,0:T(8,128)S(1)} %broadcast_add_fusion.2), channel_id=1, source_target_pairs={{0,4},{4,0},{8,12},{12,8},{16,20},{20,16},{24,28},{28,24},{1,5},{5... | collective-permute-start | bytes 285704 | tf_op jit(solution)/shard_map/ppermute | solution.py:971
  577.4 16.8 %collective-permute-start.36 = (bf16[1,4,96,768]{3,2,1,0:T(8,128)(2,1)}, bf16[1,4,96,768]{3,2,1,0:T(8,128)(2,1)S(1)}, u32[]{:S(2)}, u32[]{:S(2)}) collective-permute-start(bf16[1,4,96,768]{3,2,1,0:T(8,128)(2,1)} %get-tuple-element.137), channel_id=1, source_target_pairs={{0,4},{8,0},{16,8},{24,16},{28,24},{20,28},{12,20},{4,12},{1,5},{9... | collective-permute-start | bytes 1769480 | tf_op jit(solution)/shard_map/ppermute | solution.py:784
  580.4 13.8 %collective-permute-start.35 = (bf16[1,4,96,768]{3,2,1,0:T(8,128)(2,1)}, bf16[1,4,96,768]{3,2,1,0:T(8,128)(2,1)S(1)}, u32[]{:S(2)}, u32[]{:S(2)}) collective-permute-start(bf16[1,4,96,768]{3,2,1,0:T(8,128)(2,1)} %get-tuple-element.138), channel_id=1, source_target_pairs={{0,8},{8,16},{16,24},{24,28},{28,20},{20,12},{12,4},{4,0},{1,9},{9... | collective-permute-start | bytes 1769480 | tf_op jit(solution)/shard_map/ppermute | solution.py:784
  581.3 12.2 %collective-permute-start.34 = (f32[31,768]{1,0:T(8,128)S(1)}, f32[31,768]{1,0:T(8,128)S(1)}, u32[]{:S(2)}, u32[]{:S(2)}) collective-permute-start(f32[31,768]{1,0:T(8,128)S(1)} %broadcast_add_fusion.1), channel_id=1, source_target_pairs={{0,8},{4,12},{8,0},{12,4},{16,24},{20,28},{24,16},{28,20},{1,9},{5... | collective-permute-start | bytes 285704 | tf_op jit(solution)/shard_map/ppermute | solution.py:971
  601.1 5.9 collective-permute-start.37
  (40 other events, 207.9 us)
Sparse Core Ops, SparseCore 0:
  478.2 71.4 reduce-scatter.1

commit v7 on v6

--- a/solution.py
+++ b/solution.py
@@ -27,7 +27,7 @@
 
 
 def cost(us):
-    return pl.CostEstimate(flops=int(us * 2e8), bytes_accessed=0, transcendentals=0)
+    return pl.CostEstimate(flops=int(us * 1.1e9), bytes_accessed=0, transcendentals=0)
 
 
 def route_plan(routes, expert_count):
@@ -455,17 +455,16 @@
     return raised * (1.0 / jnp.sum(raised, axis=-1, keepdims=True))
 
 
-def attention_forward(x, turn, gain, shift, weight, bias, out_weight, half, kept, after):
+def attention_forward(x, turn, gain, shift, weight, bias, out_weight):
     images, seq, width = x.shape
     rows, inner = ROWS, weight.shape[2]
+    blocks = images // TRIO
 
     def kernel(
         turn_ref, x_ref, gain_ref, shift_ref, w_ref, b_ref, wo_ref,
         *refs
     ):
-        own_ref, other_ref, pad_ref, n_ref, q_ref, k_ref, v_ref, o_ref, held = refs[
-            len(kept) + len(after) :
-        ]
+        own_ref, other_ref, pad_ref, n_ref, q_ref, k_ref, v_ref, o_ref, held = refs
         held[...] = jnp.zeros_like(held)
         for i in range(TRIO):
             held[i, :seq, :] = x_ref[i].astype(jnp.float32)
@@ -488,21 +487,19 @@
         part = jnp.dot(mixed, wo_ref[...], preferred_element_type=jnp.float32)
         part = part.astype(jnp.bfloat16).reshape(TRIO, rows, width)
 
-        @pl.when(pl.program_id(0) == 0)
+        @pl.when(pl.program_id(0) < blocks // 2)
         def _():
             other_ref[...] = part
 
-        @pl.when(pl.program_id(0) == 1)
+        @pl.when(pl.program_id(0) >= blocks // 2)
         def _():
             own_ref[...] = part
 
 
     wide = shape_of((images, rows, width), jnp.bfloat16)
     slim = shape_of((images, rows, inner), jnp.bfloat16)
-    blocks = images // TRIO
-
     def place(i, turn):
-        return (2 * (1 - i) + half, 0, 0)
+        return ((i + blocks // 2) % blocks, 0, 0)
 
     def whole(array):
         return pl.BlockSpec(array.shape, lambda i, turn: (0,) * array.ndim)
@@ -512,24 +509,29 @@
         kernel,
         grid_spec=pltpu.PrefetchScalarGridSpec(
             num_scalar_prefetch=1,
-            grid=(blocks // 2,),
+            grid=(blocks,),
             in_specs=[
                 pl.BlockSpec(
-                    (TRIO, seq, width), lambda i, turn: ((2 * (1 - i) + half + turn[0]) % blocks, 0, 0)
+                    (TRIO, seq, width), lambda i, turn: ((i + blocks // 2 + turn[0]) % blocks, 0, 0)
                 )
             ]
-            + [whole(array) for array in small]
-            + [pl.BlockSpec(memory_space=pl.ANY)] * (len(kept) + len(after)),
-            out_specs=[pl.BlockSpec((TRIO, rows, width), lambda i, turn: (0, 0, 0))] * 2
+            + [whole(array) for array in small],
+            out_specs=[
+                pl.BlockSpec(
+                    (TRIO, rows, width), lambda i, turn: (jnp.maximum(i - blocks // 2, 0), 0, 0)
+                ),
+                pl.BlockSpec(
+                    (TRIO, rows, width), lambda i, turn: (jnp.minimum(i, blocks // 2 - 1), 0, 0)
+                ),
+            ]
             + [pl.BlockSpec((TRIO, *a.shape[1:]), place) for a in [wide] * 2 + [slim] * 4],
             scratch_shapes=[pltpu.VMEM((TRIO, rows, width), jnp.float32)],
         ),
-        out_shape=[shape_of((TRIO, rows, width), jnp.bfloat16)] * 2 + [wide] * 2 + [slim] * 4,
-        input_output_aliases={7 + i: 2 + i for i in range(len(kept))},
+        out_shape=[shape_of((images // 2, rows, width), jnp.bfloat16)] * 2 + [wide] * 2 + [slim] * 4,
         compiler_params=pltpu.CompilerParams(vmem_limit_bytes=VMEM),
-        cost_estimate=cost(9),
+        cost_estimate=cost(18),
         name="attention_forward",
-    )(turn, x, *small, *kept, *after)
+    )(turn, x, *small)
 
 
 def attention_backward(own_da, other_da, x, n, q, k, v, o, weight, out_weight, after):
@@ -610,34 +612,18 @@
 
 
 def middle_norm(near, far, x, out_bias, gain, shift, after):
-    each = near[0].shape[0]
-    count, (_, rows, width) = 2 * each, x.shape
-
-    def kernel(near_a, near_b, far_a, far_b, x_ref, bias_ref, gain_ref, shift_ref, *refs):
-        middle_ref, n_ref = refs[len(after) :]
-        early = pl.program_id(0) < each
-        total = jnp.where(early, near_a[0], near_b[0]).astype(jnp.float32)
-        total = total + jnp.where(early, far_a[0], far_b[0]).astype(jnp.float32)
+    def kernel(near_ref, far_ref, x_ref, bias_ref, gain_ref, shift_ref, middle_ref, n_ref):
+        total = near_ref[0].astype(jnp.float32) + far_ref[0].astype(jnp.float32)
         middle = x_ref[0].astype(jnp.float32) + total + bias_ref[...]
         middle_ref[0] = middle
         n_ref[0] = (normal(middle)[0] * gain_ref[...] + shift_ref[...]).astype(jnp.bfloat16)
 
-    block = (1, rows, width)
-    low = pl.BlockSpec(block, lambda i: (jnp.minimum(i, each - 1), 0, 0))
-    high = pl.BlockSpec(block, lambda i: (jnp.maximum(i - each, 0), 0, 0))
-    one = pl.BlockSpec(block, lambda i: (i, 0, 0))
-    flat = pl.BlockSpec((1, width), lambda i: (0, 0))
-    return pl.pallas_call(
-        kernel,
-        grid=(count,),
-        in_specs=[low, high, low, high, one, flat, flat, flat]
-        + [pl.BlockSpec(memory_space=pl.ANY)] * len(after),
-        out_specs=[one, one],
-        out_shape=[shape_of((count, rows, width), kind) for kind in (jnp.float32, jnp.bfloat16)],
-        compiler_params=pltpu.CompilerParams(vmem_limit_bytes=VMEM),
-        cost_estimate=cost(7),
-        name="middle_norm",
-    )(*near, *far, x, out_bias, gain, shift, *after)
+    return call(
+        kernel, "middle_norm", near.shape[0],
+        [(near, True), (far, True), (x, True), (out_bias, False), (gain, False), (shift, False)],
+        [(shape_of(near.shape, jnp.float32), True), (shape_of(near.shape, jnp.bfloat16), True)],
+        after=after, us=8,
+    )
 
 
 def norm_back(dn, unit, spread_of, gain):
@@ -784,7 +770,7 @@
     return lax.ppermute(value, "dp", path)
 
 
-def ring_add(got, sources, steps, kinds, after):
+def ring_add(got, sources, steps, kinds, after, carry=()):
     groups, came = len(sources), got[0].shape[0]
     many, total, cols = sources[0][0].shape
     rows, part = total // 8, 2
@@ -792,7 +778,8 @@
     joint = all(kind == kinds[0] for kind in kinds)
 
     def kernel(owners_ref, *refs):
-        held, locals_, outs = refs[:2], refs[2 : 2 + 2 * groups], refs[2 + 2 * groups + len(after) :]
+        held, locals_ = refs[:2], refs[2 : 2 + 2 * groups]
+        outs = refs[2 + 2 * groups + len(after) + len(carry) :]
         for g in range(groups):
             for d in range(2):
                 value = locals_[2 * g + d][...]
@@ -820,14 +807,19 @@
             grid=(many // part,),
             in_specs=[stack(came)] * 2
             + [source(i) for i in range(2 * groups)]
-            + [pl.BlockSpec(memory_space=pl.ANY)] * len(after),
-            out_specs=[stack(dims[0]) for dims, _ in outs],
+            + [pl.BlockSpec(memory_space=pl.ANY)] * (len(after) + len(carry)),
+            out_specs=[stack(dims[0]) for dims, _ in outs]
+            + [pl.BlockSpec(memory_space=pl.ANY)] * len(carry),
         ),
-        out_shape=[jax.ShapeDtypeStruct(dims, kind) for dims, kind in outs],
+        out_shape=[jax.ShapeDtypeStruct(dims, kind) for dims, kind in outs]
+        + [jax.ShapeDtypeStruct(value.shape, value.dtype) for value in carry],
+        input_output_aliases={
+            3 + 2 * groups + len(after) + i: len(outs) + i for i in range(len(carry))
+        },
         compiler_params=pltpu.CompilerParams(vmem_limit_bytes=VMEM),
         cost_estimate=cost(5),
         name="ring_add",
-    )(owners, *got, *[piece for pair in sources for piece in pair], *after)
+    )(owners, *got, *[piece for pair in sources for piece in pair], *after, *carry)
 
 
 def on_device(
@@ -875,15 +867,11 @@
     turn = (half * core).astype(jnp.int32)[None]
     bias_rows = jnp.stack([qv_bias[0], jnp.zeros_like(qv_bias[0]), qv_bias[1]]).astype(f32)
     images_in = embedded.reshape(images, SEQ, width)
-    kept, near, far = (), [], []
-    for i in range(2):
-        own, other, *kept = attention_forward(
-            images_in, turn // TRIO, row(attn_gain), row(attn_shift),
-            qkv_weight, bias_rows, out_weight, i, tuple(kept), tuple(near),
-        )
-        near.append(core_sum(own, other, 0.0))
-        far.append(across(near[i]))
-    x, normed, queries, keys, values, mixed = kept
+    own, other, x, normed, queries, keys, values, mixed = attention_forward(
+        images_in, turn // TRIO, row(attn_gain), row(attn_shift), qkv_weight, bias_rows, out_weight
+    )
+    near = core_sum(own, other, 0.0)
+    far = across(near)
 
     chosen = own_first(routes, -1).reshape(images * ROWS, 2)
     rows, columns, plan, tiles = route_plan(chosen, expert_count)
@@ -927,13 +915,13 @@
         ]
     y_second, back_second, *second, bias_second = experts_of(1, tuple(moving))
 
-    def round_trip(step, kinds, *after):
+    def round_trip(step, kinds, after=(), carry=()):
         if not ringed:
-            return ()
+            return carry
         got = [ring_hop(value, way) for value, way in zip(moving, (1, -1))]
         if step < 8:
-            return ring_add(got, [first, second], [step, step - 1], kinds, after)
-        return ring_add(got, [second], [step - 1], kinds, after)
+            return ring_add(got, [first, second], [step, step - 1], kinds, after, carry)
+        return ring_add(got, [second], [step - 1], kinds, after, carry)
 
     moving = round_trip(1, [low, low])
     own, other, dots = collect((back_first, back_second), columns, plan, width, tuple(moving))
@@ -943,67 +931,90 @@
     dots = dots[:expert_count] + dots[expert_count:]
     dots = dots[:, :own_rows] + to_core(dots[:, own_rows:])
     dots = (dots + across(dots)).T.reshape(half, ROWS, expert_count)
-    moving = round_trip(2, [low, low], back_near)
+    moving = round_trip(2, [low, low], (back_near,))
     own_y, other_y = collect((y_first, y_second), columns, plan, width, (back_near, *moving))
-    moving = round_trip(3, [low, low], other_y)
+    moving = round_trip(3, [low, low], (other_y,))
     middle_grad, own_da, moe_sums, router_sums, bias_sums = middle_back(
         back_near, back_far, dots, gates, chosen, mix_pair, own_normed, router_weight,
         down_bias, middle, upstream, row(moe_gain), tuple(moving),
     )
-    y_near = core_sum(imaged(own_y), imaged(other_y), zero_of(back_far))
+    *moving, own_da = round_trip(4, [low, low], (), (own_da,))
+    other_da, other_grad = to_core(own_da), to_core(middle_grad)
+    y_near = core_sum(imaged(own_y), imaged(other_y), zero_of(own_da))
     y_far = across(y_near)
-    other_da, other_grad = to_core(own_da), to_core(middle_grad)
-    moving = round_trip(4, [low, low], own_da)
     own, other, grad_qkv, grad_out, grad_qv_bias, sums = attention_backward(
         own_da, other_da, x, normed, queries, keys, values, mixed, qkv_weight, out_weight,
-        (y_far, *moving),
-    )
+        (y_near, *moving),
+    )
+    *moving, own, other = round_trip(5, [low, low], (y_far,), (own, other))
     last_near = core_sum(own, other, 0.0)
     last_far = across(last_near)
-    slim = jnp.concatenate([grad_qkv, grad_out]).astype(low)
-    slim = lax.psum_scatter(slim, "dp", scatter_dimension=1, tiled=True).astype(f32)
-    moving = round_trip(5, [low, low], last_near)
 
     def after_round(value):
-        return value + zero_of(moving[1]) if ringed else value
+        return value + zero_of(moving[1]).astype(value.dtype) if ringed else value
 
     def meet(value, axis, bit):
         return value + lax.ppermute(value, axis, pairs(lax.axis_size(axis), bit))
+
+    def halve(values, bit, axis):
+        mine = (lax.axis_index("dp") >> bit) % 2
+        keep = lax.dynamic_index_in_dim(values, mine, axis, keepdims=True)
+        give = lax.dynamic_index_in_dim(values, 1 - mine, axis, keepdims=True).astype(low)
+        return keep, lax.ppermute(give, "dp", pairs(8, 1 << bit))
 
     own_out = finish(y_near, y_far, middle, mix_pair, bias_twice, (last_near, *moving))
     layer_out = in_order(own_out, to_core(own_out))
     router_bias = [router_sums, bias_sums[:expert_count] + bias_sums[expert_count : 2 * expert_count]]
-    tensor_parts = jnp.concatenate([sums[:2]] + [0.5 * part for part in (moe_sums, *router_bias)])
-    tensor_parts = meet(meet(after_round(tensor_parts), "tensor", 1), "tensor", 2)
     packed = jnp.concatenate(
         [
-            tensor_parts,
+            sums[:2],
+            0.5 * moe_sums,
+            *[0.5 * part for part in router_bias],
             sums[2:],
             jnp.pad(grad_qv_bias, ((0, 0), (0, width - head_width))),
             bias_first[:, 0],
             bias_second[:, 0],
         ]
     )
-    moving = round_trip(6, [low, low], layer_out)
+    slim = jnp.concatenate([grad_qkv, grad_out])
+    base = 4 + 2 * expert_count
     last = (last_near.astype(f32) + last_far.astype(f32)).astype(low)
-    grad_embedded = input_back(
-        last, to_core(last), x, middle_grad, other_grad, row(attn_gain), turn, tuple(moving)
-    )
+    other_last = to_core(last)
+
+    def input_grad():
+        return input_back(
+            last, other_last, x, middle_grad, other_grad, row(attn_gain), turn, tuple(moving)
+        )
+
     if ringed:
-        packed = meet(after_round(packed), "dp", 1)
-        up_first, down_first, *moving = round_trip(7, [f32, low], grad_embedded, packed)
-        packed = meet(after_round(packed), "dp", 2)
-        up_second, down_second = round_trip(8, [f32], packed)
-        packed = meet(packed + zero_of(up_second), "dp", 4)
+        slim = slim.reshape(4, 2, 2, 2, width // 8, head_width)
+        packed = after_round(packed)
+        for step, bit, axis in ((6, 0, 3), (7, 1, 2), (8, 2, 1)):
+            keep, got = halve(after_round(slim) if step > 6 else slim, bit, axis)
+            sent = lax.ppermute(packed, "dp", pairs(8, 1 << bit))
+            if step == 6:
+                moving = round_trip(6, [low, low], (last_near, layer_out))
+            elif step == 7:
+                up_first, down_first, *moving = round_trip(7, [f32, low])
+                grad_embedded = input_grad()
+            else:
+                moving = round_trip(8, [f32], (grad_embedded,))
+            slim = keep.astype(f32) + got.astype(f32) + zero_of(moving[0])
+            packed = after_round(packed + sent)
+        up_second, down_second = moving
+        slim = slim.reshape(4, width // 8, head_width)
     else:
+        grad_embedded = input_grad()
         packed = lax.psum(packed, "dp")
+        slim = lax.psum_scatter(slim, "dp", scatter_dimension=1, tiled=True)
         up_first, down_first, up_second, down_second = [
             lax.psum_scatter(grad, "dp", scatter_dimension=1, tiled=True).astype(f32)[None]
             for grad in (*first, *second)
         ]
     grad_up = jnp.concatenate([up_first[0], up_second[0]])
     grad_down = jnp.concatenate([down_first[0], down_second[0]]).transpose(0, 2, 1)
-    base = 4 + 2 * expert_count
+    tensor_parts = meet(meet(packed[:base], "tensor", 1), "tensor", 2)
+    packed = jnp.concatenate([tensor_parts, packed[base:]])
     return (
         layer_out,
         grad_embedded,

time: 626 us -> 542 us (0.87)
  waiting for transfers between devices: 174 us -> 107 us
  between operations: 18.8 us -> 7.35 us
  Pallas kernels: 291 us -> 281 us
  local copies, waits for them, and re-layouts: 53 us -> 61.3 us
    ppermute x16, waiting for transfers between devices: 105 us -> 44.4 us  [ring_hop(): return lax.ppermute(value, 'dp', path)]
    ppermute x0 -> x6, waiting for transfers between devices: none -> 22.1 us  [the longest x3 22.1 us: on_device(): sent = lax.ppermute(packed, 'dp', pairs(8, 1 << bit))]
    reduce_scatter x1 -> x0, waiting for transfers between devices: 14.8 us -> none  [on_device(): lax.psum_scatter(slim, 'dp', scatter_dimension=1, tiled=True).astype(f32)]
    ppermute x5 -> x2, waiting for transfers between devices: 18 us -> 3.46 us  [meet(): return value + lax.ppermute(value, axis, pairs(lax.axis_size(axis), bit))]
    ppermute x0 -> x6, starting transfers between devices: none -> 7.18 us  [the longest x3 5.1 us: on_device(): sent = lax.ppermute(packed, 'dp', pairs(8, 1 << bit))]
    pallas_call x1 -> x0, Pallas kernels: 6.95 us -> none  [middle_norm(): pl.pallas_call(kernel, grid=(count,), in_specs=[low, high, low, high, one...]
    pallas_call x3 -> x4, Pallas kernels: 58.1 us -> 64.9 us  [call(): pl.pallas_call(body, grid_spec=pltpu.PrefetchScalarGridSpec(num_scalar_pr...]
    unnamed x104 -> x107, local copies, waits for them, and re-layouts: 13.3 us -> 18 us
  transfers between devices with their start and end apart: 39 -> 39, of which waited for: 21 -> 17; matrix products, arithmetic and copies ran while one was open for 12% -> 13% of each run, Pallas kernels for 22% -> 30%
where the time goes in v7:
time: 542 us; the launch traced here: 532 us
  Pallas kernels  281 us (52%)
  waiting for transfers between devices  107 us (20%)
  local copies, waits for them, and re-layouts  61.3 us (11%)
  other arithmetic  38.5 us (7%)
  starting transfers between devices  36.3 us (7%)
  between operations  7.35 us (1%)
    pallas_call x2, Pallas kernels, expert_pass(): pl.pallas_call(kernel, grid_spec=pltpu.PrefetchScalarGridSpec(num_scalar_...  73.2 us
    pallas_call x4, Pallas kernels, call(): pl.pallas_call(body, grid_spec=pltpu.PrefetchScalarGridSpec(num_scalar_pr...  64.9 us
    ppermute x16, waiting for transfers between devices, ring_hop(): return lax.ppermute(value, 'dp', path)  44.4 us
    pallas_call x2, Pallas kernels, collect(): pl.pallas_call(kernel, grid_spec=pltpu.PrefetchScalarGridSpec(num_scalar_...  36.3 us
    pallas_call x8, Pallas kernels, ring_add(): pl.pallas_call(kernel, grid_spec=pltpu.PrefetchScalarGridSpec(num_scalar_...  33.7 us
    ppermute x5, waiting for transfers between devices, across(): return lax.ppermute(value, 'tensor', pairs(lax.axis_size('tensor'), 2))  31.1 us
    ppermute x3, waiting for transfers between devices, on_device(): sent = lax.ppermute(packed, 'dp', pairs(8, 1 << bit))  22.1 us
    pallas_call x1, Pallas kernels, gated_spread(): pl.pallas_call(kernel, grid_spec=pltpu.PrefetchScalarGridSpec(num_scalar_...  21.6 us
  transfers between devices with their start and end apart: 39, of which 17 were waited for; matrix products, arithmetic and copies ran while one was open for 13% of the time, Pallas kernels for 30%

profile of v7, /device:TPU:0, one launch (start us, length us, event | category | flops | bytes accessed | tf_op | source)
XLA Modules:
  0.0 531.9 jit_solution(571358170841291801)
XLA Ops:
  1.4 2.3 copy.101.w_ref.refs_8_
  4.4 4.3 reshape.216.x_ref
  10.0 20.6 %attention_forward.1 = (bf16[6,208,768]{2,1,0:T(8,128)(2,1)}, bf16[6,208,768]{2,1,0:T(8,128)(2,1)}, bf16[12,208,768]{2,1,0:T(8,128)(2,1)}, bf16[12,208,768]{2,1,...) custom-call(s32[1]{0:T(128)S(6)} %select_n.441.turn_ref, ...), custom_call_target="tpu_custom_call" | custom-call | flops 19800000512 | tf_op jit(solution)/shard_map/attention_forward/pallas_call | solution.py:508
  35.3 4.3 reshape.217
  43.5 2.4 pad_slice_fusion.1
  46.5 2.2 add_convert_fusion.2.refs_0_
  48.7 2.6 collective-permute-start.1
  51.9 2.4 maximum_select_fusion.refs_10_
  54.2 15.4 %spread.1.refs_6_.g_ref = bf16[8,1024,768]{2,1,0:T(8,128)(2,1)} custom-call(s32[144]{0:T(256)} %pad_add_fusion.1.plan_ref, s32[6,2,416]{2,1,0:T(2,128)} %add_bitcast_fusion.rows_ref, bf16[2496,768]{1,0:T(8,128)(2,1)} %bitcast.104), custom_call_target="tpu_custom_call" | custom-call | flops 16499999744 | tf_op jit(solution)/shard_map/spread/pallas_call | solution.py:91
  69.7 24.0 %collective-permute-done.1.refs_1_ = bf16[6,208,768]{2,1,0:T(8,128)(2,1)S(1)} collective-permute-done((bf16[6,208,768]{2,1,0:T(8,128)(2,1)S(1)}, bf16[6,208,768]{2,1,0:T(8,128)(2,1)S(1)}, u32[]{:S(2)}, u32[]{:S(2)}) %collective-permute-start.1) | collective-permute-done | bytes 1916960 | tf_op jit(solution)/shard_map/ppermute | solution.py:749
  94.9 7.1 %middle_norm.1 = (f32[6,208,768]{2,1,0:T(8,128)}, bf16[6,208,768]{2,1,0:T(8,128)(2,1)}) custom-call(s32[1]{0:T(128)} %constant.451.clone.1.turn_ref, bf16[6,208,768]{2,1,0:T(8,128)(2,1)} %copy-done.14, bf16[6,208,768]{2,1,0:T(8,128)(2,1)} %copy-done.44, bf16[12,208,768]{2,1,0:T(8,128)(2,1)} %get-tuple-element.77.refs_2_.x_ref, f32[1,768]{1,0:T(1,128)} %reshape.230.refs_3_, ...), custom_call_target="tpu_custom_call" | custom-call | flops 8800000000 | tf_op jit(solution)/shard_map/middle_norm/pallas_call | solution.py:411
  107.3 21.6 %gated_spread.1 = (bf16[8,1024,896]{2,1,0:T(8,128)(2,1)}, f32[2496,128]{1,0:T(8,128)}, bf16[2496,128]{1,0:T(8,128)(2,1)}) custom-call(s32[144]{0:T(256)} %pad_add_fusion.1.plan_ref, s32[6,2,416]{2,1,0:T(2,128)} %add_bitcast_fusion.rows_ref, bf16[1248,768]{1,0:T(8,128)(2,1)} %bitcast.117, bf16[1248,768]{1,0:T(8,128)(2,1)} %bitcast.119, s32[2496,2]{1,0:T(8,128)} %bitcast.101, ...), custom_call_target="tpu_custom_call" | custom-call | flops 22000001024 | tf_op jit(solution)/shard_map/gated_spread/pallas_call | solution.py:160
  129.0 38.4 %experts.2 = (bf16[4,1024,768]{2,1,0:T(8,128)(2,1)}, bf16[4,1024,896]{2,1,0:T(8,128)(2,1)}, bf16[4,768,768]{2,1,0:T(8,128)(2,1)}, bf16[4,768,768]{2,1,0:T(8,128)(2,1)}, f32[4,1,768]{2,1,0:T(1,128)}) custom-call(s32[8]{0:T(128)} %and_select_fusion.refs_9_.tiles_ref, bf16[8,1024,896]{2,1,0:T(8,128)(2,1)} %get-tuple-element.79.x_ref, ...), custom_call_target="tpu_custom_call" | custom-call | flops 21743271936 | bytes 46137344 | tf_op jit(solution)/shard_map/experts/pallas_call | solution.py:360
  172.3 34.8 %experts.3 = (bf16[4,1024,768]{2,1,0:T(8,128)(2,1)}, bf16[4,1024,896]{2,1,0:T(8,128)(2,1)}, bf16[4,768,768]{2,1,0:T(8,128)(2,1)}, bf16[4,768,768]{2,1,0:T(8,128)(2,1)}, f32[4,1,768]{2,1,0:T(1,128)}) custom-call(s32[8]{0:T(128)} %and_select_fusion.refs_9_.tiles_ref, bf16[8,1024,896]{2,1,0:T(8,128)(2,1)} %get-tuple-element.79.x_ref, ...), custom_call_target="tpu_custom_call" | custom-call | flops 21743271936 | bytes 46137344 | tf_op jit(solution)/shard_map/experts/pallas_call | solution.py:360
  208.0 3.9 ring_add.8
  211.9 18.5 %collect.2 = (bf16[1248,768]{1,0:T(8,128)(2,1)}, bf16[1248,768]{1,0:T(8,128)(2,1)}, f32[2496,128]{1,0:T(8,128)}) custom-call(s32[144]{0:T(256)} %pad_add_fusion.1.plan_ref, s32[2496,2]{1,0:T(8,128)} %bitcast.107, bf16[4,1024,896]{2,1,0:T(8,128)(2,1)} %get-tuple-element.84.refs_0_, bf16[4,1024,896]{2,1,0:T(8,128)(2,1)} %get-tuple-element.85.refs_1_, ...), custom_call_target="tpu_custom_call" | custom-call | flops 17600000000 | tf_op jit(solution)/shard_map/collect/pallas_call | solution.py:249
  239.0 2.6 fusion.2.refs_6_.refs_2_.refs_0_
  243.1 16.6 %collective-permute-done.6.refs_0_ = bf16[2,4,96,768]{3,2,1,0:T(8,128)(2,1)} collective-permute-done((bf16[2,4,96,768]{3,2,1,0:T(8,128)(2,1)}, bf16[2,4,96,768]{3,2,1,0:T(8,128)(2,1)}, u32[]{:S(2)}, u32[]{:S(2)}) %collective-permute-start.6) | collective-permute-done | bytes 1179680 | tf_op jit(solution)/shard_map/ppermute | solution.py:770
  260.8 4.3 ring_add.9
  267.2 17.7 %collect.3 = (bf16[1248,768]{1,0:T(8,128)(2,1)}, bf16[1248,768]{1,0:T(8,128)(2,1)}) custom-call(s32[144]{0:T(256)} %pad_add_fusion.1.plan_ref, s32[2496,2]{1,0:T(8,128)} %bitcast.108, bf16[4,1024,768]{2,1,0:T(8,128)(2,1)} %get-tuple-element.80.refs_0_, bf16[4,1024,768]{2,1,0:T(8,128)(2,1)} %get-tuple-element.83.refs_1_, bf16[6,208,768]{2,1,0:T(8,128)(2,1)} %copy-done.6, ...), custom_call_target="tpu_custom_call" | custom-call | flops 17600000000 | tf_op jit(solution)/shard_map/collect/pallas_call | solution.py:249
  284.9 7.7 %collective-permute-done.10.refs_1_ = bf16[2,4,96,768]{3,2,1,0:T(8,128)(2,1)S(1)} collective-permute-done((bf16[2,4,96,768]{3,2,1,0:T(8,128)(2,1)}, bf16[2,4,96,768]{3,2,1,0:T(8,128)(2,1)S(1)}, u32[]{:S(2)}, u32[]{:S(2)}) %collective-permute-start.10) | collective-permute-done | bytes 1179680 | tf_op jit(solution)/shard_map/ppermute | solution.py:770
  294.0 4.5 ring_add.10
  306.3 11.2 %middle_back.1 = (f32[6,208,768]{2,1,0:T(8,128)}, bf16[6,208,768]{2,1,0:T(8,128)(2,1)}, f32[2,768]{1,0:T(2,128)}, f32[8,768]{1,0:T(8,128)}, f32[128,768]{1,0:T(8,128)}) custom-call(s32[1]{0:T(128)} %constant.451.clone.1.turn_ref, bf16[6,208,768]{2,1,0:T(8,128)(2,1)} %copy-done.6, bf16[6,208,768]{2,1,0:T(8,128)(2,1)} %collective-permute-done.13.refs_1_, ...), custom_call_target="tpu_custom_call" | custom-call | flops 8800000000 | tf_op jit(solution)/shard_map/middle_back/pallas_call | solution.py:411
  317.5 7.7 %collective-permute-done.11.refs_0_ = bf16[2,4,96,768]{3,2,1,0:T(8,128)(2,1)} collective-permute-done((bf16[2,4,96,768]{3,2,1,0:T(8,128)(2,1)}, bf16[2,4,96,768]{3,2,1,0:T(8,128)(2,1)}, u32[]{:S(2)}, u32[]{:S(2)}) %collective-permute-start.11) | collective-permute-done | bytes 1179680 | tf_op jit(solution)/shard_map/ppermute | solution.py:770
  326.2 4.5 ring_add.11
  333.2 2.2 fusion.1.refs_10_.refs_0_
  339.0 39.9 %attention_backward.1 = (bf16[6,208,768]{2,1,0:T(8,128)(2,1)}, bf16[6,208,768]{2,1,0:T(8,128)(2,1)}, f32[3,768,192]{2,1,0:T(8,128)}, f32[1,768,192]{2,1,0:T(8,128)}, f32[2,192]{1,0:T(2,128)}, /*index=5*/f32[3,768]{1,0:T(4,128)}) custom-call(s32[1]{0:T(128)} %constant.451.clone.1.turn_ref, bf16[6,208,768]{2,1,0:T(8,128)(2,1)} %get-tuple-element.103.refs_0_, ...), custom_call_target="tpu_custom_call" | custom-call | flops 32999999488 | tf_op jit(solution)/shard_map/attention_backward/pallas_call | solution.py:411
  380.9 4.3 ring_add.12
  385.2 4.1 collective-permute-done.20
  389.3 3.4 add_convert_fusion.1.refs_5_.refs_6_
  392.8 6.7 %finish.1 = bf16[6,208,768]{2,1,0:T(8,128)(2,1)} custom-call(s32[1]{0:T(128)} %constant.451.clone.1.turn_ref, bf16[6,208,768]{2,1,0:T(8,128)(2,1)} %copy-done.13, bf16[6,208,768]{2,1,0:T(8,128)(2,1)} %copy-done.15, f32[6,208,768]{2,1,0:T(8,128)} %get-tuple-element.101.refs_9_.refs_2_, bf16[12,208,128]{2,1,0:T(8,128)(2,1)} %bitcast.122, ...), custom_call_target="tpu_custom_call" | custom-call | flops 8800000000 | tf_op jit(solution)/shard_map/finish/pallas_call | solution.py:411
  407.7 2.2 pad_maximum_fusion.1
  414.6 2.4 broadcast_select_fusion.1
  417.0 2.1 pad_maximum_fusion
  419.1 4.2 reshape.226.refs_7_
  423.3 9.9 %collective-permute-done.25.refs_0_ = bf16[2,4,96,768]{3,2,1,0:T(8,128)(2,1)S(1)} collective-permute-done((bf16[2,4,96,768]{3,2,1,0:T(8,128)(2,1)}, bf16[2,4,96,768]{3,2,1,0:T(8,128)(2,1)S(1)}, u32[]{:S(2)}, u32[]{:S(2)}) %collective-permute-start.25) | collective-permute-done | bytes 1179680 | tf_op jit(solution)/shard_map/ppermute | solution.py:770
  434.2 4.3 ring_add.13
  440.6 5.3 collective-permute-done.22
  445.8 2.0 add_convert_fusion.own_ref
  454.2 22.1 %collective-permute-done.29 = f32[31,768]{1,0:T(8,128)S(1)} collective-permute-done((f32[31,768]{1,0:T(8,128)S(1)}, f32[31,768]{1,0:T(8,128)S(1)}, u32[]{:S(2)}, u32[]{:S(2)}) %collective-permute-start.29) | collective-permute-done | bytes 95264 | tf_op jit(solution)/shard_map/ppermute | solution.py:994
  476.4 2.1 collective-permute-start.30
  478.5 4.4 ring_add.14
  487.5 2.9 collective-permute-start.33
  491.6 2.0 collective-permute-start.31
  493.6 15.5 %input_back.1.refs_4_ = f32[2364,768]{1,0:T(8,128)} custom-call(s32[1]{0:T(128)} %bitcast.8.turn_ref, bf16[6,208,768]{2,1,0:T(8,128)(2,1)} %copy-done.12, bf16[6,208,768]{2,1,0:T(8,128)(2,1)} %collective-permute-done.23.other_ref, bf16[12,208,768]{2,1,0:T(8,128)(2,1)} %get-tuple-element.77.refs_2_.x_ref, f32[6,208,768]{2,1,0:T(8,128)} %get-tuple-element.117.own_grad_ref, ...), custom_call_target="tpu_custom_call" | custom-call | flops 16499999744 | tf_op jit(solution)/shard_map/input_back/pallas_call | solution.py:721
  510.7 3.4 ring_add.15
  518.9 3.0 maximum_bitcast_fusion
  526.7 3.5 collective-permute-done.35
  (278 shorter events, 91.2 us)
Async XLA Ops:
  10.0 21.2 %copy-start.30 = (s32[2364,2]{0,1:T(2,128)S(1)}, s32[2364,2]{0,1:T(2,128)}, u32[]{:S(2)}) copy-start(s32[2364,2]{0,1:T(2,128)} %param.30) | copy-start | bytes 56740
  30.6 15.9 %collective-permute-start = (bf16[6,208,768]{2,1,0:T(8,128)(2,1)}, bf16[6,208,768]{2,1,0:T(8,128)(2,1)}, u32[]{:S(2)}, u32[]{:S(2)}) collective-permute-start(bf16[6,208,768]{2,1,0:T(8,128)(2,1)} %get-tuple-element.76), channel_id=1, source_target_pairs={{0,1},{1,0},{2,3},{3,2},{4,5},{5,4},{6,7},{7,6},{8,9},{9,8},{10,11... | collective-permute-start | bytes 5750792 | tf_op jit(solution)/shard_map/ppermute | solution.py:745
  48.7 45.0 %collective-permute-start.1 = (bf16[6,208,768]{2,1,0:T(8,128)(2,1)S(1)}, bf16[6,208,768]{2,1,0:T(8,128)(2,1)S(1)}, u32[]{:S(2)}, u32[]{:S(2)}) collective-permute-start(bf16[6,208,768]{2,1,0:T(8,128)(2,1)S(1)} %add_convert_fusion.2.refs_0_), channel_id=1, source_target_pairs={{0,2},{1,3},{2,0},{3,1},{4,6},{5,7},{6,4},{7,5},{8,10},{9,11},{10,... | collective-permute-start | bytes 5750792 | tf_op jit(solution)/shard_map/ppermute | solution.py:749
  102.0 4.1 collective-permute-start.2
  168.5 38.5 %collective-permute-start.4 = (bf16[1,4,96,768]{3,2,1,0:T(8,128)(2,1)S(1)}, bf16[1,4,96,768]{3,2,1,0:T(8,128)(2,1)S(1)}, u32[]{:S(2)}, u32[]{:S(2)}) collective-permute-start(bf16[1,4,96,768]{3,2,1,0:T(8,128)(2,1)S(1)} %dynamic-slice_bitcast_fusion.refs_1_), channel_id=1, source_target_pairs={{0,4},{8,0},{16,8},{24,16},{28,24},{20,28},{12,20},{4,12},{1,5},{9... | collective-permute-start | bytes 1769480 | tf_op jit(solution)/shard_map/ppermute | solution.py:770
  171.5 35.6 %collective-permute-start.3 = (bf16[1,4,96,768]{3,2,1,0:T(8,128)(2,1)S(1)}, bf16[1,4,96,768]{3,2,1,0:T(8,128)(2,1)S(1)}, u32[]{:S(2)}, u32[]{:S(2)}) collective-permute-start(bf16[1,4,96,768]{3,2,1,0:T(8,128)(2,1)S(1)} %dynamic-slice_bitcast_fusion.1.refs_0_), channel_id=1, source_target_pairs={{0,8},{8,16},{16,24},{24,28},{28,20},{20,12},{12,4},{4,0},{1,9},{9... | collective-permute-start | bytes 1769480 | tf_op jit(solution)/shard_map/ppermute | solution.py:770
  230.4 7.3 %collective-permute-start.5 = (bf16[6,208,768]{2,1,0:T(8,128)(2,1)}, bf16[6,208,768]{2,1,0:T(8,128)(2,1)S(1)}, u32[]{:S(2)}, u32[]{:S(2)}) collective-permute-start(bf16[6,208,768]{2,1,0:T(8,128)(2,1)} %bitcast.118), channel_id=1, source_target_pairs={{0,1},{1,0},{2,3},{3,2},{4,5},{5,4},{6,7},{7,6},{8,9},{9,8},{10,11... | collective-permute-start | bytes 5750792 | tf_op jit(solution)/shard_map/ppermute | solution.py:745
  231.1 28.6 %collective-permute-start.6 = (bf16[2,4,96,768]{3,2,1,0:T(8,128)(2,1)}, bf16[2,4,96,768]{3,2,1,0:T(8,128)(2,1)}, u32[]{:S(2)}, u32[]{:S(2)}) collective-permute-start(bf16[2,4,96,768]{3,2,1,0:T(8,128)(2,1)} %get-tuple-element.88.refs_2_), channel_id=1, source_target_pairs={{0,8},{8,16},{16,24},{24,28},{28,20},{20,12},{12,4},{4,0},{1,9},{9... | collective-permute-start | bytes 3538952 | tf_op jit(solution)/shard_map/ppermute | solution.py:770
  232.5 28.4 %collective-permute-start.7 = (bf16[2,4,96,768]{3,2,1,0:T(8,128)(2,1)}, bf16[2,4,96,768]{3,2,1,0:T(8,128)(2,1)}, u32[]{:S(2)}, u32[]{:S(2)}) collective-permute-start(bf16[2,4,96,768]{3,2,1,0:T(8,128)(2,1)} %get-tuple-element.89.refs_3_), channel_id=1, source_target_pairs={{0,4},{8,0},{16,8},{24,16},{28,24},{20,28},{12,20},{4,12},{1,5},{9... | collective-permute-start | bytes 3538952 | tf_op jit(solution)/shard_map/ppermute | solution.py:770
  236.2 1.3 collective-permute-start.14
  241.5 19.3 %copy-start.6 = (bf16[6,208,768]{2,1,0:T(8,128)(2,1)}, bf16[6,208,768]{2,1,0:T(8,128)(2,1)S(1)}, u32[]{:S(2)}) copy-start(bf16[6,208,768]{2,1,0:T(8,128)(2,1)S(1)} %fusion.2.refs_6_.refs_2_.refs_0_) | copy-start | bytes 5750788
  241.6 64.7 %collective-permute-start.13 = (bf16[6,208,768]{2,1,0:T(8,128)(2,1)S(1)}, bf16[6,208,768]{2,1,0:T(8,128)(2,1)}, u32[]{:S(2)}, u32[]{:S(2)}) collective-permute-start(bf16[6,208,768]{2,1,0:T(8,128)(2,1)S(1)} %fusion.2.refs_6_.refs_2_.refs_0_), channel_id=1, source_target_pairs={{0,2},{1,3},{2,0},{3,1},{4,6},{5,7},{6,4},{7,5},{8,10},{9,11},{10,... | collective-permute-start | bytes 5750792 | tf_op jit(solution)/shard_map/ppermute | solution.py:749
  265.2 27.4 %collective-permute-start.10 = (bf16[2,4,96,768]{3,2,1,0:T(8,128)(2,1)}, bf16[2,4,96,768]{3,2,1,0:T(8,128)(2,1)S(1)}, u32[]{:S(2)}, u32[]{:S(2)}) collective-permute-start(bf16[2,4,96,768]{3,2,1,0:T(8,128)(2,1)} %get-tuple-element.93.refs_4_), channel_id=1, source_target_pairs={{0,4},{8,0},{16,8},{24,16},{28,24},{20,28},{12,20},{4,12},{1,5},{9... | collective-permute-start | bytes 3538952 | tf_op jit(solution)/shard_map/ppermute | solution.py:770
  265.8 27.2 %collective-permute-start.9 = (bf16[2,4,96,768]{3,2,1,0:T(8,128)(2,1)}, bf16[2,4,96,768]{3,2,1,0:T(8,128)(2,1)S(1)}, u32[]{:S(2)}, u32[]{:S(2)}) collective-permute-start(bf16[2,4,96,768]{3,2,1,0:T(8,128)(2,1)} %get-tuple-element.92.refs_3_), channel_id=1, source_target_pairs={{0,8},{8,16},{16,24},{24,28},{28,20},{20,12},{12,4},{4,0},{1,9},{9... | collective-permute-start | bytes 3538952 | tf_op jit(solution)/shard_map/ppermute | solution.py:770
  298.6 26.7 %collective-permute-start.11 = (bf16[2,4,96,768]{3,2,1,0:T(8,128)(2,1)}, bf16[2,4,96,768]{3,2,1,0:T(8,128)(2,1)}, u32[]{:S(2)}, u32[]{:S(2)}) collective-permute-start(bf16[2,4,96,768]{3,2,1,0:T(8,128)(2,1)} %get-tuple-element.96.refs_12_), channel_id=1, source_target_pairs={{0,8},{8,16},{16,24},{24,28},{28,20},{20,12},{12,4},{4,0},{1,9},{9... | collective-permute-start | bytes 3538952 | tf_op jit(solution)/shard_map/ppermute | solution.py:770
  300.0 26.2 %collective-permute-start.12 = (bf16[2,4,96,768]{3,2,1,0:T(8,128)(2,1)}, bf16[2,4,96,768]{3,2,1,0:T(8,128)(2,1)}, u32[]{:S(2)}, u32[]{:S(2)}) collective-permute-start(bf16[2,4,96,768]{3,2,1,0:T(8,128)(2,1)} %get-tuple-element.97.refs_13_), channel_id=1, source_target_pairs={{0,4},{8,0},{16,8},{24,16},{28,24},{20,28},{12,20},{4,12},{1,5},{9... | collective-permute-start | bytes 3538952 | tf_op jit(solution)/shard_map/ppermute | solution.py:770
  301.1 4.0 collective-permute-start.15
  306.3 26.9 %collective-permute-start.8 = (bf16[6,208,768]{2,1,0:T(8,128)(2,1)}, bf16[6,208,768]{2,1,0:T(8,128)(2,1)}, u32[]{:S(2)}, u32[]{:S(2)}) collective-permute-start(bf16[6,208,768]{2,1,0:T(8,128)(2,1)} %bitcast.24), channel_id=1, source_target_pairs={{0,1},{1,0},{2,3},{3,2},{4,5},{5,4},{6,7},{7,6},{8,9},{9,8},{10,11... | collective-permute-start | bytes 5750792 | tf_op jit(solution)/shard_map/ppermute | solution.py:745
  330.7 8.3 %collective-permute-start.19 = (bf16[6,208,768]{2,1,0:T(8,128)(2,1)}, bf16[6,208,768]{2,1,0:T(8,128)(2,1)}, u32[]{:S(2)}, u32[]{:S(2)}) collective-permute-start(bf16[6,208,768]{2,1,0:T(8,128)(2,1)} %get-tuple-element.103.refs_0_), channel_id=1, source_target_pairs={{0,1},{1,0},{2,3},{3,2},{4,5},{5,4},{6,7},{7,6},{8,9},{9,8},{10,11... | collective-permute-start | bytes 5750792 | tf_op jit(solution)/shard_map/ppermute | solution.py:745
  335.4 44.2 %collective-permute-start.16 = (bf16[6,208,768]{2,1,0:T(8,128)(2,1)S(1)}, bf16[6,208,768]{2,1,0:T(8,128)(2,1)S(1)}, u32[]{:S(2)}, u32[]{:S(2)}) collective-permute-start(bf16[6,208,768]{2,1,0:T(8,128)(2,1)S(1)} %fusion.1.refs_10_.refs_0_), channel_id=1, source_target_pairs={{0,2},{1,3},{2,0},{3,1},{4,6},{5,7},{6,4},{7,5},{8,10},{9,11},{10,... | collective-permute-start | bytes 5750792 | tf_op jit(solution)/shard_map/ppermute | solution.py:749
  337.0 41.9 %collective-permute-start.17 = (bf16[2,4,96,768]{3,2,1,0:T(8,128)(2,1)}, bf16[2,4,96,768]{3,2,1,0:T(8,128)(2,1)S(1)}, u32[]{:S(2)}, u32[]{:S(2)}) collective-permute-start(bf16[2,4,96,768]{3,2,1,0:T(8,128)(2,1)} %get-tuple-element.104.refs_11_), channel_id=1, source_target_pairs={{0,8},{8,16},{16,24},{24,28},{28,20},{20,12},{12,4},{4,0},{1,9},{9... | collective-permute-start | bytes 3538952 | tf_op jit(solution)/shard_map/ppermute | solution.py:770
  338.1 40.7 %collective-permute-start.18 = (bf16[2,4,96,768]{3,2,1,0:T(8,128)(2,1)S(1)}, bf16[2,4,96,768]{3,2,1,0:T(8,128)(2,1)S(1)}, u32[]{:S(2)}, u32[]{:S(2)}) collective-permute-start(bf16[2,4,96,768]{3,2,1,0:T(8,128)(2,1)S(1)} %copy-done.45), channel_id=1, source_target_pairs={{0,4},{8,0},{16,8},{24,16},{28,24},{20,28},{12,20},{4,12},{1,5},{9... | collective-permute-start | bytes 3538952 | tf_op jit(solution)/shard_map/ppermute | solution.py:770
  385.2 4.1 collective-permute-start.20
  392.8 8.7 %copy-start.32 = (f32[4,1,768]{2,1,0:T(1,128)S(1)}, f32[4,1,768]{2,1,0:T(1,128)}, u32[]{:S(2)}) copy-start(f32[4,1,768]{2,1,0:T(1,128)} %get-tuple-element.127) | copy-start | bytes 36868
  392.8 9.1 %copy-start.1 = (bf16[6,208,768]{2,1,0:T(8,128)(2,1)S(1)}, bf16[6,208,768]{2,1,0:T(8,128)(2,1)}, u32[]{:S(2)}) copy-start(bf16[6,208,768]{2,1,0:T(8,128)(2,1)} %add_convert_fusion.1.refs_5_.refs_6_) | copy-start | bytes 5750788
  392.8 13.6 %copy-start.29 = (f32[8,768]{1,0:T(8,128)S(1)}, f32[8,768]{1,0:T(8,128)}, u32[]{:S(2)}) copy-start(f32[8,768]{1,0:T(8,128)} %get-tuple-element.124) | copy-start | bytes 73732
  392.8 13.6 %copy-start.36 = (f32[2,768]{1,0:T(2,128)S(1)}, f32[2,768]{1,0:T(2,128)}, u32[]{:S(2)}) copy-start(f32[2,768]{1,0:T(2,128)} %get-tuple-element.123) | copy-start | bytes 18436
  392.8 13.6 %copy-start.35 = (f32[3,768]{1,0:T(4,128)S(1)}, f32[3,768]{1,0:T(4,128)}, u32[]{:S(2)}) copy-start(f32[3,768]{1,0:T(4,128)} %get-tuple-element.122) | copy-start | bytes 27652
  399.5 14.1 %collective-permute-start.21 = (bf16[6,208,768]{2,1,0:T(8,128)(2,1)}, bf16[6,208,768]{2,1,0:T(8,128)(2,1)}, u32[]{:S(2)}, u32[]{:S(2)}) collective-permute-start(bf16[6,208,768]{2,1,0:T(8,128)(2,1)} %finish.1), channel_id=1, source_target_pairs={{0,1},{1,0},{2,3},{3,2},{4,5},{5,4},{6,7},{7,6},{8,9},{9,8},{10,11... | collective-permute-start | bytes 5750792 | tf_op jit(solution)/shard_map/ppermute | solution.py:745
  401.5 90.1 %collective-permute-start.24 = (f32[6,208,768]{2,1,0:T(8,128)}, f32[6,208,768]{2,1,0:T(8,128)}, u32[]{:S(2)}, u32[]{:S(2)}) collective-permute-start(f32[6,208,768]{2,1,0:T(8,128)} %get-tuple-element.117.own_grad_ref), channel_id=1, source_target_pairs={{0,1},{1,0},{2,3},{3,2},{4,5},{5,4},{6,7},{7,6},{8,9},{9,8},{10,11... | collective-permute-start | bytes 11501576 | tf_op jit(solution)/shard_map/ppermute | solution.py:745
  401.9 43.9 %collective-permute-start.22 = (bf16[6,208,768]{2,1,0:T(8,128)(2,1)S(1)}, bf16[6,208,768]{2,1,0:T(8,128)(2,1)}, u32[]{:S(2)}, u32[]{:S(2)}) collective-permute-start(bf16[6,208,768]{2,1,0:T(8,128)(2,1)S(1)} %copy-done.1), channel_id=1, source_target_pairs={{0,2},{1,3},{2,0},{3,1},{4,6},{5,7},{6,4},{7,5},{8,10},{9,11},{10,... | collective-permute-start | bytes 5750792 | tf_op jit(solution)/shard_map/ppermute | solution.py:749
  404.1 29.1 %collective-permute-start.25 = (bf16[2,4,96,768]{3,2,1,0:T(8,128)(2,1)}, bf16[2,4,96,768]{3,2,1,0:T(8,128)(2,1)S(1)}, u32[]{:S(2)}, u32[]{:S(2)}) collective-permute-start(bf16[2,4,96,768]{3,2,1,0:T(8,128)(2,1)} %get-tuple-element.115.refs_6_), channel_id=1, source_target_pairs={{0,8},{8,16},{16,24},{24,28},{28,20},{20,12},{12,4},{4,0},{1,9},{9... | collective-permute-start | bytes 3538952 | tf_op jit(solution)/shard_map/ppermute | solution.py:770
  405.3 28.0 %collective-permute-start.26 = (bf16[2,4,96,768]{3,2,1,0:T(8,128)(2,1)}, bf16[2,4,96,768]{3,2,1,0:T(8,128)(2,1)}, u32[]{:S(2)}, u32[]{:S(2)}) collective-permute-start(bf16[2,4,96,768]{3,2,1,0:T(8,128)(2,1)} %get-tuple-element.116.refs_7_), channel_id=1, source_target_pairs={{0,4},{8,0},{16,8},{24,16},{28,24},{20,28},{12,20},{4,12},{1,5},{9... | collective-permute-start | bytes 3538952 | tf_op jit(solution)/shard_map/ppermute | solution.py:770
  413.6 38.1 %collective-permute-start.36 = (bf16[4,2,2,1,96,192]{5,4,0,3,2,1:T(8,128)(2,1)}, bf16[4,2,2,1,96,192]{5,4,0,3,2,1:T(8,128)(2,1)}, u32[]{:S(2)}, u32[]{:S(2)}) collective-permute-start(bf16[4,2,2,1,96,192]{5,4,0,3,2,1:T(8,128)(2,1)} %copy.127), channel_id=1, source_target_pairs={{0,4},{4,0},{8,12},{12,8},{16,20},{20,16},{24,28},{28,24},{1,5},{5... | collective-permute-start | bytes 1769480 | tf_op jit(solution)/shard_map/ppermute | solution.py:963
  423.3 22.5 %copy-start.2 = (bf16[6,208,768]{2,1,0:T(8,128)(2,1)S(1)}, bf16[6,208,768]{2,1,0:T(8,128)(2,1)}, u32[]{:S(2)}) copy-start(bf16[6,208,768]{2,1,0:T(8,128)(2,1)} %add_convert_fusion.1.refs_5_.refs_6_) | copy-start | bytes 5750788
  438.5 37.8 %collective-permute-start.27 = (bf16[2,4,96,768]{3,2,1,0:T(8,128)(2,1)}, bf16[2,4,96,768]{3,2,1,0:T(8,128)(2,1)S(1)}, u32[]{:S(2)}, u32[]{:S(2)}) collective-permute-start(bf16[2,4,96,768]{3,2,1,0:T(8,128)(2,1)} %get-tuple-element.118), channel_id=1, source_target_pairs={{0,8},{8,16},{16,24},{24,28},{28,20},{20,12},{12,4},{4,0},{1,9},{9... | collective-permute-start | bytes 3538952 | tf_op jit(solution)/shard_map/ppermute | solution.py:770
  438.7 14.1 %copy-start.5 = (f32[4,768,192]{2,1,0:T(8,128)S(1)}, f32[4,768,192]{2,1,0:T(8,128)}, u32[]{:S(2)}) copy-start(f32[4,768,192]{2,1,0:T(8,128)} %copy-done.4) | copy-start | bytes 7077892
  438.7 39.8 %collective-permute-start.28 = (bf16[2,4,96,768]{3,2,1,0:T(8,128)(2,1)}, bf16[2,4,96,768]{3,2,1,0:T(8,128)(2,1)}, u32[]{:S(2)}, u32[]{:S(2)}) collective-permute-start(bf16[2,4,96,768]{3,2,1,0:T(8,128)(2,1)} %get-tuple-element.119), channel_id=1, source_target_pairs={{0,4},{8,0},{16,8},{24,16},{28,24},{20,28},{12,20},{4,12},{1,5},{9... | collective-permute-start | bytes 3538952 | tf_op jit(solution)/shard_map/ppermute | solution.py:770
  447.9 45.7 %collective-permute-start.23 = (bf16[6,208,768]{2,1,0:T(8,128)(2,1)S(1)}, bf16[6,208,768]{2,1,0:T(8,128)(2,1)}, u32[]{:S(2)}, u32[]{:S(2)}) collective-permute-start(bf16[6,208,768]{2,1,0:T(8,128)(2,1)S(1)} %add_convert_fusion.own_ref), channel_id=1, source_target_pairs={{0,1},{1,0},{2,3},{3,2},{4,5},{5,4},{6,7},{7,6},{8,9},{9,8},{10,11... | collective-permute-start | bytes 5750792 | tf_op jit(solution)/shard_map/ppermute | solution.py:745
  451.7 24.6 %collective-permute-start.29 = (f32[31,768]{1,0:T(8,128)S(1)}, f32[31,768]{1,0:T(8,128)S(1)}, u32[]{:S(2)}, u32[]{:S(2)}) collective-permute-start(f32[31,768]{1,0:T(8,128)S(1)} %broadcast_add_fusion), channel_id=1, source_target_pairs={{0,4},{4,0},{8,12},{12,8},{16,20},{20,16},{24,28},{28,24},{1,5},{5... | collective-permute-start | bytes 285704 | tf_op jit(solution)/shard_map/ppermute | solution.py:994
  476.3 11.2 %collective-permute-start.37 = (bf16[4,2,1,1,96,192]{5,4,0,3,2,1:T(8,128)(2,1)S(1)}, bf16[4,2,1,1,96,192]{5,4,0,3,2,1:T(8,128)(2,1)S(1)}, u32[]{:S(2)}, u32[]{:S(2)}) collective-permute-start(bf16[4,2,1,1,96,192]{5,4,0,3,2,1:T(8,128)(2,1)S(1)} %dynamic-slice_convert_fusion), channel_id=1, source_target_pairs={{0,8},{4,12},{8,0},{12,4},{16,24},{20,28},{24,16},{28,20},{1,9},{5... | collective-permute-start | bytes 884744 | tf_op jit(solution)/shard_map/ppermute | solution.py:963
  476.4 14.1 %collective-permute-start.30 = (f32[31,768]{1,0:T(8,128)S(1)}, f32[31,768]{1,0:T(8,128)S(1)}, u32[]{:S(2)}, u32[]{:S(2)}) collective-permute-start(f32[31,768]{1,0:T(8,128)S(1)} %add_add_fusion.4), channel_id=1, source_target_pairs={{0,8},{4,12},{8,0},{12,4},{16,24},{20,28},{24,16},{28,20},{1,9},{5... | collective-permute-start | bytes 285704 | tf_op jit(solution)/shard_map/ppermute | solution.py:994
  482.9 26.2 %collective-permute-start.32 = (bf16[1,4,96,768]{3,2,1,0:T(8,128)(2,1)}, bf16[1,4,96,768]{3,2,1,0:T(8,128)(2,1)S(1)}, u32[]{:S(2)}, u32[]{:S(2)}) collective-permute-start(bf16[1,4,96,768]{3,2,1,0:T(8,128)(2,1)} %get-tuple-element.120.refs_0_), channel_id=1, source_target_pairs={{0,8},{8,16},{16,24},{24,28},{28,20},{20,12},{12,4},{4,0},{1,9},{9... | collective-permute-start | bytes 1769480 | tf_op jit(solution)/shard_map/ppermute | solution.py:770
  487.5 21.6 %collective-permute-start.33 = (bf16[1,4,96,768]{3,2,1,0:T(8,128)(2,1)}, bf16[1,4,96,768]{3,2,1,0:T(8,128)(2,1)S(1)}, u32[]{:S(2)}, u32[]{:S(2)}) collective-permute-start(bf16[1,4,96,768]{3,2,1,0:T(8,128)(2,1)} %get-tuple-element.121.refs_1_), channel_id=1, source_target_pairs={{0,4},{8,0},{16,8},{24,16},{28,24},{20,28},{12,20},{4,12},{1,5},{9... | collective-permute-start | bytes 1769480 | tf_op jit(solution)/shard_map/ppermute | solution.py:770
  490.5 25.6 %collective-permute-start.38 = (bf16[4,1,1,1,96,192]{5,4,0,3,2,1:T(8,128)(2,1)S(1)}, bf16[4,1,1,1,96,192]{5,4,0,3,2,1:T(8,128)(2,1)S(1)}, u32[]{:S(2)}, u32[]{:S(2)}) collective-permute-start(bf16[4,1,1,1,96,192]{5,4,0,3,2,1:T(8,128)(2,1)S(1)} %dynamic-slice_convert_fusion.1), channel_id=1, source_target_pairs={{0,16},{4,20},{8,24},{12,28},{16,0},{20,4},{24,8},{28,12},{1,17},{... | collective-permute-start | bytes 442376 | tf_op jit(solution)/shard_map/ppermute | solution.py:963
  491.6 27.1 %collective-permute-start.31 = (f32[31,768]{1,0:T(8,128)S(1)}, f32[31,768]{1,0:T(8,128)S(1)}, u32[]{:S(2)}, u32[]{:S(2)}) collective-permute-start(f32[31,768]{1,0:T(8,128)S(1)} %add_add_fusion.3), channel_id=1, source_target_pairs={{0,16},{4,20},{8,24},{12,28},{16,0},{20,4},{24,8},{28,12},{1,17},{... | collective-permute-start | bytes 285704 | tf_op jit(solution)/shard_map/ppermute | solution.py:994
  518.8 6.7 %collective-permute-start.34 = (f32[20,768]{1,0:T(8,128)S(1)}, f32[20,768]{1,0:T(8,128)S(1)}, u32[]{:S(2)}, u32[]{:S(2)}) collective-permute-start(f32[20,768]{1,0:T(8,128)S(1)} %slice.173), channel_id=1, source_target_pairs={{0,1},{1,0},{2,3},{3,2},{4,5},{5,4},{6,7},{7,6},{8,9},{9,8},{10,11... | collective-permute-start | bytes 184328 | tf_op jit(solution)/shard_map/ppermute | solution.py:957
  525.5 4.7 collective-permute-start.35
  (41 other events, 138.6 us)

commit v8 on v7

--- a/solution.py
+++ b/solution.py
@@ -17,7 +17,6 @@
 
 ROWS = 208
 PAIR = 2
-TRIO = 3
 BLOCK = 416
 GROUPS = 2
 LOCAL = 960
@@ -458,7 +457,7 @@
 def attention_forward(x, turn, gain, shift, weight, bias, out_weight):
     images, seq, width = x.shape
     rows, inner = ROWS, weight.shape[2]
-    blocks = images // TRIO
+    blocks = images // PAIR
 
     def kernel(
         turn_ref, x_ref, gain_ref, shift_ref, w_ref, b_ref, wo_ref,
@@ -466,16 +465,16 @@
     ):
         own_ref, other_ref, pad_ref, n_ref, q_ref, k_ref, v_ref, o_ref, held = refs
         held[...] = jnp.zeros_like(held)
-        for i in range(TRIO):
+        for i in range(PAIR):
             held[i, :seq, :] = x_ref[i].astype(jnp.float32)
-        value = held[...].reshape(TRIO * rows, width)
-        pad_ref[...] = value.astype(jnp.bfloat16).reshape(TRIO, rows, width)
+        value = held[...].reshape(PAIR * rows, width)
+        pad_ref[...] = value.astype(jnp.bfloat16).reshape(PAIR, rows, width)
         n = (normal(value)[0] * gain_ref[...] + shift_ref[...]).astype(jnp.bfloat16)
-        n_ref[...] = n.reshape(TRIO, rows, width)
+        n_ref[...] = n.reshape(PAIR, rows, width)
         for j, ref in enumerate((q_ref, k_ref, v_ref)):
             made = jnp.dot(n, w_ref[j], preferred_element_type=jnp.float32) + b_ref[j : j + 1, :]
-            ref[...] = made.astype(jnp.bfloat16).reshape(TRIO, rows, inner)
-        for i in range(TRIO):
+            ref[...] = made.astype(jnp.bfloat16).reshape(PAIR, rows, inner)
+        for i in range(PAIR):
             q, k, v = q_ref[i], k_ref[i], v_ref[i]
             mixed = jnp.zeros((rows, inner), jnp.float32)
             for mask in head_masks(inner):
@@ -483,9 +482,9 @@
                 head = jnp.dot(probs, v, preferred_element_type=jnp.float32)
                 mixed = jnp.where(mask, head, mixed)
             o_ref[i] = mixed.astype(jnp.bfloat16)
-        mixed = o_ref[...].reshape(TRIO * rows, inner)
+        mixed = o_ref[...].reshape(PAIR * rows, inner)
         part = jnp.dot(mixed, wo_ref[...], preferred_element_type=jnp.float32)
-        part = part.astype(jnp.bfloat16).reshape(TRIO, rows, width)
+        part = part.astype(jnp.bfloat16).reshape(PAIR, rows, width)
 
         @pl.when(pl.program_id(0) < blocks // 2)
         def _():
@@ -512,20 +511,20 @@
             grid=(blocks,),
             in_specs=[
                 pl.BlockSpec(
-                    (TRIO, seq, width), lambda i, turn: ((i + blocks // 2 + turn[0]) % blocks, 0, 0)
+                    (PAIR, seq, width), lambda i, turn: ((i + blocks // 2 + turn[0]) % blocks, 0, 0)
                 )
             ]
             + [whole(array) for array in small],
             out_specs=[
                 pl.BlockSpec(
-                    (TRIO, rows, width), lambda i, turn: (jnp.maximum(i - blocks // 2, 0), 0, 0)
+                    (PAIR, rows, width), lambda i, turn: (jnp.maximum(i - blocks // 2, 0), 0, 0)
                 ),
                 pl.BlockSpec(
-                    (TRIO, rows, width), lambda i, turn: (jnp.minimum(i, blocks // 2 - 1), 0, 0)
+                    (PAIR, rows, width), lambda i, turn: (jnp.minimum(i, blocks // 2 - 1), 0, 0)
                 ),
             ]
-            + [pl.BlockSpec((TRIO, *a.shape[1:]), place) for a in [wide] * 2 + [slim] * 4],
-            scratch_shapes=[pltpu.VMEM((TRIO, rows, width), jnp.float32)],
+            + [pl.BlockSpec((PAIR, *a.shape[1:]), place) for a in [wide] * 2 + [slim] * 4],
+            scratch_shapes=[pltpu.VMEM((PAIR, rows, width), jnp.float32)],
         ),
         out_shape=[shape_of((images // 2, rows, width), jnp.bfloat16)] * 2 + [wide] * 2 + [slim] * 4,
         compiler_params=pltpu.CompilerParams(vmem_limit_bytes=VMEM),
@@ -868,14 +867,15 @@
     bias_rows = jnp.stack([qv_bias[0], jnp.zeros_like(qv_bias[0]), qv_bias[1]]).astype(f32)
     images_in = embedded.reshape(images, SEQ, width)
     own, other, x, normed, queries, keys, values, mixed = attention_forward(
-        images_in, turn // TRIO, row(attn_gain), row(attn_shift), qkv_weight, bias_rows, out_weight
+        images_in, turn // PAIR, row(attn_gain), row(attn_shift), qkv_weight, bias_rows, out_weight
     )
     near = core_sum(own, other, 0.0)
     far = across(near)
 
-    chosen = own_first(routes, -1).reshape(images * ROWS, 2)
+    near_zero = zero_of(near)
+    chosen = own_first(routes + near_zero.astype(jnp.int32), -1).reshape(images * ROWS, 2)
     rows, columns, plan, tiles = route_plan(chosen, expert_count)
-    upstream = own_first(cotangent, 0)
+    upstream = own_first(cotangent, 0) + near_zero.astype(jnp.bfloat16)
     grad_buffers = spread(upstream.reshape(images * ROWS, width), rows, plan, expert_count)
 
     extra = 128
@@ -925,13 +925,14 @@
 
     moving = round_trip(1, [low, low])
     own, other, dots = collect((back_first, back_second), columns, plan, width, tuple(moving))
-    back_near = core_sum(imaged(own), imaged(other), 0.0)
+    sent = to_core(imaged(other))
+    *moving, own = round_trip(2, [low, low], (), (own,))
+    back_near = (imaged(own).astype(f32) + sent.astype(f32)).astype(low)
     back_far = across(back_near)
-    dots = dots[:, : 2 * expert_count].T
+    dots = dots[:, : 2 * expert_count].T + zero_of(back_near)
     dots = dots[:expert_count] + dots[expert_count:]
     dots = dots[:, :own_rows] + to_core(dots[:, own_rows:])
     dots = (dots + across(dots)).T.reshape(half, ROWS, expert_count)
-    moving = round_trip(2, [low, low], (back_near,))
     own_y, other_y = collect((y_first, y_second), columns, plan, width, (back_near, *moving))
     moving = round_trip(3, [low, low], (other_y,))
     middle_grad, own_da, moe_sums, router_sums, bias_sums = middle_back(
@@ -962,8 +963,10 @@
         give = lax.dynamic_index_in_dim(values, 1 - mine, axis, keepdims=True).astype(low)
         return keep, lax.ppermute(give, "dp", pairs(8, 1 << bit))
 
-    own_out = finish(y_near, y_far, middle, mix_pair, bias_twice, (last_near, *moving))
-    layer_out = in_order(own_out, to_core(own_out))
+    def output():
+        own_out = finish(y_near, y_far, middle, mix_pair, bias_twice, tuple(moving))
+        return in_order(own_out, to_core(own_out))
+
     router_bias = [router_sums, bias_sums[:expert_count] + bias_sums[expert_count : 2 * expert_count]]
     packed = jnp.concatenate(
         [
@@ -990,20 +993,22 @@
         slim = slim.reshape(4, 2, 2, 2, width // 8, head_width)
         packed = after_round(packed)
         for step, bit, axis in ((6, 0, 3), (7, 1, 2), (8, 2, 1)):
-            keep, got = halve(after_round(slim) if step > 6 else slim, bit, axis)
+            keep, got = halve(after_round(slim), bit, axis)
             sent = lax.ppermute(packed, "dp", pairs(8, 1 << bit))
             if step == 6:
-                moving = round_trip(6, [low, low], (last_near, layer_out))
+                moving = round_trip(6, [low, low], (last_near, sent, got))
+                layer_out = output()
             elif step == 7:
-                up_first, down_first, *moving = round_trip(7, [f32, low])
+                up_first, down_first, *moving = round_trip(7, [f32, low], (layer_out, sent, got))
                 grad_embedded = input_grad()
             else:
-                moving = round_trip(8, [f32], (grad_embedded,))
+                moving = round_trip(8, [f32], (grad_embedded, sent, got))
             slim = keep.astype(f32) + got.astype(f32) + zero_of(moving[0])
             packed = after_round(packed + sent)
         up_second, down_second = moving
         slim = slim.reshape(4, width // 8, head_width)
     else:
+        layer_out = output()
         grad_embedded = input_grad()
         packed = lax.psum(packed, "dp")
         slim = lax.psum_scatter(slim, "dp", scatter_dimension=1, tiled=True)

time: 542 us -> 567 us (1.046)
  waiting for transfers between devices: 107 us -> 125 us
  other arithmetic: 38.5 us -> 44.8 us
    ppermute x5, waiting for transfers between devices: 31.1 us -> 53.2 us  [across(): return lax.ppermute(value, 'tensor', pairs(lax.axis_size('tensor'), 2))]
    ppermute x16, waiting for transfers between devices: 44.4 us -> 26.1 us  [ring_hop(): return lax.ppermute(value, 'dp', path)]
    ppermute x3, waiting for transfers between devices: 22.1 us -> 40.2 us  [on_device(): sent = lax.ppermute(packed, 'dp', pairs(8, 1 << bit))]
    unnamed x107 -> x100, local copies, waits for them, and re-layouts: 18 us -> 12.7 us
    slice x8 -> x10, local copies, waits for them, and re-layouts: 9.66 us -> 11.3 us  [zero_of(): return value[(0,) * value.ndim].astype(jnp.float32) * 0.0]
  transfers between devices with their start and end apart: 39 -> 39, of which waited for: 17 -> 14; matrix products, arithmetic and copies ran while one was open for 13% -> 14% of each run, Pallas kernels for 30% -> 30%
where the time goes in v8:
time: 567 us; the launch traced here: 558 us
  Pallas kernels  281 us (50%)
  waiting for transfers between devices  125 us (22%)
  local copies, waits for them, and re-layouts  61.3 us (11%)
  other arithmetic  44.8 us (8%)
  starting transfers between devices  35.5 us (6%)
  between operations  8.62 us (2%)
    pallas_call x2, Pallas kernels, expert_pass(): pl.pallas_call(kernel, grid_spec=pltpu.PrefetchScalarGridSpec(num_scalar_...  73.2 us
    pallas_call x4, Pallas kernels, call(): pl.pallas_call(body, grid_spec=pltpu.PrefetchScalarGridSpec(num_scalar_pr...  64.3 us
    ppermute x5, waiting for transfers between devices, across(): return lax.ppermute(value, 'tensor', pairs(lax.axis_size('tensor'), 2))  53.2 us
    ppermute x3, waiting for transfers between devices, on_device(): sent = lax.ppermute(packed, 'dp', pairs(8, 1 << bit))  40.2 us
    pallas_call x2, Pallas kernels, collect(): pl.pallas_call(kernel, grid_spec=pltpu.PrefetchScalarGridSpec(num_scalar_...  36.2 us
    pallas_call x8, Pallas kernels, ring_add(): pl.pallas_call(kernel, grid_spec=pltpu.PrefetchScalarGridSpec(num_scalar_...  33.8 us
    ppermute x16, waiting for transfers between devices, ring_hop(): return lax.ppermute(value, 'dp', path)  26.1 us
    pallas_call x1, Pallas kernels, gated_spread(): pl.pallas_call(kernel, grid_spec=pltpu.PrefetchScalarGridSpec(num_scalar_...  22.1 us
  transfers between devices with their start and end apart: 39, of which 14 were waited for; matrix products, arithmetic and copies ran while one was open for 14% of the time, Pallas kernels for 30%

profile of v8, /device:TPU:0, one launch (start us, length us, event | category | flops | bytes accessed | tf_op | source)
XLA Modules:
  0.0 558.0 jit_solution(8649340323012074863)
XLA Ops:
  1.4 2.3 copy.90.w_ref.refs_8_
  4.4 4.3 reshape.222.x_ref
  9.9 20.2 %attention_forward.1 = (bf16[6,208,768]{2,1,0:T(8,128)(2,1)}, bf16[6,208,768]{2,1,0:T(8,128)(2,1)}, bf16[12,208,768]{2,1,0:T(8,128)(2,1)}, bf16[12,208,768]{2,1,...) custom-call(s32[1]{0:T(128)S(6)} %select_n.435.turn_ref, ...), custom_call_target="tpu_custom_call" | custom-call | flops 19800000512 | tf_op jit(solution)/shard_map/attention_forward/pallas_call | solution.py:507
  30.6 4.3 reshape.229
  38.4 4.4 pad_slice_fusion.1
  48.3 2.5 collective-permute-start.1
  52.4 1.8 convolution_convert_fusion
  57.7 4.6 fusion.refs_10_
  62.4 15.4 %spread.1.refs_6_.g_ref = bf16[8,1024,768]{2,1,0:T(8,128)(2,1)} custom-call(s32[144]{0:T(256)} %pad_add_fusion.1.plan_ref, s32[6,2,416]{2,1,0:T(2,128)} %add_bitcast_fusion.1.rows_ref, bf16[2496,768]{1,0:T(8,128)(2,1)} %bitcast.108), custom_call_target="tpu_custom_call" | custom-call | flops 16499999744 | tf_op jit(solution)/shard_map/spread/pallas_call | solution.py:90
  77.8 15.8 %collective-permute-done.1.refs_1_ = bf16[6,208,768]{2,1,0:T(8,128)(2,1)} collective-permute-done((bf16[6,208,768]{2,1,0:T(8,128)(2,1)}, bf16[6,208,768]{2,1,0:T(8,128)(2,1)}, u32[]{:S(2)}, u32[]{:S(2)}) %collective-permute-start.1) | collective-permute-done | bytes 1916960 | tf_op jit(solution)/shard_map/ppermute | solution.py:748
  93.6 6.6 %middle_norm.1 = (f32[6,208,768]{2,1,0:T(8,128)}, bf16[6,208,768]{2,1,0:T(8,128)(2,1)}) custom-call(s32[1]{0:T(128)} %constant.460.clone.1.turn_ref, bf16[6,208,768]{2,1,0:T(8,128)(2,1)} %copy-done.6, bf16[6,208,768]{2,1,0:T(8,128)(2,1)} %collective-permute-done.1.refs_1_, bf16[12,208,768]{2,1,0:T(8,128)(2,1)} %get-tuple-element.78.refs_2_.x_ref, ...), custom_call_target="tpu_custom_call" | custom-call | flops 8800000000 | tf_op jit(solution)/shard_map/middle_norm/pallas_call | solution.py:410
  104.4 22.1 %gated_spread.1 = (bf16[8,1024,896]{2,1,0:T(8,128)(2,1)}, f32[2496,128]{1,0:T(8,128)}, bf16[2496,128]{1,0:T(8,128)(2,1)}) custom-call(s32[144]{0:T(256)} %pad_add_fusion.1.plan_ref, s32[6,2,416]{2,1,0:T(2,128)} %add_bitcast_fusion.1.rows_ref, bf16[1248,768]{1,0:T(8,128)(2,1)} %bitcast.121, bf16[1248,768]{1,0:T(8,128)(2,1)} %bitcast.13.other_ref, ...), custom_call_target="tpu_custom_call" | custom-call | flops 22000001024 | tf_op jit(solution)/shard_map/gated_spread/pallas_call | solution.py:159
  126.5 32.3 %experts.2 = (bf16[4,1024,768]{2,1,0:T(8,128)(2,1)}, bf16[4,1024,896]{2,1,0:T(8,128)(2,1)}, bf16[4,768,768]{2,1,0:T(8,128)(2,1)}, bf16[4,768,768]{2,1,0:T(8,128)(2,1)}, f32[4,1,768]{2,1,0:T(1,128)}) custom-call(s32[8]{0:T(128)} %and_select_fusion.refs_9_.tiles_ref, bf16[8,1024,896]{2,1,0:T(8,128)(2,1)} %get-tuple-element.80.x_ref, ...), custom_call_target="tpu_custom_call" | custom-call | flops 21743271936 | bytes 46137344 | tf_op jit(solution)/shard_map/experts/pallas_call | solution.py:359
  159.9 3.4 collective-permute-start.4
  165.3 40.9 %experts.3 = (bf16[4,1024,768]{2,1,0:T(8,128)(2,1)}, bf16[4,1024,896]{2,1,0:T(8,128)(2,1)}, bf16[4,768,768]{2,1,0:T(8,128)(2,1)}, bf16[4,768,768]{2,1,0:T(8,128)(2,1)}, f32[4,1,768]{2,1,0:T(1,128)}) custom-call(s32[8]{0:T(128)} %and_select_fusion.refs_9_.tiles_ref, bf16[8,1024,896]{2,1,0:T(8,128)(2,1)} %get-tuple-element.80.x_ref, ...), custom_call_target="tpu_custom_call" | custom-call | flops 21743271936 | bytes 46137344 | tf_op jit(solution)/shard_map/experts/pallas_call | solution.py:359
  207.2 3.8 ring_add.8
  211.0 18.5 %collect.2 = (bf16[1248,768]{1,0:T(8,128)(2,1)}, bf16[1248,768]{1,0:T(8,128)(2,1)}, f32[2496,128]{1,0:T(8,128)}) custom-call(s32[144]{0:T(256)} %pad_add_fusion.1.plan_ref, s32[2496,2]{1,0:T(8,128)} %bitcast.111, bf16[4,1024,896]{2,1,0:T(8,128)(2,1)} %get-tuple-element.89.refs_0_, bf16[4,1024,896]{2,1,0:T(8,128)(2,1)} %get-tuple-element.90.refs_1_, ...), custom_call_target="tpu_custom_call" | custom-call | flops 17600000000 | tf_op jit(solution)/shard_map/collect/pallas_call | solution.py:248
  229.6 2.0 collective-permute-start.6
  232.8 25.3 %collective-permute-done.5.refs_0_ = bf16[2,4,96,768]{3,2,1,0:T(8,128)(2,1)S(1)} collective-permute-done((bf16[2,4,96,768]{3,2,1,0:T(8,128)(2,1)}, bf16[2,4,96,768]{3,2,1,0:T(8,128)(2,1)S(1)}, u32[]{:S(2)}, u32[]{:S(2)}) %collective-permute-start.5) | collective-permute-done | bytes 1179680 | tf_op jit(solution)/shard_map/ppermute | solution.py:769
  259.2 4.3 ring_add.9
  265.5 3.4 fusion.3.refs_2_.refs_0_
  273.0 17.7 %collect.3 = (bf16[1248,768]{1,0:T(8,128)(2,1)}, bf16[1248,768]{1,0:T(8,128)(2,1)}) custom-call(s32[144]{0:T(256)} %pad_add_fusion.1.plan_ref, s32[2496,2]{1,0:T(8,128)} %bitcast.112, bf16[4,1024,768]{2,1,0:T(8,128)(2,1)} %get-tuple-element.81.refs_0_, bf16[4,1024,768]{2,1,0:T(8,128)(2,1)} %get-tuple-element.84.refs_1_, ...), custom_call_target="tpu_custom_call" | custom-call | flops 17600000000 | tf_op jit(solution)/shard_map/collect/pallas_call | solution.py:248
  291.6 4.4 ring_add.10
  301.4 12.6 %collective-permute-done.15 = f32[8,1248]{1,0:T(8,128)S(1)} collective-permute-done((f32[8,1248]{1,0:T(8,128)S(1)}, f32[8,1248]{1,0:T(8,128)S(1)}, u32[]{:S(2)}, u32[]{:S(2)}) %collective-permute-start.15) | collective-permute-done | bytes 39968 | tf_op jit(solution)/shard_map/ppermute | solution.py:748
  315.2 11.2 %middle_back.1 = (f32[6,208,768]{2,1,0:T(8,128)}, bf16[6,208,768]{2,1,0:T(8,128)(2,1)}, f32[2,768]{1,0:T(2,128)}, f32[8,768]{1,0:T(8,128)}, f32[128,768]{1,0:T(8,128)}) custom-call(s32[1]{0:T(128)} %constant.460.clone.1.turn_ref, bf16[6,208,768]{2,1,0:T(8,128)(2,1)} %fusion.3.refs_2_.refs_0_, bf16[6,208,768]{2,1,0:T(8,128)(2,1)} %collective-permute-done.13.refs_1_, ...), custom_call_target="tpu_custom_call" | custom-call | flops 8800000000 | tf_op jit(solution)/shard_map/middle_back/pallas_call | solution.py:410
  326.5 4.5 ring_add.11
  333.5 2.2 fusion.2.refs_10_.refs_0_
  339.4 39.9 %attention_backward.1 = (bf16[6,208,768]{2,1,0:T(8,128)(2,1)}, bf16[6,208,768]{2,1,0:T(8,128)(2,1)}, f32[3,768,192]{2,1,0:T(8,128)}, f32[1,768,192]{2,1,0:T(8,128)}, f32[2,192]{1,0:T(2,128)}, /*index=5*/f32[3,768]{1,0:T(4,128)}) custom-call(s32[1]{0:T(128)} %constant.460.clone.1.turn_ref, bf16[6,208,768]{2,1,0:T(8,128)(2,1)} %get-tuple-element.105.refs_0_, ...), custom_call_target="tpu_custom_call" | custom-call | flops 32999999488 | tf_op jit(solution)/shard_map/attention_backward/pallas_call | solution.py:410
  381.3 4.5 ring_add.12
  391.3 2.2 maximum_add_fusion
  397.0 3.8 add_convert_fusion.1.refs_6_
  400.8 34.0 %collective-permute-done.23.refs_7_ = f32[31,768]{1,0:T(8,128)S(1)} collective-permute-done((f32[31,768]{1,0:T(8,128)S(1)}, f32[31,768]{1,0:T(8,128)S(1)}, u32[]{:S(2)}, u32[]{:S(2)}) %collective-permute-start.23) | collective-permute-done | bytes 95264 | tf_op jit(solution)/shard_map/ppermute | solution.py:997
  436.3 4.3 ring_add.13
  440.6 6.6 %finish.1 = bf16[6,208,768]{2,1,0:T(8,128)(2,1)} custom-call(s32[1]{0:T(128)} %constant.460.clone.1.turn_ref, bf16[6,208,768]{2,1,0:T(8,128)(2,1)} %copy-done.4, bf16[6,208,768]{2,1,0:T(8,128)(2,1)} %copy-done.8, f32[6,208,768]{2,1,0:T(8,128)} %get-tuple-element.103.refs_9_.refs_2_, bf16[12,208,128]{2,1,0:T(8,128)(2,1)} %bitcast.125, ...), custom_call_target="tpu_custom_call" | custom-call | flops 8800000000 | tf_op jit(solution)/shard_map/finish/pallas_call | solution.py:410
  450.8 2.3 collective-permute-start.30
  454.4 24.1 %collective-permute-done.26 = bf16[6,208,768]{2,1,0:T(8,128)(2,1)} collective-permute-done((bf16[6,208,768]{2,1,0:T(8,128)(2,1)}, bf16[6,208,768]{2,1,0:T(8,128)(2,1)}, u32[]{:S(2)}, u32[]{:S(2)}) %collective-permute-start.26) | collective-permute-done | bytes 1916960 | tf_op jit(solution)/shard_map/ppermute | solution.py:748
  478.4 3.8 add_convert_fusion.own_ref
  487.0 2.0 broadcast_select_fusion.1
  489.0 2.1 pad_maximum_fusion
  491.1 4.2 reshape.238.refs_6_
  495.3 1.9 collective-permute-done.32.refs_8_
  498.0 4.5 ring_add.14
  510.1 2.3 collective-permute-start.33
  512.4 15.5 %input_back.1.refs_4_ = f32[2364,768]{1,0:T(8,128)} custom-call(s32[1]{0:T(128)} %bitcast.turn_ref, bf16[6,208,768]{2,1,0:T(8,128)(2,1)} %add_convert_fusion.own_ref, bf16[6,208,768]{2,1,0:T(8,128)(2,1)} %collective-permute-done.27.other_ref, bf16[12,208,768]{2,1,0:T(8,128)(2,1)} %get-tuple-element.78.refs_2_.x_ref, ...), custom_call_target="tpu_custom_call" | custom-call | flops 16499999744 | tf_op jit(solution)/shard_map/input_back/pallas_call | solution.py:720
  527.9 5.4 collective-permute-done.33.refs_5_
  535.0 3.4 ring_add.15
  545.0 3.0 maximum_bitcast_fusion
  553.7 2.6 collective-permute-done.38
  (274 shorter events, 86.1 us)
Async XLA Ops:
  30.1 12.6 %collective-permute-start = (bf16[6,208,768]{2,1,0:T(8,128)(2,1)}, bf16[6,208,768]{2,1,0:T(8,128)(2,1)S(1)}, u32[]{:S(2)}, u32[]{:S(2)}) collective-permute-start(bf16[6,208,768]{2,1,0:T(8,128)(2,1)} %get-tuple-element.77), channel_id=1, source_target_pairs={{0,1},{1,0},{2,3},{3,2},{4,5},{5,4},{6,7},{7,6},{8,9},{9,8},{10,11... | collective-permute-start | bytes 5750792 | tf_op jit(solution)/shard_map/ppermute | solution.py:744
  30.6 7.1 %copy-start.30 = (bf16[8,768]{1,0:T(8,128)(2,1)S(1)}, bf16[8,768]{1,0:T(8,128)(2,1)}, u32[]{:S(2)}) copy-start(bf16[8,768]{1,0:T(8,128)(2,1)} %refs_8_.2) | copy-start | bytes 36868
  46.5 7.6 %copy-start = (s32[12,208,2]{2,1,0:T(8,128)}, s32[12,208,2]{2,1,0:T(8,128)S(1)}, u32[]{:S(2)}) copy-start(s32[12,208,2]{2,1,0:T(8,128)S(1)} %add_select_fusion.refs_4_) | copy-start | bytes 59908
  46.5 11.2 %copy-start.1 = (bf16[6,208,768]{2,1,0:T(8,128)(2,1)S(1)}, bf16[6,208,768]{2,1,0:T(8,128)(2,1)}, u32[]{:S(2)}) copy-start(bf16[6,208,768]{2,1,0:T(8,128)(2,1)} %get-tuple-element.224) | copy-start | bytes 5750788
  48.3 45.2 %collective-permute-start.1 = (bf16[6,208,768]{2,1,0:T(8,128)(2,1)}, bf16[6,208,768]{2,1,0:T(8,128)(2,1)}, u32[]{:S(2)}, u32[]{:S(2)}) collective-permute-start(bf16[6,208,768]{2,1,0:T(8,128)(2,1)} %copy-done.6), channel_id=1, source_target_pairs={{0,2},{1,3},{2,0},{3,1},{4,6},{5,7},{6,4},{7,5},{8,10},{9,11},{10,... | collective-permute-start | bytes 5750792 | tf_op jit(solution)/shard_map/ppermute | solution.py:748
  100.2 4.2 collective-permute-start.2
  159.9 46.2 %collective-permute-start.4 = (bf16[1,4,96,768]{3,2,1,0:T(8,128)(2,1)S(1)}, bf16[1,4,96,768]{3,2,1,0:T(8,128)(2,1)S(1)}, u32[]{:S(2)}, u32[]{:S(2)}) collective-permute-start(bf16[1,4,96,768]{3,2,1,0:T(8,128)(2,1)S(1)} %dynamic-slice_bitcast_fusion.refs_1_), channel_id=1, source_target_pairs={{0,4},{8,0},{16,8},{24,16},{28,24},{20,28},{12,20},{4,12},{1,5},{9... | collective-permute-start | bytes 1769480 | tf_op jit(solution)/shard_map/ppermute | solution.py:769
  164.5 41.7 %collective-permute-start.3 = (bf16[1,4,96,768]{3,2,1,0:T(8,128)(2,1)S(1)}, bf16[1,4,96,768]{3,2,1,0:T(8,128)(2,1)S(1)}, u32[]{:S(2)}, u32[]{:S(2)}) collective-permute-start(bf16[1,4,96,768]{3,2,1,0:T(8,128)(2,1)S(1)} %dynamic-slice_bitcast_fusion.1.refs_0_), channel_id=1, source_target_pairs={{0,8},{8,16},{16,24},{24,28},{28,20},{20,12},{12,4},{4,0},{1,9},{9... | collective-permute-start | bytes 1769480 | tf_op jit(solution)/shard_map/ppermute | solution.py:769
  229.5 36.0 %collective-permute-start.7 = (bf16[6,208,768]{2,1,0:T(8,128)(2,1)}, bf16[6,208,768]{2,1,0:T(8,128)(2,1)S(1)}, u32[]{:S(2)}, u32[]{:S(2)}) collective-permute-start(bf16[6,208,768]{2,1,0:T(8,128)(2,1)} %bitcast.122), channel_id=1, source_target_pairs={{0,1},{1,0},{2,3},{3,2},{4,5},{5,4},{6,7},{7,6},{8,9},{9,8},{10,11... | collective-permute-start | bytes 5750792 | tf_op jit(solution)/shard_map/ppermute | solution.py:744
  229.5 28.6 %collective-permute-start.5 = (bf16[2,4,96,768]{3,2,1,0:T(8,128)(2,1)}, bf16[2,4,96,768]{3,2,1,0:T(8,128)(2,1)S(1)}, u32[]{:S(2)}, u32[]{:S(2)}) collective-permute-start(bf16[2,4,96,768]{3,2,1,0:T(8,128)(2,1)} %get-tuple-element.87.refs_2_), channel_id=1, source_target_pairs={{0,8},{8,16},{16,24},{24,28},{28,20},{20,12},{12,4},{4,0},{1,9},{9... | collective-permute-start | bytes 3538952 | tf_op jit(solution)/shard_map/ppermute | solution.py:769
  229.6 28.7 %collective-permute-start.6 = (bf16[2,4,96,768]{3,2,1,0:T(8,128)(2,1)}, bf16[2,4,96,768]{3,2,1,0:T(8,128)(2,1)}, u32[]{:S(2)}, u32[]{:S(2)}) collective-permute-start(bf16[2,4,96,768]{3,2,1,0:T(8,128)(2,1)} %get-tuple-element.88.refs_3_), channel_id=1, source_target_pairs={{0,4},{8,0},{16,8},{24,16},{28,24},{20,28},{12,20},{4,12},{1,5},{9... | collective-permute-start | bytes 3538952 | tf_op jit(solution)/shard_map/ppermute | solution.py:769
  263.5 28.0 %collective-permute-start.10 = (bf16[2,4,96,768]{3,2,1,0:T(8,128)(2,1)}, bf16[2,4,96,768]{3,2,1,0:T(8,128)(2,1)}, u32[]{:S(2)}, u32[]{:S(2)}) collective-permute-start(bf16[2,4,96,768]{3,2,1,0:T(8,128)(2,1)} %get-tuple-element.95.refs_4_), channel_id=1, source_target_pairs={{0,4},{8,0},{16,8},{24,16},{28,24},{20,28},{12,20},{4,12},{1,5},{9... | collective-permute-start | bytes 3538952 | tf_op jit(solution)/shard_map/ppermute | solution.py:769
  264.3 27.3 %collective-permute-start.9 = (bf16[2,4,96,768]{3,2,1,0:T(8,128)(2,1)}, bf16[2,4,96,768]{3,2,1,0:T(8,128)(2,1)}, u32[]{:S(2)}, u32[]{:S(2)}) collective-permute-start(bf16[2,4,96,768]{3,2,1,0:T(8,128)(2,1)} %get-tuple-element.94.refs_3_), channel_id=1, source_target_pairs={{0,8},{8,16},{16,24},{24,28},{28,20},{20,12},{12,4},{4,0},{1,9},{9... | collective-permute-start | bytes 3538952 | tf_op jit(solution)/shard_map/ppermute | solution.py:769
  270.1 45.2 %collective-permute-start.13 = (bf16[6,208,768]{2,1,0:T(8,128)(2,1)}, bf16[6,208,768]{2,1,0:T(8,128)(2,1)}, u32[]{:S(2)}, u32[]{:S(2)}) collective-permute-start(bf16[6,208,768]{2,1,0:T(8,128)(2,1)} %fusion.3.refs_2_.refs_0_), channel_id=1, source_target_pairs={{0,2},{1,3},{2,0},{3,1},{4,6},{5,7},{6,4},{7,5},{8,10},{9,11},{10,... | collective-permute-start | bytes 5750792 | tf_op jit(solution)/shard_map/ppermute | solution.py:748
  273.0 17.8 %collective-permute-start.14 = (f32[8,1248]{1,0:T(8,128)S(1)}, f32[8,1248]{1,0:T(8,128)S(1)}, u32[]{:S(2)}, u32[]{:S(2)}) collective-permute-start(f32[8,1248]{1,0:T(8,128)S(1)} %copy.108), channel_id=1, source_target_pairs={{0,1},{1,0},{2,3},{3,2},{4,5},{5,4},{6,7},{7,6},{8,9},{9,8},{10,11... | collective-permute-start | bytes 119816 | tf_op jit(solution)/shard_map/ppermute | solution.py:744
  296.0 30.5 %collective-permute-start.11 = (bf16[2,4,96,768]{3,2,1,0:T(8,128)(2,1)}, bf16[2,4,96,768]{3,2,1,0:T(8,128)(2,1)}, u32[]{:S(2)}, u32[]{:S(2)}) collective-permute-start(bf16[2,4,96,768]{3,2,1,0:T(8,128)(2,1)} %get-tuple-element.98.refs_12_), channel_id=1, source_target_pairs={{0,8},{8,16},{16,24},{24,28},{28,20},{20,12},{12,4},{4,0},{1,9},{9... | collective-permute-start | bytes 3538952 | tf_op jit(solution)/shard_map/ppermute | solution.py:769
  297.7 28.8 %collective-permute-start.12 = (bf16[2,4,96,768]{3,2,1,0:T(8,128)(2,1)}, bf16[2,4,96,768]{3,2,1,0:T(8,128)(2,1)}, u32[]{:S(2)}, u32[]{:S(2)}) collective-permute-start(bf16[2,4,96,768]{3,2,1,0:T(8,128)(2,1)} %get-tuple-element.99.refs_13_), channel_id=1, source_target_pairs={{0,4},{8,0},{16,8},{24,16},{28,24},{20,28},{12,20},{4,12},{1,5},{9... | collective-permute-start | bytes 3538952 | tf_op jit(solution)/shard_map/ppermute | solution.py:769
  298.5 15.6 %collective-permute-start.15 = (f32[8,1248]{1,0:T(8,128)S(1)}, f32[8,1248]{1,0:T(8,128)S(1)}, u32[]{:S(2)}, u32[]{:S(2)}) collective-permute-start(f32[8,1248]{1,0:T(8,128)S(1)} %copy.101), channel_id=1, source_target_pairs={{0,2},{1,3},{2,0},{3,1},{4,6},{5,7},{6,4},{7,5},{8,10},{9,11},{10,... | collective-permute-start | bytes 119816 | tf_op jit(solution)/shard_map/ppermute | solution.py:748
  301.4 32.1 %collective-permute-start.8 = (bf16[6,208,768]{2,1,0:T(8,128)(2,1)}, bf16[6,208,768]{2,1,0:T(8,128)(2,1)}, u32[]{:S(2)}, u32[]{:S(2)}) collective-permute-start(bf16[6,208,768]{2,1,0:T(8,128)(2,1)} %bitcast.110), channel_id=1, source_target_pairs={{0,1},{1,0},{2,3},{3,2},{4,5},{5,4},{6,7},{7,6},{8,9},{9,8},{10,11... | collective-permute-start | bytes 5750792 | tf_op jit(solution)/shard_map/ppermute | solution.py:744
  331.0 8.3 %collective-permute-start.19 = (bf16[6,208,768]{2,1,0:T(8,128)(2,1)}, bf16[6,208,768]{2,1,0:T(8,128)(2,1)}, u32[]{:S(2)}, u32[]{:S(2)}) collective-permute-start(bf16[6,208,768]{2,1,0:T(8,128)(2,1)} %get-tuple-element.105.refs_0_), channel_id=1, source_target_pairs={{0,1},{1,0},{2,3},{3,2},{4,5},{5,4},{6,7},{7,6},{8,9},{9,8},{10,11... | collective-permute-start | bytes 5750792 | tf_op jit(solution)/shard_map/ppermute | solution.py:744
  335.8 44.2 %collective-permute-start.16 = (bf16[6,208,768]{2,1,0:T(8,128)(2,1)S(1)}, bf16[6,208,768]{2,1,0:T(8,128)(2,1)S(1)}, u32[]{:S(2)}, u32[]{:S(2)}) collective-permute-start(bf16[6,208,768]{2,1,0:T(8,128)(2,1)S(1)} %fusion.2.refs_10_.refs_0_), channel_id=1, source_target_pairs={{0,2},{1,3},{2,0},{3,1},{4,6},{5,7},{6,4},{7,5},{8,10},{9,11},{10,... | collective-permute-start | bytes 5750792 | tf_op jit(solution)/shard_map/ppermute | solution.py:748
  337.3 41.9 %collective-permute-start.17 = (bf16[2,4,96,768]{3,2,1,0:T(8,128)(2,1)}, bf16[2,4,96,768]{3,2,1,0:T(8,128)(2,1)S(1)}, u32[]{:S(2)}, u32[]{:S(2)}) collective-permute-start(bf16[2,4,96,768]{3,2,1,0:T(8,128)(2,1)} %get-tuple-element.106.refs_11_), channel_id=1, source_target_pairs={{0,8},{8,16},{16,24},{24,28},{28,20},{20,12},{12,4},{4,0},{1,9},{9... | collective-permute-start | bytes 3538952 | tf_op jit(solution)/shard_map/ppermute | solution.py:769
  337.7 41.5 %collective-permute-start.18 = (bf16[2,4,96,768]{3,2,1,0:T(8,128)(2,1)S(1)}, bf16[2,4,96,768]{3,2,1,0:T(8,128)(2,1)S(1)}, u32[]{:S(2)}, u32[]{:S(2)}) collective-permute-start(bf16[2,4,96,768]{3,2,1,0:T(8,128)(2,1)S(1)} %copy-done.42), channel_id=1, source_target_pairs={{0,4},{8,0},{16,8},{24,16},{28,24},{20,28},{12,20},{4,12},{1,5},{9... | collective-permute-start | bytes 3538952 | tf_op jit(solution)/shard_map/ppermute | solution.py:769
  381.3 8.1 %copy-start.35 = (f32[2,768]{1,0:T(2,128)S(1)}, f32[2,768]{1,0:T(2,128)}, u32[]{:S(2)}) copy-start(f32[2,768]{1,0:T(2,128)} %get-tuple-element.120) | copy-start | bytes 18436
  381.3 8.1 %copy-start.28 = (f32[8,768]{1,0:T(8,128)S(1)}, f32[8,768]{1,0:T(8,128)}, u32[]{:S(2)}) copy-start(f32[8,768]{1,0:T(8,128)} %get-tuple-element.121) | copy-start | bytes 73732
  381.3 9.3 %copy-start.34 = (f32[3,768]{1,0:T(4,128)S(1)}, f32[3,768]{1,0:T(4,128)}, u32[]{:S(2)}) copy-start(f32[3,768]{1,0:T(4,128)} %get-tuple-element.119) | copy-start | bytes 27652
  385.8 9.4 %collective-permute-start.22 = (bf16[6,208,768]{2,1,0:T(8,128)(2,1)}, bf16[6,208,768]{2,1,0:T(8,128)(2,1)}, u32[]{:S(2)}, u32[]{:S(2)}) collective-permute-start(bf16[6,208,768]{2,1,0:T(8,128)(2,1)} %get-tuple-element.118), channel_id=1, source_target_pairs={{0,1},{1,0},{2,3},{3,2},{4,5},{5,4},{6,7},{7,6},{8,9},{9,8},{10,11... | collective-permute-start | bytes 5750792 | tf_op jit(solution)/shard_map/ppermute | solution.py:744
  387.3 48.9 %collective-permute-start.20 = (bf16[2,4,96,768]{3,2,1,0:T(8,128)(2,1)}, bf16[2,4,96,768]{3,2,1,0:T(8,128)(2,1)}, u32[]{:S(2)}, u32[]{:S(2)}) collective-permute-start(bf16[2,4,96,768]{3,2,1,0:T(8,128)(2,1)} %get-tuple-element.115), channel_id=1, source_target_pairs={{0,8},{8,16},{16,24},{24,28},{28,20},{20,12},{12,4},{4,0},{1,9},{9... | collective-permute-start | bytes 3538952 | tf_op jit(solution)/shard_map/ppermute | solution.py:769
  387.7 48.6 %collective-permute-start.21 = (bf16[2,4,96,768]{3,2,1,0:T(8,128)(2,1)}, bf16[2,4,96,768]{3,2,1,0:T(8,128)(2,1)}, u32[]{:S(2)}, u32[]{:S(2)}) collective-permute-start(bf16[2,4,96,768]{3,2,1,0:T(8,128)(2,1)} %get-tuple-element.116), channel_id=1, source_target_pairs={{0,4},{8,0},{16,8},{24,16},{28,24},{20,28},{12,20},{4,12},{1,5},{9... | collective-permute-start | bytes 3538952 | tf_op jit(solution)/shard_map/ppermute | solution.py:769
  389.3 120.8 %collective-permute-start.28 = (f32[6,208,768]{2,1,0:T(8,128)}, f32[6,208,768]{2,1,0:T(8,128)}, u32[]{:S(2)}, u32[]{:S(2)}) collective-permute-start(f32[6,208,768]{2,1,0:T(8,128)} %get-tuple-element.130.own_grad_ref), channel_id=1, source_target_pairs={{0,1},{1,0},{2,3},{3,2},{4,5},{5,4},{6,7},{7,6},{8,9},{9,8},{10,11... | collective-permute-start | bytes 11501576 | tf_op jit(solution)/shard_map/ppermute | solution.py:744
  394.5 41.8 %collective-permute-start.24 = (bf16[4,2,2,1,96,192]{5,4,3,2,1,0:T(8,128)(2,1)}, bf16[4,2,2,1,96,192]{5,4,3,2,1,0:T(8,128)(2,1)}, u32[]{:S(2)}, u32[]{:S(2)}) collective-permute-start(bf16[4,2,2,1,96,192]{5,4,3,2,1,0:T(8,128)(2,1)} %dynamic-slice_convert_fusion), channel_id=1, source_target_pairs={{0,4},{4,0},{8,12},{12,8},{16,20},{20,16},{24,28},{28,24},{1,5},{5... | collective-permute-start | bytes 1769480 | tf_op jit(solution)/shard_map/ppermute | solution.py:964
  395.2 39.5 %collective-permute-start.23 = (f32[31,768]{1,0:T(8,128)S(1)}, f32[31,768]{1,0:T(8,128)S(1)}, u32[]{:S(2)}, u32[]{:S(2)}) collective-permute-start(f32[31,768]{1,0:T(8,128)S(1)} %broadcast_add_fusion), channel_id=1, source_target_pairs={{0,4},{4,0},{8,12},{12,8},{16,20},{20,16},{24,28},{28,24},{1,5},{5... | collective-permute-start | bytes 285704 | tf_op jit(solution)/shard_map/ppermute | solution.py:997
  434.8 43.6 %collective-permute-start.26 = (bf16[6,208,768]{2,1,0:T(8,128)(2,1)}, bf16[6,208,768]{2,1,0:T(8,128)(2,1)}, u32[]{:S(2)}, u32[]{:S(2)}) collective-permute-start(bf16[6,208,768]{2,1,0:T(8,128)(2,1)} %add_convert_fusion.1.refs_6_), channel_id=1, source_target_pairs={{0,2},{1,3},{2,0},{3,1},{4,6},{5,7},{6,4},{7,5},{8,10},{9,11},{10,... | collective-permute-start | bytes 5750792 | tf_op jit(solution)/shard_map/ppermute | solution.py:748
  440.6 13.7 %copy-start.21 = (f32[31,768]{1,0:T(8,128)S(1)}, f32[31,768]{1,0:T(8,128)}, u32[]{:S(2)}) copy-start(f32[31,768]{1,0:T(8,128)} %copy-done.20) | copy-start | bytes 285700
  447.2 37.4 %collective-permute-start.25 = (bf16[6,208,768]{2,1,0:T(8,128)(2,1)}, bf16[6,208,768]{2,1,0:T(8,128)(2,1)}, u32[]{:S(2)}, u32[]{:S(2)}) collective-permute-start(bf16[6,208,768]{2,1,0:T(8,128)(2,1)} %finish.1), channel_id=1, source_target_pairs={{0,1},{1,0},{2,3},{3,2},{4,5},{5,4},{6,7},{7,6},{8,9},{9,8},{10,11... | collective-permute-start | bytes 5750792 | tf_op jit(solution)/shard_map/ppermute | solution.py:744
  450.8 46.5 %collective-permute-start.29 = (bf16[2,4,96,768]{3,2,1,0:T(8,128)(2,1)}, bf16[2,4,96,768]{3,2,1,0:T(8,128)(2,1)}, u32[]{:S(2)}, u32[]{:S(2)}) collective-permute-start(bf16[2,4,96,768]{3,2,1,0:T(8,128)(2,1)} %get-tuple-element.128.refs_5_), channel_id=1, source_target_pairs={{0,8},{8,16},{16,24},{24,28},{28,20},{20,12},{12,4},{4,0},{1,9},{9... | collective-permute-start | bytes 3538952 | tf_op jit(solution)/shard_map/ppermute | solution.py:769
  450.8 46.5 %collective-permute-start.30 = (bf16[2,4,96,768]{3,2,1,0:T(8,128)(2,1)}, bf16[2,4,96,768]{3,2,1,0:T(8,128)(2,1)}, u32[]{:S(2)}, u32[]{:S(2)}) collective-permute-start(bf16[2,4,96,768]{3,2,1,0:T(8,128)(2,1)} %get-tuple-element.129.refs_6_), channel_id=1, source_target_pairs={{0,4},{8,0},{16,8},{24,16},{28,24},{20,28},{12,20},{4,12},{1,5},{9... | collective-permute-start | bytes 3538952 | tf_op jit(solution)/shard_map/ppermute | solution.py:769
  478.4 4.6 collective-permute-start.31
  483.0 29.4 %collective-permute-start.27 = (bf16[6,208,768]{2,1,0:T(8,128)(2,1)}, bf16[6,208,768]{2,1,0:T(8,128)(2,1)}, u32[]{:S(2)}, u32[]{:S(2)}) collective-permute-start(bf16[6,208,768]{2,1,0:T(8,128)(2,1)} %add_convert_fusion.own_ref), channel_id=1, source_target_pairs={{0,1},{1,0},{2,3},{3,2},{4,5},{5,4},{6,7},{7,6},{8,9},{9,8},{10,11... | collective-permute-start | bytes 5750792 | tf_op jit(solution)/shard_map/ppermute | solution.py:744
  485.7 11.5 %collective-permute-start.32 = (bf16[4,2,1,1,96,192]{5,4,3,2,1,0:T(8,128)(2,1)S(1)}, bf16[4,2,1,1,96,192]{5,4,3,2,1,0:T(8,128)(2,1)S(1)}, u32[]{:S(2)}, u32[]{:S(2)}) collective-permute-start(bf16[4,2,1,1,96,192]{5,4,3,2,1,0:T(8,128)(2,1)S(1)} %dynamic-slice_convert_fusion.1), channel_id=1, source_target_pairs={{0,8},{4,12},{8,0},{12,4},{16,24},{20,28},{24,16},{28,20},{1,9},{5... | collective-permute-start | bytes 884744 | tf_op jit(solution)/shard_map/ppermute | solution.py:964
  495.3 12.9 %copy-start.3 = (f32[4,2,2,1,96,192]{5,4,3,2,1,0:T(8,128)S(1)}, f32[4,2,2,1,96,192]{5,4,3,2,1,0:T(8,128)}, u32[]{:S(2)}) copy-start(f32[4,2,2,1,96,192]{5,4,3,2,1,0:T(8,128)} %copy-done.2) | copy-start | bytes 3538948
  502.5 7.6 %copy-start.23 = (f32[31,768]{1,0:T(8,128)S(1)}, f32[31,768]{1,0:T(8,128)}, u32[]{:S(2)}) copy-start(f32[31,768]{1,0:T(8,128)} %copy-done.22) | copy-start | bytes 285700
  503.7 29.6 %collective-permute-start.34 = (bf16[1,4,96,768]{3,2,1,0:T(8,128)(2,1)}, bf16[1,4,96,768]{3,2,1,0:T(8,128)(2,1)S(1)}, u32[]{:S(2)}, u32[]{:S(2)}) collective-permute-start(bf16[1,4,96,768]{3,2,1,0:T(8,128)(2,1)} %get-tuple-element.131.refs_0_), channel_id=1, source_target_pairs={{0,8},{8,16},{16,24},{24,28},{28,20},{20,12},{12,4},{4,0},{1,9},{9... | collective-permute-start | bytes 1769480 | tf_op jit(solution)/shard_map/ppermute | solution.py:769
  506.1 27.3 %collective-permute-start.35 = (bf16[1,4,96,768]{3,2,1,0:T(8,128)(2,1)}, bf16[1,4,96,768]{3,2,1,0:T(8,128)(2,1)S(1)}, u32[]{:S(2)}, u32[]{:S(2)}) collective-permute-start(bf16[1,4,96,768]{3,2,1,0:T(8,128)(2,1)} %get-tuple-element.132.refs_1_), channel_id=1, source_target_pairs={{0,4},{8,0},{16,8},{24,16},{28,24},{20,28},{12,20},{4,12},{1,5},{9... | collective-permute-start | bytes 1769480 | tf_op jit(solution)/shard_map/ppermute | solution.py:769
  509.3 24.0 %collective-permute-start.36 = (bf16[4,1,1,1,96,192]{5,4,3,2,1,0:T(8,128)(2,1)S(1)}, bf16[4,1,1,1,96,192]{5,4,3,2,1,0:T(8,128)(2,1)S(1)}, u32[]{:S(2)}, u32[]{:S(2)}) collective-permute-start(bf16[4,1,1,1,96,192]{5,4,3,2,1,0:T(8,128)(2,1)S(1)} %dynamic-slice_convert_fusion.2), channel_id=1, source_target_pairs={{0,16},{4,20},{8,24},{12,28},{16,0},{20,4},{24,8},{28,12},{1,17},{... | collective-permute-start | bytes 442376 | tf_op jit(solution)/shard_map/ppermute | solution.py:964
  510.1 23.2 %collective-permute-start.33 = (f32[31,768]{1,0:T(8,128)S(1)}, f32[31,768]{1,0:T(8,128)S(1)}, u32[]{:S(2)}, u32[]{:S(2)}) collective-permute-start(f32[31,768]{1,0:T(8,128)S(1)} %add_add_fusion.4), channel_id=1, source_target_pairs={{0,16},{4,20},{8,24},{12,28},{16,0},{20,4},{24,8},{28,12},{1,17},{... | collective-permute-start | bytes 285704 | tf_op jit(solution)/shard_map/ppermute | solution.py:997
  544.9 6.7 %collective-permute-start.37 = (f32[20,768]{1,0:T(8,128)S(1)}, f32[20,768]{1,0:T(8,128)S(1)}, u32[]{:S(2)}, u32[]{:S(2)}) collective-permute-start(f32[20,768]{1,0:T(8,128)S(1)} %slice.184), channel_id=1, source_target_pairs={{0,1},{1,0},{2,3},{3,2},{4,5},{5,4},{6,7},{7,6},{8,9},{9,8},{10,11... | collective-permute-start | bytes 184328 | tf_op jit(solution)/shard_map/ppermute | solution.py:958
  551.6 4.7 collective-permute-start.38
  (38 other events, 121.7 us)

commit v9 on v8

--- a/solution.py
+++ b/solution.py
@@ -925,11 +925,10 @@
 
     moving = round_trip(1, [low, low])
     own, other, dots = collect((back_first, back_second), columns, plan, width, tuple(moving))
-    sent = to_core(imaged(other))
-    *moving, own = round_trip(2, [low, low], (), (own,))
-    back_near = (imaged(own).astype(f32) + sent.astype(f32)).astype(low)
+    *moving, own, other = round_trip(2, [low, low], (), (own, other))
+    back_near = core_sum(imaged(own), imaged(other), 0.0)
     back_far = across(back_near)
-    dots = dots[:, : 2 * expert_count].T + zero_of(back_near)
+    dots = dots[:, : 2 * expert_count].T + zero_of(own)
     dots = dots[:expert_count] + dots[expert_count:]
     dots = dots[:, :own_rows] + to_core(dots[:, own_rows:])
     dots = (dots + across(dots)).T.reshape(half, ROWS, expert_count)
@@ -963,10 +962,9 @@
         give = lax.dynamic_index_in_dim(values, 1 - mine, axis, keepdims=True).astype(low)
         return keep, lax.ppermute(give, "dp", pairs(8, 1 << bit))
 
-    def output():
-        own_out = finish(y_near, y_far, middle, mix_pair, bias_twice, tuple(moving))
-        return in_order(own_out, to_core(own_out))
-
+    moving = round_trip(6, [low, low], (last_near,))
+    own_out = finish(y_near, y_far, middle, mix_pair, bias_twice, tuple(moving))
+    layer_out = in_order(own_out, to_core(own_out))
     router_bias = [router_sums, bias_sums[:expert_count] + bias_sums[expert_count : 2 * expert_count]]
     packed = jnp.concatenate(
         [
@@ -992,23 +990,19 @@
     if ringed:
         slim = slim.reshape(4, 2, 2, 2, width // 8, head_width)
         packed = after_round(packed)
-        for step, bit, axis in ((6, 0, 3), (7, 1, 2), (8, 2, 1)):
+        for step, bit, axis in ((7, 0, 3), (8, 1, 2), (9, 2, 1)):
             keep, got = halve(after_round(slim), bit, axis)
             sent = lax.ppermute(packed, "dp", pairs(8, 1 << bit))
-            if step == 6:
-                moving = round_trip(6, [low, low], (last_near, sent, got))
-                layer_out = output()
-            elif step == 7:
-                up_first, down_first, *moving = round_trip(7, [f32, low], (layer_out, sent, got))
-                grad_embedded = input_grad()
-            else:
-                moving = round_trip(8, [f32], (grad_embedded, sent, got))
-            slim = keep.astype(f32) + got.astype(f32) + zero_of(moving[0])
+            if step == 7:
+                up_first, down_first, *moving = round_trip(7, [f32, low], (layer_out,))
+            elif step == 8:
+                moving = round_trip(8, [f32])
+            slim = keep.astype(f32) + got.astype(f32)
             packed = after_round(packed + sent)
+        grad_embedded = input_grad()
         up_second, down_second = moving
         slim = slim.reshape(4, width // 8, head_width)
     else:
-        layer_out = output()
         grad_embedded = input_grad()
         packed = lax.psum(packed, "dp")
         slim = lax.psum_scatter(slim, "dp", scatter_dimension=1, tiled=True)

time: 567 us -> 535 us (0.944)
  waiting for transfers between devices: 125 us -> 107 us
    ppermute x3, waiting for transfers between devices: 40.2 us -> 7.7 us  [on_device(): sent = lax.ppermute(packed, 'dp', pairs(8, 1 << bit))]
    ppermute x16, waiting for transfers between devices: 26.1 us -> 55.2 us  [ring_hop(): return lax.ppermute(value, 'dp', path)]
    ppermute x5, waiting for transfers between devices: 53.2 us -> 28.5 us  [across(): return lax.ppermute(value, 'tensor', pairs(lax.axis_size('tensor'), 2))]
    ppermute x3, waiting for transfers between devices: 1.92 us -> 10.1 us  [halve(): return (keep, lax.ppermute(give, 'dp', pairs(8, 1 << bit)))]
    slice x10 -> x6, local copies, waits for them, and re-layouts: 11.3 us -> 6.64 us  [zero_of(): return value[(0,) * value.ndim].astype(jnp.float32) * 0.0]
    unnamed x100 -> x99, local copies, waits for them, and re-layouts: 12.7 us -> 15.4 us
  transfers between devices with their start and end apart: 39 -> 39, of which waited for: 14 -> 20; matrix products, arithmetic and copies ran while one was open for 14% -> 15% of each run, Pallas kernels for 30% -> 29%
where the time goes in v9:
time: 535 us; the launch traced here: 526 us
  Pallas kernels  279 us (52%)
  waiting for transfers between devices  107 us (20%)
  local copies, waits for them, and re-layouts  60.1 us (11%)
  other arithmetic  39.2 us (7%)
  starting transfers between devices  32.8 us (6%)
  between operations  5.94 us (1%)
    pallas_call x2, Pallas kernels, expert_pass(): pl.pallas_call(kernel, grid_spec=pltpu.PrefetchScalarGridSpec(num_scalar_...  71.5 us
    pallas_call x4, Pallas kernels, call(): pl.pallas_call(body, grid_spec=pltpu.PrefetchScalarGridSpec(num_scalar_pr...  64.4 us
    ppermute x16, waiting for transfers between devices, ring_hop(): return lax.ppermute(value, 'dp', path)  55.2 us
    pallas_call x2, Pallas kernels, collect(): pl.pallas_call(kernel, grid_spec=pltpu.PrefetchScalarGridSpec(num_scalar_...  36.4 us
    pallas_call x8, Pallas kernels, ring_add(): pl.pallas_call(kernel, grid_spec=pltpu.PrefetchScalarGridSpec(num_scalar_...  33.8 us
    ppermute x5, waiting for transfers between devices, across(): return lax.ppermute(value, 'tensor', pairs(lax.axis_size('tensor'), 2))  28.5 us
    pallas_call x1, Pallas kernels, gated_spread(): pl.pallas_call(kernel, grid_spec=pltpu.PrefetchScalarGridSpec(num_scalar_...  22.1 us
    pallas_call x1, Pallas kernels, attention_forward(): pl.pallas_call(kernel, grid_spec=pltpu.PrefetchScalarGridSpec(num_scalar_...  20.1 us
  transfers between devices with their start and end apart: 39, of which 20 were waited for; matrix products, arithmetic and copies ran while one was open for 15% of the time, Pallas kernels for 29%

profile of v9, /device:TPU:0, one launch (start us, length us, event | category | flops | bytes accessed | tf_op | source)
XLA Modules:
  0.0 525.7 jit_solution(283081342077162505)
XLA Ops:
  1.4 2.3 copy.98.w_ref.refs_8_
  4.4 4.3 reshape.211.x_ref
  10.0 20.1 %attention_forward.1 = (bf16[6,208,768]{2,1,0:T(8,128)(2,1)}, bf16[6,208,768]{2,1,0:T(8,128)(2,1)}, bf16[12,208,768]{2,1,0:T(8,128)(2,1)}, bf16[12,208,768]{2,1,...) custom-call(s32[1]{0:T(128)S(6)} %select_n.435.turn_ref, ...), custom_call_target="tpu_custom_call" | custom-call | flops 19800000512 | tf_op jit(solution)/shard_map/attention_forward/pallas_call | solution.py:507
  30.6 4.3 reshape.218
  38.4 4.4 pad_slice_fusion.1
  48.3 2.5 collective-permute-start.1
  57.7 4.7 fusion.refs_10_
  62.4 15.4 %spread.1.refs_6_.g_ref = bf16[8,1024,768]{2,1,0:T(8,128)(2,1)} custom-call(s32[144]{0:T(256)} %pad_add_fusion.1.plan_ref, s32[6,2,416]{2,1,0:T(2,128)} %add_bitcast_fusion.1.rows_ref, bf16[2496,768]{1,0:T(8,128)(2,1)} %bitcast.104), custom_call_target="tpu_custom_call" | custom-call | flops 16499999744 | tf_op jit(solution)/shard_map/spread/pallas_call | solution.py:90
  77.8 15.7 %collective-permute-done.1.refs_1_ = bf16[6,208,768]{2,1,0:T(8,128)(2,1)} collective-permute-done((bf16[6,208,768]{2,1,0:T(8,128)(2,1)}, bf16[6,208,768]{2,1,0:T(8,128)(2,1)}, u32[]{:S(2)}, u32[]{:S(2)}) %collective-permute-start.1) | collective-permute-done | bytes 1916960 | tf_op jit(solution)/shard_map/ppermute | solution.py:748
  93.5 6.6 %middle_norm.1 = (f32[6,208,768]{2,1,0:T(8,128)}, bf16[6,208,768]{2,1,0:T(8,128)(2,1)}) custom-call(s32[1]{0:T(128)} %constant.456.clone.1.turn_ref, bf16[6,208,768]{2,1,0:T(8,128)(2,1)} %copy-done.9, bf16[6,208,768]{2,1,0:T(8,128)(2,1)} %collective-permute-done.1.refs_1_, bf16[12,208,768]{2,1,0:T(8,128)(2,1)} %get-tuple-element.79.refs_2_.x_ref, ...), custom_call_target="tpu_custom_call" | custom-call | flops 8800000000 | tf_op jit(solution)/shard_map/middle_norm/pallas_call | solution.py:410
  104.4 22.1 %gated_spread.1 = (bf16[8,1024,896]{2,1,0:T(8,128)(2,1)}, f32[2496,128]{1,0:T(8,128)}, bf16[2496,128]{1,0:T(8,128)(2,1)}) custom-call(s32[144]{0:T(256)} %pad_add_fusion.1.plan_ref, s32[6,2,416]{2,1,0:T(2,128)} %add_bitcast_fusion.1.rows_ref, bf16[1248,768]{1,0:T(8,128)(2,1)} %bitcast.118, bf16[1248,768]{1,0:T(8,128)(2,1)} %bitcast.13.other_ref, ...), custom_call_target="tpu_custom_call" | custom-call | flops 22000001024 | tf_op jit(solution)/shard_map/gated_spread/pallas_call | solution.py:159
  126.5 38.4 %experts.2 = (bf16[4,1024,768]{2,1,0:T(8,128)(2,1)}, bf16[4,1024,896]{2,1,0:T(8,128)(2,1)}, bf16[4,768,768]{2,1,0:T(8,128)(2,1)}, bf16[4,768,768]{2,1,0:T(8,128)(2,1)}, f32[4,1,768]{2,1,0:T(1,128)}) custom-call(s32[8]{0:T(128)} %and_select_fusion.refs_9_.tiles_ref, bf16[8,1024,896]{2,1,0:T(8,128)(2,1)} %get-tuple-element.81.x_ref, ...), custom_call_target="tpu_custom_call" | custom-call | flops 21743271936 | bytes 46137344 | tf_op jit(solution)/shard_map/experts/pallas_call | solution.py:359
  166.0 1.8 collective-permute-start.4
  169.8 33.2 %experts.3 = (bf16[4,1024,768]{2,1,0:T(8,128)(2,1)}, bf16[4,1024,896]{2,1,0:T(8,128)(2,1)}, bf16[4,768,768]{2,1,0:T(8,128)(2,1)}, bf16[4,768,768]{2,1,0:T(8,128)(2,1)}, f32[4,1,768]{2,1,0:T(1,128)}) custom-call(s32[8]{0:T(128)} %and_select_fusion.refs_9_.tiles_ref, bf16[8,1024,896]{2,1,0:T(8,128)(2,1)} %get-tuple-element.81.x_ref, ...), custom_call_target="tpu_custom_call" | custom-call | flops 21743271936 | bytes 46137344 | tf_op jit(solution)/shard_map/experts/pallas_call | solution.py:359
  203.9 3.8 ring_add.8
  207.8 1.9 collective-permute-start.5
  209.8 18.6 %collect.2 = (bf16[1248,768]{1,0:T(8,128)(2,1)}, bf16[1248,768]{1,0:T(8,128)(2,1)}, f32[2496,128]{1,0:T(8,128)}) custom-call(s32[144]{0:T(256)} %pad_add_fusion.1.plan_ref, s32[2496,2]{1,0:T(8,128)} %bitcast.108, bf16[4,1024,896]{2,1,0:T(8,128)(2,1)} %get-tuple-element.90.refs_0_, bf16[4,1024,896]{2,1,0:T(8,128)(2,1)} %get-tuple-element.91.refs_1_, ...), custom_call_target="tpu_custom_call" | custom-call | flops 17600000000 | tf_op jit(solution)/shard_map/collect/pallas_call | solution.py:248
  228.4 7.3 %collective-permute-done.5.refs_0_ = bf16[2,4,96,768]{3,2,1,0:T(8,128)(2,1)S(1)} collective-permute-done((bf16[2,4,96,768]{3,2,1,0:T(8,128)(2,1)}, bf16[2,4,96,768]{3,2,1,0:T(8,128)(2,1)S(1)}, u32[]{:S(2)}, u32[]{:S(2)}) %collective-permute-start.5) | collective-permute-done | bytes 1179680 | tf_op jit(solution)/shard_map/ppermute | solution.py:769
  235.7 3.9 collective-permute-done.6.refs_1_
  240.7 4.5 ring_add.9
  253.9 3.3 fusion.3.refs_2_.refs_0_
  258.6 17.8 %collect.3 = (bf16[1248,768]{1,0:T(8,128)(2,1)}, bf16[1248,768]{1,0:T(8,128)(2,1)}) custom-call(s32[144]{0:T(256)} %pad_add_fusion.1.plan_ref, s32[2496,2]{1,0:T(8,128)} %bitcast.109, bf16[4,1024,768]{2,1,0:T(8,128)(2,1)} %get-tuple-element.82.refs_0_, bf16[4,1024,768]{2,1,0:T(8,128)(2,1)} %get-tuple-element.85.refs_1_, ...), custom_call_target="tpu_custom_call" | custom-call | flops 17600000000 | tf_op jit(solution)/shard_map/collect/pallas_call | solution.py:248
  276.4 2.6 collective-permute-done.10.refs_1_
  279.3 4.5 ring_add.10
  289.3 12.1 %collective-permute-done.15 = f32[8,1248]{1,0:T(8,128)S(1)} collective-permute-done((f32[8,1248]{1,0:T(8,128)S(1)}, f32[8,1248]{1,0:T(8,128)S(1)}, u32[]{:S(2)}, u32[]{:S(2)}) %collective-permute-start.15) | collective-permute-done | bytes 39968 | tf_op jit(solution)/shard_map/ppermute | solution.py:748
  302.6 11.2 %middle_back.1 = (f32[6,208,768]{2,1,0:T(8,128)}, bf16[6,208,768]{2,1,0:T(8,128)(2,1)}, f32[2,768]{1,0:T(2,128)}, f32[8,768]{1,0:T(8,128)}, f32[128,768]{1,0:T(8,128)}) custom-call(s32[1]{0:T(128)} %constant.456.clone.1.turn_ref, bf16[6,208,768]{2,1,0:T(8,128)(2,1)} %fusion.3.refs_2_.refs_0_, bf16[6,208,768]{2,1,0:T(8,128)(2,1)} %collective-permute-done.13.refs_1_, ...), custom_call_target="tpu_custom_call" | custom-call | flops 8800000000 | tf_op jit(solution)/shard_map/middle_back/pallas_call | solution.py:410
  314.9 4.5 ring_add.11
  322.4 2.2 fusion.2.refs_10_.refs_0_
  328.2 39.8 %attention_backward.1 = (bf16[6,208,768]{2,1,0:T(8,128)(2,1)}, bf16[6,208,768]{2,1,0:T(8,128)(2,1)}, f32[3,768,192]{2,1,0:T(8,128)}, f32[1,768,192]{2,1,0:T(8,128)}, f32[2,192]{1,0:T(2,128)}, /*index=5*/f32[3,768]{1,0:T(4,128)}) custom-call(s32[1]{0:T(128)} %constant.456.clone.1.turn_ref, bf16[6,208,768]{2,1,0:T(8,128)(2,1)} %get-tuple-element.107.refs_0_, ...), custom_call_target="tpu_custom_call" | custom-call | flops 32999999488 | tf_op jit(solution)/shard_map/attention_backward/pallas_call | solution.py:410
  370.1 4.4 ring_add.12
  378.6 3.3 add_convert_fusion.1.refs_6_
  381.8 21.2 %collective-permute-done.20.refs_0_ = bf16[2,4,96,768]{3,2,1,0:T(8,128)(2,1)S(1)} collective-permute-done((bf16[2,4,96,768]{3,2,1,0:T(8,128)(2,1)}, bf16[2,4,96,768]{3,2,1,0:T(8,128)(2,1)S(1)}, u32[]{:S(2)}, u32[]{:S(2)}) %collective-permute-start.20) | collective-permute-done | bytes 1179680 | tf_op jit(solution)/shard_map/ppermute | solution.py:769
  404.6 4.3 ring_add.13
  409.0 6.7 %finish.1 = bf16[6,208,768]{2,1,0:T(8,128)(2,1)} custom-call(s32[1]{0:T(128)} %constant.456.clone.1.turn_ref, bf16[6,208,768]{2,1,0:T(8,128)(2,1)} %copy-done.8, bf16[6,208,768]{2,1,0:T(8,128)(2,1)} %copy-done.12, f32[6,208,768]{2,1,0:T(8,128)} %get-tuple-element.105.refs_9_.refs_2_, bf16[12,208,128]{2,1,0:T(8,128)(2,1)} %bitcast.121, ...), custom_call_target="tpu_custom_call" | custom-call | flops 8800000000 | tf_op jit(solution)/shard_map/finish/pallas_call | solution.py:410
  423.3 2.2 maximum_add_fusion
  428.6 2.0 broadcast_select_fusion.1
  430.7 2.1 pad_maximum_fusion
  432.7 4.2 reshape.227.refs_6_
  437.0 9.7 %collective-permute-done.27.refs_0_ = bf16[2,4,96,768]{3,2,1,0:T(8,128)(2,1)S(1)} collective-permute-done((bf16[2,4,96,768]{3,2,1,0:T(8,128)(2,1)}, bf16[2,4,96,768]{3,2,1,0:T(8,128)(2,1)S(1)}, u32[]{:S(2)}, u32[]{:S(2)}) %collective-permute-start.27) | collective-permute-done | bytes 1179680 | tf_op jit(solution)/shard_map/ppermute | solution.py:769
  447.7 4.4 ring_add.14
  455.4 8.3 %collective-permute-done.36 = bf16[4,2,2,1,96,192]{5,4,0,3,2,1:T(8,128)(2,1)} collective-permute-done((bf16[4,2,2,1,96,192]{5,4,0,3,2,1:T(8,128)(2,1)}, bf16[4,2,2,1,96,192]{5,4,0,3,2,1:T(8,128)(2,1)}, u32[]{:S(2)}, u32[]{:S(2)}) %collective-permute-start.36) | collective-permute-done | bytes 589856 | tf_op jit(solution)/shard_map/ppermute | solution.py:963
  467.6 3.3 add_convert_fusion.own_ref
  470.9 7.6 %collective-permute-done.29.refs_0_ = bf16[1,4,96,768]{3,2,1,0:T(8,128)(2,1)} collective-permute-done((bf16[1,4,96,768]{3,2,1,0:T(8,128)(2,1)}, bf16[1,4,96,768]{3,2,1,0:T(8,128)(2,1)}, u32[]{:S(2)}, u32[]{:S(2)}) %collective-permute-start.29) | collective-permute-done | bytes 589856 | tf_op jit(solution)/shard_map/ppermute | solution.py:769
  478.6 3.4 ring_add.15
  485.9 2.9 collective-permute-start.38
  493.8 7.3 %collective-permute-done.33 = f32[31,768]{1,0:T(8,128)S(1)} collective-permute-done((f32[31,768]{1,0:T(8,128)S(1)}, f32[31,768]{1,0:T(8,128)S(1)}, u32[]{:S(2)}, u32[]{:S(2)}) %collective-permute-start.33) | collective-permute-done | bytes 95264 | tf_op jit(solution)/shard_map/ppermute | solution.py:995
  505.6 2.9 collective-permute-done.35
  509.7 15.5 %input_back.1 = f32[2364,768]{1,0:T(8,128)} custom-call(s32[1]{0:T(128)} %bitcast.turn_ref, bf16[6,208,768]{2,1,0:T(8,128)(2,1)} %add_convert_fusion.own_ref, bf16[6,208,768]{2,1,0:T(8,128)(2,1)} %collective-permute-done.25.other_ref, bf16[12,208,768]{2,1,0:T(8,128)(2,1)} %get-tuple-element.79.refs_2_.x_ref, f32[6,208,768]{2,1,0:T(8,128)} %get-tuple-element.123.own_grad_ref, ...), custom_call_target="tpu_custom_call" | custom-call | flops 16499999744 | tf_op jit(solution)/shard_map/input_back/pallas_call | solution.py:720
  (269 shorter events, 90.2 us)
Async XLA Ops:
  30.1 12.6 %collective-permute-start = (bf16[6,208,768]{2,1,0:T(8,128)(2,1)}, bf16[6,208,768]{2,1,0:T(8,128)(2,1)S(1)}, u32[]{:S(2)}, u32[]{:S(2)}) collective-permute-start(bf16[6,208,768]{2,1,0:T(8,128)(2,1)} %get-tuple-element.78), channel_id=1, source_target_pairs={{0,1},{1,0},{2,3},{3,2},{4,5},{5,4},{6,7},{7,6},{8,9},{9,8},{10,11... | collective-permute-start | bytes 5750792 | tf_op jit(solution)/shard_map/ppermute | solution.py:744
  46.5 11.2 %copy-start.4 = (bf16[6,208,768]{2,1,0:T(8,128)(2,1)S(1)}, bf16[6,208,768]{2,1,0:T(8,128)(2,1)}, u32[]{:S(2)}) copy-start(bf16[6,208,768]{2,1,0:T(8,128)(2,1)} %get-tuple-element.211) | copy-start | bytes 5750788
  48.3 45.2 %collective-permute-start.1 = (bf16[6,208,768]{2,1,0:T(8,128)(2,1)}, bf16[6,208,768]{2,1,0:T(8,128)(2,1)}, u32[]{:S(2)}, u32[]{:S(2)}) collective-permute-start(bf16[6,208,768]{2,1,0:T(8,128)(2,1)} %copy-done.9), channel_id=1, source_target_pairs={{0,2},{1,3},{2,0},{3,1},{4,6},{5,7},{6,4},{7,5},{8,10},{9,11},{10,... | collective-permute-start | bytes 5750792 | tf_op jit(solution)/shard_map/ppermute | solution.py:748
  100.2 4.2 collective-permute-start.2
  166.0 36.9 %collective-permute-start.4 = (bf16[1,4,96,768]{3,2,1,0:T(8,128)(2,1)S(1)}, bf16[1,4,96,768]{3,2,1,0:T(8,128)(2,1)S(1)}, u32[]{:S(2)}, u32[]{:S(2)}) collective-permute-start(bf16[1,4,96,768]{3,2,1,0:T(8,128)(2,1)S(1)} %dynamic-slice_bitcast_fusion.refs_1_), channel_id=1, source_target_pairs={{0,4},{8,0},{16,8},{24,16},{28,24},{20,28},{12,20},{4,12},{1,5},{9... | collective-permute-start | bytes 1769480 | tf_op jit(solution)/shard_map/ppermute | solution.py:769
  169.0 34.0 %collective-permute-start.3 = (bf16[1,4,96,768]{3,2,1,0:T(8,128)(2,1)S(1)}, bf16[1,4,96,768]{3,2,1,0:T(8,128)(2,1)S(1)}, u32[]{:S(2)}, u32[]{:S(2)}) collective-permute-start(bf16[1,4,96,768]{3,2,1,0:T(8,128)(2,1)S(1)} %dynamic-slice_bitcast_fusion.1.refs_0_), channel_id=1, source_target_pairs={{0,8},{8,16},{16,24},{24,28},{28,20},{20,12},{12,4},{4,0},{1,9},{9... | collective-permute-start | bytes 1769480 | tf_op jit(solution)/shard_map/ppermute | solution.py:769
  207.8 27.9 %collective-permute-start.5 = (bf16[2,4,96,768]{3,2,1,0:T(8,128)(2,1)}, bf16[2,4,96,768]{3,2,1,0:T(8,128)(2,1)S(1)}, u32[]{:S(2)}, u32[]{:S(2)}) collective-permute-start(bf16[2,4,96,768]{3,2,1,0:T(8,128)(2,1)} %get-tuple-element.88.refs_2_), channel_id=1, source_target_pairs={{0,8},{8,16},{16,24},{24,28},{28,20},{20,12},{12,4},{4,0},{1,9},{9... | collective-permute-start | bytes 3538952 | tf_op jit(solution)/shard_map/ppermute | solution.py:769
  209.7 29.9 %collective-permute-start.6 = (bf16[2,4,96,768]{3,2,1,0:T(8,128)(2,1)}, bf16[2,4,96,768]{3,2,1,0:T(8,128)(2,1)S(1)}, u32[]{:S(2)}, u32[]{:S(2)}) collective-permute-start(bf16[2,4,96,768]{3,2,1,0:T(8,128)(2,1)} %get-tuple-element.89.refs_3_), channel_id=1, source_target_pairs={{0,4},{8,0},{16,8},{24,16},{28,24},{20,28},{12,20},{4,12},{1,5},{9... | collective-permute-start | bytes 3538952 | tf_op jit(solution)/shard_map/ppermute | solution.py:769
  245.1 8.8 %collective-permute-start.7 = (bf16[6,208,768]{2,1,0:T(8,128)(2,1)}, bf16[6,208,768]{2,1,0:T(8,128)(2,1)}, u32[]{:S(2)}, u32[]{:S(2)}) collective-permute-start(bf16[6,208,768]{2,1,0:T(8,128)(2,1)} %bitcast.107), channel_id=1, source_target_pairs={{0,1},{1,0},{2,3},{3,2},{4,5},{5,4},{6,7},{7,6},{8,9},{9,8},{10,11... | collective-permute-start | bytes 5750792 | tf_op jit(solution)/shard_map/ppermute | solution.py:744
  249.7 3.1 collective-permute-start.14
  250.8 28.2 %collective-permute-start.10 = (bf16[2,4,96,768]{3,2,1,0:T(8,128)(2,1)}, bf16[2,4,96,768]{3,2,1,0:T(8,128)(2,1)}, u32[]{:S(2)}, u32[]{:S(2)}) collective-permute-start(bf16[2,4,96,768]{3,2,1,0:T(8,128)(2,1)} %get-tuple-element.97.refs_4_), channel_id=1, source_target_pairs={{0,4},{8,0},{16,8},{24,16},{28,24},{20,28},{12,20},{4,12},{1,5},{9... | collective-permute-start | bytes 3538952 | tf_op jit(solution)/shard_map/ppermute | solution.py:769
  251.4 28.0 %collective-permute-start.9 = (bf16[2,4,96,768]{3,2,1,0:T(8,128)(2,1)}, bf16[2,4,96,768]{3,2,1,0:T(8,128)(2,1)}, u32[]{:S(2)}, u32[]{:S(2)}) collective-permute-start(bf16[2,4,96,768]{3,2,1,0:T(8,128)(2,1)} %get-tuple-element.96.refs_3_), channel_id=1, source_target_pairs={{0,8},{8,16},{16,24},{24,28},{28,20},{20,12},{12,4},{4,0},{1,9},{9... | collective-permute-start | bytes 3538952 | tf_op jit(solution)/shard_map/ppermute | solution.py:769
  257.1 45.5 %collective-permute-start.13 = (bf16[6,208,768]{2,1,0:T(8,128)(2,1)}, bf16[6,208,768]{2,1,0:T(8,128)(2,1)}, u32[]{:S(2)}, u32[]{:S(2)}) collective-permute-start(bf16[6,208,768]{2,1,0:T(8,128)(2,1)} %fusion.3.refs_2_.refs_0_), channel_id=1, source_target_pairs={{0,2},{1,3},{2,0},{3,1},{4,6},{5,7},{6,4},{7,5},{8,10},{9,11},{10,... | collective-permute-start | bytes 5750792 | tf_op jit(solution)/shard_map/ppermute | solution.py:748
  283.9 30.0 %collective-permute-start.11 = (bf16[2,4,96,768]{3,2,1,0:T(8,128)(2,1)}, bf16[2,4,96,768]{3,2,1,0:T(8,128)(2,1)S(1)}, u32[]{:S(2)}, u32[]{:S(2)}) collective-permute-start(bf16[2,4,96,768]{3,2,1,0:T(8,128)(2,1)} %get-tuple-element.100.refs_12_), channel_id=1, source_target_pairs={{0,8},{8,16},{16,24},{24,28},{28,20},{20,12},{12,4},{4,0},{1,9},{9... | collective-permute-start | bytes 3538952 | tf_op jit(solution)/shard_map/ppermute | solution.py:769
  285.3 28.5 %collective-permute-start.12 = (bf16[2,4,96,768]{3,2,1,0:T(8,128)(2,1)}, bf16[2,4,96,768]{3,2,1,0:T(8,128)(2,1)}, u32[]{:S(2)}, u32[]{:S(2)}) collective-permute-start(bf16[2,4,96,768]{3,2,1,0:T(8,128)(2,1)} %get-tuple-element.101.refs_13_), channel_id=1, source_target_pairs={{0,4},{8,0},{16,8},{24,16},{28,24},{20,28},{12,20},{4,12},{1,5},{9... | collective-permute-start | bytes 3538952 | tf_op jit(solution)/shard_map/ppermute | solution.py:769
  286.4 15.0 %collective-permute-start.15 = (f32[8,1248]{1,0:T(8,128)S(1)}, f32[8,1248]{1,0:T(8,128)S(1)}, u32[]{:S(2)}, u32[]{:S(2)}) collective-permute-start(f32[8,1248]{1,0:T(8,128)S(1)} %copy.109), channel_id=1, source_target_pairs={{0,2},{1,3},{2,0},{3,1},{4,6},{5,7},{6,4},{7,5},{8,10},{9,11},{10,... | collective-permute-start | bytes 119816 | tf_op jit(solution)/shard_map/ppermute | solution.py:748
  302.6 19.8 %collective-permute-start.8 = (bf16[6,208,768]{2,1,0:T(8,128)(2,1)}, bf16[6,208,768]{2,1,0:T(8,128)(2,1)}, u32[]{:S(2)}, u32[]{:S(2)}) collective-permute-start(bf16[6,208,768]{2,1,0:T(8,128)(2,1)} %bitcast.106), channel_id=1, source_target_pairs={{0,1},{1,0},{2,3},{3,2},{4,5},{5,4},{6,7},{7,6},{8,9},{9,8},{10,11... | collective-permute-start | bytes 5750792 | tf_op jit(solution)/shard_map/ppermute | solution.py:744
  319.4 8.8 %collective-permute-start.19 = (bf16[6,208,768]{2,1,0:T(8,128)(2,1)}, bf16[6,208,768]{2,1,0:T(8,128)(2,1)}, u32[]{:S(2)}, u32[]{:S(2)}) collective-permute-start(bf16[6,208,768]{2,1,0:T(8,128)(2,1)} %get-tuple-element.107.refs_0_), channel_id=1, source_target_pairs={{0,1},{1,0},{2,3},{3,2},{4,5},{5,4},{6,7},{7,6},{8,9},{9,8},{10,11... | collective-permute-start | bytes 5750792 | tf_op jit(solution)/shard_map/ppermute | solution.py:744
  324.6 43.8 %collective-permute-start.16 = (bf16[6,208,768]{2,1,0:T(8,128)(2,1)S(1)}, bf16[6,208,768]{2,1,0:T(8,128)(2,1)S(1)}, u32[]{:S(2)}, u32[]{:S(2)}) collective-permute-start(bf16[6,208,768]{2,1,0:T(8,128)(2,1)S(1)} %fusion.2.refs_10_.refs_0_), channel_id=1, source_target_pairs={{0,2},{1,3},{2,0},{3,1},{4,6},{5,7},{6,4},{7,5},{8,10},{9,11},{10,... | collective-permute-start | bytes 5750792 | tf_op jit(solution)/shard_map/ppermute | solution.py:748
  326.1 41.9 %collective-permute-start.17 = (bf16[2,4,96,768]{3,2,1,0:T(8,128)(2,1)}, bf16[2,4,96,768]{3,2,1,0:T(8,128)(2,1)S(1)}, u32[]{:S(2)}, u32[]{:S(2)}) collective-permute-start(bf16[2,4,96,768]{3,2,1,0:T(8,128)(2,1)} %get-tuple-element.108.refs_11_), channel_id=1, source_target_pairs={{0,8},{8,16},{16,24},{24,28},{28,20},{20,12},{12,4},{4,0},{1,9},{9... | collective-permute-start | bytes 3538952 | tf_op jit(solution)/shard_map/ppermute | solution.py:769
  327.9 40.2 %collective-permute-start.18 = (bf16[2,4,96,768]{3,2,1,0:T(8,128)(2,1)S(1)}, bf16[2,4,96,768]{3,2,1,0:T(8,128)(2,1)S(1)}, u32[]{:S(2)}, u32[]{:S(2)}) collective-permute-start(bf16[2,4,96,768]{3,2,1,0:T(8,128)(2,1)S(1)} %copy-done.43), channel_id=1, source_target_pairs={{0,4},{8,0},{16,8},{24,16},{28,24},{20,28},{12,20},{4,12},{1,5},{9... | collective-permute-start | bytes 3538952 | tf_op jit(solution)/shard_map/ppermute | solution.py:769
  374.4 4.1 collective-permute-start.22
  374.4 28.6 %collective-permute-start.20 = (bf16[2,4,96,768]{3,2,1,0:T(8,128)(2,1)}, bf16[2,4,96,768]{3,2,1,0:T(8,128)(2,1)S(1)}, u32[]{:S(2)}, u32[]{:S(2)}) collective-permute-start(bf16[2,4,96,768]{3,2,1,0:T(8,128)(2,1)} %get-tuple-element.117), channel_id=1, source_target_pairs={{0,8},{8,16},{16,24},{24,28},{28,20},{20,12},{12,4},{4,0},{1,9},{9... | collective-permute-start | bytes 3538952 | tf_op jit(solution)/shard_map/ppermute | solution.py:769
  376.2 28.4 %collective-permute-start.21 = (bf16[2,4,96,768]{3,2,1,0:T(8,128)(2,1)}, bf16[2,4,96,768]{3,2,1,0:T(8,128)(2,1)}, u32[]{:S(2)}, u32[]{:S(2)}) collective-permute-start(bf16[2,4,96,768]{3,2,1,0:T(8,128)(2,1)} %get-tuple-element.118), channel_id=1, source_target_pairs={{0,4},{8,0},{16,8},{24,16},{28,24},{20,28},{12,20},{4,12},{1,5},{9... | collective-permute-start | bytes 3538952 | tf_op jit(solution)/shard_map/ppermute | solution.py:769
  408.9 8.0 %copy-start.33 = (f32[4,1,768]{2,1,0:T(1,128)S(1)}, f32[4,1,768]{2,1,0:T(1,128)}, u32[]{:S(2)}) copy-start(f32[4,1,768]{2,1,0:T(1,128)} %get-tuple-element.134) | copy-start | bytes 36868
  408.9 8.0 %copy-start.32 = (f32[4,1,768]{2,1,0:T(1,128)S(1)}, f32[4,1,768]{2,1,0:T(1,128)}, u32[]{:S(2)}) copy-start(f32[4,1,768]{2,1,0:T(1,128)} %get-tuple-element.133) | copy-start | bytes 36868
  408.9 8.7 %copy-start.29 = (f32[8,768]{1,0:T(8,128)S(1)}, f32[8,768]{1,0:T(8,128)}, u32[]{:S(2)}) copy-start(f32[8,768]{1,0:T(8,128)} %get-tuple-element.130) | copy-start | bytes 73732
  409.0 11.0 %copy-start.36 = (f32[2,768]{1,0:T(2,128)S(1)}, f32[2,768]{1,0:T(2,128)}, u32[]{:S(2)}) copy-start(f32[2,768]{1,0:T(2,128)} %get-tuple-element.129) | copy-start | bytes 18436
  409.0 11.1 %copy-start.35 = (f32[3,768]{1,0:T(4,128)S(1)}, f32[3,768]{1,0:T(4,128)}, u32[]{:S(2)}) copy-start(f32[3,768]{1,0:T(4,128)} %get-tuple-element.128) | copy-start | bytes 27652
  409.0 11.1 %copy-start.37 = (f32[2,192]{1,0:T(2,128)S(1)}, f32[2,192]{1,0:T(2,128)}, u32[]{:S(2)}) copy-start(f32[2,192]{1,0:T(2,128)} %get-tuple-element.132) | copy-start | bytes 4612
  409.0 12.7 %copy-start = (bf16[6,208,768]{2,1,0:T(8,128)(2,1)S(1)}, bf16[6,208,768]{2,1,0:T(8,128)(2,1)}, u32[]{:S(2)}) copy-start(bf16[6,208,768]{2,1,0:T(8,128)(2,1)} %add_convert_fusion.1.refs_6_) | copy-start | bytes 5750788
  415.7 12.6 %collective-permute-start.23 = (bf16[6,208,768]{2,1,0:T(8,128)(2,1)}, bf16[6,208,768]{2,1,0:T(8,128)(2,1)}, u32[]{:S(2)}, u32[]{:S(2)}) collective-permute-start(bf16[6,208,768]{2,1,0:T(8,128)(2,1)} %finish.1), channel_id=1, source_target_pairs={{0,1},{1,0},{2,3},{3,2},{4,5},{5,4},{6,7},{7,6},{8,9},{9,8},{10,11... | collective-permute-start | bytes 5750792 | tf_op jit(solution)/shard_map/ppermute | solution.py:744
  417.7 29.0 %collective-permute-start.27 = (bf16[2,4,96,768]{3,2,1,0:T(8,128)(2,1)}, bf16[2,4,96,768]{3,2,1,0:T(8,128)(2,1)S(1)}, u32[]{:S(2)}, u32[]{:S(2)}) collective-permute-start(bf16[2,4,96,768]{3,2,1,0:T(8,128)(2,1)} %get-tuple-element.121.refs_5_), channel_id=1, source_target_pairs={{0,8},{8,16},{16,24},{24,28},{28,20},{20,12},{12,4},{4,0},{1,9},{9... | collective-permute-start | bytes 3538952 | tf_op jit(solution)/shard_map/ppermute | solution.py:769
  418.9 28.6 %collective-permute-start.28 = (bf16[2,4,96,768]{3,2,1,0:T(8,128)(2,1)}, bf16[2,4,96,768]{3,2,1,0:T(8,128)(2,1)}, u32[]{:S(2)}, u32[]{:S(2)}) collective-permute-start(bf16[2,4,96,768]{3,2,1,0:T(8,128)(2,1)} %get-tuple-element.122.refs_6_), channel_id=1, source_target_pairs={{0,4},{8,0},{16,8},{24,16},{28,24},{20,28},{12,20},{4,12},{1,5},{9... | collective-permute-start | bytes 3538952 | tf_op jit(solution)/shard_map/ppermute | solution.py:769
  420.0 89.7 %collective-permute-start.26 = (f32[6,208,768]{2,1,0:T(8,128)}, f32[6,208,768]{2,1,0:T(8,128)}, u32[]{:S(2)}, u32[]{:S(2)}) collective-permute-start(f32[6,208,768]{2,1,0:T(8,128)} %get-tuple-element.123.own_grad_ref), channel_id=1, source_target_pairs={{0,1},{1,0},{2,3},{3,2},{4,5},{5,4},{6,7},{7,6},{8,9},{9,8},{10,11... | collective-permute-start | bytes 11501576 | tf_op jit(solution)/shard_map/ppermute | solution.py:744
  421.6 44.3 %collective-permute-start.24 = (bf16[6,208,768]{2,1,0:T(8,128)(2,1)S(1)}, bf16[6,208,768]{2,1,0:T(8,128)(2,1)}, u32[]{:S(2)}, u32[]{:S(2)}) collective-permute-start(bf16[6,208,768]{2,1,0:T(8,128)(2,1)S(1)} %copy-done), channel_id=1, source_target_pairs={{0,2},{1,3},{2,0},{3,1},{4,6},{5,7},{6,4},{7,5},{8,10},{9,11},{10,... | collective-permute-start | bytes 5750792 | tf_op jit(solution)/shard_map/ppermute | solution.py:748
  428.3 35.4 %collective-permute-start.36 = (bf16[4,2,2,1,96,192]{5,4,0,3,2,1:T(8,128)(2,1)}, bf16[4,2,2,1,96,192]{5,4,0,3,2,1:T(8,128)(2,1)}, u32[]{:S(2)}, u32[]{:S(2)}) collective-permute-start(bf16[4,2,2,1,96,192]{5,4,0,3,2,1:T(8,128)(2,1)} %copy.127), channel_id=1, source_target_pairs={{0,4},{4,0},{8,12},{12,8},{16,20},{20,16},{24,28},{28,24},{1,5},{5... | collective-permute-start | bytes 1769480 | tf_op jit(solution)/shard_map/ppermute | solution.py:963
  437.0 26.7 %copy-start.3 = (f32[4,768,192]{2,1,0:T(8,128)S(1)}, f32[4,768,192]{2,1,0:T(8,128)}, u32[]{:S(2)}) copy-start(f32[4,768,192]{2,1,0:T(8,128)} %copy-done.2) | copy-start | bytes 7077892
  446.7 18.8 %collective-permute-start.31 = (f32[31,768]{1,0:T(8,128)S(1)}, f32[31,768]{1,0:T(8,128)S(1)}, u32[]{:S(2)}, u32[]{:S(2)}) collective-permute-start(f32[31,768]{1,0:T(8,128)S(1)} %broadcast_add_fusion), channel_id=1, source_target_pairs={{0,4},{4,0},{8,12},{12,8},{16,20},{20,16},{24,28},{28,24},{1,5},{5... | collective-permute-start | bytes 285704 | tf_op jit(solution)/shard_map/ppermute | solution.py:995
  452.1 26.5 %collective-permute-start.30 = (bf16[1,4,96,768]{3,2,1,0:T(8,128)(2,1)}, bf16[1,4,96,768]{3,2,1,0:T(8,128)(2,1)}, u32[]{:S(2)}, u32[]{:S(2)}) collective-permute-start(bf16[1,4,96,768]{3,2,1,0:T(8,128)(2,1)} %get-tuple-element.125), channel_id=1, source_target_pairs={{0,4},{8,0},{16,8},{24,16},{28,24},{20,28},{12,20},{4,12},{1,5},{9... | collective-permute-start | bytes 1769480 | tf_op jit(solution)/shard_map/ppermute | solution.py:769
  463.7 14.9 %collective-permute-start.29 = (bf16[1,4,96,768]{3,2,1,0:T(8,128)(2,1)}, bf16[1,4,96,768]{3,2,1,0:T(8,128)(2,1)}, u32[]{:S(2)}, u32[]{:S(2)}) collective-permute-start(bf16[1,4,96,768]{3,2,1,0:T(8,128)(2,1)} %get-tuple-element.124), channel_id=1, source_target_pairs={{0,8},{8,16},{16,24},{24,28},{28,20},{20,12},{12,4},{4,0},{1,9},{9... | collective-permute-start | bytes 1769480 | tf_op jit(solution)/shard_map/ppermute | solution.py:769
  465.5 20.3 %collective-permute-start.37 = (bf16[4,2,1,1,96,192]{5,4,0,3,2,1:T(8,128)(2,1)S(1)}, bf16[4,2,1,1,96,192]{5,4,0,3,2,1:T(8,128)(2,1)S(1)}, u32[]{:S(2)}, u32[]{:S(2)}) collective-permute-start(bf16[4,2,1,1,96,192]{5,4,0,3,2,1:T(8,128)(2,1)S(1)} %dynamic-slice_convert_fusion), channel_id=1, source_target_pairs={{0,8},{4,12},{8,0},{12,4},{16,24},{20,28},{24,16},{28,20},{1,9},{5... | collective-permute-start | bytes 884744 | tf_op jit(solution)/shard_map/ppermute | solution.py:963
  465.9 22.8 %collective-permute-start.32 = (f32[31,768]{1,0:T(8,128)S(1)}, f32[31,768]{1,0:T(8,128)S(1)}, u32[]{:S(2)}, u32[]{:S(2)}) collective-permute-start(f32[31,768]{1,0:T(8,128)S(1)} %add_add_fusion.3), channel_id=1, source_target_pairs={{0,8},{4,12},{8,0},{12,4},{16,24},{20,28},{24,16},{28,20},{1,9},{5... | collective-permute-start | bytes 285704 | tf_op jit(solution)/shard_map/ppermute | solution.py:995
  478.6 31.1 %collective-permute-start.25 = (bf16[6,208,768]{2,1,0:T(8,128)(2,1)}, bf16[6,208,768]{2,1,0:T(8,128)(2,1)}, u32[]{:S(2)}, u32[]{:S(2)}) collective-permute-start(bf16[6,208,768]{2,1,0:T(8,128)(2,1)} %add_convert_fusion.own_ref), channel_id=1, source_target_pairs={{0,1},{1,0},{2,3},{3,2},{4,5},{5,4},{6,7},{7,6},{8,9},{9,8},{10,11... | collective-permute-start | bytes 5750792 | tf_op jit(solution)/shard_map/ppermute | solution.py:744
  485.9 17.0 %collective-permute-start.38 = (bf16[4,1,1,1,96,192]{5,4,0,3,2,1:T(8,128)(2,1)S(1)}, bf16[4,1,1,1,96,192]{5,4,0,3,2,1:T(8,128)(2,1)S(1)}, u32[]{:S(2)}, u32[]{:S(2)}) collective-permute-start(bf16[4,1,1,1,96,192]{5,4,0,3,2,1:T(8,128)(2,1)S(1)} %dynamic-slice_convert_fusion.1), channel_id=1, source_target_pairs={{0,16},{4,20},{8,24},{12,28},{16,0},{20,4},{24,8},{28,12},{1,17},{... | collective-permute-start | bytes 442376 | tf_op jit(solution)/shard_map/ppermute | solution.py:963
  488.7 12.3 %collective-permute-start.33 = (f32[31,768]{1,0:T(8,128)S(1)}, f32[31,768]{1,0:T(8,128)S(1)}, u32[]{:S(2)}, u32[]{:S(2)}) collective-permute-start(f32[31,768]{1,0:T(8,128)S(1)} %add_add_fusion.2), channel_id=1, source_target_pairs={{0,16},{4,20},{8,24},{12,28},{16,0},{20,4},{24,8},{28,12},{1,17},{... | collective-permute-start | bytes 285704 | tf_op jit(solution)/shard_map/ppermute | solution.py:995
  502.3 1.4 collective-permute-start.34
  503.7 4.7 collective-permute-start.35
  (37 other events, 143.1 us)
